TPU v7x, 32 devices: a whole 2x2x4 slice. The times are simulated.
32 devices in a mesh: dp: 16 (over z, y, x), copy: 2 (over core).
Axes of the slice: x: 2, y: 2, z: 4, core: 2. Of those that a mesh axis runs over, the one named last changes fastest.
Arguments:
- patches: bfloat16 [16, 1024, 64], P('dp'), may hold values from -6 to 6
- noise_copies: bfloat16 [2, 16, 1024, 64], P('copy', 'dp'), may hold values from -6 to 6
- image_ids: int32 [16, 1024], P('dp'), may hold values from 0 to 2, never falling along the last dimension, each value on 1 to 512 neighbouring positions
- buffer_flags: int32 [16, 1024], P('dp'), may hold values 0 or 1
- loss_mask: int32 [16, 1024], P('dp'), may hold values 0 or 1
- timesteps: int32 [2, 16, 1024], P('copy', 'dp'), may hold values from 0 to 999
- attend_weight: float32 [8, 768, 768], P(None, ('dp', 'copy'))
- attend_velocity: float32 [8, 768, 768], P(None, ('dp', 'copy')), may hold values from -1.1920929e-06 to 1.1920929e-06
- expand_weight: float32 [4, 3072, 768], P(None, ('dp', 'copy')), may hold values from -0.21875 to 0.21875
- expand_velocity: float32 [4, 3072, 768], P(None, ('dp', 'copy')), may hold values from -1.1920929e-06 to 1.1920929e-06
- dense_weight: float32 [2, 1024, 1024], P(None, ('dp', 'copy')), may hold values from -0.1875 to 0.1875
- dense_velocity: float32 [2, 1024, 1024], P(None, ('dp', 'copy')), may hold values from -1.1920929e-06 to 1.1920929e-06
- modulate_weight: float32 [5120, 1024], P(('dp', 'copy')), may hold values from -0.1875 to 0.1875
- modulate_velocity: float32 [5120, 1024], P(('dp', 'copy')), may hold values from -1.1920929e-06 to 1.1920929e-06
- condition_weight: float32 [1024, 768], P(('dp', 'copy')), may hold values from -0.21875 to 0.21875
- condition_velocity: float32 [1024, 768], P(('dp', 'copy')), may hold values from -1.1920929e-06 to 1.1920929e-06
- encoder_table: float32 [1100, 768], P(None, ('dp', 'copy'))
- encoder_first: float32 [1100, 768], P(None, ('dp', 'copy')), may hold values from -1.1920929e-07 to 1.1920929e-07
- encoder_second: float32 [1100, 768], P(None, ('dp', 'copy')), may hold values from 1.1054302e-15 to 1.7856949e-14
- head_table: float32 [384, 1024], P(None, ('dp', 'copy'))
- head_first: float32 [384, 1024], P(None, ('dp', 'copy')), may hold values from -1.1920929e-07 to 1.1920929e-07
- head_second: float32 [384, 1024], P(None, ('dp', 'copy')), may hold values from 1.1054302e-15 to 1.7856949e-14
Outputs:
- loss_sum: float32 [], replicated
- loss_count: float32 [], replicated
- clip_norm: float32 [], replicated
- attend_master: float32 [8, 768, 768], P(None, ('dp', 'copy'))
- attend_momentum: float32 [8, 768, 768], P(None, ('dp', 'copy'))
- expand_master: float32 [4, 3072, 768], P(None, ('dp', 'copy'))
- expand_momentum: float32 [4, 3072, 768], P(None, ('dp', 'copy'))
- dense_master: float32 [2, 1024, 1024], P(None, ('dp', 'copy'))
- dense_momentum: float32 [2, 1024, 1024], P(None, ('dp', 'copy'))
- modulate_master: float32 [5120, 1024], P(('dp', 'copy'))
- modulate_momentum: float32 [5120, 1024], P(('dp', 'copy'))
- condition_master: float32 [1024, 768], P(('dp', 'copy'))
- condition_momentum: float32 [1024, 768], P(('dp', 'copy'))
- encoder_master: float32 [1100, 768], P(None, ('dp', 'copy'))
- encoder_firsts: float32 [1100, 768], P(None, ('dp', 'copy'))
- encoder_seconds: float32 [1100, 768], P(None, ('dp', 'copy'))
- table_master: float32 [384, 1024], P(None, ('dp', 'copy'))
- table_firsts: float32 [384, 1024], P(None, ('dp', 'copy'))
- table_seconds: float32 [384, 1024], P(None, ('dp', 'copy'))
Inputs may be any that keep to these rules, and one draw needn't show every extreme that they name: `image_ids`: numbered from 0 along each sequence, never falling; each image has 1 to 512 tokens, one exactly that many.
All inputs are finite; a program needn't handle non-finite values. No bound on the sum of `buffer_flags` or of `loss_mask` on one device may be relied on, other than what follows from the above.
Results may differ from a plain program's by a relative error of at most 0.0023.
The roundings to bfloat16 on the way count: a program that leaves them out, or rounds other values in their place, can miss the bound.
Values may be sent and summed in bfloat16 or wider, within the bound.
No kernel may reach another device: no remote copies, remote signals or barrier semaphores. Data moves between devices by JAX's collectives and lax.ppermute only.
A program may use at most 448 MiB of HBM per device.

v0:
```python
import math

import jax
import jax.numpy as jnp
from jax import lax
from jax.sharding import PartitionSpec as P

D = 768
HEADS = 12
HD = 64
HW = 1024
PATCH = 64
FREQ = 256
SEQ = 1024
NS_STEPS = 2
STEP = 10
TSTEPS = 1000


precise_mode = lax.Precision.HIGHEST
norm_floor = 1e-06
score_factor = 0.125
newton_first = 3.4445
newton_second = -4.775
newton_third = 2.0315
muon_rate = 1.0
muon_decay = 0.01
muon_keep = 0.95
clip_bound = 0.001
adam_rate = 0.02
beta_first = 0.9
beta_second = 0.95
adam_floor = 1e-08
adam_decay = 0.1


def product(left_side, right_side):
    return jnp.dot(left_side, right_side, preferred_element_type=jnp.float32)


def product_left(left_side, right_side):
    return lax.dot_general(
        left_side, right_side, (((0,), (0,)), ((), ())), preferred_element_type=jnp.float32
    )


def product_right(left_side, right_side):
    return lax.dot_general(
        left_side, right_side, (((1,), (1,)), ((), ())), preferred_element_type=jnp.float32
    )


def to_low(values):
    return values.astype(jnp.bfloat16)


def layer_norm(values, gain_row, bias_row):
    centered = values - jnp.mean(values, axis=-1, keepdims=True)
    spread = jnp.mean(centered * centered, axis=-1, keepdims=True)
    return centered * lax.rsqrt(spread + norm_floor) * gain_row + bias_row


def plain_norm(values):
    centered = values - jnp.mean(values, axis=-1, keepdims=True)
    spread = jnp.mean(centered * centered, axis=-1, keepdims=True)
    return centered * lax.rsqrt(spread + norm_floor)


def alpha_bar(step_float):
    return jnp.cos(0.5 * math.pi * (step_float + 0.5) / TSTEPS) ** 2


def time_features(step_float):
    halfway = FREQ // 2
    frequency = jnp.exp(-math.log(10000.0) * jnp.arange(halfway).astype(jnp.float32) / halfway)
    angles = step_float[:, None] * frequency[None, :]
    return jnp.concatenate([jnp.cos(angles), jnp.sin(angles)], axis=1)


def first_modulate(lifted, modulation):
    return plain_norm(lifted) * (1.0 + modulation[:, HW : 2 * HW]) + modulation[:, :HW]


def last_modulate(lifted, modulation, branch):
    joined = lifted + modulation[:, 2 * HW : 3 * HW] * branch
    return plain_norm(joined) * (1.0 + modulation[:, 4 * HW :]) + modulation[:, 3 * HW : 4 * HW]


def attention_scores(query_heads, key_heads, same_image):
    raw_scores = jnp.einsum(
        "qhd,khd->hqk", query_heads, key_heads, preferred_element_type=jnp.float32
    )
    return jnp.where(same_image[None], raw_scores * score_factor, -1e30)


def block_forward(entered, attend_low, expand_low, gain_rows, same_image):
    halfway = entered.shape[0]
    normed, first_back = jax.vjp(layer_norm, entered, gain_rows[0], gain_rows[1])
    normed_low = to_low(normed)
    query_low = to_low(product(normed_low, attend_low[0]))
    key_low = to_low(product(normed_low, attend_low[1]))
    value_low = to_low(product(normed_low, attend_low[2]))
    key_all, value_all = (
        lax.all_gather(key_low, "copy", axis=0, tiled=True),
        lax.all_gather(value_low, "copy", axis=0, tiled=True),
    )
    query_heads = query_low.reshape(halfway, HEADS, HD)
    key_heads = key_all.reshape(SEQ, HEADS, HD)
    value_heads = value_all.reshape(SEQ, HEADS, HD)
    scores = attention_scores(query_heads, key_heads, same_image)
    highest = jnp.max(scores, axis=-1, keepdims=True)
    exponent_rows = jnp.exp(scores - highest)
    row_total = jnp.sum(exponent_rows, axis=-1, keepdims=True)
    log_total = highest + jnp.log(row_total)
    attended = to_low(
        jnp.einsum(
            "hqk,khd->qhd",
            to_low(exponent_rows / row_total),
            value_heads,
            preferred_element_type=jnp.float32,
        ).reshape(halfway, D)
    )
    middle = entered + product(attended, attend_low[3])
    normed_two, second_back = jax.vjp(layer_norm, middle, gain_rows[2], gain_rows[3])
    normed_two_low = to_low(normed_two)
    hidden, gelu_back = jax.vjp(jax.nn.gelu, product_right(normed_two_low, expand_low[0]))
    hidden_low = to_low(hidden)
    output_rows = middle + product(hidden_low, expand_low[1])
    kept = (
        first_back,
        normed_low,
        query_heads,
        key_heads,
        value_heads,
        log_total,
        attended,
        second_back,
        normed_two_low,
        gelu_back,
        hidden_low,
    )
    return (output_rows, kept)


def block_backward(output_grad, kept, attend_low, expand_low, same_image):
    (
        first_back,
        normed_low,
        query_heads,
        key_heads,
        value_heads,
        log_total,
        attended,
        second_back,
        normed_two_low,
        gelu_back,
        hidden_low,
    ) = kept
    halfway = attended.shape[0]
    upper_low = to_low(output_grad)
    upper_delta = product_left(hidden_low, upper_low)
    (hidden_grad,) = gelu_back(product_right(upper_low, expand_low[1]))
    hidden_grad_low = to_low(hidden_grad)
    lower_delta = product_left(hidden_grad_low, normed_two_low)
    middle_extra, gain_three, gain_four = second_back(product(hidden_grad_low, expand_low[0]))
    middle_grad = output_grad + middle_extra
    projected_low = to_low(middle_grad)
    output_delta = product_left(attended, projected_low)
    attended_grad = to_low(product_right(projected_low, attend_low[3])).reshape(halfway, HEADS, HD)
    probability = jnp.exp(attention_scores(query_heads, key_heads, same_image) - log_total)
    soft_grad = jnp.einsum(
        "qhd,khd->hqk", attended_grad, value_heads, preferred_element_type=jnp.float32
    )
    value_part = jnp.einsum(
        "hqk,qhd->khd", to_low(probability), attended_grad, preferred_element_type=jnp.float32
    )
    score_low = to_low(
        probability
        * (soft_grad - jnp.sum(probability * soft_grad, axis=-1, keepdims=True))
        * score_factor
    )
    query_grad = to_low(
        jnp.einsum(
            "hqk,khd->qhd", score_low, key_heads, preferred_element_type=jnp.float32
        ).reshape(halfway, D)
    )
    key_part = jnp.einsum(
        "hqk,qhd->khd", score_low, query_heads, preferred_element_type=jnp.float32
    )
    key_sum, value_sum = (
        lax.psum_scatter(
            key_part.reshape(SEQ, D).astype(jnp.bfloat16), "copy", scatter_dimension=0, tiled=True
        ).astype(jnp.float32),
        lax.psum_scatter(
            value_part.reshape(SEQ, D).astype(jnp.bfloat16), "copy", scatter_dimension=0, tiled=True
        ).astype(jnp.float32),
    )
    key_grad = to_low(key_sum)
    value_grad = to_low(value_sum)
    normed_grad = (
        product_right(query_grad, attend_low[0])
        + product_right(key_grad, attend_low[1])
        + product_right(value_grad, attend_low[2])
    )
    entered_extra, gain_one, gain_two = first_back(normed_grad)
    attend_delta = jnp.stack(
        [
            product_left(normed_low, query_grad),
            product_left(normed_low, key_grad),
            product_left(normed_low, value_grad),
            output_delta,
        ]
    )
    expand_delta = jnp.stack([lower_delta, upper_delta])
    gain_delta = jnp.stack([gain_one, gain_two, gain_three, gain_four])
    return (middle_grad + entered_extra, attend_delta, expand_delta, gain_delta)


def local_gram(member):
    return jnp.einsum("krn,krm->knm", member, member, precision=precise_mode)


def newton_update(member, gram_matrix):
    once = jnp.einsum("krn,knm->krm", member, gram_matrix, precision=precise_mode)
    twice = jnp.einsum("krn,knm->krm", once, gram_matrix, precision=precise_mode)
    return newton_first * member + newton_second * once + newton_third * twice


def scale_first(current, whole):
    inverse = tuple(
        (
            (1.0 / (jnp.sqrt(jnp.einsum("knn->k", member)) + 1e-07))[:, None, None]
            for member in whole
        )
    )
    current = tuple((current[i] * inverse[i] for i in range(5)))
    whole = tuple((whole[i] * inverse[i] * inverse[i] for i in range(5)))
    return (current, whole)


def adam_shard(master, first, second, gradient):
    first_new = beta_first * first + (1.0 - beta_first) * gradient
    second_new = beta_second * second + (1.0 - beta_second) * gradient * gradient
    corrected_first = first_new / (1.0 - beta_first**STEP)
    corrected_second = second_new / (1.0 - beta_second**STEP)
    master_new = master - adam_rate * (
        corrected_first / (jnp.sqrt(corrected_second) + adam_floor) + adam_decay * master
    )
    return (master_new, first_new, second_new)


def per_device(
    patches,
    noise_copies,
    image_ids,
    buffer_flags,
    loss_mask,
    timesteps,
    attend_weight,
    attend_velocity,
    expand_weight,
    expand_velocity,
    dense_weight,
    dense_velocity,
    modulate_weight,
    modulate_velocity,
    condition_weight,
    condition_velocity,
    encoder_table,
    encoder_first,
    encoder_second,
    head_table,
    head_first,
    head_second,
):
    attend_all, expand_all, dense_all, modulate_all, condition_all, encoder_all, head_all = (
        lax.all_gather(to_low(attend_weight), ("dp", "copy"), axis=1, tiled=True),
        lax.all_gather(to_low(expand_weight), ("dp", "copy"), axis=1, tiled=True),
        lax.all_gather(to_low(dense_weight), ("dp", "copy"), axis=1, tiled=True),
        lax.all_gather(to_low(modulate_weight), ("dp", "copy"), axis=0, tiled=True),
        lax.all_gather(to_low(condition_weight), ("dp", "copy"), axis=0, tiled=True),
        lax.all_gather(to_low(encoder_table), ("dp", "copy"), axis=1, tiled=True),
        lax.all_gather(to_low(head_table), ("dp", "copy"), axis=1, tiled=True),
    )
    halfway = SEQ // lax.axis_size("copy")
    offset = lax.axis_index("copy") * halfway
    patch_seq = patches[0]
    weight_row = (loss_mask[0] * (1 - buffer_flags[0])).astype(jnp.float32)
    token_count = lax.psum(jnp.sum(weight_row), ("dp", "copy"))
    own_patch = lax.dynamic_slice_in_dim(patch_seq, offset, halfway, 0)
    own_image = lax.dynamic_slice_in_dim(image_ids[0], offset, halfway, 0)
    buffer_on = lax.dynamic_slice_in_dim(buffer_flags[0], offset, halfway, 0)[:, None] > 0
    masked_on = lax.dynamic_slice_in_dim(loss_mask[0], offset, halfway, 0)[:, None] > 0
    same_image = own_image[:, None] == image_ids[0][None, :]
    gain_rows = encoder_all[:12].astype(jnp.float32)
    position = lax.dynamic_slice_in_dim(encoder_all, 12 + PATCH + offset, halfway, 0).astype(
        jnp.float32
    )
    embedded = product(own_patch, encoder_all[12 : 12 + PATCH])

    def entry(embedded_rows, token_pair, position_rows):
        return (
            jnp.where(buffer_on, token_pair[1], jnp.where(masked_on, token_pair[0], embedded_rows))
            + position_rows
        )

    entered, entry_back = jax.vjp(entry, embedded, gain_rows[10:12], position)
    state_rows = entered
    kept_all = []
    for depth_index in range(2):
        state_rows, kept = block_forward(
            state_rows,
            attend_all[4 * depth_index : 4 * depth_index + 4],
            expand_all[2 * depth_index : 2 * depth_index + 2],
            gain_rows[4 * depth_index : 4 * depth_index + 4],
            same_image,
        )
        kept_all.append(kept)
    latent, third_back = jax.vjp(layer_norm, state_rows, gain_rows[8], gain_rows[9])
    latent_low = to_low(latent)
    condition_rows = lax.all_gather(
        to_low(product_right(latent_low, condition_all)), "copy", axis=0, tiled=True
    )
    step_float = timesteps[0, 0].astype(jnp.float32)
    alpha_row = alpha_bar(step_float)[:, None]
    target = noise_copies[0, 0].astype(jnp.float32)
    noisy_low = to_low(
        jnp.sqrt(alpha_row) * patch_seq.astype(jnp.float32) + jnp.sqrt(1.0 - alpha_row) * target
    )
    lifted = product(noisy_low, head_all[:PATCH])
    feature_low = to_low(time_features(step_float))
    summed = condition_rows.astype(jnp.float32) + product(
        feature_low, head_all[PATCH : PATCH + FREQ]
    )
    activated, silu_back = jax.vjp(jax.nn.silu, summed)
    activated_low = to_low(activated)
    modulation = product_right(activated_low, modulate_all)
    inner_rows, inner_back = jax.vjp(first_modulate, lifted, modulation)
    inner_low = to_low(inner_rows)
    expanded, dense_back = jax.vjp(jax.nn.gelu, product(inner_low, dense_all[0]))
    expanded_low = to_low(expanded)
    branch = product(expanded_low, dense_all[1])
    outer_rows, outer_back = jax.vjp(last_modulate, lifted, modulation, branch)
    outer_low = to_low(outer_rows)
    predicted = product_right(outer_low, head_all[PATCH + FREQ :])
    residue = predicted - target
    loss_local = jnp.sum(weight_row[:, None] * residue * residue) / PATCH
    predicted_grad = to_low(2.0 * weight_row[:, None] * residue / (PATCH * token_count))
    final_delta = product_left(predicted_grad, outer_low)
    lifted_grad, modulation_grad, branch_grad = outer_back(
        product(predicted_grad, head_all[PATCH + FREQ :])
    )
    branch_low = to_low(branch_grad)
    second_delta = product_left(expanded_low, branch_low)
    (expanded_grad,) = dense_back(product_right(branch_low, dense_all[1]))
    expanded_grad_low = to_low(expanded_grad)
    first_delta = product_left(inner_low, expanded_grad_low)
    lifted_extra, modulation_extra = inner_back(product_right(expanded_grad_low, dense_all[0]))
    modulation_low = to_low(modulation_grad + modulation_extra)
    modulate_delta = product_left(modulation_low, activated_low)
    (summed_grad,) = silu_back(product(modulation_low, modulate_all))
    time_delta = product_left(feature_low, to_low(summed_grad))
    lift_delta = product_left(noisy_low, to_low(lifted_grad + lifted_extra))
    condition_grad = to_low(
        lax.psum_scatter(
            summed_grad.astype(jnp.bfloat16), "copy", scatter_dimension=0, tiled=True
        ).astype(jnp.float32)
    )
    condition_delta = product_left(condition_grad, latent_low)
    state_grad, gain_nine, gain_ten = third_back(product(condition_grad, condition_all))
    attend_parts = [None, None]
    expand_parts = [None, None]
    gain_parts = [None, None]
    for depth_index in (1, 0):
        (
            state_grad,
            attend_parts[depth_index],
            expand_parts[depth_index],
            gain_parts[depth_index],
        ) = block_backward(
            state_grad,
            kept_all[depth_index],
            attend_all[4 * depth_index : 4 * depth_index + 4],
            expand_all[2 * depth_index : 2 * depth_index + 2],
            same_image,
        )
    embedded_grad, token_grad, position_grad = entry_back(state_grad)
    embed_delta = product_left(own_patch, to_low(embedded_grad))
    gain_delta = jnp.concatenate(
        [gain_parts[0], gain_parts[1], jnp.stack([gain_nine, gain_ten]), token_grad], axis=0
    )
    position_full = lax.dynamic_update_slice_in_dim(
        jnp.zeros((SEQ, D), jnp.float32), position_grad, offset, 0
    )
    encoder_delta = jnp.concatenate([gain_delta, embed_delta, position_full], axis=0)
    head_delta = jnp.concatenate([lift_delta, time_delta, final_delta], axis=0)
    attend_delta = jnp.concatenate([attend_parts[0], attend_parts[1]], axis=0)
    expand_delta = jnp.concatenate([expand_parts[0], expand_parts[1]], axis=0)
    dense_delta = jnp.stack([first_delta, second_delta])
    reduced = (
        lax.psum_scatter(attend_delta, ("dp", "copy"), scatter_dimension=1, tiled=True),
        lax.psum_scatter(expand_delta, ("dp", "copy"), scatter_dimension=1, tiled=True),
        lax.psum_scatter(dense_delta, ("dp", "copy"), scatter_dimension=1, tiled=True),
        lax.psum_scatter(modulate_delta, ("dp", "copy"), scatter_dimension=0, tiled=True),
        lax.psum_scatter(condition_delta, ("dp", "copy"), scatter_dimension=0, tiled=True),
        lax.psum_scatter(encoder_delta, ("dp", "copy"), scatter_dimension=1, tiled=True),
        lax.psum_scatter(head_delta, ("dp", "copy"), scatter_dimension=1, tiled=True),
    )
    squares = sum((jnp.sum(member * member) for member in reduced))
    square_total, loss_sum = lax.psum((squares, loss_local), ("dp", "copy"))
    clip_norm = jnp.sqrt(square_total)
    factor = jnp.minimum(1.0, clip_bound / (clip_norm + 1e-06))
    velocities = (
        attend_velocity,
        expand_velocity,
        dense_velocity,
        modulate_velocity,
        condition_velocity,
    )
    moments = tuple((muon_keep * velocities[i] + factor * reduced[i] for i in range(5)))
    current = (moments[0], moments[1], moments[2], moments[3][None], moments[4][None])
    for sweep_index in range(NS_STEPS):
        grams = tuple((local_gram(member) for member in current))
        parts = (
            lax.psum_scatter(grams[0], ("dp", "copy"), scatter_dimension=1, tiled=True),
            lax.psum_scatter(grams[1], ("dp", "copy"), scatter_dimension=1, tiled=True),
            lax.psum_scatter(grams[2], ("dp", "copy"), scatter_dimension=1, tiled=True),
            lax.psum_scatter(grams[3], ("dp", "copy"), scatter_dimension=1, tiled=True),
            lax.psum_scatter(grams[4], ("dp", "copy"), scatter_dimension=1, tiled=True),
        )
        whole = (
            lax.all_gather(
                parts[0].astype(jnp.bfloat16), ("dp", "copy"), axis=1, tiled=True
            ).astype(jnp.float32),
            lax.all_gather(
                parts[1].astype(jnp.bfloat16), ("dp", "copy"), axis=1, tiled=True
            ).astype(jnp.float32),
            lax.all_gather(
                parts[2].astype(jnp.bfloat16), ("dp", "copy"), axis=1, tiled=True
            ).astype(jnp.float32),
            lax.all_gather(
                parts[3].astype(jnp.bfloat16), ("dp", "copy"), axis=1, tiled=True
            ).astype(jnp.float32),
            lax.all_gather(
                parts[4].astype(jnp.bfloat16), ("dp", "copy"), axis=1, tiled=True
            ).astype(jnp.float32),
        )
        if sweep_index == 0:
            current, whole = scale_first(current, whole)
        current = tuple((newton_update(current[i], whole[i]) for i in range(5)))
    devices = lax.axis_size(("dp", "copy"))
    masters = (
        attend_weight,
        expand_weight,
        dense_weight,
        modulate_weight[None],
        condition_weight[None],
    )
    updated = tuple(
        (
            masters[i] * (1.0 - muon_rate * muon_decay)
            - muon_rate
            * max(1.0, current[i].shape[1] * devices / current[i].shape[2]) ** 0.5
            * current[i]
            for i in range(5)
        )
    )
    encoder_master, encoder_firsts, encoder_seconds = adam_shard(
        encoder_table, encoder_first, encoder_second, factor * reduced[5]
    )
    table_master, table_firsts, table_seconds = adam_shard(
        head_table, head_first, head_second, factor * reduced[6]
    )
    return (
        loss_sum,
        token_count,
        clip_norm,
        updated[0],
        moments[0],
        updated[1],
        moments[1],
        updated[2],
        moments[2],
        updated[3][0],
        moments[3],
        updated[4][0],
        moments[4],
        encoder_master,
        encoder_firsts,
        encoder_seconds,
        table_master,
        table_firsts,
        table_seconds,
    )


def solution(mesh):
    placed = (
        P("dp", None, None),
        P("copy", "dp", None, None),
        P("dp", None),
        P("dp", None),
        P("dp", None),
        P("copy", "dp", None),
        P(None, ("dp", "copy"), None),
        P(None, ("dp", "copy"), None),
        P(None, ("dp", "copy"), None),
        P(None, ("dp", "copy"), None),
        P(None, ("dp", "copy"), None),
        P(None, ("dp", "copy"), None),
        P(("dp", "copy"), None),
        P(("dp", "copy"), None),
        P(("dp", "copy"), None),
        P(("dp", "copy"), None),
        P(None, ("dp", "copy")),
        P(None, ("dp", "copy")),
        P(None, ("dp", "copy")),
        P(None, ("dp", "copy")),
        P(None, ("dp", "copy")),
        P(None, ("dp", "copy")),
    )
    return jax.shard_map(
        per_device,
        mesh=mesh,
        in_specs=placed,
        out_specs=(
            P(),
            P(),
            P(),
            P(None, ("dp", "copy"), None),
            P(None, ("dp", "copy"), None),
            P(None, ("dp", "copy"), None),
            P(None, ("dp", "copy"), None),
            P(None, ("dp", "copy"), None),
            P(None, ("dp", "copy"), None),
            P(("dp", "copy"), None),
            P(("dp", "copy"), None),
            P(("dp", "copy"), None),
            P(("dp", "copy"), None),
            P(None, ("dp", "copy")),
            P(None, ("dp", "copy")),
            P(None, ("dp", "copy")),
            P(None, ("dp", "copy")),
            P(None, ("dp", "copy")),
            P(None, ("dp", "copy")),
        ),
        check_vma=False,
    )
```

profile of v0, /device:TPU:0, one launch (start us, length us, event | category | flops | bytes accessed | tf_op | source)
XLA Modules:
  0.0 4410.2 jit_solution(13976795343557423090)
XLA Ops:
  11.5 58.3 %all-gather.22.cloned.1.call-done = bf16[1100,768]{0,1:T(8,128)(2,1)} async-done(((bf16[1100,24]{0,1:T(8,128)(2,1)}), bf16[1100,768]{0,1:T(8,128)(2,1)}) %all-gather.22.cloned.1.call-update) | async-done | bytes 1689616 | tf_op jit(solution)/shard_map/all_gather | solution.py:282
  77.7 76.7 %all-gather.24.cloned.1.call-done = bf16[8,768,768]{2,1,0:T(8,128)(2,1)} async-done(((bf16[8,24,768]{2,1,0:T(8,128)(2,1)}), bf16[8,768,768]{2,1,0:T(8,128)(2,1)}) %all-gather.24.cloned.1.call-update) | async-done | bytes 9437200 | tf_op jit(solution)/shard_map/all_gather | solution.py:277
  220.2 87.3 %all-gather.30.cloned.1.call-done = bf16[4,3072,768]{2,1,0:T(8,128)(2,1)} async-done(((bf16[4,96,768]{2,1,0:T(8,128)(2,1)}), bf16[4,3072,768]{2,1,0:T(8,128)(2,1)}) %all-gather.30.cloned.1.call-update) | async-done | bytes 18874384 | tf_op jit(solution)/shard_map/all_gather | solution.py:278
  451.7 45.5 %all_gather.66 = bf16[384,1024]{0,1:T(8,128)(2,1)S(1)} all-gather(bf16[384,32]{0,1:T(8,128)(2,1)S(1)} %convert_element_type.349), channel_id=1, replica_groups=mesh['dp'=16,'copy'=2] {'dp','copy'}, dimensions={1}, use_global_device_ids=true | all-gather | bytes 811008 | tf_op jit(solution)/shard_map/all_gather | solution.py:283
  721.1 46.5 %fusion.118 = bf16[12,64,1024]{2,1,0:T(8,128)(2,1)} fusion(bf16[512,12,64]{0,2,1:T(8,128)(2,1)} %bitcast.348, f32[12,512,1024]{2,1,0:T(8,128)} %fusion.313, f32[12,512]{1,0:T(8,128)S(1)} %log_add_fusion, f32[12,512,1024]{2,1,0:T(8,128)} %get-tuple-element.168, pred[512,1024]{1,0:T(8,128)(4,1)S(1)} %copy-done.30), kind=kOutput, calls=%fused_computation.179 | convolution fusion | flops 875305984 | bytes 53239808 | tf_op jit(solution)/shard_map/hqk,qhd->khd/dot_general | solution.py:187
  781.1 45.6 %fusion.132 = bf16[12,64,512]{2,1,0:T(8,128)(2,1)} fusion(bf16[1024,12,64]{0,2,1:T(8,128)(2,1)} %bitcast.344, f32[12,512,1024]{2,1,0:T(8,128)} %fusion.313, f32[12,512]{1,0:T(8,128)S(1)} %log_add_fusion, f32[12,512,1024]{2,1,0:T(8,128)} %get-tuple-element.168, pred[512,1024]{1,0:T(8,128)(4,1)S(1)} %copy-done.30), kind=kOutput, calls=%fused_computation.222 | convolution fusion | flops 874912768 | bytes 53239808 | tf_op jit(solution)/shard_map/hqk,khd->qhd/dot_general | solution.py:183
  869.0 46.3 %fusion.115 = bf16[12,64,1024]{2,1,0:T(8,128)(2,1)} fusion(bf16[512,12,64]{0,2,1:T(8,128)(2,1)} %bitcast.346, f32[12,512,1024]{2,1,0:T(8,128)} %fusion.314, f32[12,512]{1,0:T(8,128)S(1)} %log_add_fusion.1, f32[12,512,1024]{2,1,0:T(8,128)} %get-tuple-element.162, pred[512,1024]{1,0:T(8,128)(4,1)S(1)} %copy-done.31), kind=kOutput, calls=%fused_computation.178 | convolution fusion | flops 875305984 | bytes 53239808 | tf_op jit(solution)/shard_map/hqk,qhd->khd/dot_general | solution.py:187
  950.9 45.0 %fusion.129 = bf16[12,64,512]{2,1,0:T(8,128)(2,1)} fusion(bf16[1024,12,64]{0,2,1:T(8,128)(2,1)S(1)} %bitcast.342, f32[12,512,1024]{2,1,0:T(8,128)} %fusion.314, f32[12,512]{1,0:T(8,128)S(1)} %log_add_fusion.1, f32[12,512,1024]{2,1,0:T(8,128)} %get-tuple-element.162, pred[512,1024]{1,0:T(8,128)(4,1)S(1)} %copy-done.31), kind=kOutput, calls=%fused_computation.221 | convolution fusion | flops 874912768 | bytes 53239808 | tf_op jit(solution)/shard_map/hqk,khd->qhd/dot_general | solution.py:183
  1152.0 106.9 %reduce-scatter.69.cloned.1.call-done = f32[1100,24]{0,1:T(8,128)} async-done(((f32[1100,768]{0,1:T(8,128)}), f32[1100,24]{0,1:T(8,128)}) %reduce-scatter.69.cloned.1.call-update) | async-done | bytes 105616
  1260.4 148.8 %reduce-scatter.41.cloned.1.call-done = f32[2,32,1024]{2,1,0:T(8,128)} async-done(((f32[2,1024,1024]{2,1,0:T(8,128)}), f32[2,32,1024]{2,1,0:T(8,128)}) %reduce-scatter.41.cloned.1.call-update) | async-done | bytes 262160 | tf_op jit(solution)/shard_map/reduce_scatter | solution.py:403
  1410.8 206.9 %reduce-scatter.37.cloned.1.call-done = f32[8,24,768]{2,1,0:T(8,128)} async-done(((f32[8,768,768]{2,1,0:T(8,128)}), f32[8,24,768]{2,1,0:T(8,128)}) %reduce-scatter.37.cloned.1.call-update) | async-done | bytes 589840 | tf_op jit(solution)/shard_map/reduce_scatter | solution.py:401
  1619.5 224.8 %reduce-scatter.43.cloned.1.call-done = f32[160,1024]{1,0:T(8,128)} async-done(((f32[5120,1024]{1,0:T(8,128)}), f32[160,1024]{1,0:T(8,128)}) %reduce-scatter.43.cloned.1.call-update) | async-done | bytes 655376 | tf_op jit(solution)/shard_map/reduce_scatter | solution.py:404
  1846.2 357.1 %reduce-scatter.39.cloned.1.call-done = f32[4,96,768]{2,1,0:T(8,128)} async-done(((f32[4,3072,768]{2,1,0:T(8,128)}), f32[4,96,768]{2,1,0:T(8,128)}) %reduce-scatter.39.cloned.1.call-update) | async-done | bytes 1179664 | tf_op jit(solution)/shard_map/reduce_scatter | solution.py:402
  2302.4 51.4 %reduce-scatter.63.cloned.1.call-done = f32[1,24,768]{2,1,0:T(8,128)} async-done(((f32[1,768,768]{2,1,0:T(8,128)}), f32[1,24,768]{2,1,0:T(8,128)}) %reduce-scatter.63.cloned.1.call-update) | async-done | bytes 73744 | tf_op jit(solution)/shard_map/reduce_scatter | solution.py:429
  2355.4 140.7 %reduce-scatter.59.cloned.1.call-done = f32[1,32,1024]{2,1,0:T(8,128)} async-done(((f32[1,1024,1024]{2,1,0:T(8,128)}), f32[1,32,1024]{2,1,0:T(8,128)}) %reduce-scatter.59.cloned.1.call-update) | async-done | bytes 131088 | tf_op jit(solution)/shard_map/reduce_scatter | solution.py:428
  2497.7 136.7 %reduce-scatter.51.cloned.1.call-done = f32[4,24,768]{2,1,0:T(8,128)} async-done(((f32[4,768,768]{2,1,0:T(8,128)}), f32[4,24,768]{2,1,0:T(8,128)}) %reduce-scatter.51.cloned.1.call-update) | async-done | bytes 294928 | tf_op jit(solution)/shard_map/reduce_scatter | solution.py:426
  2636.1 148.1 %reduce-scatter.55.cloned.1.call-done = f32[2,32,1024]{2,1,0:T(8,128)} async-done(((f32[2,1024,1024]{2,1,0:T(8,128)}), f32[2,32,1024]{2,1,0:T(8,128)}) %reduce-scatter.55.cloned.1.call-update) | async-done | bytes 262160 | tf_op jit(solution)/shard_map/reduce_scatter | solution.py:427
  2786.0 205.6 %reduce-scatter.47.cloned.1.call-done = f32[8,24,768]{2,1,0:T(8,128)} async-done(((f32[8,768,768]{2,1,0:T(8,128)}), f32[8,24,768]{2,1,0:T(8,128)}) %reduce-scatter.47.cloned.1.call-update) | async-done | bytes 589840 | tf_op jit(solution)/shard_map/reduce_scatter | solution.py:425
  2993.6 54.3 %all-gather.60.cloned.1.call-done = bf16[1,768,768]{2,1,0:T(8,128)(2,1)} async-done(((bf16[1,24,768]{2,1,0:T(8,128)(2,1)}), bf16[1,768,768]{2,1,0:T(8,128)(2,1)}) %all-gather.60.cloned.1.call-update) | async-done | bytes 1179664 | tf_op jit(solution)/shard_map/all_gather | solution.py:444
  3060.1 46.5 %all-gather.56.cloned.1.call-done = bf16[1,1024,1024]{2,1,0:T(8,128)(2,1)} async-done(((bf16[1,32,1024]{2,1,0:T(8,128)(2,1)}), bf16[1,1024,1024]{2,1,0:T(8,128)(2,1)}) %all-gather.56.cloned.1.call-update) | async-done | bytes 2097168 | tf_op jit(solution)/shard_map/all_gather | solution.py:441
  3124.5 48.2 %all-gather.48.cloned.1.call-done = bf16[4,768,768]{2,1,0:T(8,128)(2,1)} async-done(((bf16[4,24,768]{2,1,0:T(8,128)(2,1)}), bf16[4,768,768]{2,1,0:T(8,128)(2,1)}) %all-gather.48.cloned.1.call-update) | async-done | bytes 4718608 | tf_op jit(solution)/shard_map/all_gather | solution.py:435
  3261.6 59.2 %all-gather.44.cloned.1.call-done = bf16[8,768,768]{2,1,0:T(8,128)(2,1)} async-done(((bf16[8,24,768]{2,1,0:T(8,128)(2,1)}), bf16[8,768,768]{2,1,0:T(8,128)(2,1)}) %all-gather.44.cloned.1.call-update) | async-done | bytes 9437200 | tf_op jit(solution)/shard_map/all_gather | solution.py:432
  3367.8 55.8 %reduce-scatter.65.cloned.1.call-done = f32[1,24,768]{2,1,0:T(8,128)} async-done(((f32[1,768,768]{2,1,0:T(8,128)}), f32[1,24,768]{2,1,0:T(8,128)}) %reduce-scatter.65.cloned.1.call-update) | async-done | bytes 73744 | tf_op jit(solution)/shard_map/reduce_scatter | solution.py:429
  3425.2 140.7 %reduce-scatter.61.cloned.1.call-done = f32[1,32,1024]{2,1,0:T(8,128)} async-done(((f32[1,1024,1024]{2,1,0:T(8,128)}), f32[1,32,1024]{2,1,0:T(8,128)}) %reduce-scatter.61.cloned.1.call-update) | async-done | bytes 131088 | tf_op jit(solution)/shard_map/reduce_scatter | solution.py:428
  3567.6 136.6 %reduce-scatter.53.cloned.1.call-done = f32[4,24,768]{2,1,0:T(8,128)} async-done(((f32[4,768,768]{2,1,0:T(8,128)}), f32[4,24,768]{2,1,0:T(8,128)}) %reduce-scatter.53.cloned.1.call-update) | async-done | bytes 294928 | tf_op jit(solution)/shard_map/reduce_scatter | solution.py:426
  3705.8 148.3 %reduce-scatter.57.cloned.1.call-done = f32[2,32,1024]{2,1,0:T(8,128)} async-done(((f32[2,1024,1024]{2,1,0:T(8,128)}), f32[2,32,1024]{2,1,0:T(8,128)}) %reduce-scatter.57.cloned.1.call-update) | async-done | bytes 262160 | tf_op jit(solution)/shard_map/reduce_scatter | solution.py:427
  3855.9 205.6 %reduce-scatter.49.cloned.1.call-done = f32[8,24,768]{2,1,0:T(8,128)} async-done(((f32[8,768,768]{2,1,0:T(8,128)}), f32[8,24,768]{2,1,0:T(8,128)}) %reduce-scatter.49.cloned.1.call-update) | async-done | bytes 589840 | tf_op jit(solution)/shard_map/reduce_scatter | solution.py:425
  4066.6 50.6 %all-gather.62.cloned.1.call-done = bf16[1,768,768]{2,1,0:T(8,128)(2,1)} async-done(((bf16[1,24,768]{2,1,0:T(8,128)(2,1)}), bf16[1,768,768]{2,1,0:T(8,128)(2,1)}) %all-gather.62.cloned.1.call-update) | async-done | bytes 1179664 | tf_op jit(solution)/shard_map/all_gather | solution.py:444
  4121.8 54.2 %all-gather.58.cloned.1.call-done = bf16[1,1024,1024]{2,1,0:T(8,128)(2,1)} async-done(((bf16[1,32,1024]{2,1,0:T(8,128)(2,1)}), bf16[1,1024,1024]{2,1,0:T(8,128)(2,1)}) %all-gather.58.cloned.1.call-update) | async-done | bytes 2097168 | tf_op jit(solution)/shard_map/all_gather | solution.py:441
  4181.2 60.9 %all-gather.50.cloned.1.call-done = bf16[4,768,768]{2,1,0:T(8,128)(2,1)} async-done(((bf16[4,24,768]{2,1,0:T(8,128)(2,1)}), bf16[4,768,768]{2,1,0:T(8,128)(2,1)}) %all-gather.50.cloned.1.call-update) | async-done | bytes 4718608 | tf_op jit(solution)/shard_map/all_gather | solution.py:435
  4250.6 55.2 %all-gather.54.cloned.1.call-done = bf16[2,1024,1024]{2,1,0:T(8,128)(2,1)} async-done(((bf16[2,32,1024]{2,1,0:T(8,128)(2,1)}), bf16[2,1024,1024]{2,1,0:T(8,128)(2,1)}) %all-gather.54.cloned.1.call-update) | async-done | bytes 4194320 | tf_op jit(solution)/shard_map/all_gather | solution.py:438
  4313.1 76.6 %all-gather.46.cloned.1.call-done = bf16[8,768,768]{2,1,0:T(8,128)(2,1)} async-done(((bf16[8,24,768]{2,1,0:T(8,128)(2,1)}), bf16[8,768,768]{2,1,0:T(8,128)(2,1)}) %all-gather.46.cloned.1.call-update) | async-done | bytes 9437200 | tf_op jit(solution)/shard_map/all_gather | solution.py:432
  (736 shorter events, 1012.6 us)
Async XLA Ops:
  162.6 172.3 %all-gather.32.cloned.1.call-start = ((), (), s32[]{:S(2)}) async-start(), calls=%async_computation.27 | async-start | bytes 2359296 | tf_op jit(solution)/shard_map/all_gather | solution.py:105
  329.3 177.2 %all-gather.40.cloned.1.call-start = ((), (), s32[]{:S(2)}) async-start(), calls=%async_computation.31 | async-start | bytes 10813440 | tf_op jit(solution)/shard_map/all_gather | solution.py:280
  330.2 181.9 %all-gather.38.cloned.1.call-start = ((), (), s32[]{:S(2)}) async-start(), calls=%async_computation.30 | async-start | bytes 3145728 | tf_op jit(solution)/shard_map/all_gather | solution.py:321
  410.5 272.3 %reduce-scatter.27.cloned.1.call-start = ((), (), s32[]{:S(2)}) async-start(), calls=%async_computation.33 | async-start | bytes 3145728 | tf_op jit(solution)/shard_map/reduce_scatter | solution.py:365
  781.0 217.3 %reduce-scatter.33.cloned.1.call-start = ((), (), s32[]{:S(2)}) async-start(), calls=%async_computation.36 | async-start | bytes 2359296 | tf_op jit(solution)/shard_map/reduce_scatter | solution.py:191
  929.1 194.4 %reduce-scatter.67.cloned.1.call-start = ((), (), s32[]{:S(2)}) async-start(), calls=%async_computation.63 | async-start | bytes 1622016
  938.6 211.8 %reduce-scatter.45.cloned.1.call-start = ((), (), s32[]{:S(2)}) async-start(), calls=%async_computation.42 | async-start | bytes 3244032 | tf_op jit(solution)/shard_map/reduce_scatter | solution.py:405
  943.4 315.4 %reduce-scatter.69.cloned.1.call-start = ((), (), s32[]{:S(2)}) async-start(), calls=%async_computation.64 | async-start | bytes 3649536
  1022.3 386.9 %reduce-scatter.41.cloned.1.call-start = ((), (), s32[]{:S(2)}) async-start(), calls=%async_computation.40 | async-start | bytes 8650752 | tf_op jit(solution)/shard_map/reduce_scatter | solution.py:403
  1034.1 583.7 %reduce-scatter.37.cloned.1.call-start = ((), (), s32[]{:S(2)}) async-start(), calls=%async_computation.38 | async-start | bytes 19464192 | tf_op jit(solution)/shard_map/reduce_scatter | solution.py:401
  1054.3 790.0 %reduce-scatter.43.cloned.1.call-start = ((), (), s32[]{:S(2)}) async-start(), calls=%async_computation.41 | async-start | bytes 21626880 | tf_op jit(solution)/shard_map/reduce_scatter | solution.py:404
  1079.0 1124.3 %reduce-scatter.39.cloned.1.call-start = ((), (), s32[]{:S(2)}) async-start(), calls=%async_computation.39 | async-start | bytes 38928384 | tf_op jit(solution)/shard_map/reduce_scatter | solution.py:402
  1122.4 1231.4 %reduce-scatter.63.cloned.1.call-start = ((), (), s32[]{:S(2)}) async-start(), calls=%async_computation.59 | async-start | bytes 2433024 | tf_op jit(solution)/shard_map/reduce_scatter | solution.py:429
  2254.7 241.4 %reduce-scatter.59.cloned.1.call-start = ((), (), s32[]{:S(2)}) async-start(), calls=%async_computation.55 | async-start | bytes 4325376 | tf_op jit(solution)/shard_map/reduce_scatter | solution.py:428
  2260.2 374.3 %reduce-scatter.51.cloned.1.call-start = ((), (), s32[]{:S(2)}) async-start(), calls=%async_computation.47 | async-start | bytes 9732096 | tf_op jit(solution)/shard_map/reduce_scatter | solution.py:426
  2272.0 512.3 %reduce-scatter.55.cloned.1.call-start = ((), (), s32[]{:S(2)}) async-start(), calls=%async_computation.51 | async-start | bytes 8650752 | tf_op jit(solution)/shard_map/reduce_scatter | solution.py:427
  2282.1 709.4 %reduce-scatter.47.cloned.1.call-start = ((), (), s32[]{:S(2)}) async-start(), calls=%async_computation.43 | async-start | bytes 19464192 | tf_op jit(solution)/shard_map/reduce_scatter | solution.py:425
  2302.4 745.6 %all-gather.60.cloned.1.call-start = ((), (), s32[]{:S(2)}) async-start(), calls=%async_computation.60 | async-start | bytes 1216512 | tf_op jit(solution)/shard_map/all_gather | solution.py:444
  2355.4 751.2 %all-gather.56.cloned.1.call-start = ((), (), s32[]{:S(2)}) async-start(), calls=%async_computation.56 | async-start | bytes 2162688 | tf_op jit(solution)/shard_map/all_gather | solution.py:441
  2497.7 675.0 %all-gather.48.cloned.1.call-start = ((), (), s32[]{:S(2)}) async-start(), calls=%async_computation.48 | async-start | bytes 4866048 | tf_op jit(solution)/shard_map/all_gather | solution.py:435
  2636.1 600.8 %all-gather.52.cloned.1.call-start = ((), (), s32[]{:S(2)}) async-start(), calls=%async_computation.52 | async-start | bytes 4325376 | tf_op jit(solution)/shard_map/all_gather | solution.py:438
  2785.9 534.9 %all-gather.44.cloned.1.call-start = ((), (), s32[]{:S(2)}) async-start(), calls=%async_computation.44 | async-start | bytes 9732096 | tf_op jit(solution)/shard_map/all_gather | solution.py:432
  2993.4 430.3 %reduce-scatter.65.cloned.1.call-start = ((), (), s32[]{:S(2)}) async-start(), calls=%async_computation.61 | async-start | bytes 2433024 | tf_op jit(solution)/shard_map/reduce_scatter | solution.py:429
  3060.1 505.9 %reduce-scatter.61.cloned.1.call-start = ((), (), s32[]{:S(2)}) async-start(), calls=%async_computation.57 | async-start | bytes 4325376 | tf_op jit(solution)/shard_map/reduce_scatter | solution.py:428
  3123.8 580.4 %reduce-scatter.53.cloned.1.call-start = ((), (), s32[]{:S(2)}) async-start(), calls=%async_computation.49 | async-start | bytes 9732096 | tf_op jit(solution)/shard_map/reduce_scatter | solution.py:426
  3200.1 654.1 %reduce-scatter.57.cloned.1.call-start = ((), (), s32[]{:S(2)}) async-start(), calls=%async_computation.53 | async-start | bytes 8650752 | tf_op jit(solution)/shard_map/reduce_scatter | solution.py:427
  3261.6 799.9 %reduce-scatter.49.cloned.1.call-start = ((), (), s32[]{:S(2)}) async-start(), calls=%async_computation.45 | async-start | bytes 19464192 | tf_op jit(solution)/shard_map/reduce_scatter | solution.py:425
  3367.8 749.4 %all-gather.62.cloned.1.call-start = ((), (), s32[]{:S(2)}) async-start(), calls=%async_computation.62 | async-start | bytes 1216512 | tf_op jit(solution)/shard_map/all_gather | solution.py:444
  3425.1 750.8 %all-gather.58.cloned.1.call-start = ((), (), s32[]{:S(2)}) async-start(), calls=%async_computation.58 | async-start | bytes 2162688 | tf_op jit(solution)/shard_map/all_gather | solution.py:441
  3567.5 674.6 %all-gather.50.cloned.1.call-start = ((), (), s32[]{:S(2)}) async-start(), calls=%async_computation.50 | async-start | bytes 4866048 | tf_op jit(solution)/shard_map/all_gather | solution.py:435
  3705.8 599.9 %all-gather.54.cloned.1.call-start = ((), (), s32[]{:S(2)}) async-start(), calls=%async_computation.54 | async-start | bytes 4325376 | tf_op jit(solution)/shard_map/all_gather | solution.py:438
  3855.8 533.9 %all-gather.46.cloned.1.call-start = ((), (), s32[]{:S(2)}) async-start(), calls=%async_computation.46 | async-start | bytes 9732096 | tf_op jit(solution)/shard_map/all_gather | solution.py:432
  (209 other events, 13884.7 us)
Sparse Core Ops, SparseCore 0:
  11.4 58.3 all-gather.21
  73.3 80.9 all-gather.23
  181.6 125.7 all-gather.29
  349.7 56.1 all-gather.35
  409.3 90.7 all-gather.39
  515.6 63.0 all-gather.41
  945.4 98.2 reduce-scatter.66
  1049.9 100.4 reduce-scatter.44
  1156.8 102.0 reduce-scatter.68
  1261.1 148.0 reduce-scatter.40
  1416.7 200.9 reduce-scatter.36
  1620.1 224.1 reduce-scatter.42
  1851.9 351.3 reduce-scatter.38
  2254.8 99.0 reduce-scatter.62
  2356.2 139.8 reduce-scatter.58
  2502.9 131.5 reduce-scatter.50
  2636.6 147.6 reduce-scatter.54
  2790.7 200.8 reduce-scatter.46
  3051.2 55.2 all-gather.55
  3110.1 62.5 all-gather.47
  3176.1 60.7 all-gather.51
  3240.3 80.4 all-gather.43
  3326.1 97.4 reduce-scatter.64
  3426.0 139.8 reduce-scatter.60
  3572.7 131.3 reduce-scatter.52
  3706.3 147.8 reduce-scatter.56
  3860.6 200.8 reduce-scatter.48
  4064.2 52.9 all-gather.61
  4120.7 55.2 all-gather.57
  4179.5 62.5 all-gather.49
  4245.0 60.7 all-gather.53
  4309.1 80.6 all-gather.45
  (11 shorter events, 149.7 us)
where the time goes:
time: 4420 us; the launch traced here: 4410 us
  waiting for transfers between devices  3280 us (74%)
  matrix products  759 us (17%)
  other arithmetic  153 us (3%)
  blocking collectives  125 us (3%)
  local copies, waits for them, and re-layouts  64.3 us (1%)
    reduce_scatter x2, waiting for transfers between devices, per_device(): lax.psum_scatter(grams[0], ('dp', 'copy'), scatter_dimension=1, tiled=True)  411 us
    reduce_scatter x1, waiting for transfers between devices, per_device(): lax.psum_scatter(expand_delta, ('dp', 'copy'), scatter_dimension=1, tiled...  357 us
    reduce_scatter x2, waiting for transfers between devices, per_device(): lax.psum_scatter(grams[2], ('dp', 'copy'), scatter_dimension=1, tiled=True)  296 us
    reduce_scatter x2, waiting for transfers between devices, per_device(): lax.psum_scatter(grams[3], ('dp', 'copy'), scatter_dimension=1, tiled=True)  281 us
    reduce_scatter x2, waiting for transfers between devices, per_device(): lax.psum_scatter(grams[1], ('dp', 'copy'), scatter_dimension=1, tiled=True)  273 us
    reduce_scatter x1, waiting for transfers between devices, per_device(): lax.psum_scatter(modulate_delta, ('dp', 'copy'), scatter_dimension=0, til...  225 us
    reduce_scatter x1, waiting for transfers between devices, per_device(): lax.psum_scatter(attend_delta, ('dp', 'copy'), scatter_dimension=1, tiled...  207 us
    reduce_scatter x1, waiting for transfers between devices, per_device(): lax.psum_scatter(dense_delta, ('dp', 'copy'), scatter_dimension=1, tiled=...  149 us
  transfers between devices with their start and end apart: 43, of which 35 were waited for; matrix products, arithmetic and copies ran while one was open for 15% of the time, Pallas kernels for 0%

commit v1 on v0

--- a/solution.py
+++ b/solution.py
@@ -86,6 +86,102 @@
     return plain_norm(joined) * (1.0 + modulation[:, 4 * HW :]) + modulation[:, 3 * HW : 4 * HW]
 
 
+def grid_of(count):
+    side = 1
+    while 2 * side**3 < count:
+        side *= 2
+    if 2 * side**3 == count:
+        return (2 * side, side, side)
+    return (count, 1, 1)
+
+
+def place_of(index, grid):
+    return (index // (grid[1] * grid[2]), index // grid[2] % grid[1], index % grid[2])
+
+
+def index_of(place, grid):
+    return (place[0] * grid[1] + place[1]) * grid[2] + place[2]
+
+
+def shift_pairs(grid, axis, shift):
+    pairs = []
+    for source in range(grid[0] * grid[1] * grid[2]):
+        place = list(place_of(source, grid))
+        place[axis] = (place[axis] + shift) % grid[axis]
+        pairs.append((source, index_of(place, grid)))
+    return pairs
+
+
+def swap_core(values):
+    return lax.ppermute(values, "copy", [(0, 1), (1, 0)])
+
+
+def sum_all(values):
+    values = values + swap_core(values)
+    count = lax.axis_size("dp")
+    if count & (count - 1):
+        return lax.psum(values, "dp")
+    step = 1
+    while step < count:
+        values = values + lax.ppermute(values, "dp", [(i, i ^ step) for i in range(count)])
+        step *= 2
+    return values
+
+
+def scatter_axis(values, grid, axis, position, sent_type):
+    size = grid[axis]
+    mine = place_of(lax.axis_index("dp"), grid)[axis]
+    total = lax.dynamic_index_in_dim(values, mine, position, keepdims=False)
+    for shift in range(1, size):
+        sent = lax.dynamic_index_in_dim(
+            values, (mine + shift) % size, position, keepdims=False
+        ).astype(sent_type)
+        arrived = lax.ppermute(sent, "dp", shift_pairs(grid, axis, shift))
+        total = total + arrived.astype(jnp.float32)
+    return total
+
+
+def scatter_rows(values, order):
+    grid = grid_of(lax.axis_size("dp"))
+    rows, columns = values.shape
+    values = values.reshape(*grid, rows // lax.axis_size("dp"), columns)
+    left = [0, 1, 2]
+    for axis in order:
+        sent_type = jnp.float32 if axis == order[-1] else jnp.bfloat16
+        values = scatter_axis(values, grid, axis, left.index(axis), sent_type)
+        left.remove(axis)
+    return values
+
+
+def share_columns(values):
+    core = lax.axis_index("copy")
+    rows = values.shape[0] // 2
+    mine = lax.dynamic_slice_in_dim(values, core * rows, rows, 0)
+    arrived = swap_core(lax.dynamic_slice_in_dim(values, (1 - core) * rows, rows, 0))
+    first = jnp.where(core == 0, mine, arrived)
+    last = jnp.where(core == 0, arrived, mine)
+    return (first, last)
+
+
+def columns_of(values, core):
+    half = values.shape[1] // 2
+    return lax.dynamic_slice_in_dim(values, core * half, half, 1)
+
+
+def weight_grad(left_side, right_side):
+    core = lax.axis_index("copy")
+    arrived = swap_core(product_left(left_side, columns_of(right_side, 1 - core)))
+    return product_left(left_side, columns_of(right_side, core)) + arrived
+
+
+forward_order = (2, 1, 0)
+crossed_order = (1, 2, 0)
+
+
+def rows_whole(values, order):
+    return jnp.concatenate(share_columns(scatter_rows(values, order)), axis=1)
+
+
 def attention_scores(query_heads, key_heads, same_image):
     raw_scores = jnp.einsum(
         "qhd,khd->hqk", query_heads, key_heads, preferred_element_type=jnp.float32
@@ -97,13 +193,11 @@
     halfway = entered.shape[0]
     normed, first_back = jax.vjp(layer_norm, entered, gain_rows[0], gain_rows[1])
     normed_low = to_low(normed)
-    query_low = to_low(product(normed_low, attend_low[0]))
     key_low = to_low(product(normed_low, attend_low[1]))
     value_low = to_low(product(normed_low, attend_low[2]))
-    key_all, value_all = (
-        lax.all_gather(key_low, "copy", axis=0, tiled=True),
-        lax.all_gather(value_low, "copy", axis=0, tiled=True),
-    )
+    key_all = jnp.concatenate([key_low, swap_core(key_low)], axis=0)
+    value_all = jnp.concatenate([value_low, swap_core(value_low)], axis=0)
+    query_low = to_low(product(normed_low, attend_low[0]))
     query_heads = query_low.reshape(halfway, HEADS, HD)
     key_heads = key_all.reshape(SEQ, HEADS, HD)
     value_heads = value_all.reshape(SEQ, HEADS, HD)
@@ -158,14 +252,14 @@
     ) = kept
     halfway = attended.shape[0]
     upper_low = to_low(output_grad)
-    upper_delta = product_left(hidden_low, upper_low)
+    upper_delta = rows_whole(weight_grad(hidden_low, upper_low), forward_order)
     (hidden_grad,) = gelu_back(product_right(upper_low, expand_low[1]))
     hidden_grad_low = to_low(hidden_grad)
-    lower_delta = product_left(hidden_grad_low, normed_two_low)
+    lower_delta = rows_whole(weight_grad(hidden_grad_low, normed_two_low), crossed_order)
     middle_extra, gain_three, gain_four = second_back(product(hidden_grad_low, expand_low[0]))
     middle_grad = output_grad + middle_extra
     projected_low = to_low(middle_grad)
-    output_delta = product_left(attended, projected_low)
+    output_delta = rows_whole(weight_grad(attended, projected_low), forward_order)
     attended_grad = to_low(product_right(projected_low, attend_low[3])).reshape(halfway, HEADS, HD)
     probability = jnp.exp(attention_scores(query_heads, key_heads, same_image) - log_total)
     soft_grad = jnp.einsum(
@@ -179,24 +273,22 @@
         * (soft_grad - jnp.sum(probability * soft_grad, axis=-1, keepdims=True))
         * score_factor
     )
+    key_part = jnp.einsum(
+        "hqk,qhd->khd", score_low, query_heads, preferred_element_type=jnp.float32
+    )
     query_grad = to_low(
         jnp.einsum(
             "hqk,khd->qhd", score_low, key_heads, preferred_element_type=jnp.float32
         ).reshape(halfway, D)
     )
-    key_part = jnp.einsum(
-        "hqk,qhd->khd", score_low, query_heads, preferred_element_type=jnp.float32
-    )
-    key_sum, value_sum = (
-        lax.psum_scatter(
-            key_part.reshape(SEQ, D).astype(jnp.bfloat16), "copy", scatter_dimension=0, tiled=True
-        ).astype(jnp.float32),
-        lax.psum_scatter(
-            value_part.reshape(SEQ, D).astype(jnp.bfloat16), "copy", scatter_dimension=0, tiled=True
-        ).astype(jnp.float32),
-    )
-    key_grad = to_low(key_sum)
-    value_grad = to_low(value_sum)
+    key_part = key_part.reshape(SEQ, D)
+    value_part = value_part.reshape(SEQ, D)
+    value_grad = to_low(
+        value_part[:halfway] + swap_core(to_low(value_part[halfway:])).astype(jnp.float32)
+    )
+    key_grad = to_low(
+        key_part[:halfway] + swap_core(to_low(key_part[halfway:])).astype(jnp.float32)
+    )
     normed_grad = (
         product_right(query_grad, attend_low[0])
         + product_right(key_grad, attend_low[1])
@@ -205,9 +297,9 @@
     entered_extra, gain_one, gain_two = first_back(normed_grad)
     attend_delta = jnp.stack(
         [
-            product_left(normed_low, query_grad),
-            product_left(normed_low, key_grad),
-            product_left(normed_low, value_grad),
+            rows_whole(weight_grad(normed_low, query_grad), forward_order),
+            rows_whole(weight_grad(normed_low, key_grad), crossed_order),
+            rows_whole(weight_grad(normed_low, value_grad), crossed_order),
             output_delta,
         ]
     )
@@ -216,26 +308,83 @@
     return (middle_grad + entered_extra, attend_delta, expand_delta, gain_delta)
 
 
-def local_gram(member):
-    return jnp.einsum("krn,krm->knm", member, member, precision=precise_mode)
-
-
-def newton_update(member, gram_matrix):
-    once = jnp.einsum("krn,knm->krm", member, gram_matrix, precision=precise_mode)
-    twice = jnp.einsum("krn,knm->krm", once, gram_matrix, precision=precise_mode)
-    return newton_first * member + newton_second * once + newton_third * twice
-
-
-def scale_first(current, whole):
-    inverse = tuple(
-        (
-            (1.0 / (jnp.sqrt(jnp.einsum("knn->k", member)) + 1e-07))[:, None, None]
-            for member in whole
+def fine(left_side, right_side):
+    return jnp.dot(
+        left_side, right_side, precision=lax.Precision.HIGH, preferred_element_type=jnp.float32
+    )
+
+
+def newton_extra(gram_matrix):
+    first_tail = newton_second * gram_matrix + newton_third * fine(gram_matrix, gram_matrix)
+    once = newton_first * gram_matrix + fine(gram_matrix, first_tail)
+    later = newton_first * once + fine(once, first_tail)
+    last_tail = newton_second * later + newton_third * fine(later, later)
+    return newton_first * (first_tail + last_tail) + fine(first_tail, last_tail)
+
+
+def slots_of(devices):
+    slots = [(14, 0, 2), (14, 1, 2)]
+    for matrix in range(8, 12):
+        slots += [(matrix, 0, 2), (matrix, 1, 2)]
+    slots += [(matrix, 0, 1) for matrix in list(range(8)) + [12, 13, 15]]
+    return slots + [None] * (devices - len(slots))
+
+
+def padded(piece, rows, columns):
+    return jnp.pad(piece, ((0, rows - piece.shape[0]), (0, columns - piece.shape[1])))
+
+
+def muon_steps(moments):
+    devices = lax.axis_size(("dp", "copy"))
+    pieces = (
+        [moments[0][i] for i in range(8)]
+        + [moments[1][i] for i in range(4)]
+        + [moments[2][i] for i in range(2)]
+        + [moments[3], moments[4]]
+    )
+    slots = slots_of(devices)
+    highest = max(pieces[slot[0]].shape[0] // slot[2] for slot in slots if slot)
+    widest = max(piece.shape[1] for piece in pieces)
+    sending = []
+    for slot in slots:
+        if slot is None:
+            sending.append(jnp.zeros((highest, widest), jnp.bfloat16))
+        else:
+            rows = pieces[slot[0]].shape[0] // slot[2]
+            piece = to_low(pieces[slot[0]][slot[1] * rows : (slot[1] + 1) * rows])
+            sending.append(padded(piece, highest, widest))
+    held = lax.all_to_all(jnp.stack(sending), ("dp", "copy"), 0, 0).reshape(
+        devices * highest, widest
+    )
+    squares = sum_all(jnp.stack([jnp.sum(piece * piece) for piece in pieces]))
+    inverse = 1.0 / (jnp.sqrt(squares) + 1e-07)
+    me = lax.axis_index(("dp", "copy"))
+    matrix_here = jnp.asarray([slot[0] if slot else 0 for slot in slots], jnp.int32)[me]
+    shared_here = jnp.asarray([1.0 if slot and slot[2] == 2 else 0.0 for slot in slots])[me]
+    scale_here = inverse[matrix_here]
+    gram_matrix = product_left(held, held)
+    gram_matrix = gram_matrix + shared_here * swap_core(gram_matrix)
+    extra = newton_extra(gram_matrix * (scale_here * scale_here))
+    result = to_low(product(held, to_low(extra)) * scale_here)
+    back = lax.all_to_all(result.reshape(devices, highest, widest), ("dp", "copy"), 0, 0)
+    found = []
+    for matrix, piece in enumerate(pieces):
+        parts = [
+            back[device, : piece.shape[0] // slot[2], : piece.shape[1]]
+            for device, slot in enumerate(slots)
+            if slot and slot[0] == matrix
+        ]
+        whole = jnp.concatenate(parts, axis=0) if len(parts) > 1 else parts[0]
+        found.append(
+            newton_first * newton_first * inverse[matrix] * piece + whole.astype(jnp.float32)
         )
-    )
-    current = tuple((current[i] * inverse[i] for i in range(5)))
-    whole = tuple((whole[i] * inverse[i] * inverse[i] for i in range(5)))
-    return (current, whole)
+    return (
+        jnp.stack(found[:8]),
+        jnp.stack(found[8:12]),
+        jnp.stack(found[12:14]),
+        found[14],
+        found[15],
+    )
 
 
 def adam_shard(master, first, second, gradient):
@@ -273,25 +422,46 @@
     head_first,
     head_second,
 ):
-    attend_all, expand_all, dense_all, modulate_all, condition_all, encoder_all, head_all = (
-        lax.all_gather(to_low(attend_weight), ("dp", "copy"), axis=1, tiled=True),
-        lax.all_gather(to_low(expand_weight), ("dp", "copy"), axis=1, tiled=True),
-        lax.all_gather(to_low(dense_weight), ("dp", "copy"), axis=1, tiled=True),
-        lax.all_gather(to_low(modulate_weight), ("dp", "copy"), axis=0, tiled=True),
-        lax.all_gather(to_low(condition_weight), ("dp", "copy"), axis=0, tiled=True),
-        lax.all_gather(to_low(encoder_table), ("dp", "copy"), axis=1, tiled=True),
-        lax.all_gather(to_low(head_table), ("dp", "copy"), axis=1, tiled=True),
-    )
-    halfway = SEQ // lax.axis_size("copy")
-    offset = lax.axis_index("copy") * halfway
-    patch_seq = patches[0]
-    weight_row = (loss_mask[0] * (1 - buffer_flags[0])).astype(jnp.float32)
-    token_count = lax.psum(jnp.sum(weight_row), ("dp", "copy"))
-    own_patch = lax.dynamic_slice_in_dim(patch_seq, offset, halfway, 0)
-    own_image = lax.dynamic_slice_in_dim(image_ids[0], offset, halfway, 0)
-    buffer_on = lax.dynamic_slice_in_dim(buffer_flags[0], offset, halfway, 0)[:, None] > 0
-    masked_on = lax.dynamic_slice_in_dim(loss_mask[0], offset, halfway, 0)[:, None] > 0
-    same_image = own_image[:, None] == image_ids[0][None, :]
+    everywhere = ("dp", "copy")
+    core = lax.axis_index("copy")
+    encoder_turned = lax.all_gather(to_low(encoder_table).T, everywhere, axis=0, tiled=True)
+    attend_low, expand_low = (to_low(attend_weight), to_low(expand_weight))
+    attend_all, expand_all = ([], [])
+    for depth_index in range(2):
+        attend_all.append(
+            lax.all_gather(
+                attend_low[4 * depth_index : 4 * depth_index + 4], everywhere, axis=1, tiled=True
+            )
+        )
+        expand_all.append(
+            lax.all_gather(
+                expand_low[2 * depth_index : 2 * depth_index + 2], everywhere, axis=1, tiled=True
+            )
+        )
+    condition_all = lax.all_gather(to_low(condition_weight), everywhere, axis=0, tiled=True)
+    head_turned = lax.all_gather(to_low(head_table).T, everywhere, axis=0, tiled=True)
+    modulate_all = lax.all_gather(to_low(modulate_weight), everywhere, axis=0, tiled=True)
+    dense_all = lax.all_gather(to_low(dense_weight), everywhere, axis=1, tiled=True)
+    encoder_all = encoder_turned.T
+    head_all = head_turned.T
+    halfway = SEQ // 2
+    offset = core * halfway
+
+    def own_first(values):
+        return jnp.where(
+            core == 0, values, jnp.concatenate([values[halfway:], values[:halfway]], axis=0)
+        )
+
+    patch_seq = own_first(patches[0])
+    image_row = own_first(image_ids[0])
+    buffer_row = own_first(buffer_flags[0])
+    masked_row = own_first(loss_mask[0])
+    weight_row = (masked_row * (1 - buffer_row)).astype(jnp.float32)
+    token_count = sum_all(jnp.sum(weight_row))
+    own_patch = patch_seq[:halfway]
+    buffer_on = buffer_row[:halfway, None] > 0
+    masked_on = masked_row[:halfway, None] > 0
+    same_image = image_row[:halfway, None] == image_row[None, :]
     gain_rows = encoder_all[:12].astype(jnp.float32)
     position = lax.dynamic_slice_in_dim(encoder_all, 12 + PATCH + offset, halfway, 0).astype(
         jnp.float32
@@ -310,20 +480,19 @@
     for depth_index in range(2):
         state_rows, kept = block_forward(
             state_rows,
-            attend_all[4 * depth_index : 4 * depth_index + 4],
-            expand_all[2 * depth_index : 2 * depth_index + 2],
+            attend_all[depth_index],
+            expand_all[depth_index],
             gain_rows[4 * depth_index : 4 * depth_index + 4],
             same_image,
         )
         kept_all.append(kept)
     latent, third_back = jax.vjp(layer_norm, state_rows, gain_rows[8], gain_rows[9])
     latent_low = to_low(latent)
-    condition_rows = lax.all_gather(
-        to_low(product_right(latent_low, condition_all)), "copy", axis=0, tiled=True
-    )
-    step_float = timesteps[0, 0].astype(jnp.float32)
+    condition_own = to_low(product_right(latent_low, condition_all))
+    condition_rows = jnp.concatenate([condition_own, swap_core(condition_own)], axis=0)
+    step_float = own_first(timesteps[0, 0]).astype(jnp.float32)
     alpha_row = alpha_bar(step_float)[:, None]
-    target = noise_copies[0, 0].astype(jnp.float32)
+    target = own_first(noise_copies[0, 0]).astype(jnp.float32)
     noisy_low = to_low(
         jnp.sqrt(alpha_row) * patch_seq.astype(jnp.float32) + jnp.sqrt(1.0 - alpha_row) * target
     )
@@ -346,27 +515,36 @@
     residue = predicted - target
     loss_local = jnp.sum(weight_row[:, None] * residue * residue) / PATCH
     predicted_grad = to_low(2.0 * weight_row[:, None] * residue / (PATCH * token_count))
-    final_delta = product_left(predicted_grad, outer_low)
+    final_turned = product_left(outer_low, predicted_grad)
     lifted_grad, modulation_grad, branch_grad = outer_back(
         product(predicted_grad, head_all[PATCH + FREQ :])
     )
     branch_low = to_low(branch_grad)
-    second_delta = product_left(expanded_low, branch_low)
+    second_delta = rows_whole(weight_grad(expanded_low, branch_low), forward_order)
     (expanded_grad,) = dense_back(product_right(branch_low, dense_all[1]))
     expanded_grad_low = to_low(expanded_grad)
-    first_delta = product_left(inner_low, expanded_grad_low)
+    first_delta = rows_whole(weight_grad(inner_low, expanded_grad_low), crossed_order)
     lifted_extra, modulation_extra = inner_back(product_right(expanded_grad_low, dense_all[0]))
     modulation_low = to_low(modulation_grad + modulation_extra)
-    modulate_delta = product_left(modulation_low, activated_low)
+    modulate_half = weight_grad(modulation_low, activated_low)
+    quarter = modulate_half.shape[1] // 2
+    modulate_left = share_columns(scatter_rows(modulate_half[:, :quarter], forward_order))
+    modulate_right = share_columns(scatter_rows(modulate_half[:, quarter:], crossed_order))
+    modulate_delta = jnp.concatenate(
+        [modulate_left[0], modulate_right[0], modulate_left[1], modulate_right[1]], axis=1
+    )
     (summed_grad,) = silu_back(product(modulation_low, modulate_all))
-    time_delta = product_left(feature_low, to_low(summed_grad))
-    lift_delta = product_left(noisy_low, to_low(lifted_grad + lifted_extra))
+    time_turned = product_left(to_low(summed_grad), feature_low)
+    lift_turned = product_left(to_low(lifted_grad + lifted_extra), noisy_low)
+    head_turned_grad = jnp.concatenate([lift_turned, time_turned, final_turned], axis=1)
+    head_delta = rows_whole(
+        columns_of(head_turned_grad, core) + swap_core(columns_of(head_turned_grad, 1 - core)),
+        forward_order,
+    ).T
     condition_grad = to_low(
-        lax.psum_scatter(
-            summed_grad.astype(jnp.bfloat16), "copy", scatter_dimension=0, tiled=True
-        ).astype(jnp.float32)
-    )
-    condition_delta = product_left(condition_grad, latent_low)
+        summed_grad[:halfway] + swap_core(to_low(summed_grad[halfway:])).astype(jnp.float32)
+    )
+    condition_delta = rows_whole(weight_grad(condition_grad, latent_low), crossed_order)
     state_grad, gain_nine, gain_ten = third_back(product(condition_grad, condition_all))
     attend_parts = [None, None]
     expand_parts = [None, None]
@@ -380,34 +558,52 @@
         ) = block_backward(
             state_grad,
             kept_all[depth_index],
-            attend_all[4 * depth_index : 4 * depth_index + 4],
-            expand_all[2 * depth_index : 2 * depth_index + 2],
+            attend_all[depth_index],
+            expand_all[depth_index],
             same_image,
         )
     embedded_grad, token_grad, position_grad = entry_back(state_grad)
     embed_delta = product_left(own_patch, to_low(embedded_grad))
-    gain_delta = jnp.concatenate(
-        [gain_parts[0], gain_parts[1], jnp.stack([gain_nine, gain_ten]), token_grad], axis=0
-    )
-    position_full = lax.dynamic_update_slice_in_dim(
-        jnp.zeros((SEQ, D), jnp.float32), position_grad, offset, 0
-    )
-    encoder_delta = jnp.concatenate([gain_delta, embed_delta, position_full], axis=0)
-    head_delta = jnp.concatenate([lift_delta, time_delta, final_delta], axis=0)
-    attend_delta = jnp.concatenate([attend_parts[0], attend_parts[1]], axis=0)
-    expand_delta = jnp.concatenate([expand_parts[0], expand_parts[1]], axis=0)
-    dense_delta = jnp.stack([first_delta, second_delta])
+    small_delta = jnp.concatenate(
+        [
+            gain_parts[0],
+            gain_parts[1],
+            jnp.stack([gain_nine, gain_ten]),
+            token_grad,
+            embed_delta,
+        ],
+        axis=0,
+    )
+    small_delta = small_delta + swap_core(small_delta)
+    small_half = small_delta.shape[0] // 2
+    encoder_half = jnp.concatenate(
+        [position_grad, lax.dynamic_slice_in_dim(small_delta, core * small_half, small_half, 0)],
+        axis=0,
+    ).T
+    encoder_first_half, encoder_last_half = share_columns(
+        scatter_rows(encoder_half, crossed_order)
+    )
+    encoder_delta = jnp.concatenate(
+        [
+            encoder_first_half[:, halfway:],
+            encoder_last_half[:, halfway:],
+            encoder_first_half[:, :halfway],
+            encoder_last_half[:, :halfway],
+        ],
+        axis=1,
+    ).T
     reduced = (
-        lax.psum_scatter(attend_delta, ("dp", "copy"), scatter_dimension=1, tiled=True),
-        lax.psum_scatter(expand_delta, ("dp", "copy"), scatter_dimension=1, tiled=True),
-        lax.psum_scatter(dense_delta, ("dp", "copy"), scatter_dimension=1, tiled=True),
-        lax.psum_scatter(modulate_delta, ("dp", "copy"), scatter_dimension=0, tiled=True),
-        lax.psum_scatter(condition_delta, ("dp", "copy"), scatter_dimension=0, tiled=True),
-        lax.psum_scatter(encoder_delta, ("dp", "copy"), scatter_dimension=1, tiled=True),
-        lax.psum_scatter(head_delta, ("dp", "copy"), scatter_dimension=1, tiled=True),
+        jnp.concatenate(attend_parts, axis=0),
+        jnp.concatenate(expand_parts, axis=0),
+        jnp.stack([first_delta, second_delta]),
+        modulate_delta,
+        condition_delta,
+        encoder_delta,
+        head_delta,
     )
     squares = sum((jnp.sum(member * member) for member in reduced))
-    square_total, loss_sum = lax.psum((squares, loss_local), ("dp", "copy"))
+    totals = sum_all(jnp.stack([squares, loss_local]))
+    square_total, loss_sum = (totals[0], totals[1])
     clip_norm = jnp.sqrt(square_total)
     factor = jnp.minimum(1.0, clip_bound / (clip_norm + 1e-06))
     velocities = (
@@ -418,49 +614,14 @@
         condition_velocity,
     )
     moments = tuple((muon_keep * velocities[i] + factor * reduced[i] for i in range(5)))
-    current = (moments[0], moments[1], moments[2], moments[3][None], moments[4][None])
-    for sweep_index in range(NS_STEPS):
-        grams = tuple((local_gram(member) for member in current))
-        parts = (
-            lax.psum_scatter(grams[0], ("dp", "copy"), scatter_dimension=1, tiled=True),
-            lax.psum_scatter(grams[1], ("dp", "copy"), scatter_dimension=1, tiled=True),
-            lax.psum_scatter(grams[2], ("dp", "copy"), scatter_dimension=1, tiled=True),
-            lax.psum_scatter(grams[3], ("dp", "copy"), scatter_dimension=1, tiled=True),
-            lax.psum_scatter(grams[4], ("dp", "copy"), scatter_dimension=1, tiled=True),
-        )
-        whole = (
-            lax.all_gather(
-                parts[0].astype(jnp.bfloat16), ("dp", "copy"), axis=1, tiled=True
-            ).astype(jnp.float32),
-            lax.all_gather(
-                parts[1].astype(jnp.bfloat16), ("dp", "copy"), axis=1, tiled=True
-            ).astype(jnp.float32),
-            lax.all_gather(
-                parts[2].astype(jnp.bfloat16), ("dp", "copy"), axis=1, tiled=True
-            ).astype(jnp.float32),
-            lax.all_gather(
-                parts[3].astype(jnp.bfloat16), ("dp", "copy"), axis=1, tiled=True
-            ).astype(jnp.float32),
-            lax.all_gather(
-                parts[4].astype(jnp.bfloat16), ("dp", "copy"), axis=1, tiled=True
-            ).astype(jnp.float32),
-        )
-        if sweep_index == 0:
-            current, whole = scale_first(current, whole)
-        current = tuple((newton_update(current[i], whole[i]) for i in range(5)))
-    devices = lax.axis_size(("dp", "copy"))
-    masters = (
-        attend_weight,
-        expand_weight,
-        dense_weight,
-        modulate_weight[None],
-        condition_weight[None],
-    )
+    current = muon_steps(moments)
+    devices = lax.axis_size(everywhere)
+    masters = (attend_weight, expand_weight, dense_weight, modulate_weight, condition_weight)
     updated = tuple(
         (
             masters[i] * (1.0 - muon_rate * muon_decay)
             - muon_rate
-            * max(1.0, current[i].shape[1] * devices / current[i].shape[2]) ** 0.5
+            * max(1.0, current[i].shape[-2] * devices / current[i].shape[-1]) ** 0.5
             * current[i]
             for i in range(5)
         )
@@ -481,9 +642,9 @@
         moments[1],
         updated[2],
         moments[2],
-        updated[3][0],
+        updated[3],
         moments[3],
-        updated[4][0],
+        updated[4],
         moments[4],
         encoder_master,
         encoder_firsts,

time: 4420 us -> 1960 us (0.44)
  waiting for transfers between devices: 3280 us -> 735 us
  matrix products: 759 us -> 609 us
  starting transfers between devices: 3.61 us -> 147 us
    reduce_scatter x20 -> x0, waiting for transfers between devices: 2340 us -> none  [the longest x2 411 us: per_device(): lax.psum_scatter(grams[0], ('dp', 'copy'), scatter_dimension=1, tiled=True)]
    all_gather x21 -> x8, waiting for transfers between devices: 830 us -> 303 us  [the longest x2 92.1 us: per_device(): lax.all_gather(attend_low[4 * depth_index:4 * depth_index + 4], everywher...]
    ppermute x0 -> x158, waiting for transfers between devices: none -> 328 us  [the longest x95 291 us: scatter_axis(): arrived = lax.ppermute(sent, 'dp', shift_pairs(grid, axis, shift))]
    ppermute x0 -> x158, starting transfers between devices: none -> 143 us  [the longest x95 117 us: scatter_axis(): arrived = lax.ppermute(sent, 'dp', shift_pairs(grid, axis, shift))]
    dot_general x30 -> x5, matrix products: 190 us -> 50.9 us  [fine(): jnp.dot(left_side, right_side, precision=lax.Precision.HIGH, preferred_el...]
    all_to_all x0 -> x1, blocking collectives: none -> 118 us  [muon_steps(): lax.all_to_all(jnp.stack(sending), ('dp', 'copy'), 0, 0)]
    unnamed x45 -> x8, waiting for transfers between devices: 108 us -> 1.15 us
    all_to_all x0 -> x1, waiting for transfers between devices: none -> 103 us  [muon_steps(): lax.all_to_all(result.reshape(devices, highest, widest), ('dp', 'copy'),...]
  transfers between devices with their start and end apart: 43 -> 167, of which waited for: 35 -> 97; matrix products, arithmetic and copies ran while one was open for 15% -> 33% of each run, Pallas kernels for 0% -> 0%
where the time goes in v1:
time: 1960 us; the launch traced here: 1950 us
  waiting for transfers between devices  735 us (38%)
  matrix products  609 us (31%)
  blocking collectives  164 us (8%)
  other arithmetic  158 us (8%)
  starting transfers between devices  147 us (8%)
  local copies, waits for them, and re-layouts  91 us (5%)
  between operations  44.9 us (2%)
    ppermute x95, waiting for transfers between devices, scatter_axis(): arrived = lax.ppermute(sent, 'dp', shift_pairs(grid, axis, shift))  291 us
    all_to_all x1, blocking collectives, muon_steps(): lax.all_to_all(jnp.stack(sending), ('dp', 'copy'), 0, 0)  118 us
    dot_general x37, matrix products, product_left(): lax.dot_general(left_side, right_side, (((0,), (0,)), ((), ())), preferre...  117 us
    ppermute x95, starting transfers between devices, scatter_axis(): arrived = lax.ppermute(sent, 'dp', shift_pairs(grid, axis, shift))  117 us
    all_to_all x1, waiting for transfers between devices, muon_steps(): lax.all_to_all(result.reshape(devices, highest, widest), ('dp', 'copy'),...  103 us
    dot_general x21, matrix products, product(): return jnp.dot(left_side, right_side, preferred_element_type=jnp.float32)  93.9 us
    dot_general x2, matrix products, block_backward(): jnp.einsum('hqk,qhd->khd', score_low, query_heads, preferred_element_type...  93.2 us
    all_gather x2, waiting for transfers between devices, per_device(): lax.all_gather(attend_low[4 * depth_index:4 * depth_index + 4], everywher...  92.1 us
  transfers between devices with their start and end apart: 167, of which 97 were waited for; matrix products, arithmetic and copies ran while one was open for 33% of the time, Pallas kernels for 0%

profile of v1, /device:TPU:0, one launch (start us, length us, event | category | flops | bytes accessed | tf_op | source)
XLA Modules:
  0.0 1949.6 jit_solution(12646539716262007380)
XLA Ops:
  19.2 50.8 %all-gather.9.cloned.1.call-done = bf16[768,1100]{1,0:T(8,128)(2,1)} async-done(((bf16[24,1100]{1,0:T(8,128)(2,1)}), bf16[768,1100]{1,0:T(8,128)(2,1)}) %all-gather.9.cloned.1.call-update) | async-done | bytes 1689616 | tf_op jit(solution)/shard_map/all_gather | solution.py:427
  77.8 58.2 %all-gather.11.cloned.1.call-done = bf16[4,768,768]{2,1,0:T(8,128)(2,1)} async-done(((bf16[4,24,768]{2,1,0:T(8,128)(2,1)}), bf16[4,768,768]{2,1,0:T(8,128)(2,1)}) %all-gather.11.cloned.1.call-update) | async-done | bytes 4718608 | tf_op jit(solution)/shard_map/all_gather | solution.py:432
  142.5 46.1 %all_gather.29 = bf16[1024,384]{1,0:T(8,128)(2,1)} all-gather(bf16[32,384]{1,0:T(8,128)(2,1)S(1)} %convert_bitcast_fusion.1), channel_id=1, replica_groups=mesh['dp'=16,'copy'=2] {'dp','copy'}, dimensions={0}, use_global_device_ids=true | all-gather | bytes 811008 | tf_op jit(solution)/shard_map/all_gather | solution.py:442
  204.5 12.3 fusion.6
  216.8 12.6 fusion.4
  254.9 33.9 %all-gather.15.cloned.1.call-done = bf16[4,768,768]{2,1,0:T(8,128)(2,1)} async-done(((bf16[4,24,768]{2,1,0:T(8,128)(2,1)}), bf16[4,768,768]{2,1,0:T(8,128)(2,1)}) %all-gather.15.cloned.1.call-update) | async-done | bytes 4718608 | tf_op jit(solution)/shard_map/all_gather | solution.py:432
  314.3 12.1 fusion.7
  326.4 12.3 fusion.5
  355.0 18.1 all-gather.17.cloned.1.call-done
  383.5 46.4 %all-gather.19.cloned.1.call-done = bf16[1024,768]{1,0:T(8,128)(2,1)} async-done(((bf16[32,768]{1,0:T(8,128)(2,1)}), bf16[1024,768]{1,0:T(8,128)(2,1)}) %all-gather.19.cloned.1.call-update) | async-done | bytes 1572880 | tf_op jit(solution)/shard_map/all_gather | solution.py:441
  461.8 57.2 %all-gather.21.cloned.1.call-done = bf16[5120,1024]{1,0:T(8,128)(2,1)} async-done(((bf16[160,1024]{1,0:T(8,128)(2,1)}), bf16[5120,1024]{1,0:T(8,128)(2,1)}) %all-gather.21.cloned.1.call-update) | async-done | bytes 10485776 | tf_op jit(solution)/shard_map/all_gather | solution.py:443
  519.0 18.6 fusion.406
  544.1 38.3 %all-gather.23.cloned.1.call-done = bf16[2,1024,1024]{2,1,0:T(8,128)(2,1)} async-done(((bf16[2,32,1024]{2,1,0:T(8,128)(2,1)}), bf16[2,1024,1024]{2,1,0:T(8,128)(2,1)}) %all-gather.23.cloned.1.call-update) | async-done | bytes 4194320 | tf_op jit(solution)/shard_map/all_gather | solution.py:444
  650.0 20.0 %fusion.381 = (bf16[1024,1024]{0,1:T(8,128)(2,1)S(1)}, f32[1024,1024]{0,1:T(8,128)}) fusion(f32[1024,1024]{0,1:T(8,128)} %get-tuple-element.290, bf16[512,1024]{0,1:T(8,128)(2,1)} %collective-permute-done.4, bf16[512,1024]{0,1:T(8,128)(2,1)} %convolution_convert_fusion, bf16[1024,5120]{0,1:T(8,128)(2,1)} %add_convert_fusion, ...), kind=kOutput, calls=%fused_computation.887 | convolution fusion | flops 10753146880 | bytes 33554432 | tf_op jit(solution)/shard_map/dot_general | solution.py:38
  730.3 11.6 fusion.402
  742.0 13.1 fusion.75
  755.1 44.8 %fusion.95 = bf16[12,64,512]{2,1,0:T(8,128)(2,1)} fusion(bf16[1024,12,64]{0,2,1:T(8,128)(2,1)} %bitcast.877, f32[12,512,1024]{2,1,0:T(8,128)} %fusion.402, f32[12,512]{1,0:T(8,128)S(1)} %copy-done.180, f32[12,512,1024]{2,1,0:T(8,128)} %get-tuple-element.284, pred[512,1024]{1,0:T(8,128)(4,1)S(1)} %copy-done.30), kind=kOutput, calls=%fused_computation.204 | convolution fusion | flops 874912768 | bytes 53239808 | tf_op jit(solution)/shard_map/hqk,khd->qhd/dot_general | solution.py:280
  799.9 46.5 %fusion.72 = f32[1024,12,64]{0,2,1:T(8,128)} fusion(bf16[512,12,64]{0,2,1:T(8,128)(2,1)} %bitcast.905, f32[12,512,1024]{2,1,0:T(8,128)} %fusion.402, f32[12,512]{1,0:T(8,128)S(1)} %copy-done.180, f32[12,512,1024]{2,1,0:T(8,128)} %get-tuple-element.284, pred[512,1024]{1,0:T(8,128)(4,1)S(1)} %copy-done.30), kind=kOutput, calls=%fused_computation.138 | convolution fusion | flops 874519552 | bytes 54812672 | tf_op jit(solution)/shard_map/hqk,qhd->khd/dot_general | solution.py:276
  891.0 11.3 fusion.403
  902.3 13.1 fusion.78
  915.4 44.5 %fusion.92 = bf16[12,64,512]{2,1,0:T(8,128)(2,1)} fusion(bf16[1024,12,64]{0,2,1:T(8,128)(2,1)S(1)} %bitcast.875, f32[12,512,1024]{2,1,0:T(8,128)} %fusion.403, f32[12,512]{1,0:T(8,128)S(1)} %copy-done.179, f32[12,512,1024]{2,1,0:T(8,128)} %get-tuple-element.278, pred[512,1024]{1,0:T(8,128)(4,1)S(1)} %copy-done.30), kind=kOutput, calls=%fused_computation.203 | convolution fusion | flops 874912768 | bytes 53239808 | tf_op jit(solution)/shard_map/hqk,khd->qhd/dot_general | solution.py:280
  960.0 46.8 %fusion.69 = f32[1024,12,64]{0,2,1:T(8,128)} fusion(bf16[512,12,64]{0,2,1:T(8,128)(2,1)} %bitcast.902, f32[12,512,1024]{2,1,0:T(8,128)} %fusion.403, f32[12,512]{1,0:T(8,128)S(1)} %copy-done.179, f32[12,512,1024]{2,1,0:T(8,128)} %get-tuple-element.278, pred[512,1024]{1,0:T(8,128)(4,1)S(1)} %copy-done.30), kind=kOutput, calls=%fused_computation.137 | convolution fusion | flops 874519552 | bytes 54812672 | tf_op jit(solution)/shard_map/hqk,qhd->khd/dot_general | solution.py:276
  1308.4 11.0 collective-permute-done.93
  1338.7 18.1 collective-permute-done.87
  1376.8 14.2 collective-permute-done.96
  1445.5 15.5 collective-permute-done.75
  1511.7 18.2 collective-permute-done.117
  1530.1 16.9 collective-permute-done.123
  1577.1 118.2 %all_to_all.10 = bf16[32,80,1024]{2,1,0:T(8,128)(2,1)S(1)} all-to-all(bf16[32,80,1024]{2,1,0:T(8,128)(2,1)S(1)} %broadcast_dynamic-update-slice_fusion), channel_id=1, replica_groups=mesh['dp'=16,'copy'=2] {'dp','copy'}, dimensions={0} | all-to-all | bytes 10485760 | tf_op jit(solution)/shard_map/all_to_all | solution.py:356
  1764.0 16.7 multiply_add_fusion
  1780.6 11.1 fusion.405
  1819.9 103.1 %all-to-all-done.1 = bf16[32,80,1024]{2,1,0:T(8,128)(2,1)} async-done(((bf16[32,80,1024]{2,1,0:T(8,128)(2,1)}), bf16[32,80,1024]{2,1,0:T(8,128)(2,1)}, u32[]{:S(2)}, u32[]{:S(2)}) %all-to-all-start.1) | async-done | bytes 5242912 | tf_op jit(solution)/shard_map/all_to_all | solution.py:369
  (1290 shorter events, 892.8 us)
Async XLA Ops:
  7.3 62.6 %all-gather.9.cloned.1.call-start = ((), (), s32[]{:S(2)}) async-start(), calls=%async_computation.2 | async-start | bytes 1824768 | tf_op jit(solution)/shard_map/all_gather | solution.py:427
  9.0 127.0 %all-gather.11.cloned.1.call-start = ((), (), s32[]{:S(2)}) async-start(), calls=%async_computation.3 | async-start | bytes 4866048 | tf_op jit(solution)/shard_map/all_gather | solution.py:432
  10.9 233.4 %all-gather.13.cloned.1.call-start = ((), (), s32[]{:S(2)}) async-start(), calls=%async_computation.4 | async-start | bytes 9732096 | tf_op jit(solution)/shard_map/all_gather | solution.py:437
  13.2 275.6 %all-gather.15.cloned.1.call-start = ((), (), s32[]{:S(2)}) async-start(), calls=%async_computation.5 | async-start | bytes 4866048 | tf_op jit(solution)/shard_map/all_gather | solution.py:432
  13.8 359.3 %all-gather.17.cloned.1.call-start = ((), (), s32[]{:S(2)}) async-start(), calls=%async_computation.6 | async-start | bytes 9732096 | tf_op jit(solution)/shard_map/all_gather | solution.py:437
  14.4 415.6 %all-gather.19.cloned.1.call-start = ((), (), s32[]{:S(2)}) async-start(), calls=%async_computation.7 | async-start | bytes 1622016 | tf_op jit(solution)/shard_map/all_gather | solution.py:441
  15.1 503.9 %all-gather.21.cloned.1.call-start = ((), (), s32[]{:S(2)}) async-start(), calls=%async_computation.8 | async-start | bytes 10813440 | tf_op jit(solution)/shard_map/all_gather | solution.py:443
  15.9 566.4 %all-gather.23.cloned.1.call-start = ((), (), s32[]{:S(2)}) async-start(), calls=%async_computation.9 | async-start | bytes 4325376 | tf_op jit(solution)/shard_map/all_gather | solution.py:444
  17.2 419.5 %collective-permute-start.5 = (f32[]{:T(128)}, f32[]{:T(128)}, u32[]{:S(2)}, u32[]{:S(2)}) collective-permute-start(f32[]{:T(128)} %reduce_sum.637), channel_id=1, source_target_pairs={{0,1},{1,0},{2,3},{3,2},{4,5},{5,4},{6,7},{7,6},{8,9},{9,8},{10,11... | collective-permute-start | bytes 20 | tf_op jit(solution)/shard_map/ppermute | solution.py:116
  139.0 54.9 %collective-permute-start = (bf16[512,768]{1,0:T(8,128)(2,1)}, bf16[512,768]{1,0:T(8,128)(2,1)}, u32[]{:S(2)}, u32[]{:S(2)}) collective-permute-start(bf16[512,768]{1,0:T(8,128)(2,1)} %convolution_convert_fusion.8), channel_id=1, source_target_pairs={{0,1},{1,0},{2,3},{3,2},{4,5},{5,4},{6,7},{7,6},{8,9},{9,8},{10,11... | collective-permute-start | bytes 2359304 | tf_op jit(solution)/shard_map/ppermute | solution.py:116
  142.2 57.0 %collective-permute-start.1 = (bf16[512,768]{1,0:T(8,128)(2,1)}, bf16[512,768]{1,0:T(8,128)(2,1)}, u32[]{:S(2)}, u32[]{:S(2)}) collective-permute-start(bf16[512,768]{1,0:T(8,128)(2,1)} %convolution_convert_fusion.6), channel_id=1, source_target_pairs={{0,1},{1,0},{2,3},{3,2},{4,5},{5,4},{6,7},{7,6},{8,9},{9,8},{10,11... | collective-permute-start | bytes 2359304 | tf_op jit(solution)/shard_map/ppermute | solution.py:116
  678.6 349.8 %collective-permute-start.106 = (f32[1024,512]{1,0:T(8,128)}, f32[1024,512]{1,0:T(8,128)}, u32[]{:S(2)}, u32[]{:S(2)}) collective-permute-start(f32[1024,512]{1,0:T(8,128)} %fusion.110), channel_id=1, source_target_pairs={{0,1},{1,0},{2,3},{3,2},{4,5},{5,4},{6,7},{7,6},{8,9},{9,8},{10,11... | collective-permute-start | bytes 6291464 | tf_op jit(solution)/shard_map/ppermute | solution.py:116
  695.2 338.6 %collective-permute-start.99 = (f32[1024,512]{1,0:T(8,128)}, f32[1024,512]{1,0:T(8,128)}, u32[]{:S(2)}, u32[]{:S(2)}) collective-permute-start(f32[1024,512]{1,0:T(8,128)} %fusion.113), channel_id=1, source_target_pairs={{0,1},{1,0},{2,3},{3,2},{4,5},{5,4},{6,7},{7,6},{8,9},{9,8},{10,11... | collective-permute-start | bytes 6291464 | tf_op jit(solution)/shard_map/ppermute | solution.py:116
  697.8 151.6 %collective-permute-start.142 = (bf16[4,64,192]{2,1,0:T(8,128)(2,1)S(1)}, bf16[4,64,192]{2,1,0:T(8,128)(2,1)S(1)}, u32[]{:S(2)}, u32[]{:S(2)}) collective-permute-start(bf16[4,64,192]{2,1,0:T(8,128)(2,1)S(1)} %fusion.223), channel_id=1, source_target_pairs={{0,4},{2,6},{4,0},{6,2},{8,12},{10,14},{12,8},{14,10},{16,20},{18,... | collective-permute-start | bytes 294920 | tf_op jit(solution)/shard_map/ppermute | solution.py:139
  857.4 223.9 %collective-permute-start.126 = (f32[1024,384]{1,0:T(8,128)}, f32[1024,384]{1,0:T(8,128)}, u32[]{:S(2)}, u32[]{:S(2)}) collective-permute-start(f32[1024,384]{1,0:T(8,128)} %fusion.138), channel_id=1, source_target_pairs={{0,1},{1,0},{2,3},{3,2},{4,5},{5,4},{6,7},{7,6},{8,9},{9,8},{10,11... | collective-permute-start | bytes 4718600 | tf_op jit(solution)/shard_map/ppermute | solution.py:116
  863.8 173.3 %collective-permute-start.64 = (f32[768,384]{1,0:T(8,128)}, f32[768,384]{1,0:T(8,128)}, u32[]{:S(2)}, u32[]{:S(2)}) collective-permute-start(f32[768,384]{1,0:T(8,128)} %fusion.153), channel_id=1, source_target_pairs={{0,1},{1,0},{2,3},{3,2},{4,5},{5,4},{6,7},{7,6},{8,9},{9,8},{10,11... | collective-permute-start | bytes 3538952 | tf_op jit(solution)/shard_map/ppermute | solution.py:116
  865.9 174.5 %collective-permute-start.43 = (f32[768,384]{1,0:T(8,128)}, f32[768,384]{1,0:T(8,128)}, u32[]{:S(2)}, u32[]{:S(2)}) collective-permute-start(f32[768,384]{1,0:T(8,128)} %fusion.162), channel_id=1, source_target_pairs={{0,1},{1,0},{2,3},{3,2},{4,5},{5,4},{6,7},{7,6},{8,9},{9,8},{10,11... | collective-permute-start | bytes 3538952 | tf_op jit(solution)/shard_map/ppermute | solution.py:116
  1028.3 115.5 %collective-permute-start.57 = (f32[768,384]{1,0:T(8,128)}, f32[768,384]{1,0:T(8,128)}, u32[]{:S(2)}, u32[]{:S(2)}) collective-permute-start(f32[768,384]{1,0:T(8,128)} %fusion.156), channel_id=1, source_target_pairs={{0,1},{1,0},{2,3},{3,2},{4,5},{5,4},{6,7},{7,6},{8,9},{9,8},{10,11... | collective-permute-start | bytes 3538952 | tf_op jit(solution)/shard_map/ppermute | solution.py:116
  1033.8 36.2 %collective-permute-start.20 = (bf16[512,768]{0,1:T(8,128)(2,1)S(1)}, bf16[512,768]{0,1:T(8,128)(2,1)S(1)}, u32[]{:S(2)}, u32[]{:S(2)}) collective-permute-start(bf16[512,768]{0,1:T(8,128)(2,1)S(1)} %bitcast.923), channel_id=1, source_target_pairs={{0,1},{1,0},{2,3},{3,2},{4,5},{5,4},{6,7},{7,6},{8,9},{9,8},{10,11... | collective-permute-start | bytes 2359304 | tf_op jit(solution)/shard_map/ppermute | solution.py:116
  1065.9 80.2 %collective-permute-start.50 = (f32[768,384]{1,0:T(8,128)}, f32[768,384]{1,0:T(8,128)}, u32[]{:S(2)}, u32[]{:S(2)}) collective-permute-start(f32[768,384]{1,0:T(8,128)} %fusion.159), channel_id=1, source_target_pairs={{0,1},{1,0},{2,3},{3,2},{4,5},{5,4},{6,7},{7,6},{8,9},{9,8},{10,11... | collective-permute-start | bytes 3538952 | tf_op jit(solution)/shard_map/ppermute | solution.py:116
  1143.9 98.5 %collective-permute-start.29 = (f32[768,384]{1,0:T(8,128)S(1)}, f32[768,384]{1,0:T(8,128)S(1)}, u32[]{:S(2)}, u32[]{:S(2)}) collective-permute-start(f32[768,384]{1,0:T(8,128)S(1)} %copy-done.105), channel_id=1, source_target_pairs={{0,1},{1,0},{2,3},{3,2},{4,5},{5,4},{6,7},{7,6},{8,9},{9,8},{10,11... | collective-permute-start | bytes 3538952 | tf_op jit(solution)/shard_map/ppermute | solution.py:116
  1146.0 97.4 %collective-permute-start.21 = (f32[768,384]{1,0:T(8,128)S(1)}, f32[768,384]{1,0:T(8,128)S(1)}, u32[]{:S(2)}, u32[]{:S(2)}) collective-permute-start(f32[768,384]{1,0:T(8,128)S(1)} %copy-done.104), channel_id=1, source_target_pairs={{0,1},{1,0},{2,3},{3,2},{4,5},{5,4},{6,7},{7,6},{8,9},{9,8},{10,11... | collective-permute-start | bytes 3538952 | tf_op jit(solution)/shard_map/ppermute | solution.py:116
  1235.3 47.8 %collective-permute-start.92 = (f32[3072,384]{1,0:T(8,128)}, f32[3072,384]{1,0:T(8,128)}, u32[]{:S(2)}, u32[]{:S(2)}) collective-permute-start(f32[3072,384]{1,0:T(8,128)} %fusion.141), channel_id=1, source_target_pairs={{0,1},{1,0},{2,3},{3,2},{4,5},{5,4},{6,7},{7,6},{8,9},{9,8},{10,11... | collective-permute-start | bytes 14155784 | tf_op jit(solution)/shard_map/ppermute | solution.py:116
  1236.3 55.7 %collective-permute-start.85 = (f32[3072,384]{1,0:T(8,128)}, f32[3072,384]{1,0:T(8,128)}, u32[]{:S(2)}, u32[]{:S(2)}) collective-permute-start(f32[3072,384]{1,0:T(8,128)} %fusion.144), channel_id=1, source_target_pairs={{0,1},{1,0},{2,3},{3,2},{4,5},{5,4},{6,7},{7,6},{8,9},{9,8},{10,11... | collective-permute-start | bytes 14155784 | tf_op jit(solution)/shard_map/ppermute | solution.py:116
  1280.7 132.1 %collective-permute-start.113 = (f32[5120,512]{1,0:T(8,128)}, f32[5120,512]{1,0:T(8,128)}, u32[]{:S(2)}, u32[]{:S(2)}) collective-permute-start(f32[5120,512]{1,0:T(8,128)} %fusion.107), channel_id=1, source_target_pairs={{0,1},{1,0},{2,3},{3,2},{4,5},{5,4},{6,7},{7,6},{8,9},{9,8},{10,11... | collective-permute-start | bytes 31457288 | tf_op jit(solution)/shard_map/ppermute | solution.py:116
  1302.3 55.8 %collective-permute-start.79 = (bf16[4,2,192,384]{3,2,1,0:T(8,128)(2,1)S(1)}, bf16[4,2,192,384]{3,2,1,0:T(8,128)(2,1)S(1)}, u32[]{:S(2)}, u32[]{:S(2)}) collective-permute-start(bf16[4,2,192,384]{3,2,1,0:T(8,128)(2,1)S(1)} %fusion.103), channel_id=1, source_target_pairs={{0,2},{2,0},{4,6},{6,4},{8,10},{10,8},{12,14},{14,12},{16,18},{18,... | collective-permute-start | bytes 3538952 | tf_op jit(solution)/shard_map/ppermute | solution.py:139
  1327.0 36.0 %collective-permute-start.72 = (bf16[4,2,192,384]{3,2,1,0:T(8,128)(2,1)S(1)}, bf16[4,2,192,384]{3,2,1,0:T(8,128)(2,1)S(1)}, u32[]{:S(2)}, u32[]{:S(2)}) collective-permute-start(bf16[4,2,192,384]{3,2,1,0:T(8,128)(2,1)S(1)} %fusion.102), channel_id=1, source_target_pairs={{0,4},{2,6},{4,0},{6,2},{8,12},{10,14},{12,8},{14,10},{16,20},{18,... | collective-permute-start | bytes 3538952 | tf_op jit(solution)/shard_map/ppermute | solution.py:139
  1367.8 34.3 %collective-permute-start.89 = (f32[192,384]{1,0:T(8,128)S(1)}, f32[192,384]{1,0:T(8,128)S(1)}, u32[]{:S(2)}, u32[]{:S(2)}) collective-permute-start(f32[192,384]{1,0:T(8,128)S(1)} %get-tuple-element.139), channel_id=1, source_target_pairs={{0,16},{2,18},{4,20},{6,22},{8,24},{10,26},{12,28},{14,30},{16,0},... | collective-permute-start | bytes 884744 | tf_op jit(solution)/shard_map/ppermute | solution.py:139
  1410.8 34.6 %collective-permute-start.74 = (f32[192,384]{1,0:T(8,128)}, f32[192,384]{1,0:T(8,128)}, u32[]{:S(2)}, u32[]{:S(2)}) collective-permute-start(f32[192,384]{1,0:T(8,128)} %get-tuple-element.131), channel_id=1, source_target_pairs={{0,8},{2,10},{4,12},{6,14},{8,16},{10,18},{12,20},{14,22},{16,24},... | collective-permute-start | bytes 884744 | tf_op jit(solution)/shard_map/ppermute | solution.py:139
  1494.6 35.4 %collective-permute-start.117 = (f32[320,256]{1,0:T(8,128)S(1)}, f32[320,256]{1,0:T(8,128)S(1)}, u32[]{:S(2)}, u32[]{:S(2)}) collective-permute-start(f32[320,256]{1,0:T(8,128)S(1)} %get-tuple-element.123), channel_id=1, source_target_pairs={{0,16},{2,18},{4,20},{6,22},{8,24},{10,26},{12,28},{14,30},{16,0},... | collective-permute-start | bytes 983048 | tf_op jit(solution)/shard_map/ppermute | solution.py:139
  1503.2 43.8 %collective-permute-start.123 = (f32[320,256]{1,0:T(8,128)S(1)}, f32[320,256]{1,0:T(8,128)S(1)}, u32[]{:S(2)}, u32[]{:S(2)}) collective-permute-start(f32[320,256]{1,0:T(8,128)S(1)} %get-tuple-element.126), channel_id=1, source_target_pairs={{0,16},{2,18},{4,20},{6,22},{8,24},{10,26},{12,28},{14,30},{16,0},... | collective-permute-start | bytes 983048 | tf_op jit(solution)/shard_map/ppermute | solution.py:139
  1802.4 120.6 %all-to-all-start.1 = ((bf16[32,80,1024]{2,1,0:T(8,128)(2,1)}), bf16[32,80,1024]{2,1,0:T(8,128)(2,1)}, u32[]{:S(2)}, u32[]{:S(2)}) async-start(bf16[32,80,1024]{2,1,0:T(8,128)(2,1)} %bitcast.881), calls=%async_computation.1 | async-start | bytes 10485760 | tf_op jit(solution)/shard_map/all_to_all | solution.py:369
  (380 other events, 8039.2 us)
Sparse Core Ops, SparseCore 0:
  11.5 58.3 all-gather.8
  73.5 62.5 all-gather.10
  139.6 83.5 all-gather.12
  226.5 62.2 all-gather.14
  292.2 80.8 all-gather.16
  376.4 53.5 all-gather.18
  433.3 85.6 all-gather.20
  521.9 60.4 all-gather.22

commit v2 on v1

--- a/solution.py
+++ b/solution.py
@@ -3,6 +3,8 @@
 import jax
 import jax.numpy as jnp
 from jax import lax
+from jax.experimental import pallas as pl
+from jax.experimental.pallas import tpu as pltpu
 from jax.sharding import PartitionSpec as P
 
 D = 768
@@ -128,58 +130,180 @@
     return values
 
 
-def scatter_axis(values, grid, axis, position, sent_type):
+def assemble(pieces, places, shape):
+    indices = jnp.stack(
+        [jnp.asarray(i, jnp.int32) for place in places for i in place if i is not None]
+    )
+
+    def kernel(index_ref, *refs):
+        sources, target, semaphores = (refs[: len(pieces)], refs[-2], refs[-1])
+        copies, number = ([], 0)
+        for i, place in enumerate(places):
+            view = []
+            for wanted in place:
+                if wanted is None:
+                    view.append(slice(None))
+                else:
+                    view.append(index_ref[number])
+                    number += 1
+            copies.append(
+                pltpu.make_async_copy(sources[i], target.at[tuple(view)], semaphores.at[i])
+            )
+            copies[-1].start()
+        for copy in copies:
+            copy.wait()
+
+    size = 2 * math.prod(shape)
+    return pl.pallas_call(
+        kernel,
+        out_shape=jax.ShapeDtypeStruct(shape, pieces[0].dtype),
+        in_specs=[pl.BlockSpec(memory_space=pltpu.SMEM)]
+        + [pl.BlockSpec(memory_space=pl.ANY)] * len(pieces),
+        out_specs=pl.BlockSpec(memory_space=pl.ANY),
+        scratch_shapes=[pltpu.SemaphoreType.DMA((len(pieces),))],
+        cost_estimate=pl.CostEstimate(flops=0, bytes_accessed=2 * size, transcendentals=0),
+    )(indices, *pieces)
+
+
+class Flow:
+    def __init__(self):
+        self.live, self.results = ([], {})
+
+    def begin(self, name, task):
+        self.live.append([name, task, *next(task)])
+
+    def tick(self, *carry):
+        due = [entry for entry in self.live if entry[3] <= 1]
+        for entry in self.live:
+            entry[3] -= 1
+        carry, arrived = lax.optimization_barrier((carry, [entry[2] for entry in due]))
+        for entry, values in zip(due, arrived):
+            try:
+                entry[2], entry[3] = entry[1].send(values)
+            except StopIteration as stop:
+                self.results[entry[0]] = stop.value
+                self.live.remove(entry)
+        return carry if len(carry) > 1 else (carry[0] if carry else None)
+
+    def take(self, *names):
+        while any(name not in self.results for name in names):
+            self.tick()
+        return [self.results[name] for name in names]
+
+
+forward_order = (2, 1, 0)
+crossed_order = (1, 2, 0)
+
+
+def gather_task(own, order):
+    grid = grid_of(lax.axis_size("dp"))
+    here = place_of(lax.axis_index("dp"), grid)
+    core = lax.axis_index("copy")
+    slots, rows, columns = own.shape
+    values, found = (own, [])
+    for axis in order[::-1][:-1]:
+        size = grid[axis]
+        arrived = yield (
+            [lax.ppermute(values, "dp", shift_pairs(grid, axis, shift)) for shift in range(1, size)],
+            1,
+        )
+        position = 1 + sum(1 for other in found if other < axis)
+        shape = values.shape[:position] + (size,) + values.shape[position:]
+        places = [
+            (None,) * position + ((here[axis] - shift) % size,) for shift in range(size)
+        ]
+        values = assemble([values] + arrived, places, shape)
+        found.append(axis)
+    axis = order[0]
     size = grid[axis]
-    mine = place_of(lax.axis_index("dp"), grid)[axis]
-    total = lax.dynamic_index_in_dim(values, mine, position, keepdims=False)
-    for shift in range(1, size):
-        sent = lax.dynamic_index_in_dim(
-            values, (mine + shift) % size, position, keepdims=False
-        ).astype(sent_type)
-        arrived = lax.ppermute(sent, "dp", shift_pairs(grid, axis, shift))
-        total = total + arrived.astype(jnp.float32)
-    return total
-
-
-def scatter_rows(values, order):
+    arrived = yield (
+        [swap_core(values)]
+        + [lax.ppermute(values, "dp", shift_pairs(grid, axis, shift)) for shift in range(1, size)],
+        1,
+    )
+    mine = [values] + arrived[1:]
+    others = yield ([swap_core(piece) for piece in arrived[1:]], 1)
+    others = [arrived[0]] + others
+    position = 1 + sum(1 for other in found if other < axis)
+    places = []
+    for owner in (core, 1 - core):
+        for shift in range(size):
+            place = [None] * 4
+            place[position] = (here[axis] - shift) % size
+            places.append(tuple(place) + (owner,))
+    whole = assemble(mine + others, places, (slots, *grid, 2, rows, columns))
+    return whole.reshape(slots, 2 * math.prod(grid) * rows, columns)
+
+
+def columns_of(values, core):
+    half = values.shape[-1] // 2
+    return lax.dynamic_slice_in_dim(values, core * half, half, values.ndim - 1)
+
+
+def scatter_task(values, order):
     grid = grid_of(lax.axis_size("dp"))
-    rows, columns = values.shape
-    values = values.reshape(*grid, rows // lax.axis_size("dp"), columns)
+    here = place_of(lax.axis_index("dp"), grid)
+    core = lax.axis_index("copy")
+    slots, rows, columns = values.shape
+    values = values.reshape(slots, *grid, rows // math.prod(grid), columns)
     left = [0, 1, 2]
     for axis in order:
-        sent_type = jnp.float32 if axis == order[-1] else jnp.bfloat16
-        values = scatter_axis(values, grid, axis, left.index(axis), sent_type)
+        position, size = (1 + left.index(axis), grid[axis])
+        sent = [
+            to_low(
+                lax.dynamic_index_in_dim(
+                    values, (here[axis] + shift) % size, position, keepdims=False
+                )
+            )
+            for shift in range(1, size)
+        ]
+        arrived = yield (
+            [
+                lax.ppermute(sent[shift - 1], "dp", shift_pairs(grid, axis, shift))
+                for shift in range(1, size)
+            ],
+            1,
+        )
+        total = lax.dynamic_index_in_dim(values, here[axis], position, keepdims=False)
+        for part in arrived:
+            total = total + part.astype(jnp.float32)
+        values = total
         left.remove(axis)
-    return values
-
-
-def share_columns(values):
-    core = lax.axis_index("copy")
-    rows = values.shape[0] // 2
-    mine = lax.dynamic_slice_in_dim(values, core * rows, rows, 0)
-    arrived = swap_core(lax.dynamic_slice_in_dim(values, (1 - core) * rows, rows, 0))
+    half = values.shape[1] // 2
+    mine = lax.dynamic_slice_in_dim(values, core * half, half, 1)
+    (arrived,) = yield (
+        [swap_core(lax.dynamic_slice_in_dim(values, (1 - core) * half, half, 1))],
+        1,
+    )
     first = jnp.where(core == 0, mine, arrived)
     last = jnp.where(core == 0, arrived, mine)
     return (first, last)
 
 
-def columns_of(values, core):
-    half = values.shape[1] // 2
-    return lax.dynamic_slice_in_dim(values, core * half, half, 1)
-
-
-def weight_grad(left_side, right_side):
+def weight_task(left_side, right_side, order, slots=1):
     core = lax.axis_index("copy")
-    arrived = swap_core(product_left(left_side, columns_of(right_side, 1 - core)))
-    return product_left(left_side, columns_of(right_side, core)) + arrived
-
-
-forward_order = (2, 1, 0)
-crossed_order = (1, 2, 0)
-
-
-def rows_whole(values, order):
-    return jnp.concatenate(share_columns(scatter_rows(values, order)), axis=1)
+    (arrived,) = yield ([swap_core(product_left(left_side, columns_of(right_side, 1 - core)))], 1)
+    total = product_left(left_side, columns_of(right_side, core)) + arrived
+    total = total.reshape(slots, total.shape[0] // slots, total.shape[1])
+    first, last = yield from scatter_task(total, order)
+    return jnp.concatenate([first, last], axis=-1)
+
+
+def split_weight_task(left_side, right_side, flow, names):
+    core = lax.axis_index("copy")
+    (arrived,) = yield ([swap_core(product_left(left_side, columns_of(right_side, 1 - core)))], 1)
+    total = (product_left(left_side, columns_of(right_side, core)) + arrived)[None]
+    quarter = total.shape[-1] // 2
+    flow.begin(names[0], scatter_task(total[..., :quarter], forward_order))
+    flow.begin(names[1], scatter_task(total[..., quarter:], crossed_order))
+    return None
+
+
+def shared_task(values, order):
+    core = lax.axis_index("copy")
+    (arrived,) = yield ([swap_core(columns_of(values, 1 - core))], 1)
+    first, last = yield from scatter_task((columns_of(values, core) + arrived)[None], order)
+    return jnp.concatenate([first, last], axis=-1)[0]
 
 
 def attention_scores(query_heads, key_heads, same_image):
@@ -189,7 +313,7 @@
     return jnp.where(same_image[None], raw_scores * score_factor, -1e30)
 
 
-def block_forward(entered, attend_low, expand_low, gain_rows, same_image):
+def block_forward(entered, attend_low, flow, depth, gain_rows, same_image):
     halfway = entered.shape[0]
     normed, first_back = jax.vjp(layer_norm, entered, gain_rows[0], gain_rows[1])
     normed_low = to_low(normed)
@@ -198,6 +322,7 @@
     key_all = jnp.concatenate([key_low, swap_core(key_low)], axis=0)
     value_all = jnp.concatenate([value_low, swap_core(value_low)], axis=0)
     query_low = to_low(product(normed_low, attend_low[0]))
+    query_low, key_all, value_all = flow.tick(query_low, key_all, value_all)
     query_heads = query_low.reshape(halfway, HEADS, HD)
     key_heads = key_all.reshape(SEQ, HEADS, HD)
     value_heads = value_all.reshape(SEQ, HEADS, HD)
@@ -214,11 +339,14 @@
             preferred_element_type=jnp.float32,
         ).reshape(halfway, D)
     )
+    attended = flow.tick(attended)
     middle = entered + product(attended, attend_low[3])
     normed_two, second_back = jax.vjp(layer_norm, middle, gain_rows[2], gain_rows[3])
     normed_two_low = to_low(normed_two)
+    first_expand, last_expand = flow.take("expand%d.0" % depth, "expand%d.1" % depth)
+    expand_low = (first_expand.reshape(-1, D), last_expand.reshape(-1, D))
     hidden, gelu_back = jax.vjp(jax.nn.gelu, product_right(normed_two_low, expand_low[0]))
-    hidden_low = to_low(hidden)
+    hidden_low = flow.tick(to_low(hidden))
     output_rows = middle + product(hidden_low, expand_low[1])
     kept = (
         first_back,
@@ -232,11 +360,12 @@
         normed_two_low,
         gelu_back,
         hidden_low,
+        expand_low,
     )
     return (output_rows, kept)
 
 
-def block_backward(output_grad, kept, attend_low, expand_low, same_image):
+def block_backward(output_grad, kept, attend_low, flow, depth, same_image):
     (
         first_back,
         normed_low,
@@ -249,18 +378,21 @@
         normed_two_low,
         gelu_back,
         hidden_low,
+        expand_low,
     ) = kept
     halfway = attended.shape[0]
+    copies = expand_low[0].shape[0] // D
     upper_low = to_low(output_grad)
-    upper_delta = rows_whole(weight_grad(hidden_low, upper_low), forward_order)
+    flow.begin("upper%d" % depth, weight_task(hidden_low, upper_low, forward_order, copies))
     (hidden_grad,) = gelu_back(product_right(upper_low, expand_low[1]))
-    hidden_grad_low = to_low(hidden_grad)
-    lower_delta = rows_whole(weight_grad(hidden_grad_low, normed_two_low), crossed_order)
+    hidden_grad_low = flow.tick(to_low(hidden_grad))
+    flow.begin("lower%d" % depth, weight_task(hidden_grad_low, normed_two_low, crossed_order, copies))
     middle_extra, gain_three, gain_four = second_back(product(hidden_grad_low, expand_low[0]))
-    middle_grad = output_grad + middle_extra
+    middle_grad = flow.tick(output_grad + middle_extra)
     projected_low = to_low(middle_grad)
-    output_delta = rows_whole(weight_grad(attended, projected_low), forward_order)
+    flow.begin("joined%d" % depth, weight_task(attended, projected_low, forward_order))
     attended_grad = to_low(product_right(projected_low, attend_low[3])).reshape(halfway, HEADS, HD)
+    attended_grad = flow.tick(attended_grad)
     probability = jnp.exp(attention_scores(query_heads, key_heads, same_image) - log_total)
     soft_grad = jnp.einsum(
         "qhd,khd->hqk", attended_grad, value_heads, preferred_element_type=jnp.float32
@@ -273,9 +405,11 @@
         * (soft_grad - jnp.sum(probability * soft_grad, axis=-1, keepdims=True))
         * score_factor
     )
+    score_low, value_part = flow.tick(score_low, value_part)
     key_part = jnp.einsum(
         "hqk,qhd->khd", score_low, query_heads, preferred_element_type=jnp.float32
     )
+    key_part = flow.tick(key_part)
     query_grad = to_low(
         jnp.einsum(
             "hqk,khd->qhd", score_low, key_heads, preferred_element_type=jnp.float32
@@ -289,23 +423,18 @@
     key_grad = to_low(
         key_part[:halfway] + swap_core(to_low(key_part[halfway:])).astype(jnp.float32)
     )
+    query_grad, key_grad, value_grad = flow.tick(query_grad, key_grad, value_grad)
+    flow.begin("value%d" % depth, weight_task(normed_low, value_grad, crossed_order))
+    flow.begin("key%d" % depth, weight_task(normed_low, key_grad, crossed_order))
+    flow.begin("query%d" % depth, weight_task(normed_low, query_grad, forward_order))
     normed_grad = (
         product_right(query_grad, attend_low[0])
         + product_right(key_grad, attend_low[1])
         + product_right(value_grad, attend_low[2])
     )
     entered_extra, gain_one, gain_two = first_back(normed_grad)
-    attend_delta = jnp.stack(
-        [
-            rows_whole(weight_grad(normed_low, query_grad), forward_order),
-            rows_whole(weight_grad(normed_low, key_grad), crossed_order),
-            rows_whole(weight_grad(normed_low, value_grad), crossed_order),
-            output_delta,
-        ]
-    )
-    expand_delta = jnp.stack([lower_delta, upper_delta])
     gain_delta = jnp.stack([gain_one, gain_two, gain_three, gain_four])
-    return (middle_grad + entered_extra, attend_delta, expand_delta, gain_delta)
+    return (flow.tick(middle_grad + entered_extra), gain_delta)
 
 
 def fine(left_side, right_side):
@@ -424,26 +553,29 @@
 ):
     everywhere = ("dp", "copy")
     core = lax.axis_index("copy")
-    encoder_turned = lax.all_gather(to_low(encoder_table).T, everywhere, axis=0, tiled=True)
-    attend_low, expand_low = (to_low(attend_weight), to_low(expand_weight))
-    attend_all, expand_all = ([], [])
-    for depth_index in range(2):
-        attend_all.append(
-            lax.all_gather(
-                attend_low[4 * depth_index : 4 * depth_index + 4], everywhere, axis=1, tiled=True
-            )
-        )
-        expand_all.append(
-            lax.all_gather(
-                expand_low[2 * depth_index : 2 * depth_index + 2], everywhere, axis=1, tiled=True
-            )
-        )
-    condition_all = lax.all_gather(to_low(condition_weight), everywhere, axis=0, tiled=True)
-    head_turned = lax.all_gather(to_low(head_table).T, everywhere, axis=0, tiled=True)
-    modulate_all = lax.all_gather(to_low(modulate_weight), everywhere, axis=0, tiled=True)
-    dense_all = lax.all_gather(to_low(dense_weight), everywhere, axis=1, tiled=True)
-    encoder_all = encoder_turned.T
-    head_all = head_turned.T
+    flow = Flow()
+    attend_low, expand_low, dense_low = (
+        to_low(attend_weight),
+        to_low(expand_weight),
+        to_low(dense_weight),
+    )
+    rows = attend_weight.shape[1]
+    table_slots = -(-encoder_table.shape[0] // D)
+    encoder_turned = padded(to_low(encoder_table).T, rows, table_slots * D)
+    encoder_turned = encoder_turned.reshape(rows, table_slots, D).transpose(1, 0, 2)
+    flow.begin(
+        "table",
+        gather_task(jnp.concatenate([encoder_turned, attend_low[0:1]], axis=0), forward_order),
+    )
+    flow.begin("attend0", gather_task(attend_low[1:4], crossed_order))
+    flow.tick()
+    flow.begin("expand0.0", gather_task(expand_low[0].reshape(-1, rows, D), forward_order))
+    flow.begin("expand0.1", gather_task(expand_low[1].reshape(-1, rows, D), crossed_order))
+    table_part, attend_part = flow.take("table", "attend0")
+    attend_all = [[table_part[-1], attend_part[0], attend_part[1], attend_part[2]]]
+    encoder_all = jnp.concatenate([table_part[i] for i in range(table_slots)], axis=1).T[
+        : encoder_table.shape[0]
+    ]
     halfway = SEQ // 2
     offset = core * halfway
 
@@ -457,6 +589,8 @@
     buffer_row = own_first(buffer_flags[0])
     masked_row = own_first(loss_mask[0])
     weight_row = (masked_row * (1 - buffer_row)).astype(jnp.float32)
+    flow.begin("attend1.0", gather_task(attend_low[4:6], forward_order))
+    flow.begin("attend1.1", gather_task(attend_low[6:8], crossed_order))
     token_count = sum_all(jnp.sum(weight_row))
     own_patch = patch_seq[:halfway]
     buffer_on = buffer_row[:halfway, None] > 0
@@ -478,14 +612,43 @@
     state_rows = entered
     kept_all = []
     for depth_index in range(2):
+        if depth_index == 1:
+            attend_all.append([m for pair in flow.take("attend1.0", "attend1.1") for m in pair])
         state_rows, kept = block_forward(
             state_rows,
             attend_all[depth_index],
-            expand_all[depth_index],
+            flow,
+            depth_index,
             gain_rows[4 * depth_index : 4 * depth_index + 4],
             same_image,
         )
         kept_all.append(kept)
+        if depth_index == 0:
+            flow.begin("expand1.0", gather_task(expand_low[2].reshape(-1, rows, D), forward_order))
+            flow.begin("expand1.1", gather_task(expand_low[3].reshape(-1, rows, D), crossed_order))
+            state_rows = flow.tick(state_rows)
+            wide = dense_weight.shape[1]
+            flow.begin(
+                "head",
+                gather_task(
+                    jnp.stack(
+                        [
+                            padded(to_low(condition_weight), wide, HW),
+                            padded(to_low(head_table).T, wide, HW),
+                        ]
+                    ),
+                    forward_order,
+                ),
+            )
+            flow.begin("dense", gather_task(dense_low, crossed_order))
+    middle_rows = modulate_weight.shape[1] // 2
+    modulate_low = to_low(modulate_weight)[None]
+    flow.begin("modulate.0", gather_task(modulate_low[..., :middle_rows], forward_order))
+    flow.begin("modulate.1", gather_task(modulate_low[..., middle_rows:], crossed_order))
+    state_rows = flow.tick(state_rows)
+    head_part, dense_all = flow.take("head", "dense")
+    condition_all = head_part[0][:, :D]
+    head_all = head_part[1][:, : head_table.shape[0]].T
     latent, third_back = jax.vjp(layer_norm, state_rows, gain_rows[8], gain_rows[9])
     latent_low = to_low(latent)
     condition_own = to_low(product_right(latent_low, condition_all))
@@ -502,7 +665,9 @@
         feature_low, head_all[PATCH : PATCH + FREQ]
     )
     activated, silu_back = jax.vjp(jax.nn.silu, summed)
-    activated_low = to_low(activated)
+    activated_low = flow.tick(to_low(activated))
+    modulate_halves = [member[0] for member in flow.take("modulate.0", "modulate.1")]
+    modulate_all = jnp.concatenate(modulate_halves, axis=1)
     modulation = product_right(activated_low, modulate_all)
     inner_rows, inner_back = jax.vjp(first_modulate, lifted, modulation)
     inner_low = to_low(inner_rows)
@@ -520,46 +685,35 @@
         product(predicted_grad, head_all[PATCH + FREQ :])
     )
     branch_low = to_low(branch_grad)
-    second_delta = rows_whole(weight_grad(expanded_low, branch_low), forward_order)
+    flow.begin("dense.1", weight_task(expanded_low, branch_low, forward_order))
     (expanded_grad,) = dense_back(product_right(branch_low, dense_all[1]))
-    expanded_grad_low = to_low(expanded_grad)
-    first_delta = rows_whole(weight_grad(inner_low, expanded_grad_low), crossed_order)
+    expanded_grad_low = flow.tick(to_low(expanded_grad))
+    flow.begin("dense.0", weight_task(inner_low, expanded_grad_low, crossed_order))
     lifted_extra, modulation_extra = inner_back(product_right(expanded_grad_low, dense_all[0]))
-    modulation_low = to_low(modulation_grad + modulation_extra)
-    modulate_half = weight_grad(modulation_low, activated_low)
-    quarter = modulate_half.shape[1] // 2
-    modulate_left = share_columns(scatter_rows(modulate_half[:, :quarter], forward_order))
-    modulate_right = share_columns(scatter_rows(modulate_half[:, quarter:], crossed_order))
-    modulate_delta = jnp.concatenate(
-        [modulate_left[0], modulate_right[0], modulate_left[1], modulate_right[1]], axis=1
+    modulation_low = flow.tick(to_low(modulation_grad + modulation_extra))
+    flow.begin(
+        "spread",
+        split_weight_task(modulation_low, activated_low, flow, ("modulate.2", "modulate.3")),
     )
     (summed_grad,) = silu_back(product(modulation_low, modulate_all))
     time_turned = product_left(to_low(summed_grad), feature_low)
     lift_turned = product_left(to_low(lifted_grad + lifted_extra), noisy_low)
     head_turned_grad = jnp.concatenate([lift_turned, time_turned, final_turned], axis=1)
-    head_delta = rows_whole(
-        columns_of(head_turned_grad, core) + swap_core(columns_of(head_turned_grad, 1 - core)),
-        forward_order,
-    ).T
+    flow.begin("head_table", shared_task(head_turned_grad, forward_order))
     condition_grad = to_low(
         summed_grad[:halfway] + swap_core(to_low(summed_grad[halfway:])).astype(jnp.float32)
     )
-    condition_delta = rows_whole(weight_grad(condition_grad, latent_low), crossed_order)
+    condition_grad = flow.tick(condition_grad)
+    flow.begin("condition", weight_task(condition_grad, latent_low, crossed_order))
     state_grad, gain_nine, gain_ten = third_back(product(condition_grad, condition_all))
-    attend_parts = [None, None]
-    expand_parts = [None, None]
     gain_parts = [None, None]
     for depth_index in (1, 0):
-        (
-            state_grad,
-            attend_parts[depth_index],
-            expand_parts[depth_index],
-            gain_parts[depth_index],
-        ) = block_backward(
+        state_grad, gain_parts[depth_index] = block_backward(
             state_grad,
             kept_all[depth_index],
             attend_all[depth_index],
-            expand_all[depth_index],
+            flow,
+            depth_index,
             same_image,
         )
     embedded_grad, token_grad, position_grad = entry_back(state_grad)
@@ -580,9 +734,8 @@
         [position_grad, lax.dynamic_slice_in_dim(small_delta, core * small_half, small_half, 0)],
         axis=0,
     ).T
-    encoder_first_half, encoder_last_half = share_columns(
-        scatter_rows(encoder_half, crossed_order)
-    )
+    flow.begin("encoder", scatter_task(encoder_half[None], crossed_order))
+    encoder_first_half, encoder_last_half = (m[0] for m in flow.take("encoder")[0])
     encoder_delta = jnp.concatenate(
         [
             encoder_first_half[:, halfway:],
@@ -592,14 +745,23 @@
         ],
         axis=1,
     ).T
+    flow.take("value0", "key0", "query0")
+    results = flow.results
+    attend_parts, expand_parts = ([], [])
+    for depth_index in range(2):
+        for name in ("query", "key", "value", "joined"):
+            attend_parts.append(results[name + str(depth_index)][0])
+        for name in ("lower", "upper"):
+            expand_parts.append(results[name + str(depth_index)].reshape(-1, D))
+    left_parts, right_parts = (results["modulate.2"], results["modulate.3"])
     reduced = (
-        jnp.concatenate(attend_parts, axis=0),
-        jnp.concatenate(expand_parts, axis=0),
-        jnp.stack([first_delta, second_delta]),
-        modulate_delta,
-        condition_delta,
+        jnp.stack(attend_parts),
+        jnp.stack(expand_parts),
+        jnp.stack([results["dense.0"][0], results["dense.1"][0]]),
+        jnp.concatenate([left_parts[0], right_parts[0], left_parts[1], right_parts[1]], axis=-1)[0],
+        results["condition"][0],
         encoder_delta,
-        head_delta,
+        results["head_table"].T,
     )
     squares = sum((jnp.sum(member * member) for member in reduced))
     totals = sum_all(jnp.stack([squares, loss_local]))

time: 1960 us -> 3780 us (1.93)
  Pallas kernels: 0 us -> 2130 us
  waiting for transfers between devices: 735 us -> 468 us
  matrix products: 609 us -> 449 us
  starting transfers between devices: 147 us -> 251 us
  local copies, waits for them, and re-layouts: 91 us -> 137 us
  blocking collectives: 164 us -> 118 us
    pallas_call x0 -> x36, Pallas kernels: none -> 2130 us  [assemble(): pl.pallas_call(kernel, out_shape=jax.ShapeDtypeStruct(shape, pieces[0].dt...]
    all_gather x8 -> x0, waiting for transfers between devices: 303 us -> none  [the longest x2 92.1 us: per_device(): lax.all_gather(attend_low[4 * depth_index:4 * depth_index + 4], everywher...]
    dot_general x2, matrix products: 93.2 us -> 5.96 us  [block_backward(): jnp.einsum('hqk,qhd->khd', score_low, query_heads, preferred_element_type...]
    dot_general x2, matrix products: 89.3 us -> 12.5 us  [block_backward(): jnp.einsum('hqk,khd->qhd', score_low, key_heads, preferred_element_type=j...]
    ppermute x95 -> x155, starting transfers between devices: 117 us -> 192 us  [the longest x95 117 us: scatter_task(): lax.ppermute(sent[shift - 1], 'dp', shift_pairs(grid, axis, shift))]
    sub x0 -> x2, matrix products: none -> 60.1 us  [block_backward(): soft_grad - jnp.sum(probability * soft_grad, axis=-1, keepdims=True)]
    all_gather x1 -> x0, blocking collectives: 46.1 us -> none  [per_device(): lax.all_gather(to_low(head_table).T, everywhere, axis=0, tiled=True)]
    ppermute x95 -> x155, waiting for transfers between devices: 291 us -> 332 us  [the longest x95 201 us: scatter_task(): lax.ppermute(sent[shift - 1], 'dp', shift_pairs(grid, axis, shift))]
  transfers between devices with their start and end apart: 167 -> 243, of which waited for: 97 -> 80; matrix products, arithmetic and copies ran while one was open for 33% -> 13% of each run, Pallas kernels for 0% -> 44%
where the time goes in v2:
time: 3780 us; the launch traced here: 3770 us
  Pallas kernels  2130 us (56%)
  waiting for transfers between devices  468 us (12%)
  matrix products  449 us (12%)
  starting transfers between devices  251 us (7%)
  other arithmetic  183 us (5%)
  local copies, waits for them, and re-layouts  137 us (4%)
  blocking collectives  118 us (3%)
    pallas_call x36, Pallas kernels, assemble(): pl.pallas_call(kernel, out_shape=jax.ShapeDtypeStruct(shape, pieces[0].dt...  2130 us
    ppermute x95, waiting for transfers between devices, scatter_task(): lax.ppermute(sent[shift - 1], 'dp', shift_pairs(grid, axis, shift))  201 us
    ppermute x60, waiting for transfers between devices, gather_task(): lax.ppermute(values, 'dp', shift_pairs(grid, axis, shift))  131 us
    all_to_all x1, blocking collectives, muon_steps(): lax.all_to_all(jnp.stack(sending), ('dp', 'copy'), 0, 0)  118 us
    ppermute x95, starting transfers between devices, scatter_task(): lax.ppermute(sent[shift - 1], 'dp', shift_pairs(grid, axis, shift))  117 us
    all_to_all x1, waiting for transfers between devices, muon_steps(): lax.all_to_all(result.reshape(devices, highest, widest), ('dp', 'copy'),...  104 us
    dot_general x37, matrix products, product_left(): lax.dot_general(left_side, right_side, (((0,), (0,)), ((), ())), preferre...  92.1 us
    dot_general x21, matrix products, product(): return jnp.dot(left_side, right_side, preferred_element_type=jnp.float32)  79.3 us
  transfers between devices with their start and end apart: 243, of which 80 were waited for; matrix products, arithmetic and copies ran while one was open for 13% of the time, Pallas kernels for 44%

profile of v2, /device:TPU:0, one launch (start us, length us, event | category | flops | bytes accessed | tf_op | source)
XLA Modules:
  0.0 3768.8 jit_solution(11966420468758142665)
XLA Ops:
  110.2 28.6 shard_map.378.refs_0_
  139.4 28.6 shard_map.377.refs_0_
  206.6 37.6 shard_map.382.refs_0_
  245.8 37.5 shard_map.381.refs_0_
  312.1 109.0 %shard_map.383 = bf16[3,4,2,2,2,24,768]{6,5,4,3,2,1,0:T(8,128)(2,1)} custom-call(s32[8]{0:T(128)} %stack.140.index_ref, bf16[3,4,2,24,768]{4,3,2,1,0:T(8,128)(2,1)} %shard_map.377.refs_0_, bf16[3,4,2,24,768]{4,3,2,1,0:T(8,128)(2,1)} %collective-permute-done.15.refs_1_, bf16[3,4,2,24,768]{4,3,2,1,0:T(8,128)(2,1)} %copy-done.196, ...), custom_call_target="tpu_custom_call" | custom-call | bytes 7077888 | tf_op jit(solution)/shard_map/pallas_call | solution.py:157
  427.4 109.0 %shard_map.384 = bf16[3,4,2,2,2,24,768]{6,5,4,3,2,1,0:T(8,128)(2,1)} custom-call(s32[8]{0:T(128)} %stack.150.index_ref, bf16[3,4,2,24,768]{4,3,2,1,0:T(8,128)(2,1)} %shard_map.378.refs_0_, bf16[3,4,2,24,768]{4,3,2,1,0:T(8,128)(2,1)} %copy-done.194, bf16[3,4,2,24,768]{4,3,2,1,0:T(8,128)(2,1)} %copy-done.195, bf16[3,4,2,24,768]{4,3,2,1,0:T(8,128)(2,1)} %copy-done.197), custom_call_target="tpu_custom_call" | custom-call | bytes 7077888 | tf_op jit(solution)/shard_map/pallas_call | solution.py:157
  636.7 144.7 %shard_map.387 = bf16[4,4,2,2,2,24,768]{6,5,4,3,2,1,0:T(8,128)(2,1)} custom-call(s32[8]{0:T(128)} %stack.140.index_ref, bf16[4,4,2,24,768]{4,3,2,1,0:T(8,128)(2,1)} %shard_map.381.refs_0_, bf16[4,4,2,24,768]{4,3,2,1,0:T(8,128)(2,1)} %copy-done.154, bf16[4,4,2,24,768]{4,3,2,1,0:T(8,128)(2,1)} %collective-permute-done.22.refs_2_, ...), custom_call_target="tpu_custom_call" | custom-call | bytes 9437184 | tf_op jit(solution)/shard_map/pallas_call | solution.py:157
  781.4 144.7 %shard_map.390 = bf16[4,4,2,2,2,24,768]{6,5,4,3,2,1,0:T(8,128)(2,1)} custom-call(s32[8]{0:T(128)} %stack.150.index_ref, bf16[4,4,2,24,768]{4,3,2,1,0:T(8,128)(2,1)} %shard_map.382.refs_0_, bf16[4,4,2,24,768]{4,3,2,1,0:T(8,128)(2,1)} %copy-done.151, bf16[4,4,2,24,768]{4,3,2,1,0:T(8,128)(2,1)} %copy-done.153, ...), custom_call_target="tpu_custom_call" | custom-call | bytes 9437184 | tf_op jit(solution)/shard_map/pallas_call | solution.py:157
  1006.5 73.3 %shard_map.391 = bf16[2,4,2,2,2,24,768]{6,5,4,3,2,1,0:T(8,128)(2,1)} custom-call(s32[8]{0:T(128)} %stack.140.index_ref, bf16[2,4,2,24,768]{4,3,2,1,0:T(8,128)(2,1)} %shard_map.388.refs_0_, bf16[2,4,2,24,768]{4,3,2,1,0:T(8,128)(2,1)} %copy-done.209, bf16[2,4,2,24,768]{4,3,2,1,0:T(8,128)(2,1)} %copy-done.210, bf16[2,4,2,24,768]{4,3,2,1,0:T(8,128)(2,1)} %copy-done.211), custom_call_target="tpu_custom_call" | custom-call | bytes 4718592 | tf_op jit(solution)/shard_map/pallas_call | solution.py:157
  1083.1 73.3 %shard_map.392 = bf16[2,4,2,2,2,24,768]{6,5,4,3,2,1,0:T(8,128)(2,1)} custom-call(s32[8]{0:T(128)} %stack.150.index_ref, bf16[2,4,2,24,768]{4,3,2,1,0:T(8,128)(2,1)} %shard_map.389.refs_0_, bf16[2,4,2,24,768]{4,3,2,1,0:T(8,128)(2,1)} %collective-permute-done.41.refs_1_, bf16[2,4,2,24,768]{4,3,2,1,0:T(8,128)(2,1)} %collective-permute-done.40.refs_2_, ...), custom_call_target="tpu_custom_call" | custom-call | bytes 4718592 | tf_op jit(solution)/shard_map/pallas_call | solution.py:157
  1229.2 37.5 shard_map.397.refs_0_
  1268.3 37.5 shard_map.396.refs_0_
  1387.8 33.5 shard_map.400.refs_0_
  1422.3 33.5 shard_map.399.refs_0_
  1486.9 144.7 %shard_map.401 = bf16[4,4,2,2,2,24,768]{6,5,4,3,2,1,0:T(8,128)(2,1)} custom-call(s32[8]{0:T(128)} %stack.140.index_ref, bf16[4,4,2,24,768]{4,3,2,1,0:T(8,128)(2,1)} %shard_map.396.refs_0_, bf16[4,4,2,24,768]{4,3,2,1,0:T(8,128)(2,1)} %collective-permute-done.61.refs_1_, bf16[4,4,2,24,768]{4,3,2,1,0:T(8,128)(2,1)} %collective-permute-done.60.refs_2_, ...), custom_call_target="tpu_custom_call" | custom-call | bytes 9437184 | tf_op jit(solution)/shard_map/pallas_call | solution.py:157
  1631.7 144.7 %shard_map.403 = bf16[4,4,2,2,2,24,768]{6,5,4,3,2,1,0:T(8,128)(2,1)} custom-call(s32[8]{0:T(128)} %stack.150.index_ref, bf16[4,4,2,24,768]{4,3,2,1,0:T(8,128)(2,1)} %shard_map.397.refs_0_, bf16[4,4,2,24,768]{4,3,2,1,0:T(8,128)(2,1)} %collective-permute-done.63.refs_1_, bf16[4,4,2,24,768]{4,3,2,1,0:T(8,128)(2,1)} %collective-permute-done.62.refs_2_, ...), custom_call_target="tpu_custom_call" | custom-call | bytes 9437184 | tf_op jit(solution)/shard_map/pallas_call | solution.py:157
  1790.2 128.9 %shard_map.402 = bf16[2,4,2,2,2,32,1024]{6,5,4,3,2,1,0:T(8,128)(2,1)} custom-call(s32[8]{0:T(128)} %stack.140.index_ref, bf16[2,4,2,32,1024]{4,3,2,1,0:T(8,128)(2,1)} %shard_map.399.refs_0_, bf16[2,4,2,32,1024]{4,3,2,1,0:T(8,128)(2,1)} %collective-permute-done.69.refs_1_, bf16[2,4,2,32,1024]{4,3,2,1,0:T(8,128)(2,1)} %copy-done.189, ...), custom_call_target="tpu_custom_call" | custom-call | bytes 8388608 | tf_op jit(solution)/shard_map/pallas_call | solution.py:157
  1932.6 21.7 shard_map.405.refs_0_
  1955.0 21.7 shard_map.404.refs_0_
  1993.8 41.5 %shard_map.407.refs_0_ = bf16[1,4,2,160,512]{4,3,2,1,0:T(8,128)(2,1)} custom-call(s32[2]{0:T(128)} %pad_add_fusion.3.index_ref, bf16[1,4,160,512]{3,2,1,0:T(8,128)(2,1)} %shard_map.405.refs_0_, bf16[1,4,160,512]{3,2,1,0:T(8,128)(2,1)} %copy-done.208), custom_call_target="tpu_custom_call" | custom-call | bytes 2621440 | tf_op jit(solution)/shard_map/pallas_call | solution.py:157
  2036.6 41.5 %shard_map.406.refs_0_ = bf16[1,4,2,160,512]{4,3,2,1,0:T(8,128)(2,1)} custom-call(s32[2]{0:T(128)} %pad_add_fusion.1.index_ref, bf16[1,4,160,512]{3,2,1,0:T(8,128)(2,1)} %shard_map.404.refs_0_, bf16[1,4,160,512]{3,2,1,0:T(8,128)(2,1)} %copy-done.207), custom_call_target="tpu_custom_call" | custom-call | bytes 2621440 | tf_op jit(solution)/shard_map/pallas_call | solution.py:157
  2084.3 24.4 collective-permute-start.90
  2123.8 129.0 %shard_map.410 = bf16[2,4,2,2,2,32,1024]{6,5,4,3,2,1,0:T(8,128)(2,1)} custom-call(s32[8]{0:T(128)} %stack.150.index_ref, bf16[2,4,2,32,1024]{4,3,2,1,0:T(8,128)(2,1)} %shard_map.400.refs_0_, bf16[2,4,2,32,1024]{4,3,2,1,0:T(8,128)(2,1)} %collective-permute-done.71.refs_1_, bf16[2,4,2,32,1024]{4,3,2,1,0:T(8,128)(2,1)} %collective-permute-done.70.refs_2_, ...), custom_call_target="tpu_custom_call" | custom-call | bytes 8388608 | tf_op jit(solution)/shard_map/pallas_call | solution.py:157
  2259.7 160.6 %shard_map.408 = bf16[1,4,2,2,2,160,512]{6,5,4,3,2,1,0:T(8,128)(2,1)} custom-call(s32[8]{0:T(128)} %stack.140.index_ref, bf16[1,4,2,160,512]{4,3,2,1,0:T(8,128)(2,1)} %shard_map.406.refs_0_, bf16[1,4,2,160,512]{4,3,2,1,0:T(8,128)(2,1)} %collective-permute-done.84.refs_1_, bf16[1,4,2,160,512]{4,3,2,1,0:T(8,128)(2,1)} %collective-permute-done.83.refs_2_, ...), custom_call_target="tpu_custom_call" | custom-call | bytes 10485760 | tf_op jit(solution)/shard_map/pallas_call | solution.py:157
  2420.3 160.6 %shard_map.409 = bf16[1,4,2,2,2,160,512]{6,5,4,3,2,1,0:T(8,128)(2,1)} custom-call(s32[8]{0:T(128)} %stack.150.index_ref, bf16[1,4,2,160,512]{4,3,2,1,0:T(8,128)(2,1)} %shard_map.407.refs_0_, bf16[1,4,2,160,512]{4,3,2,1,0:T(8,128)(2,1)} %collective-permute-done.86.refs_1_, bf16[1,4,2,160,512]{4,3,2,1,0:T(8,128)(2,1)} %copy-done.150, ...), custom_call_target="tpu_custom_call" | custom-call | bytes 10485760 | tf_op jit(solution)/shard_map/pallas_call | solution.py:157
  2851.5 20.9 collective-permute-done.118
  2942.6 27.8 multiply_convert_fusion.1
  3101.9 21.6 collective-permute-done.167
  3153.5 22.9 collective-permute-done.180
  3193.2 32.3 multiply_convert_fusion
  3405.1 118.2 %all_to_all.10 = bf16[32,80,1024]{2,1,0:T(8,128)(2,1)S(1)} all-to-all(bf16[32,80,1024]{2,1,0:T(8,128)(2,1)S(1)} %broadcast_dynamic-update-slice_fusion), channel_id=1, replica_groups=mesh['dp'=16,'copy'=2] {'dp','copy'}, dimensions={0} | all-to-all | bytes 10485760 | tf_op jit(solution)/shard_map/all_to_all | solution.py:485
  3646.2 104.1 %all-to-all-done.1 = bf16[32,80,1024]{2,1,0:T(8,128)(2,1)} async-done(((bf16[32,80,1024]{2,1,0:T(8,128)(2,1)}), bf16[32,80,1024]{2,1,0:T(8,128)(2,1)}, u32[]{:S(2)}, u32[]{:S(2)}) %all-to-all-start.1) | async-done | bytes 5242912 | tf_op jit(solution)/shard_map/all_to_all | solution.py:498
  (1864 shorter events, 1439.7 us)
Async XLA Ops:
  108.3 81.1 %collective-permute-start.19 = (bf16[4,4,24,768]{3,2,1,0:T(8,128)(2,1)}, bf16[4,4,24,768]{3,2,1,0:T(8,128)(2,1)S(1)}, u32[]{:S(2)}, u32[]{:S(2)}) collective-permute-start(bf16[4,4,24,768]{3,2,1,0:T(8,128)(2,1)} %shard_map.380.refs_0_), channel_id=1, source_target_pairs={{0,2},{2,0},{4,6},{6,4},{8,10},{10,8},{12,14},{14,12},{16,18},{18,... | collective-permute-start | bytes 1769480 | tf_op jit(solution)/shard_map/ppermute | solution.py:207
  138.8 66.6 %collective-permute-start.17 = (bf16[3,4,2,24,768]{4,3,2,1,0:T(8,128)(2,1)}, bf16[3,4,2,24,768]{4,3,2,1,0:T(8,128)(2,1)S(1)}, u32[]{:S(2)}, u32[]{:S(2)}) collective-permute-start(bf16[3,4,2,24,768]{4,3,2,1,0:T(8,128)(2,1)} %shard_map.378.refs_0_), channel_id=1, source_target_pairs={{0,4},{2,6},{4,0},{6,2},{8,12},{10,14},{12,8},{14,10},{16,20},{18,... | collective-permute-start | bytes 2654216 | tf_op jit(solution)/shard_map/ppermute | solution.py:221
  139.4 66.0 %collective-permute-start.16 = (bf16[3,4,2,24,768]{4,3,2,1,0:T(8,128)(2,1)}, bf16[3,4,2,24,768]{4,3,2,1,0:T(8,128)(2,1)S(1)}, u32[]{:S(2)}, u32[]{:S(2)}) collective-permute-start(bf16[3,4,2,24,768]{4,3,2,1,0:T(8,128)(2,1)} %shard_map.378.refs_0_), channel_id=1, source_target_pairs={{0,1},{1,0},{2,3},{3,2},{4,5},{5,4},{6,7},{7,6},{8,9},{9,8},{10,11... | collective-permute-start | bytes 2654216 | tf_op jit(solution)/shard_map/ppermute | solution.py:118
  205.4 81.3 %collective-permute-start.20 = (bf16[3,4,2,24,768]{4,3,2,1,0:T(8,128)(2,1)}, bf16[3,4,2,24,768]{4,3,2,1,0:T(8,128)(2,1)}, u32[]{:S(2)}, u32[]{:S(2)}) collective-permute-start(bf16[3,4,2,24,768]{4,3,2,1,0:T(8,128)(2,1)} %collective-permute-done.15.refs_1_), channel_id=1, source_target_pairs={{0,1},{1,0},{2,3},{3,2},{4,5},{5,4},{6,7},{7,6},{8,9},{9,8},{10,11... | collective-permute-start | bytes 2654216 | tf_op jit(solution)/shard_map/ppermute | solution.py:118
  291.7 257.7 %collective-permute-start.35 = (bf16[2,24,768]{2,1,0:T(8,128)(2,1)}, bf16[2,24,768]{2,1,0:T(8,128)(2,1)}, u32[]{:S(2)}, u32[]{:S(2)}) collective-permute-start(bf16[2,24,768]{2,1,0:T(8,128)(2,1)} %get-tuple-element.724.refs_0_), channel_id=1, source_target_pairs={{0,24},{2,26},{4,28},{6,30},{8,0},{10,2},{12,4},{14,6},{16,8},{18,... | collective-permute-start | bytes 221192 | tf_op jit(solution)/shard_map/ppermute | solution.py:207
  561.0 429.7 %collective-permute-start.46 = (bf16[4,24,768]{2,1,0:T(8,128)(2,1)S(1)}, bf16[4,24,768]{2,1,0:T(8,128)(2,1)S(1)}, u32[]{:S(2)}, u32[]{:S(2)}) collective-permute-start(bf16[4,24,768]{2,1,0:T(8,128)(2,1)S(1)} %bitcast.961), channel_id=1, source_target_pairs={{0,24},{2,26},{4,28},{6,30},{8,0},{10,2},{12,4},{14,6},{16,8},{18,... | collective-permute-start | bytes 442376 | tf_op jit(solution)/shard_map/ppermute | solution.py:207
  565.4 426.1 %collective-permute-start.45 = (bf16[4,24,768]{2,1,0:T(8,128)(2,1)S(1)}, bf16[4,24,768]{2,1,0:T(8,128)(2,1)}, u32[]{:S(2)}, u32[]{:S(2)}) collective-permute-start(bf16[4,24,768]{2,1,0:T(8,128)(2,1)S(1)} %bitcast.962), channel_id=1, source_target_pairs={{0,16},{2,18},{4,20},{6,22},{8,24},{10,26},{12,28},{14,30},{16,0},... | collective-permute-start | bytes 442376 | tf_op jit(solution)/shard_map/ppermute | solution.py:207
  565.4 426.1 %collective-permute-start.44 = (bf16[4,24,768]{2,1,0:T(8,128)(2,1)S(1)}, bf16[4,24,768]{2,1,0:T(8,128)(2,1)}, u32[]{:S(2)}, u32[]{:S(2)}) collective-permute-start(bf16[4,24,768]{2,1,0:T(8,128)(2,1)S(1)} %bitcast.963), channel_id=1, source_target_pairs={{0,8},{2,10},{4,12},{6,14},{8,16},{10,18},{12,20},{14,22},{16,24},... | collective-permute-start | bytes 442376 | tf_op jit(solution)/shard_map/ppermute | solution.py:207
  582.6 343.5 %collective-permute-start.37 = (bf16[2,4,24,768]{3,2,1,0:T(8,128)(2,1)}, bf16[2,4,24,768]{3,2,1,0:T(8,128)(2,1)}, u32[]{:S(2)}, u32[]{:S(2)}) collective-permute-start(bf16[2,4,24,768]{3,2,1,0:T(8,128)(2,1)} %shard_map.386.refs_0_), channel_id=1, source_target_pairs={{0,2},{2,0},{4,6},{6,4},{8,10},{10,8},{12,14},{14,12},{16,18},{18,... | collective-permute-start | bytes 884744 | tf_op jit(solution)/shard_map/ppermute | solution.py:207
  593.9 332.2 %collective-permute-start.36 = (bf16[2,4,24,768]{3,2,1,0:T(8,128)(2,1)}, bf16[2,4,24,768]{3,2,1,0:T(8,128)(2,1)}, u32[]{:S(2)}, u32[]{:S(2)}) collective-permute-start(bf16[2,4,24,768]{3,2,1,0:T(8,128)(2,1)} %shard_map.385.refs_0_), channel_id=1, source_target_pairs={{0,4},{2,6},{4,0},{6,2},{8,12},{10,14},{12,8},{14,10},{16,20},{18,... | collective-permute-start | bytes 884744 | tf_op jit(solution)/shard_map/ppermute | solution.py:207
  994.7 212.4 %collective-permute-start.59 = (bf16[2,32,1024]{2,1,0:T(8,128)(2,1)}, bf16[2,32,1024]{2,1,0:T(8,128)(2,1)}, u32[]{:S(2)}, u32[]{:S(2)}) collective-permute-start(bf16[2,32,1024]{2,1,0:T(8,128)(2,1)} %convert_element_type.1970.refs_0_), channel_id=1, source_target_pairs={{0,24},{2,26},{4,28},{6,30},{8,0},{10,2},{12,4},{14,6},{16,8},{18,... | collective-permute-start | bytes 393224 | tf_op jit(solution)/shard_map/ppermute | solution.py:207
  1163.1 54.2 %collective-permute-start.51 = (bf16[512,768]{1,0:T(8,128)(2,1)}, bf16[512,768]{1,0:T(8,128)(2,1)}, u32[]{:S(2)}, u32[]{:S(2)}) collective-permute-start(bf16[512,768]{1,0:T(8,128)(2,1)} %convolution_convert_fusion.3), channel_id=1, source_target_pairs={{0,1},{1,0},{2,3},{3,2},{4,5},{5,4},{6,7},{7,6},{8,9},{9,8},{10,11... | collective-permute-start | bytes 2359304 | tf_op jit(solution)/shard_map/ppermute | solution.py:118
  1266.7 121.1 %collective-permute-start.63 = (bf16[4,4,2,24,768]{4,3,2,1,0:T(8,128)(2,1)}, bf16[4,4,2,24,768]{4,3,2,1,0:T(8,128)(2,1)}, u32[]{:S(2)}, u32[]{:S(2)}) collective-permute-start(bf16[4,4,2,24,768]{4,3,2,1,0:T(8,128)(2,1)} %shard_map.397.refs_0_), channel_id=1, source_target_pairs={{0,4},{2,6},{4,0},{6,2},{8,12},{10,14},{12,8},{14,10},{16,20},{18,... | collective-permute-start | bytes 3538952 | tf_op jit(solution)/shard_map/ppermute | solution.py:221
  1268.3 119.5 %collective-permute-start.62 = (bf16[4,4,2,24,768]{4,3,2,1,0:T(8,128)(2,1)}, bf16[4,4,2,24,768]{4,3,2,1,0:T(8,128)(2,1)}, u32[]{:S(2)}, u32[]{:S(2)}) collective-permute-start(bf16[4,4,2,24,768]{4,3,2,1,0:T(8,128)(2,1)} %shard_map.397.refs_0_), channel_id=1, source_target_pairs={{0,1},{1,0},{2,3},{3,2},{4,5},{5,4},{6,7},{7,6},{8,9},{9,8},{10,11... | collective-permute-start | bytes 3538952 | tf_op jit(solution)/shard_map/ppermute | solution.py:118
  1305.9 81.9 %collective-permute-start.61 = (bf16[4,4,2,24,768]{4,3,2,1,0:T(8,128)(2,1)}, bf16[4,4,2,24,768]{4,3,2,1,0:T(8,128)(2,1)}, u32[]{:S(2)}, u32[]{:S(2)}) collective-permute-start(bf16[4,4,2,24,768]{4,3,2,1,0:T(8,128)(2,1)} %shard_map.396.refs_0_), channel_id=1, source_target_pairs={{0,2},{2,0},{4,6},{6,4},{8,10},{10,8},{12,14},{14,12},{16,18},{18,... | collective-permute-start | bytes 3538952 | tf_op jit(solution)/shard_map/ppermute | solution.py:221
  1306.5 81.3 %collective-permute-start.60 = (bf16[4,4,2,24,768]{4,3,2,1,0:T(8,128)(2,1)}, bf16[4,4,2,24,768]{4,3,2,1,0:T(8,128)(2,1)}, u32[]{:S(2)}, u32[]{:S(2)}) collective-permute-start(bf16[4,4,2,24,768]{4,3,2,1,0:T(8,128)(2,1)} %shard_map.396.refs_0_), channel_id=1, source_target_pairs={{0,1},{1,0},{2,3},{3,2},{4,5},{5,4},{6,7},{7,6},{8,9},{9,8},{10,11... | collective-permute-start | bytes 3538952 | tf_op jit(solution)/shard_map/ppermute | solution.py:118
  1460.1 458.9 %collective-permute-start.79 = (bf16[1,160,512]{2,1,0:T(8,128)(2,1)S(1)}, bf16[1,160,512]{2,1,0:T(8,128)(2,1)}, u32[]{:S(2)}, u32[]{:S(2)}) collective-permute-start(bf16[1,160,512]{2,1,0:T(8,128)(2,1)S(1)} %get-tuple-element.698.refs_0_), channel_id=1, source_target_pairs={{0,24},{2,26},{4,28},{6,30},{8,0},{10,2},{12,4},{14,6},{16,8},{18,... | collective-permute-start | bytes 491528 | tf_op jit(solution)/shard_map/ppermute | solution.py:207
  1481.8 443.3 %collective-permute-start.78 = (bf16[1,160,512]{2,1,0:T(8,128)(2,1)S(1)}, bf16[1,160,512]{2,1,0:T(8,128)(2,1)}, u32[]{:S(2)}, u32[]{:S(2)}) collective-permute-start(bf16[1,160,512]{2,1,0:T(8,128)(2,1)S(1)} %get-tuple-element.698.refs_0_), channel_id=1, source_target_pairs={{0,16},{2,18},{4,20},{6,22},{8,24},{10,26},{12,28},{14,30},{16,0},... | collective-permute-start | bytes 491528 | tf_op jit(solution)/shard_map/ppermute | solution.py:207
  1484.7 440.4 %collective-permute-start.77 = (bf16[1,160,512]{2,1,0:T(8,128)(2,1)S(1)}, bf16[1,160,512]{2,1,0:T(8,128)(2,1)}, u32[]{:S(2)}, u32[]{:S(2)}) collective-permute-start(bf16[1,160,512]{2,1,0:T(8,128)(2,1)S(1)} %get-tuple-element.698.refs_0_), channel_id=1, source_target_pairs={{0,8},{2,10},{4,12},{6,14},{8,16},{10,18},{12,20},{14,22},{16,24},... | collective-permute-start | bytes 491528 | tf_op jit(solution)/shard_map/ppermute | solution.py:207
  1484.8 299.2 %collective-permute-start.72 = (bf16[2,4,2,32,1024]{4,3,2,1,0:T(8,128)(2,1)}, bf16[2,4,2,32,1024]{4,3,2,1,0:T(8,128)(2,1)}, u32[]{:S(2)}, u32[]{:S(2)}) collective-permute-start(bf16[2,4,2,32,1024]{4,3,2,1,0:T(8,128)(2,1)} %collective-permute-done.69.refs_1_), channel_id=1, source_target_pairs={{0,1},{1,0},{2,3},{3,2},{4,5},{5,4},{6,7},{7,6},{8,9},{9,8},{10,11... | collective-permute-start | bytes 3145736 | tf_op jit(solution)/shard_map/ppermute | solution.py:118
  1484.9 302.6 %collective-permute-start.73 = (bf16[2,4,2,32,1024]{4,3,2,1,0:T(8,128)(2,1)}, bf16[2,4,2,32,1024]{4,3,2,1,0:T(8,128)(2,1)}, u32[]{:S(2)}, u32[]{:S(2)}) collective-permute-start(bf16[2,4,2,32,1024]{4,3,2,1,0:T(8,128)(2,1)} %collective-permute-done.71.refs_1_), channel_id=1, source_target_pairs={{0,1},{1,0},{2,3},{3,2},{4,5},{5,4},{6,7},{7,6},{8,9},{9,8},{10,11... | collective-permute-start | bytes 3145736 | tf_op jit(solution)/shard_map/ppermute | solution.py:118
  1784.0 141.1 %collective-permute-start.76 = (bf16[1,160,512]{2,1,0:T(8,128)(2,1)S(1)}, bf16[1,160,512]{2,1,0:T(8,128)(2,1)}, u32[]{:S(2)}, u32[]{:S(2)}) collective-permute-start(bf16[1,160,512]{2,1,0:T(8,128)(2,1)S(1)} %get-tuple-element.699.refs_0_), channel_id=1, source_target_pairs={{0,24},{2,26},{4,28},{6,30},{8,0},{10,2},{12,4},{14,6},{16,8},{18,... | collective-permute-start | bytes 491528 | tf_op jit(solution)/shard_map/ppermute | solution.py:207
  1787.5 137.6 %collective-permute-start.75 = (bf16[1,160,512]{2,1,0:T(8,128)(2,1)S(1)}, bf16[1,160,512]{2,1,0:T(8,128)(2,1)}, u32[]{:S(2)}, u32[]{:S(2)}) collective-permute-start(bf16[1,160,512]{2,1,0:T(8,128)(2,1)S(1)} %get-tuple-element.699.refs_0_), channel_id=1, source_target_pairs={{0,16},{2,18},{4,20},{6,22},{8,24},{10,26},{12,28},{14,30},{16,0},... | collective-permute-start | bytes 491528 | tf_op jit(solution)/shard_map/ppermute | solution.py:207
  2035.2 217.5 %collective-permute-start.86 = (bf16[1,4,2,160,512]{4,3,2,1,0:T(8,128)(2,1)}, bf16[1,4,2,160,512]{4,3,2,1,0:T(8,128)(2,1)}, u32[]{:S(2)}, u32[]{:S(2)}) collective-permute-start(bf16[1,4,2,160,512]{4,3,2,1,0:T(8,128)(2,1)} %shard_map.407.refs_0_), channel_id=1, source_target_pairs={{0,4},{2,6},{4,0},{6,2},{8,12},{10,14},{12,8},{14,10},{16,20},{18,... | collective-permute-start | bytes 3932168 | tf_op jit(solution)/shard_map/ppermute | solution.py:221
  2036.6 216.2 %collective-permute-start.85 = (bf16[1,4,2,160,512]{4,3,2,1,0:T(8,128)(2,1)}, bf16[1,4,2,160,512]{4,3,2,1,0:T(8,128)(2,1)S(1)}, u32[]{:S(2)}, u32[]{:S(2)}) collective-permute-start(bf16[1,4,2,160,512]{4,3,2,1,0:T(8,128)(2,1)} %shard_map.407.refs_0_), channel_id=1, source_target_pairs={{0,1},{1,0},{2,3},{3,2},{4,5},{5,4},{6,7},{7,6},{8,9},{9,8},{10,11... | collective-permute-start | bytes 3932168 | tf_op jit(solution)/shard_map/ppermute | solution.py:118
  2078.1 174.7 %collective-permute-start.84 = (bf16[1,4,2,160,512]{4,3,2,1,0:T(8,128)(2,1)}, bf16[1,4,2,160,512]{4,3,2,1,0:T(8,128)(2,1)}, u32[]{:S(2)}, u32[]{:S(2)}) collective-permute-start(bf16[1,4,2,160,512]{4,3,2,1,0:T(8,128)(2,1)} %shard_map.406.refs_0_), channel_id=1, source_target_pairs={{0,2},{2,0},{4,6},{6,4},{8,10},{10,8},{12,14},{14,12},{16,18},{18,... | collective-permute-start | bytes 3932168 | tf_op jit(solution)/shard_map/ppermute | solution.py:221
  2079.6 173.2 %collective-permute-start.83 = (bf16[1,4,2,160,512]{4,3,2,1,0:T(8,128)(2,1)}, bf16[1,4,2,160,512]{4,3,2,1,0:T(8,128)(2,1)}, u32[]{:S(2)}, u32[]{:S(2)}) collective-permute-start(bf16[1,4,2,160,512]{4,3,2,1,0:T(8,128)(2,1)} %shard_map.406.refs_0_), channel_id=1, source_target_pairs={{0,1},{1,0},{2,3},{3,2},{4,5},{5,4},{6,7},{7,6},{8,9},{9,8},{10,11... | collective-permute-start | bytes 3932168 | tf_op jit(solution)/shard_map/ppermute | solution.py:118
  2687.4 52.9 %collective-permute-start.100 = (f32[5120,512]{1,0:T(8,128)}, f32[5120,512]{1,0:T(8,128)}, u32[]{:S(2)}, u32[]{:S(2)}) collective-permute-start(f32[5120,512]{1,0:T(8,128)} %fusion.75), channel_id=1, source_target_pairs={{0,1},{1,0},{2,3},{3,2},{4,5},{5,4},{6,7},{7,6},{8,9},{9,8},{10,11... | collective-permute-start | bytes 31457288 | tf_op jit(solution)/shard_map/ppermute | solution.py:118
  2749.5 67.4 %collective-permute-start.110 = (f32[3072,384]{1,0:T(8,128)}, f32[3072,384]{1,0:T(8,128)}, u32[]{:S(2)}, u32[]{:S(2)}) collective-permute-start(f32[3072,384]{1,0:T(8,128)} %fusion.137), channel_id=1, source_target_pairs={{0,1},{1,0},{2,3},{3,2},{4,5},{5,4},{6,7},{7,6},{8,9},{9,8},{10,11... | collective-permute-start | bytes 14155784 | tf_op jit(solution)/shard_map/ppermute | solution.py:118
  3188.4 56.1 %collective-permute-start.190 = (bf16[1,4,2,48,384]{4,3,1,2,0:T(8,128)(2,1)}, bf16[1,4,2,48,384]{4,3,1,2,0:T(8,128)(2,1)}, u32[]{:S(2)}, u32[]{:S(2)}) collective-permute-start(bf16[1,4,2,48,384]{4,3,1,2,0:T(8,128)(2,1)} %fusion.150), channel_id=1, source_target_pairs={{0,2},{2,0},{4,6},{6,4},{8,10},{10,8},{12,14},{14,12},{16,18},{18,... | collective-permute-start | bytes 884744 | tf_op jit(solution)/shard_map/ppermute | solution.py:262
  3190.1 54.4 %collective-permute-start.188 = (bf16[4,48,384]{2,1,0:T(8,128)(2,1)}, bf16[4,48,384]{2,1,0:T(8,128)(2,1)}, u32[]{:S(2)}, u32[]{:S(2)}) collective-permute-start(bf16[4,48,384]{2,1,0:T(8,128)(2,1)} %get-tuple-element.645), channel_id=1, source_target_pairs={{0,24},{2,26},{4,28},{6,30},{8,0},{10,2},{12,4},{14,6},{16,8},{18,... | collective-permute-start | bytes 442376 | tf_op jit(solution)/shard_map/ppermute | solution.py:262
  3629.7 120.6 %all-to-all-start.1 = ((bf16[32,80,1024]{2,1,0:T(8,128)(2,1)}), bf16[32,80,1024]{2,1,0:T(8,128)(2,1)}, u32[]{:S(2)}, u32[]{:S(2)}) async-start(bf16[32,80,1024]{2,1,0:T(8,128)(2,1)} %bitcast.870), calls=%async_computation.1 | async-start | bytes 10485760 | tf_op jit(solution)/shard_map/all_to_all | solution.py:498
  (641 other events, 14674.6 us)

commit v3 on v1

--- a/solution.py
+++ b/solution.py
@@ -95,23 +95,6 @@
     return (count, 1, 1)
 
 
-def place_of(index, grid):
-    return (index // (grid[1] * grid[2]), index // grid[2] % grid[1], index % grid[2])
-
-
-def index_of(place, grid):
-    return (place[0] * grid[1] + place[1]) * grid[2] + place[2]
-
-
-def shift_pairs(grid, axis, shift):
-    pairs = []
-    for source in range(grid[0] * grid[1] * grid[2]):
-        place = list(place_of(source, grid))
-        place[axis] = (place[axis] + shift) % grid[axis]
-        pairs.append((source, index_of(place, grid)))
-    return pairs
-
-
 def swap_core(values):
     return lax.ppermute(values, "copy", [(0, 1), (1, 0)])
 
@@ -128,58 +111,142 @@
     return values
 
 
-def scatter_axis(values, grid, axis, position, sent_type):
-    size = grid[axis]
-    mine = place_of(lax.axis_index("dp"), grid)[axis]
-    total = lax.dynamic_index_in_dim(values, mine, position, keepdims=False)
-    for shift in range(1, size):
-        sent = lax.dynamic_index_in_dim(
-            values, (mine + shift) % size, position, keepdims=False
-        ).astype(sent_type)
-        arrived = lax.ppermute(sent, "dp", shift_pairs(grid, axis, shift))
-        total = total + arrived.astype(jnp.float32)
-    return total
-
-
-def scatter_rows(values, order):
+class Flow:
+    def __init__(self):
+        self.live, self.results = ([], {})
+
+    def begin(self, name, task):
+        self.live.append([name, task, *next(task)])
+
+    def tick(self, *carry):
+        due = [entry for entry in self.live if entry[3] <= 1]
+        for entry in self.live:
+            entry[3] -= 1
+        carry, arrived = lax.optimization_barrier((carry, [entry[2] for entry in due]))
+        for entry, values in zip(due, arrived):
+            try:
+                entry[2], entry[3] = entry[1].send(values)
+            except StopIteration as stop:
+                self.results[entry[0]] = stop.value
+                self.live.remove(entry)
+        return carry if len(carry) > 1 else (carry[0] if carry else None)
+
+    def take(self, *names):
+        while any(name not in self.results for name in names):
+            self.tick()
+        return [self.results[name] for name in names]
+
+
+def columns_of(values, core):
+    half = values.shape[-1] // 2
+    return lax.dynamic_slice_in_dim(values, core * half, half, values.ndim - 1)
+
+
+def joined(parts, axis):
+    return parts[0] if len(parts) == 1 else jnp.concatenate(parts, axis=axis)
+
+
+def bits_in_order(crossed):
     grid = grid_of(lax.axis_size("dp"))
-    rows, columns = values.shape
-    values = values.reshape(*grid, rows // lax.axis_size("dp"), columns)
-    left = [0, 1, 2]
-    for axis in order:
-        sent_type = jnp.float32 if axis == order[-1] else jnp.bfloat16
-        values = scatter_axis(values, grid, axis, left.index(axis), sent_type)
-        left.remove(axis)
-    return values
-
-
-def share_columns(values):
+    counts = [size.bit_length() - 1 for size in grid]
+    z_bits = list(range(counts[2] + counts[1], sum(counts)))
+    y_bits = list(range(counts[2], counts[2] + counts[1]))
+    x_bits = list(range(counts[2]))
+    return (y_bits + x_bits if crossed else x_bits + y_bits) + z_bits
+
+
+def scatter_task(parts, crossed, axis, exact, lag=2):
     core = lax.axis_index("copy")
-    rows = values.shape[0] // 2
-    mine = lax.dynamic_slice_in_dim(values, core * rows, rows, 0)
-    arrived = swap_core(lax.dynamic_slice_in_dim(values, (1 - core) * rows, rows, 0))
+    here = lax.axis_index("dp")
+    chips = lax.axis_size("dp")
+    sizes = [part.shape[axis] for part in parts]
+    order = bits_in_order(crossed)
+    parts = [
+        part.reshape(
+            part.shape[0], *[2] * len(order), part.shape[1] // chips, part.shape[2]
+        )
+        for part in parts
+    ]
+    left = sorted(order, reverse=True)
+    for bit in order:
+        position, mine = (1 + left.index(bit), here // 2**bit % 2)
+        sent = []
+        for part, keep in zip(parts, exact):
+            half = lax.dynamic_index_in_dim(part, 1 - mine, position, keepdims=False)
+            if keep:
+                near = lax.reduce_precision(half, 8, 7)
+                sent += [to_low(near), to_low(half - near)]
+            else:
+                sent.append(to_low(half))
+        pairs = [(i, i ^ 2**bit) for i in range(chips)]
+        (arrived,) = yield ([lax.ppermute(joined(sent, axis), "dp", pairs)], lag)
+        start, totals = (0, [])
+        for part, keep, size in zip(parts, exact, sizes):
+            total = lax.dynamic_index_in_dim(part, mine, position, keepdims=False)
+            for number in range(2 if keep else 1):
+                piece = lax.slice_in_dim(
+                    arrived, start, start + size, axis=axis % arrived.ndim
+                )
+                total = total + piece.astype(jnp.float32)
+                start += size
+            totals.append(total)
+        parts = totals
+        left.remove(bit)
+    values = joined(parts, axis)
+    half = values.shape[1] // 2
+    mine = lax.dynamic_slice_in_dim(values, core * half, half, 1)
+    (arrived,) = yield (
+        [swap_core(lax.dynamic_slice_in_dim(values, (1 - core) * half, half, 1))],
+        1,
+    )
     first = jnp.where(core == 0, mine, arrived)
     last = jnp.where(core == 0, arrived, mine)
-    return (first, last)
-
-
-def columns_of(values, core):
-    half = values.shape[1] // 2
-    return lax.dynamic_slice_in_dim(values, core * half, half, 1)
-
-
-def weight_grad(left_side, right_side):
+    starts = [sum(sizes[:i]) for i in range(len(sizes))]
+    return [
+        tuple(lax.slice_in_dim(m, start, start + size, axis=axis % m.ndim) for m in (first, last))
+        for start, size in zip(starts, sizes)
+    ]
+
+
+def weight_task(products, crossed, axis, tables=(), lag=2):
     core = lax.axis_index("copy")
-    arrived = swap_core(product_left(left_side, columns_of(right_side, 1 - core)))
-    return product_left(left_side, columns_of(right_side, core)) + arrived
-
-
-forward_order = (2, 1, 0)
-crossed_order = (1, 2, 0)
-
-
-def rows_whole(values, order):
-    return jnp.concatenate(share_columns(scatter_rows(values, order)), axis=1)
+
+    def some(right_sides, which):
+        return joined([columns_of(right, which) for right in right_sides], 1)
+
+    sent = [product_left(left, some(rights, 1 - core)) for slots, left, rights in products]
+    sent += [columns_of(table, 1 - core) for table in tables]
+    arrived = yield ([swap_core(part) for part in sent], 1)
+    totals = [
+        product_left(left, some(rights, core)) + part
+        for (slots, left, rights), part in zip(products, arrived)
+    ]
+    totals = [
+        total.reshape(member[0], total.shape[0] // member[0], total.shape[1])
+        for total, member in zip(totals, products)
+    ]
+    for table, part in zip(tables, arrived[len(products) :]):
+        totals.append((columns_of(table, core) + part)[None])
+    exact = [False] * len(products) + [True] * len(tables)
+    halves = yield from scatter_task(totals, crossed, axis, exact, lag)
+    found = []
+    counts = [len(member[2]) for member in products] + [1] * len(tables)
+    for (first, last), count in zip(halves, counts):
+        width = first.shape[-1] // count
+        for i in range(count):
+            pair = [m[..., i * width : (i + 1) * width] for m in (first, last)]
+            found.append(jnp.concatenate(pair, axis=-1))
+    return found
+
+
+def split_weight_task(left_side, right_side, flow, names):
+    core = lax.axis_index("copy")
+    (arrived,) = yield ([swap_core(product_left(left_side, columns_of(right_side, 1 - core)))], 1)
+    total = (product_left(left_side, columns_of(right_side, core)) + arrived)[None]
+    quarter = total.shape[-1] // 2
+    flow.begin(names[0], scatter_task([total[..., :quarter]], False, 0, [False]))
+    flow.begin(names[1], scatter_task([total[..., quarter:]], True, 0, [False]))
+    return None
 
 
 def attention_scores(query_heads, key_heads, same_image):
@@ -189,7 +256,7 @@
     return jnp.where(same_image[None], raw_scores * score_factor, -1e30)
 
 
-def block_forward(entered, attend_low, expand_low, gain_rows, same_image):
+def block_forward(entered, attend_low, expand_low, flow, gain_rows, same_image):
     halfway = entered.shape[0]
     normed, first_back = jax.vjp(layer_norm, entered, gain_rows[0], gain_rows[1])
     normed_low = to_low(normed)
@@ -232,11 +299,12 @@
         normed_two_low,
         gelu_back,
         hidden_low,
+        expand_low,
     )
     return (output_rows, kept)
 
 
-def block_backward(output_grad, kept, attend_low, expand_low, same_image):
+def block_backward(output_grad, kept, attend_low, flow, depth, same_image):
     (
         first_back,
         normed_low,
@@ -249,18 +317,30 @@
         normed_two_low,
         gelu_back,
         hidden_low,
+        expand_low,
     ) = kept
     halfway = attended.shape[0]
+    copies = expand_low[0].shape[0] // D
     upper_low = to_low(output_grad)
-    upper_delta = rows_whole(weight_grad(hidden_low, upper_low), forward_order)
+    flow.begin(
+        "upper%d" % depth,
+        weight_task([(copies, hidden_low, [upper_low])], False, 0),
+    )
     (hidden_grad,) = gelu_back(product_right(upper_low, expand_low[1]))
-    hidden_grad_low = to_low(hidden_grad)
-    lower_delta = rows_whole(weight_grad(hidden_grad_low, normed_two_low), crossed_order)
+    hidden_grad_low = flow.tick(to_low(hidden_grad))
     middle_extra, gain_three, gain_four = second_back(product(hidden_grad_low, expand_low[0]))
-    middle_grad = output_grad + middle_extra
+    middle_grad = flow.tick(output_grad + middle_extra)
     projected_low = to_low(middle_grad)
-    output_delta = rows_whole(weight_grad(attended, projected_low), forward_order)
+    flow.begin(
+        "lower%d" % depth,
+        weight_task(
+            [(copies, hidden_grad_low, [normed_two_low]), (1, attended, [projected_low])],
+            True,
+            0,
+        ),
+    )
     attended_grad = to_low(product_right(projected_low, attend_low[3])).reshape(halfway, HEADS, HD)
+    attended_grad = flow.tick(attended_grad)
     probability = jnp.exp(attention_scores(query_heads, key_heads, same_image) - log_total)
     soft_grad = jnp.einsum(
         "qhd,khd->hqk", attended_grad, value_heads, preferred_element_type=jnp.float32
@@ -273,9 +353,11 @@
         * (soft_grad - jnp.sum(probability * soft_grad, axis=-1, keepdims=True))
         * score_factor
     )
+    score_low, value_part = flow.tick(score_low, value_part)
     key_part = jnp.einsum(
         "hqk,qhd->khd", score_low, query_heads, preferred_element_type=jnp.float32
     )
+    key_part = flow.tick(key_part)
     query_grad = to_low(
         jnp.einsum(
             "hqk,khd->qhd", score_low, key_heads, preferred_element_type=jnp.float32
@@ -289,23 +371,19 @@
     key_grad = to_low(
         key_part[:halfway] + swap_core(to_low(key_part[halfway:])).astype(jnp.float32)
     )
+    query_grad, key_grad, value_grad = flow.tick(query_grad, key_grad, value_grad)
+    flow.begin(
+        "attend%d" % depth,
+        weight_task([(1, normed_low, [query_grad, key_grad, value_grad])], False, 0, (), 1 + depth),
+    )
     normed_grad = (
         product_right(query_grad, attend_low[0])
         + product_right(key_grad, attend_low[1])
         + product_right(value_grad, attend_low[2])
     )
     entered_extra, gain_one, gain_two = first_back(normed_grad)
-    attend_delta = jnp.stack(
-        [
-            rows_whole(weight_grad(normed_low, query_grad), forward_order),
-            rows_whole(weight_grad(normed_low, key_grad), crossed_order),
-            rows_whole(weight_grad(normed_low, value_grad), crossed_order),
-            output_delta,
-        ]
-    )
-    expand_delta = jnp.stack([lower_delta, upper_delta])
     gain_delta = jnp.stack([gain_one, gain_two, gain_three, gain_four])
-    return (middle_grad + entered_extra, attend_delta, expand_delta, gain_delta)
+    return (flow.tick(middle_grad + entered_extra), gain_delta)
 
 
 def fine(left_side, right_side):
@@ -424,26 +502,54 @@
 ):
     everywhere = ("dp", "copy")
     core = lax.axis_index("copy")
-    encoder_turned = lax.all_gather(to_low(encoder_table).T, everywhere, axis=0, tiled=True)
-    attend_low, expand_low = (to_low(attend_weight), to_low(expand_weight))
-    attend_all, expand_all = ([], [])
-    for depth_index in range(2):
-        attend_all.append(
-            lax.all_gather(
-                attend_low[4 * depth_index : 4 * depth_index + 4], everywhere, axis=1, tiled=True
-            )
+    flow = Flow()
+    attend_low, expand_low, dense_low = (
+        to_low(attend_weight),
+        to_low(expand_weight),
+        to_low(dense_weight),
+    )
+    rows, wide = (attend_weight.shape[1], dense_weight.shape[1])
+    table_slots = -(-encoder_table.shape[0] // D)
+    encoder_turned = padded(to_low(encoder_table).T, rows, table_slots * D)
+    encoder_turned = encoder_turned.reshape(rows, table_slots, D).transpose(1, 0, 2)
+    expand_slots = expand_low.reshape(expand_low.shape[0], -1, rows, D)
+    copies = expand_slots.shape[1]
+
+    def gathered(members):
+        return lax.all_gather(jnp.concatenate(members, axis=0), everywhere, axis=1, tiled=True)
+
+    entry_part = gathered([attend_low[:4], encoder_turned])
+    expand_part = gathered([expand_slots[0], expand_slots[1]])
+    later_part = gathered([attend_low[4:], expand_slots[2], expand_slots[3]])
+    modulate_slots = to_low(modulate_weight).reshape(-1, wide, HW)
+    head_part = gathered(
+        [
+            padded(to_low(head_table).T, wide, HW)[None],
+            padded(to_low(condition_weight), wide, HW)[None],
+            dense_low,
+            modulate_slots,
+        ]
+    )
+    attend_all = [entry_part[:4], later_part[:4]]
+    expand_all = [
+        (
+            member[: copies].reshape(copies * D, D),
+            member[copies:].reshape(copies * D, D),
         )
-        expand_all.append(
-            lax.all_gather(
-                expand_low[2 * depth_index : 2 * depth_index + 2], everywhere, axis=1, tiled=True
-            )
-        )
-    condition_all = lax.all_gather(to_low(condition_weight), everywhere, axis=0, tiled=True)
-    head_turned = lax.all_gather(to_low(head_table).T, everywhere, axis=0, tiled=True)
-    modulate_all = lax.all_gather(to_low(modulate_weight), everywhere, axis=0, tiled=True)
-    dense_all = lax.all_gather(to_low(dense_weight), everywhere, axis=1, tiled=True)
-    encoder_all = encoder_turned.T
-    head_all = head_turned.T
+        for member in (expand_part, later_part[4:])
+    ]
+    encoder_all = jnp.concatenate([entry_part[4 + i] for i in range(table_slots)], axis=1).T[
+        : encoder_table.shape[0]
+    ]
+    head_all = head_part[0][:, : head_table.shape[0]].T
+    condition_all = head_part[1][:, :D]
+    dense_all = head_part[2:4]
+    modulate_all = (
+        head_part[4:]
+        .reshape(modulate_slots.shape[0], -1, wide, HW)
+        .transpose(1, 0, 2, 3)
+        .reshape(modulate_slots.shape[0] * HW, HW)
+    )
     halfway = SEQ // 2
     offset = core * halfway
 
@@ -482,6 +588,7 @@
             state_rows,
             attend_all[depth_index],
             expand_all[depth_index],
+            flow,
             gain_rows[4 * depth_index : 4 * depth_index + 4],
             same_image,
         )
@@ -520,46 +627,44 @@
         product(predicted_grad, head_all[PATCH + FREQ :])
     )
     branch_low = to_low(branch_grad)
-    second_delta = rows_whole(weight_grad(expanded_low, branch_low), forward_order)
     (expanded_grad,) = dense_back(product_right(branch_low, dense_all[1]))
     expanded_grad_low = to_low(expanded_grad)
-    first_delta = rows_whole(weight_grad(inner_low, expanded_grad_low), crossed_order)
     lifted_extra, modulation_extra = inner_back(product_right(expanded_grad_low, dense_all[0]))
-    modulation_low = to_low(modulation_grad + modulation_extra)
-    modulate_half = weight_grad(modulation_low, activated_low)
-    quarter = modulate_half.shape[1] // 2
-    modulate_left = share_columns(scatter_rows(modulate_half[:, :quarter], forward_order))
-    modulate_right = share_columns(scatter_rows(modulate_half[:, quarter:], crossed_order))
-    modulate_delta = jnp.concatenate(
-        [modulate_left[0], modulate_right[0], modulate_left[1], modulate_right[1]], axis=1
+    modulation_low = flow.tick(to_low(modulation_grad + modulation_extra))
+    flow.begin(
+        "spread",
+        split_weight_task(modulation_low, activated_low, flow, ("modulate.2", "modulate.3")),
     )
     (summed_grad,) = silu_back(product(modulation_low, modulate_all))
     time_turned = product_left(to_low(summed_grad), feature_low)
     lift_turned = product_left(to_low(lifted_grad + lifted_extra), noisy_low)
     head_turned_grad = jnp.concatenate([lift_turned, time_turned, final_turned], axis=1)
-    head_delta = rows_whole(
-        columns_of(head_turned_grad, core) + swap_core(columns_of(head_turned_grad, 1 - core)),
-        forward_order,
-    ).T
     condition_grad = to_low(
         summed_grad[:halfway] + swap_core(to_low(summed_grad[halfway:])).astype(jnp.float32)
     )
-    condition_delta = rows_whole(weight_grad(condition_grad, latent_low), crossed_order)
+    condition_grad = flow.tick(condition_grad)
+    flow.begin(
+        "head",
+        weight_task(
+            [
+                (1, inner_low, [expanded_grad_low]),
+                (1, expanded_low, [branch_low]),
+                (1, condition_grad, [latent_low]),
+            ],
+            True,
+            -1,
+            [head_turned_grad],
+        ),
+    )
     state_grad, gain_nine, gain_ten = third_back(product(condition_grad, condition_all))
-    attend_parts = [None, None]
-    expand_parts = [None, None]
     gain_parts = [None, None]
     for depth_index in (1, 0):
-        (
-            state_grad,
-            attend_parts[depth_index],
-            expand_parts[depth_index],
-            gain_parts[depth_index],
-        ) = block_backward(
+        state_grad, gain_parts[depth_index] = block_backward(
             state_grad,
             kept_all[depth_index],
             attend_all[depth_index],
-            expand_all[depth_index],
+            flow,
+            depth_index,
             same_image,
         )
     embedded_grad, token_grad, position_grad = entry_back(state_grad)
@@ -580,9 +685,8 @@
         [position_grad, lax.dynamic_slice_in_dim(small_delta, core * small_half, small_half, 0)],
         axis=0,
     ).T
-    encoder_first_half, encoder_last_half = share_columns(
-        scatter_rows(encoder_half, crossed_order)
-    )
+    flow.begin("encoder", scatter_task([encoder_half[None]], True, 0, [True], 1))
+    encoder_first_half, encoder_last_half = (m[0] for m in flow.take("encoder")[0][0])
     encoder_delta = jnp.concatenate(
         [
             encoder_first_half[:, halfway:],
@@ -592,14 +696,26 @@
         ],
         axis=1,
     ).T
+    blocks = [name + str(i) for i in range(2) for name in ("upper", "lower", "attend")]
+    flow.take("head", "modulate.2", "modulate.3", *blocks)
+    results = flow.results
+    attend_parts, expand_parts = ([], [])
+    for depth_index in range(2):
+        lower_delta, output_delta = results["lower%d" % depth_index]
+        (upper_delta,) = results["upper%d" % depth_index]
+        attend_parts += [member[0] for member in results["attend%d" % depth_index]]
+        attend_parts.append(output_delta[0])
+        expand_parts += [lower_delta.reshape(-1, D), upper_delta.reshape(-1, D)]
+    first_delta, second_delta, condition_delta, head_delta = results["head"]
+    (left_parts,), (right_parts,) = (results["modulate.2"], results["modulate.3"])
     reduced = (
-        jnp.concatenate(attend_parts, axis=0),
-        jnp.concatenate(expand_parts, axis=0),
-        jnp.stack([first_delta, second_delta]),
-        modulate_delta,
-        condition_delta,
+        jnp.stack(attend_parts),
+        jnp.stack(expand_parts),
+        jnp.stack([first_delta[0], second_delta[0]]),
+        jnp.concatenate([left_parts[0], right_parts[0], left_parts[1], right_parts[1]], axis=-1)[0],
+        condition_delta[0],
         encoder_delta,
-        head_delta,
+        head_delta[0].T,
     )
     squares = sum((jnp.sum(member * member) for member in reduced))
     totals = sum_all(jnp.stack([squares, loss_local]))

time: 1960 us -> 1600 us (0.82)
  waiting for transfers between devices: 735 us -> 470 us
  matrix products: 609 us -> 481 us
  local copies, waits for them, and re-layouts: 91 us -> 186 us
  starting transfers between devices: 147 us -> 75.3 us
  other arithmetic: 158 us -> 214 us
  blocking collectives: 164 us -> 119 us
    ppermute x95 -> x40, waiting for transfers between devices: 291 us -> 137 us  [scatter_task(): arrived, = (yield ([lax.ppermute(joined(sent, axis), 'dp', pairs)], lag))]
    all_gather x8 -> x4, waiting for transfers between devices: 303 us -> 196 us  [gathered(): lax.all_gather(jnp.concatenate(members, axis=0), everywhere, axis=1, tile...]
    dot_general x2, matrix products: 93.2 us -> 7.66 us  [block_backward(): jnp.einsum('hqk,qhd->khd', score_low, query_heads, preferred_element_type...]
    dot_general x2, matrix products: 89.3 us -> 12.5 us  [block_backward(): jnp.einsum('hqk,khd->qhd', score_low, key_heads, preferred_element_type=j...]
    ppermute x95 -> x40, starting transfers between devices: 117 us -> 45.2 us  [scatter_task(): arrived, = (yield ([lax.ppermute(joined(sent, axis), 'dp', pairs)], lag))]
    sub x0 -> x2, matrix products: none -> 63.1 us  [block_backward(): soft_grad - jnp.sum(probability * soft_grad, axis=-1, keepdims=True)]
    all_gather x1 -> x0, blocking collectives: 46.1 us -> none  [per_device(): lax.all_gather(to_low(head_table).T, everywhere, axis=0, tiled=True)]
    add x58 -> x64, other arithmetic: 14.9 us -> 58.8 us  [the longest x56 46.2 us: scatter_task(): total = total + piece.astype(jnp.float32)]
  transfers between devices with their start and end apart: 167 -> 95, of which waited for: 97 -> 37; matrix products, arithmetic and copies ran while one was open for 33% -> 36% of each run, Pallas kernels for 0% -> 0%
where the time goes in v3:
time: 1600 us; the launch traced here: 1590 us
  matrix products  481 us (30%)
  waiting for transfers between devices  470 us (29%)
  other arithmetic  214 us (13%)
  local copies, waits for them, and re-layouts  186 us (12%)
  blocking collectives  119 us (7%)
  starting transfers between devices  75.3 us (5%)
  between operations  44.6 us (3%)
    all_gather x4, waiting for transfers between devices, gathered(): lax.all_gather(jnp.concatenate(members, axis=0), everywhere, axis=1, tile...  196 us
    ppermute x40, waiting for transfers between devices, scatter_task(): arrived, = (yield ([lax.ppermute(joined(sent, axis), 'dp', pairs)], lag))  137 us
    all_to_all x1, blocking collectives, muon_steps(): lax.all_to_all(jnp.stack(sending), ('dp', 'copy'), 0, 0)  119 us
    all_to_all x1, waiting for transfers between devices, muon_steps(): lax.all_to_all(result.reshape(devices, highest, widest), ('dp', 'copy'),...  103 us
    dot_general x29, matrix products, product_left(): lax.dot_general(left_side, right_side, (((0,), (0,)), ((), ())), preferre...  102 us
    dot_general x21, matrix products, product(): return jnp.dot(left_side, right_side, preferred_element_type=jnp.float32)  93.1 us
    dot_general x17, matrix products, product_right(): lax.dot_general(left_side, right_side, (((1,), (1,)), ((), ())), preferre...  81.4 us
    sub x2, matrix products, block_backward(): soft_grad - jnp.sum(probability * soft_grad, axis=-1, keepdims=True)  63.1 us
  transfers between devices with their start and end apart: 95, of which 37 were waited for; matrix products, arithmetic and copies ran while one was open for 36% of the time, Pallas kernels for 0%

profile of v3, /device:TPU:0, one launch (start us, length us, event | category | flops | bytes accessed | tf_op | source)
XLA Modules:
  0.0 1590.1 jit_solution(12422652049597356630)
XLA Ops:
  22.4 64.4 %all-gather.5.cloned.1.call-done = bf16[6,768,768]{2,1,0:T(8,128)(2,1)} async-done(((bf16[6,24,768]{2,1,0:T(8,128)(2,1)}), bf16[6,768,768]{2,1,0:T(8,128)(2,1)}) %all-gather.5.cloned.1.call-update) | async-done | bytes 7077904 | tf_op jit(solution)/shard_map/all_gather | solution.py:519
  133.1 13.1 fusion.6
  146.2 12.5 fusion.4
  191.1 85.3 %all-gather.11.cloned.1.call-done = bf16[12,768,768]{2,1,0:T(8,128)(2,1)} async-done(((bf16[12,24,768]{2,1,0:T(8,128)(2,1)}), bf16[12,768,768]{2,1,0:T(8,128)(2,1)}) %all-gather.11.cloned.1.call-update) | async-done | bytes 14155792 | tf_op jit(solution)/shard_map/all_gather | solution.py:519
  301.9 12.9 fusion.7
  314.8 12.4 fusion.5
  356.1 46.0 %all-gather.7.cloned.1.call-done = bf16[9,1024,1024]{2,1,0:T(8,128)(2,1)} async-done(((bf16[9,32,1024]{2,1,0:T(8,128)(2,1)}), bf16[9,1024,1024]{2,1,0:T(8,128)(2,1)}) %all-gather.7.cloned.1.call-update) | async-done | bytes 18874384 | tf_op jit(solution)/shard_map/all_gather | solution.py:519
  406.2 10.3 slice.1024
  416.5 10.3 copy.290
  437.6 16.3 %fusion.367 = f32[1024,5120]{0,1:T(8,128)} fusion(bf16[5120,1024]{1,0:T(8,128)(2,1)S(1)} %bitcast.734, bf16[1024,1024]{0,1:T(8,128)(2,1)} %get-tuple-element.441), kind=kOutput, calls=%fused_computation.887 | convolution fusion | flops 10737418240 | bytes 33554432 | tf_op jit(solution)/shard_map/dot_general | solution.py:48
  517.5 10.8 fusion.118
  530.0 20.1 %fusion.329 = (bf16[1024,1024]{0,1:T(8,128)(2,1)S(1)}, f32[1024,1024]{0,1:T(8,128)}) fusion(f32[1024,1024]{0,1:T(8,128)} %get-tuple-element.442, bf16[512,1024]{0,1:T(8,128)(2,1)} %copy-done.279, bf16[512,1024]{0,1:T(8,128)(2,1)} %copy-done.278, bf16[1024,5120]{0,1:T(8,128)(2,1)} %copy-done.45, bf16[5120,1024]{1,0:T(8,128)(2,1)} %bitcast.731), kind=kOutput, calls=%fused_computation.853 | convolution fusion | flops 10753146880 | bytes 33554432 | tf_op jit(solution)/shard_map/dot_general | solution.py:38
  583.2 11.0 add_bitcast_fusion
  601.1 12.6 fusion.31
  686.0 14.8 collective-permute-done.20
  703.3 31.0 %multiply_convert_fusion.1 = bf16[12,512,1024]{2,1,0:T(8,128)(2,1)} fusion(f32[12,512]{1,0:T(8,128)S(1)} %copy-done.244, f32[12,512,1024]{2,1,0:T(8,128)} %get-tuple-element.436, pred[512,1024]{1,0:T(8,128)(4,1)S(1)} %copy-done.39, bf16[512,12,64]{0,2,1:T(8,128)(2,1)} %bitcast.801, bf16[1024,12,64]{0,2,1:T(8,128)(2,1)S(1)} %bitcast.795), kind=kOutput, calls=%fused_computation.5 | convolution fusion | flops 1679825920 | bytes 40656896 | tf_op jit(solution)/shard_map/sub | solution.py:353
  734.3 13.7 fusion.49
  798.9 27.8 %collective-permute-done.26 = bf16[4,2,2,48,384]{4,3,2,1,0:T(8,128)(2,1)} collective-permute-done((bf16[4,2,2,48,384]{4,3,2,1,0:T(8,128)(2,1)}, bf16[4,2,2,48,384]{4,3,2,1,0:T(8,128)(2,1)}, u32[]{:S(2)}, u32[]{:S(2)}) %collective-permute-start.26) | collective-permute-done | bytes 589856 | tf_op jit(solution)/shard_map/ppermute | solution.py:182
  952.0 13.3 fusion.52
  965.3 32.1 %multiply_convert_fusion = bf16[12,512,1024]{2,1,0:T(8,128)(2,1)} fusion(f32[12,512]{1,0:T(8,128)S(1)} %copy-done.243, f32[12,512,1024]{2,1,0:T(8,128)} %get-tuple-element.430, pred[512,1024]{1,0:T(8,128)(4,1)S(1)} %copy-done.40, bf16[512,12,64]{0,2,1:T(8,128)(2,1)} %bitcast.799, bf16[1024,12,64]{0,2,1:T(8,128)(2,1)} %bitcast.793), kind=kOutput, calls=%fused_computation.2 | convolution fusion | flops 1679825920 | bytes 40656896 | tf_op jit(solution)/shard_map/sub | solution.py:353
  1039.6 17.1 %collective-permute-done.54 = bf16[5,2,2,2,48,384]{5,4,1,2,3,0:T(8,128)(2,1)} collective-permute-done((bf16[5,2,2,2,48,384]{5,4,1,2,3,0:T(8,128)(2,1)}, bf16[5,2,2,2,48,384]{5,4,1,2,3,0:T(8,128)(2,1)}, u32[]{:S(2)}, u32[]{:S(2)}) %collective-permute-start.54) | collective-permute-done | bytes 1474592 | tf_op jit(solution)/shard_map/ppermute | solution.py:182
  1077.4 10.0 collective-permute-done.59
  1108.9 14.6 collective-permute-done.62
  1135.4 9.3 collective-permute-done.69
  1151.3 13.8 collective-permute-done.72
  1168.4 9.8 collective-permute-done.75
  1217.3 118.9 %all_to_all.10 = bf16[32,80,1024]{2,1,0:T(8,128)(2,1)S(1)} all-to-all(bf16[32,80,1024]{2,1,0:T(8,128)(2,1)S(1)} %broadcast_dynamic-update-slice_fusion), channel_id=1, replica_groups=mesh['dp'=16,'copy'=2] {'dp','copy'}, dimensions={0} | all-to-all | bytes 10485760 | tf_op jit(solution)/shard_map/all_to_all | solution.py:434
  1346.1 10.3 stack.196
  1405.0 16.7 %multiply_add_fusion = f32[1024,1024]{1,0:T(8,128)} fusion(f32[1024,1024]{1,0:T(8,128)} %fusion.59, f32[1024,1024]{1,0:T(8,128)} %copy-done.87, f32[1024,1024]{1,0:T(8,128)S(1)} %add_multiply_fusion), kind=kOutput, calls=%fused_computation.72 | convolution fusion | flops 6453985280 | bytes 16777216 | tf_op jit(solution)/shard_map/dot_general | solution.py:390
  1421.7 11.1 fusion.366
  1432.8 10.6 multiply_convert_fusion.2
  1460.8 103.2 %all-to-all-done.1 = bf16[32,80,1024]{2,1,0:T(8,128)(2,1)} async-done(((bf16[32,80,1024]{2,1,0:T(8,128)(2,1)}), bf16[32,80,1024]{2,1,0:T(8,128)(2,1)}, u32[]{:S(2)}, u32[]{:S(2)}) %all-to-all-start.1) | async-done | bytes 5242912 | tf_op jit(solution)/shard_map/all_to_all | solution.py:447
  (1331 shorter events, 729.5 us)
Async XLA Ops:
  7.2 79.6 %all-gather.5.cloned.1.call-start = ((), (), s32[]{:S(2)}) async-start(), calls=%async_computation.2 | async-start | bytes 7299072 | tf_op jit(solution)/shard_map/all_gather | solution.py:519
  10.3 164.1 %all-gather.9.cloned.1.call-start = ((), (), s32[]{:S(2)}) async-start(), calls=%async_computation.4 | async-start | bytes 9732096 | tf_op jit(solution)/shard_map/all_gather | solution.py:519
  12.5 263.8 %all-gather.11.cloned.1.call-start = ((), (), s32[]{:S(2)}) async-start(), calls=%async_computation.5 | async-start | bytes 14598144 | tf_op jit(solution)/shard_map/all_gather | solution.py:519
  13.4 388.7 %all-gather.7.cloned.1.call-start = ((), (), s32[]{:S(2)}) async-start(), calls=%async_computation.3 | async-start | bytes 19464192 | tf_op jit(solution)/shard_map/all_gather | solution.py:519
  15.9 84.5 %collective-permute-start.5 = (f32[]{:T(128)}, f32[]{:T(128)}, u32[]{:S(2)}, u32[]{:S(2)}) collective-permute-start(f32[]{:T(128)} %reduce_sum.637), channel_id=1, source_target_pairs={{0,1},{1,0},{2,3},{3,2},{4,5},{5,4},{6,7},{7,6},{8,9},{9,8},{10,11... | collective-permute-start | bytes 20 | tf_op jit(solution)/shard_map/ppermute | solution.py:99
  528.4 45.5 %collective-permute-start.11 = (f32[5120,512]{1,0:T(8,128)}, f32[5120,512]{1,0:T(8,128)}, u32[]{:S(2)}, u32[]{:S(2)}) collective-permute-start(f32[5120,512]{1,0:T(8,128)} %fusion.118), channel_id=1, source_target_pairs={{0,1},{1,0},{2,3},{3,2},{4,5},{5,4},{6,7},{7,6},{8,9},{9,8},{10,11... | collective-permute-start | bytes 31457288 | tf_op jit(solution)/shard_map/ppermute | solution.py:99
  563.1 62.1 %collective-permute-start.15 = (f32[1024,192]{0,1:T(8,128)}, f32[1024,192]{0,1:T(8,128)}, u32[]{:S(2)}, u32[]{:S(2)}) collective-permute-start(f32[1024,192]{0,1:T(8,128)} %constant_dynamic-slice_fusion.46), channel_id=1, source_target_pairs={{0,1},{1,0},{2,3},{3,2},{4,5},{5,4},{6,7},{7,6},{8,9},{9,8},{10,11... | collective-permute-start | bytes 2359304 | tf_op jit(solution)/shard_map/ppermute | solution.py:99
  563.4 63.3 %collective-permute-start.13 = (f32[1024,512]{1,0:T(8,128)}, f32[1024,512]{1,0:T(8,128)}, u32[]{:S(2)}, u32[]{:S(2)}) collective-permute-start(f32[1024,512]{1,0:T(8,128)} %fusion.114), channel_id=1, source_target_pairs={{0,1},{1,0},{2,3},{3,2},{4,5},{5,4},{6,7},{7,6},{8,9},{9,8},{10,11... | collective-permute-start | bytes 6291464 | tf_op jit(solution)/shard_map/ppermute | solution.py:99
  563.6 63.7 %collective-permute-start.12 = (f32[1024,512]{1,0:T(8,128)}, f32[1024,512]{1,0:T(8,128)}, u32[]{:S(2)}, u32[]{:S(2)}) collective-permute-start(f32[1024,512]{1,0:T(8,128)} %fusion.116), channel_id=1, source_target_pairs={{0,1},{1,0},{2,3},{3,2},{4,5},{5,4},{6,7},{7,6},{8,9},{9,8},{10,11... | collective-permute-start | bytes 6291464 | tf_op jit(solution)/shard_map/ppermute | solution.py:99
  581.7 45.6 %collective-permute-start.16 = (f32[3072,384]{1,0:T(8,128)}, f32[3072,384]{1,0:T(8,128)}, u32[]{:S(2)}, u32[]{:S(2)}) collective-permute-start(f32[3072,384]{1,0:T(8,128)} %fusion.183), channel_id=1, source_target_pairs={{0,1},{1,0},{2,3},{3,2},{4,5},{5,4},{6,7},{7,6},{8,9},{9,8},{10,11... | collective-permute-start | bytes 14155784 | tf_op jit(solution)/shard_map/ppermute | solution.py:99
  596.1 31.2 %collective-permute-start.14 = (f32[1024,384]{1,0:T(8,128)}, f32[1024,384]{1,0:T(8,128)}, u32[]{:S(2)}, u32[]{:S(2)}) collective-permute-start(f32[1024,384]{1,0:T(8,128)} %fusion.185), channel_id=1, source_target_pairs={{0,1},{1,0},{2,3},{3,2},{4,5},{5,4},{6,7},{7,6},{8,9},{9,8},{10,11... | collective-permute-start | bytes 4718600 | tf_op jit(solution)/shard_map/ppermute | solution.py:99
  625.2 39.4 %collective-permute-start.18 = (bf16[1,2,2,2,320,256]{5,4,1,2,3,0:T(8,128)(2,1)}, bf16[1,2,2,2,320,256]{5,4,1,2,3,0:T(8,128)(2,1)}, u32[]{:S(2)}, u32[]{:S(2)}) collective-permute-start(bf16[1,2,2,2,320,256]{5,4,1,2,3,0:T(8,128)(2,1)} %fusion.70), channel_id=1, source_target_pairs={{0,4},{2,6},{4,0},{6,2},{8,12},{10,14},{12,8},{14,10},{16,20},{18,... | collective-permute-start | bytes 3932168 | tf_op jit(solution)/shard_map/ppermute | solution.py:182
  626.6 37.9 %collective-permute-start.17 = (bf16[1,2,2,2,320,256]{5,4,1,2,3,0:T(8,128)(2,1)}, bf16[1,2,2,2,320,256]{5,4,1,2,3,0:T(8,128)(2,1)}, u32[]{:S(2)}, u32[]{:S(2)}) collective-permute-start(bf16[1,2,2,2,320,256]{5,4,1,2,3,0:T(8,128)(2,1)} %fusion.69), channel_id=1, source_target_pairs={{0,2},{2,0},{4,6},{6,4},{8,10},{10,8},{12,14},{14,12},{16,18},{18,... | collective-permute-start | bytes 3932168 | tf_op jit(solution)/shard_map/ppermute | solution.py:182
  631.4 72.0 %collective-permute-start.21 = (f32[3072,384]{1,0:T(8,128)}, f32[3072,384]{1,0:T(8,128)}, u32[]{:S(2)}, u32[]{:S(2)}) collective-permute-start(f32[3072,384]{1,0:T(8,128)} %fusion.178), channel_id=1, source_target_pairs={{0,1},{1,0},{2,3},{3,2},{4,5},{5,4},{6,7},{7,6},{8,9},{9,8},{10,11... | collective-permute-start | bytes 14155784 | tf_op jit(solution)/shard_map/ppermute | solution.py:99
  660.1 43.2 %collective-permute-start.19 = (bf16[1,2,2,2,64,1792]{5,4,1,2,3,0:T(8,128)(2,1)}, bf16[1,2,2,2,64,1792]{5,4,1,2,3,0:T(8,128)(2,1)}, u32[]{:S(2)}, u32[]{:S(2)}) collective-permute-start(bf16[1,2,2,2,64,1792]{5,4,1,2,3,0:T(8,128)(2,1)} %concatenate.279), channel_id=1, source_target_pairs={{0,4},{2,6},{4,0},{6,2},{8,12},{10,14},{12,8},{14,10},{16,20},{18,... | collective-permute-start | bytes 5505032 | tf_op jit(solution)/shard_map/ppermute | solution.py:182
  676.3 76.9 %collective-permute-start.24 = (bf16[1,2,2,320,256]{4,3,1,2,0:T(8,128)(2,1)}, bf16[1,2,2,320,256]{4,3,1,2,0:T(8,128)(2,1)}, u32[]{:S(2)}, u32[]{:S(2)}) collective-permute-start(bf16[1,2,2,320,256]{4,3,1,2,0:T(8,128)(2,1)} %fusion.135), channel_id=1, source_target_pairs={{0,2},{2,0},{4,6},{6,4},{8,10},{10,8},{12,14},{14,12},{16,18},{18,... | collective-permute-start | bytes 1966088 | tf_op jit(solution)/shard_map/ppermute | solution.py:182
  700.7 52.4 %collective-permute-start.23 = (bf16[1,2,2,320,256]{4,3,1,2,0:T(8,128)(2,1)}, bf16[1,2,2,320,256]{4,3,1,2,0:T(8,128)(2,1)}, u32[]{:S(2)}, u32[]{:S(2)}) collective-permute-start(bf16[1,2,2,320,256]{4,3,1,2,0:T(8,128)(2,1)} %fusion.134), channel_id=1, source_target_pairs={{0,4},{2,6},{4,0},{6,2},{8,12},{10,14},{12,8},{14,10},{16,20},{18,... | collective-permute-start | bytes 1966088 | tf_op jit(solution)/shard_map/ppermute | solution.py:182
  780.2 46.5 %collective-permute-start.27 = (bf16[5,2,2,2,48,384]{5,4,1,2,3,0:T(8,128)(2,1)}, bf16[5,2,2,2,48,384]{5,4,1,2,3,0:T(8,128)(2,1)}, u32[]{:S(2)}, u32[]{:S(2)}) collective-permute-start(bf16[5,2,2,2,48,384]{5,4,1,2,3,0:T(8,128)(2,1)} %pad_maximum_fusion.6), channel_id=1, source_target_pairs={{0,4},{2,6},{4,0},{6,2},{8,12},{10,14},{12,8},{14,10},{16,20},{18,... | collective-permute-start | bytes 4423688 | tf_op jit(solution)/shard_map/ppermute | solution.py:182
  784.0 42.6 %collective-permute-start.26 = (bf16[4,2,2,48,384]{4,3,2,1,0:T(8,128)(2,1)}, bf16[4,2,2,48,384]{4,3,2,1,0:T(8,128)(2,1)}, u32[]{:S(2)}, u32[]{:S(2)}) collective-permute-start(bf16[4,2,2,48,384]{4,3,2,1,0:T(8,128)(2,1)} %fusion.136), channel_id=1, source_target_pairs={{0,4},{2,6},{4,0},{6,2},{8,12},{10,14},{12,8},{14,10},{16,20},{18,... | collective-permute-start | bytes 1769480 | tf_op jit(solution)/shard_map/ppermute | solution.py:182
  790.5 36.1 %collective-permute-start.25 = (bf16[1,2,2,64,1792]{4,3,1,2,0:T(8,128)(2,1)}, bf16[1,2,2,64,1792]{4,3,1,2,0:T(8,128)(2,1)S(1)}, u32[]{:S(2)}, u32[]{:S(2)}) collective-permute-start(bf16[1,2,2,64,1792]{4,3,1,2,0:T(8,128)(2,1)} %concatenate.280), channel_id=1, source_target_pairs={{0,2},{2,0},{4,6},{6,4},{8,10},{10,8},{12,14},{14,12},{16,18},{18,... | collective-permute-start | bytes 2752520 | tf_op jit(solution)/shard_map/ppermute | solution.py:182
  793.5 43.9 %collective-permute-start.31 = (bf16[1,2,320,256]{3,2,1,0:T(8,128)(2,1)}, bf16[1,2,320,256]{3,2,1,0:T(8,128)(2,1)}, u32[]{:S(2)}, u32[]{:S(2)}) collective-permute-start(bf16[1,2,320,256]{3,2,1,0:T(8,128)(2,1)} %fusion.189), channel_id=1, source_target_pairs={{0,8},{2,10},{4,12},{6,14},{8,0},{10,2},{12,4},{14,6},{16,24},{18,... | collective-permute-start | bytes 983048 | tf_op jit(solution)/shard_map/ppermute | solution.py:182
  797.2 40.2 %collective-permute-start.30 = (bf16[1,2,320,256]{3,2,1,0:T(8,128)(2,1)}, bf16[1,2,320,256]{3,2,1,0:T(8,128)(2,1)}, u32[]{:S(2)}, u32[]{:S(2)}) collective-permute-start(bf16[1,2,320,256]{3,2,1,0:T(8,128)(2,1)} %fusion.188), channel_id=1, source_target_pairs={{0,8},{2,10},{4,12},{6,14},{8,0},{10,2},{12,4},{14,6},{16,24},{18,... | collective-permute-start | bytes 983048 | tf_op jit(solution)/shard_map/ppermute | solution.py:182
  868.8 32.5 %collective-permute-start.38 = (f32[3072,384]{1,0:T(8,128)}, f32[3072,384]{1,0:T(8,128)}, u32[]{:S(2)}, u32[]{:S(2)}) collective-permute-start(f32[3072,384]{1,0:T(8,128)} %fusion.168), channel_id=1, source_target_pairs={{0,1},{1,0},{2,3},{3,2},{4,5},{5,4},{6,7},{7,6},{8,9},{9,8},{10,11... | collective-permute-start | bytes 14155784 | tf_op jit(solution)/shard_map/ppermute | solution.py:99
  876.9 39.6 %collective-permute-start.42 = (bf16[4,48,384]{2,1,0:T(8,128)(2,1)}, bf16[4,48,384]{2,1,0:T(8,128)(2,1)}, u32[]{:S(2)}, u32[]{:S(2)}) collective-permute-start(bf16[4,48,384]{2,1,0:T(8,128)(2,1)} %fusion.222), channel_id=1, source_target_pairs={{0,16},{2,18},{4,20},{6,22},{8,24},{10,26},{12,28},{14,30},{16,0},... | collective-permute-start | bytes 442376 | tf_op jit(solution)/shard_map/ppermute | solution.py:182
  883.5 33.5 %collective-permute-start.41 = (bf16[1,64,1792]{2,1,0:T(8,128)(2,1)}, bf16[1,64,1792]{2,1,0:T(8,128)(2,1)S(1)}, u32[]{:S(2)}, u32[]{:S(2)}) collective-permute-start(bf16[1,64,1792]{2,1,0:T(8,128)(2,1)} %concatenate.285), channel_id=1, source_target_pairs={{0,16},{2,18},{4,20},{6,22},{8,24},{10,26},{12,28},{14,30},{16,0},... | collective-permute-start | bytes 688136 | tf_op jit(solution)/shard_map/ppermute | solution.py:182
  915.7 32.8 %collective-permute-start.48 = (f32[3072,384]{1,0:T(8,128)}, f32[3072,384]{1,0:T(8,128)}, u32[]{:S(2)}, u32[]{:S(2)}) collective-permute-start(f32[3072,384]{1,0:T(8,128)} %fusion.161), channel_id=1, source_target_pairs={{0,1},{1,0},{2,3},{3,2},{4,5},{5,4},{6,7},{7,6},{8,9},{9,8},{10,11... | collective-permute-start | bytes 14155784 | tf_op jit(solution)/shard_map/ppermute | solution.py:99
  940.5 58.3 %collective-permute-start.50 = (bf16[5,48,384]{2,1,0:T(8,128)(2,1)}, bf16[5,48,384]{2,1,0:T(8,128)(2,1)}, u32[]{:S(2)}, u32[]{:S(2)}) collective-permute-start(bf16[5,48,384]{2,1,0:T(8,128)(2,1)} %pad_maximum_fusion.29), channel_id=1, source_target_pairs={{0,16},{2,18},{4,20},{6,22},{8,24},{10,26},{12,28},{14,30},{16,0},... | collective-permute-start | bytes 552968 | tf_op jit(solution)/shard_map/ppermute | solution.py:182
  942.0 56.8 %collective-permute-start.51 = (bf16[1,2,2,48,1152]{4,3,1,2,0:T(8,128)(2,1)}, bf16[1,2,2,48,1152]{4,3,1,2,0:T(8,128)(2,1)}, u32[]{:S(2)}, u32[]{:S(2)}) collective-permute-start(bf16[1,2,2,48,1152]{4,3,1,2,0:T(8,128)(2,1)} %fusion.150), channel_id=1, source_target_pairs={{0,4},{2,6},{4,0},{6,2},{8,12},{10,14},{12,8},{14,10},{16,20},{18,... | collective-permute-start | bytes 1327112 | tf_op jit(solution)/shard_map/ppermute | solution.py:182
  1019.1 37.6 %collective-permute-start.54 = (bf16[5,2,2,2,48,384]{5,4,1,2,3,0:T(8,128)(2,1)}, bf16[5,2,2,2,48,384]{5,4,1,2,3,0:T(8,128)(2,1)}, u32[]{:S(2)}, u32[]{:S(2)}) collective-permute-start(bf16[5,2,2,2,48,384]{5,4,1,2,3,0:T(8,128)(2,1)} %pad_maximum_fusion.7), channel_id=1, source_target_pairs={{0,4},{2,6},{4,0},{6,2},{8,12},{10,14},{12,8},{14,10},{16,20},{18,... | collective-permute-start | bytes 4423688 | tf_op jit(solution)/shard_map/ppermute | solution.py:182
  1070.7 38.2 %collective-permute-start.61 = (bf16[1,48,1152]{2,1,0:T(8,128)(2,1)}, bf16[1,48,1152]{2,1,0:T(8,128)(2,1)}, u32[]{:S(2)}, u32[]{:S(2)}) collective-permute-start(bf16[1,48,1152]{2,1,0:T(8,128)(2,1)} %fusion.234), channel_id=1, source_target_pairs={{0,16},{2,18},{4,20},{6,22},{8,24},{10,26},{12,28},{14,30},{16,0},... | collective-permute-start | bytes 331784 | tf_op jit(solution)/shard_map/ppermute | solution.py:182
  1089.8 44.4 %collective-permute-start.66 = (bf16[4,48,384]{2,1,0:T(8,128)(2,1)}, bf16[4,48,384]{2,1,0:T(8,128)(2,1)}, u32[]{:S(2)}, u32[]{:S(2)}) collective-permute-start(bf16[4,48,384]{2,1,0:T(8,128)(2,1)} %fusion.225), channel_id=1, source_target_pairs={{0,16},{2,18},{4,20},{6,22},{8,24},{10,26},{12,28},{14,30},{16,0},... | collective-permute-start | bytes 442376 | tf_op jit(solution)/shard_map/ppermute | solution.py:182
  1443.4 120.6 %all-to-all-start.1 = ((bf16[32,80,1024]{2,1,0:T(8,128)(2,1)}), bf16[32,80,1024]{2,1,0:T(8,128)(2,1)}, u32[]{:S(2)}, u32[]{:S(2)}) async-start(bf16[32,80,1024]{2,1,0:T(8,128)(2,1)} %bitcast.754), calls=%async_computation.1 | async-start | bytes 10485760 | tf_op jit(solution)/shard_map/all_to_all | solution.py:447
  (381 other events, 5800.3 us)
Sparse Core Ops, SparseCore 0:
  11.6 75.1 all-gather.4
  90.3 80.5 all-gather.8
  174.5 101.8 all-gather.10
  279.7 122.3 all-gather.6

commit v4 on v3

--- a/solution.py
+++ b/solution.py
@@ -113,10 +113,13 @@
 
 class Flow:
     def __init__(self):
-        self.live, self.results = ([], {})
+        self.live, self.results, self.waiting = ([], {}, [])
 
     def begin(self, name, task):
         self.live.append([name, task, *next(task)])
+
+    def when(self, names, name, make):
+        self.waiting.append((names, name, make))
 
     def tick(self, *carry):
         due = [entry for entry in self.live if entry[3] <= 1]
@@ -129,6 +132,10 @@
             except StopIteration as stop:
                 self.results[entry[0]] = stop.value
                 self.live.remove(entry)
+        for entry in list(self.waiting):
+            if all(name in self.results for name in entry[0]):
+                self.waiting.remove(entry)
+                self.begin(entry[1], entry[2]())
         return carry if len(carry) > 1 else (carry[0] if carry else None)
 
     def take(self, *names):
@@ -386,82 +393,96 @@
     return (flow.tick(middle_grad + entered_extra), gain_delta)
 
 
-def fine(left_side, right_side):
-    return jnp.dot(
-        left_side, right_side, precision=lax.Precision.HIGH, preferred_element_type=jnp.float32
-    )
-
-
 def newton_extra(gram_matrix):
-    first_tail = newton_second * gram_matrix + newton_third * fine(gram_matrix, gram_matrix)
-    once = newton_first * gram_matrix + fine(gram_matrix, first_tail)
-    later = newton_first * once + fine(once, first_tail)
-    last_tail = newton_second * later + newton_third * fine(later, later)
-    return newton_first * (first_tail + last_tail) + fine(first_tail, last_tail)
-
-
-def slots_of(devices):
-    slots = [(14, 0, 2), (14, 1, 2)]
-    for matrix in range(8, 12):
-        slots += [(matrix, 0, 2), (matrix, 1, 2)]
-    slots += [(matrix, 0, 1) for matrix in list(range(8)) + [12, 13, 15]]
-    return slots + [None] * (devices - len(slots))
+    gram_low = to_low(gram_matrix)
+    first_tail = newton_second * gram_matrix + newton_third * product(gram_low, gram_low)
+    tail_low = to_low(first_tail)
+    once = newton_first * gram_matrix + product(gram_low, tail_low)
+    later = newton_first * once + product(to_low(once), tail_low)
+    later_low = to_low(later)
+    last_tail = newton_second * later + newton_third * product(later_low, later_low)
+    return newton_first * (first_tail + last_tail) + product(tail_low, to_low(last_tail))
 
 
 def padded(piece, rows, columns):
-    return jnp.pad(piece, ((0, rows - piece.shape[0]), (0, columns - piece.shape[1])))
-
-
-def muon_steps(moments):
-    devices = lax.axis_size(("dp", "copy"))
-    pieces = (
-        [moments[0][i] for i in range(8)]
-        + [moments[1][i] for i in range(4)]
-        + [moments[2][i] for i in range(2)]
-        + [moments[3], moments[4]]
-    )
-    slots = slots_of(devices)
-    highest = max(pieces[slot[0]].shape[0] // slot[2] for slot in slots if slot)
-    widest = max(piece.shape[1] for piece in pieces)
-    sending = []
-    for slot in slots:
-        if slot is None:
-            sending.append(jnp.zeros((highest, widest), jnp.bfloat16))
-        else:
-            rows = pieces[slot[0]].shape[0] // slot[2]
-            piece = to_low(pieces[slot[0]][slot[1] * rows : (slot[1] + 1) * rows])
-            sending.append(padded(piece, highest, widest))
-    held = lax.all_to_all(jnp.stack(sending), ("dp", "copy"), 0, 0).reshape(
-        devices * highest, widest
-    )
-    squares = sum_all(jnp.stack([jnp.sum(piece * piece) for piece in pieces]))
-    inverse = 1.0 / (jnp.sqrt(squares) + 1e-07)
+    lead = [(0, 0)] * (piece.ndim - 2)
+    return jnp.pad(
+        piece, (*lead, (0, rows - piece.shape[-2]), (0, columns - piece.shape[-1]))
+    )
+
+
+muon_counts = (2, 8, 8, 2, 1)
+
+
+def first_owner():
+    return lax.axis_size(("dp", "copy")) // 4
+
+
+def owner_tables():
+    matrices = [14, 14] + [8 + i // 2 for i in range(8)] + list(range(8)) + [12, 13, 15]
+    shared = [1.0] * 10 + [0.0] * 11
+    devices, start = (lax.axis_size(("dp", "copy")), first_owner())
+    rest = devices - start - len(matrices)
+    return (
+        jnp.asarray([0] * start + matrices + [0] * rest, jnp.int32),
+        jnp.asarray([0.0] * start + shared + [0.0] * rest, jnp.float32),
+    )
+
+
+def owner_buffer(modulate, expand, attend, dense, condition, rows, columns):
+    devices, start = (lax.axis_size(("dp", "copy")), first_owner())
+    groups = [jnp.zeros((start, rows, columns), jnp.bfloat16)]
+    for given, count in zip((modulate, expand, attend, dense, condition), muon_counts):
+        held = 0
+        for member in given:
+            if isinstance(member, int):
+                groups.append(jnp.zeros((member, rows, columns), jnp.bfloat16))
+                held += member
+            else:
+                groups.append(padded(to_low(member), rows, columns))
+                held += member.shape[0]
+        assert held == count
+    groups.append(
+        jnp.zeros((devices - start - sum(muon_counts), rows, columns), jnp.bfloat16)
+    )
+    return jnp.concatenate(groups, axis=0)
+
+
+def two_parts(values):
+    return values.reshape(-1, values.shape[-2] // 2, values.shape[-1])
+
+
+def exchange_task(buffer, lag):
+    (arrived,) = yield ([lax.all_to_all(buffer, ("dp", "copy"), 0, 0)], lag)
+    return arrived
+
+
+def muon_steps(moments, held, inverse):
+    devices, highest, widest = held.shape
+    held = held.reshape(devices * highest, widest)
     me = lax.axis_index(("dp", "copy"))
-    matrix_here = jnp.asarray([slot[0] if slot else 0 for slot in slots], jnp.int32)[me]
-    shared_here = jnp.asarray([1.0 if slot and slot[2] == 2 else 0.0 for slot in slots])[me]
-    scale_here = inverse[matrix_here]
+    matrix_here, shared_here = owner_tables()
+    scale_here = inverse[matrix_here[me]]
     gram_matrix = product_left(held, held)
-    gram_matrix = gram_matrix + shared_here * swap_core(gram_matrix)
+    gram_matrix = gram_matrix + shared_here[me] * swap_core(gram_matrix)
     extra = newton_extra(gram_matrix * (scale_here * scale_here))
     result = to_low(product(held, to_low(extra)) * scale_here)
     back = lax.all_to_all(result.reshape(devices, highest, widest), ("dp", "copy"), 0, 0)
-    found = []
-    for matrix, piece in enumerate(pieces):
-        parts = [
-            back[device, : piece.shape[0] // slot[2], : piece.shape[1]]
-            for device, slot in enumerate(slots)
-            if slot and slot[0] == matrix
-        ]
-        whole = jnp.concatenate(parts, axis=0) if len(parts) > 1 else parts[0]
-        found.append(
-            newton_first * newton_first * inverse[matrix] * piece + whole.astype(jnp.float32)
-        )
+    scaled = newton_first * newton_first * inverse
+    found, start = ([], first_owner())
+    shapes = [moments[i].shape for i in (3, 1, 0, 2, 4)]
+    for shape, count in zip(shapes, muon_counts):
+        part = back[start : start + count]
+        rows = math.prod(shape[:-1]) // count
+        found.append(part[:, :rows, : shape[-1]].reshape(shape).astype(jnp.float32))
+        start += count
+    modulate, expand, attend, dense, condition = found
     return (
-        jnp.stack(found[:8]),
-        jnp.stack(found[8:12]),
-        jnp.stack(found[12:14]),
-        found[14],
-        found[15],
+        scaled[:8, None, None] * moments[0] + attend,
+        scaled[8:12, None, None] * moments[1] + expand,
+        scaled[12:14, None, None] * moments[2] + dense,
+        scaled[14] * moments[3] + modulate,
+        scaled[15] * moments[4] + condition,
     )
 
 
@@ -521,15 +542,26 @@
     entry_part = gathered([attend_low[:4], encoder_turned])
     expand_part = gathered([expand_slots[0], expand_slots[1]])
     later_part = gathered([attend_low[4:], expand_slots[2], expand_slots[3]])
-    modulate_slots = to_low(modulate_weight).reshape(-1, wide, HW)
-    head_part = gathered(
-        [
-            padded(to_low(head_table).T, wide, HW)[None],
-            padded(to_low(condition_weight), wide, HW)[None],
-            dense_low,
-            modulate_slots,
-        ]
-    )
+    modulate_rows = modulate_weight.shape[0]
+    head_part = lax.all_gather(
+        jnp.concatenate(
+            [
+                to_low(modulate_weight),
+                dense_low[0],
+                dense_low[1],
+                padded(to_low(condition_weight), wide, HW),
+                padded(to_low(head_table).T, wide, HW),
+            ],
+            axis=0,
+        )[None],
+        everywhere,
+        axis=0,
+        tiled=True,
+    )
+
+    def rows_of(start, count):
+        return head_part[:, start : start + count].reshape(-1, HW)
+
     attend_all = [entry_part[:4], later_part[:4]]
     expand_all = [
         (
@@ -541,15 +573,10 @@
     encoder_all = jnp.concatenate([entry_part[4 + i] for i in range(table_slots)], axis=1).T[
         : encoder_table.shape[0]
     ]
-    head_all = head_part[0][:, : head_table.shape[0]].T
-    condition_all = head_part[1][:, :D]
-    dense_all = head_part[2:4]
-    modulate_all = (
-        head_part[4:]
-        .reshape(modulate_slots.shape[0], -1, wide, HW)
-        .transpose(1, 0, 2, 3)
-        .reshape(modulate_slots.shape[0] * HW, HW)
-    )
+    modulate_all = rows_of(0, modulate_rows)
+    dense_all = [rows_of(modulate_rows, wide), rows_of(modulate_rows + wide, wide)]
+    condition_all = rows_of(modulate_rows + 2 * wide, wide)[:, :D]
+    head_all = rows_of(modulate_rows + 3 * wide, wide)[:, : head_table.shape[0]].T
     halfway = SEQ // 2
     offset = core * halfway
 
@@ -597,6 +624,28 @@
     latent_low = to_low(latent)
     condition_own = to_low(product_right(latent_low, condition_all))
     condition_rows = jnp.concatenate([condition_own, swap_core(condition_own)], axis=0)
+    highest = max(
+        modulate_weight.shape[0] // 2,
+        expand_weight.shape[1] // 2,
+        attend_weight.shape[1],
+        dense_weight.shape[1],
+        condition_weight.shape[0],
+    )
+    condition_rows, velocity_buffer = lax.optimization_barrier(
+        (
+            condition_rows,
+            owner_buffer(
+                [two_parts(modulate_velocity)],
+                [two_parts(expand_velocity)],
+                [attend_velocity],
+                [dense_velocity],
+                [condition_velocity[None]],
+                highest,
+                HW,
+            ),
+        )
+    )
+    flow.begin("velocity", exchange_task(velocity_buffer, 2))
     step_float = own_first(timesteps[0, 0]).astype(jnp.float32)
     alpha_row = alpha_bar(step_float)[:, None]
     target = own_first(noise_copies[0, 0]).astype(jnp.float32)
@@ -657,6 +706,39 @@
         ),
     )
     state_grad, gain_nine, gain_ten = third_back(product(condition_grad, condition_all))
+
+    def modulate_whole():
+        (left_parts,), (right_parts,) = (flow.results["modulate.2"], flow.results["modulate.3"])
+        quarters = [left_parts[0], right_parts[0], left_parts[1], right_parts[1]]
+        return jnp.concatenate(quarters, axis=-1)[0]
+
+    def attend_whole(depth):
+        lower = flow.results["lower%d" % depth]
+        return jnp.concatenate([*flow.results["attend%d" % depth], lower[1]], axis=0)
+
+    def expand_whole(depth):
+        lower, upper = (flow.results["lower%d" % depth], flow.results["upper%d" % depth])
+        return jnp.stack([lower[0].reshape(-1, D), upper[0].reshape(-1, D)])
+
+    def dense_whole():
+        return jnp.concatenate(flow.results["head"][:2], axis=0)
+
+    flow.when(
+        ["head", "modulate.2", "modulate.3", "upper1", "lower1", "attend1"],
+        "early",
+        lambda: exchange_task(
+            owner_buffer(
+                [two_parts(modulate_whole())],
+                [4, two_parts(expand_whole(1))],
+                [4, attend_whole(1)],
+                [dense_whole()],
+                [flow.results["head"][2]],
+                highest,
+                HW,
+            ),
+            4,
+        ),
+    )
     gain_parts = [None, None]
     for depth_index in (1, 0):
         state_grad, gain_parts[depth_index] = block_backward(
@@ -696,32 +778,25 @@
         ],
         axis=1,
     ).T
-    blocks = [name + str(i) for i in range(2) for name in ("upper", "lower", "attend")]
-    flow.take("head", "modulate.2", "modulate.3", *blocks)
-    results = flow.results
-    attend_parts, expand_parts = ([], [])
-    for depth_index in range(2):
-        lower_delta, output_delta = results["lower%d" % depth_index]
-        (upper_delta,) = results["upper%d" % depth_index]
-        attend_parts += [member[0] for member in results["attend%d" % depth_index]]
-        attend_parts.append(output_delta[0])
-        expand_parts += [lower_delta.reshape(-1, D), upper_delta.reshape(-1, D)]
-    first_delta, second_delta, condition_delta, head_delta = results["head"]
-    (left_parts,), (right_parts,) = (results["modulate.2"], results["modulate.3"])
+    flow.take("upper0", "lower0", "attend0")
+    late_rows = max(expand_weight.shape[1] // 2, attend_weight.shape[1])
+    late = lax.all_to_all(
+        owner_buffer(
+            [2], [two_parts(expand_whole(0)), 4], [attend_whole(0), 4], [2], [1], late_rows, D
+        ),
+        everywhere,
+        0,
+        0,
+    )
     reduced = (
-        jnp.stack(attend_parts),
-        jnp.stack(expand_parts),
-        jnp.stack([first_delta[0], second_delta[0]]),
-        jnp.concatenate([left_parts[0], right_parts[0], left_parts[1], right_parts[1]], axis=-1)[0],
-        condition_delta[0],
+        jnp.concatenate([attend_whole(0), attend_whole(1)], axis=0),
+        jnp.concatenate([expand_whole(0), expand_whole(1)], axis=0),
+        dense_whole(),
+        modulate_whole(),
+        flow.results["head"][2][0],
         encoder_delta,
-        head_delta[0].T,
-    )
-    squares = sum((jnp.sum(member * member) for member in reduced))
-    totals = sum_all(jnp.stack([squares, loss_local]))
-    square_total, loss_sum = (totals[0], totals[1])
-    clip_norm = jnp.sqrt(square_total)
-    factor = jnp.minimum(1.0, clip_bound / (clip_norm + 1e-06))
+        flow.results["head"][3][0].T,
+    )
     velocities = (
         attend_velocity,
         expand_velocity,
@@ -729,8 +804,43 @@
         modulate_velocity,
         condition_velocity,
     )
+
+    def pairs_of(left, right):
+        return jnp.concatenate(
+            [
+                jnp.sum((left[i] * right[i]).reshape(-1, *left[i].shape[-2:]), axis=(1, 2))
+                for i in range(5)
+            ]
+        )
+
+    table_squares = sum(jnp.sum(member * member) for member in reduced[5:])
+    totals = sum_all(
+        jnp.concatenate(
+            [
+                pairs_of(reduced, reduced),
+                pairs_of(velocities, reduced),
+                pairs_of(velocities, velocities),
+                jnp.stack([table_squares, loss_local]),
+            ]
+        )
+    )
+    loss_sum = totals[49]
+    clip_norm = jnp.sqrt(jnp.sum(totals[:16]) + totals[48])
+    factor = jnp.minimum(1.0, clip_bound / (clip_norm + 1e-06))
+    moment_squares = (
+        factor * factor * totals[:16]
+        + 2.0 * muon_keep * factor * totals[16:32]
+        + muon_keep * muon_keep * totals[32:48]
+    )
+    inverse = 1.0 / (jnp.sqrt(jnp.maximum(moment_squares, 0.0)) + 1e-07)
     moments = tuple((muon_keep * velocities[i] + factor * reduced[i] for i in range(5)))
-    current = muon_steps(moments)
+    early, velocity_held = flow.take("early", "velocity")
+    held = to_low(
+        muon_keep * velocity_held.astype(jnp.float32)
+        + factor
+        * (early.astype(jnp.float32) + padded(late, highest, HW).astype(jnp.float32))
+    )
+    current = muon_steps(moments, held, inverse)
     devices = lax.axis_size(everywhere)
     masters = (attend_weight, expand_weight, dense_weight, modulate_weight, condition_weight)
     updated = tuple(

time: 1600 us -> 1630 us (1.019)
  waiting for transfers between devices: 470 us -> 639 us
  blocking collectives: 119 us -> 0 us
  matrix products: 481 us -> 447 us
    all_to_all x1 -> x0, blocking collectives: 119 us -> none  [muon_steps(): lax.all_to_all(jnp.stack(sending), ('dp', 'copy'), 0, 0)]
    ppermute x40, waiting for transfers between devices: 137 us -> 251 us  [scatter_task(): arrived, = (yield ([lax.ppermute(joined(sent, axis), 'dp', pairs)], lag))]
    all_to_all x0 -> x3, waiting for transfers between devices: none -> 64.2 us  [the longest x2 64.2 us: exchange_task(): arrived, = (yield ([lax.all_to_all(buffer, ('dp', 'copy'), 0, 0)], lag))]
    all_gather x4 -> x3, waiting for transfers between devices: 196 us -> 140 us  [gathered(): lax.all_gather(jnp.concatenate(members, axis=0), everywhere, axis=1, tile...]
    all_gather x0 -> x1, waiting for transfers between devices: none -> 51.1 us  [per_device(): lax.all_gather(jnp.concatenate([to_low(modulate_weight), dense_low[0], de...]
    dot_general x5 -> x0, matrix products: 50.8 us -> none  [fine(): jnp.dot(left_side, right_side, precision=lax.Precision.HIGH, preferred_el...]
    dot_general x21 -> x25, matrix products: 93.1 us -> 119 us  [product(): return jnp.dot(left_side, right_side, preferred_element_type=jnp.float32)]
    unnamed x655 -> x785, local copies, waits for them, and re-layouts: 37.8 us -> 60.5 us
  transfers between devices with their start and end apart: 95 -> 93, of which waited for: 37 -> 31; matrix products, arithmetic and copies ran while one was open for 36% -> 37% of each run, Pallas kernels for 0% -> 0%
where the time goes in v4:
time: 1630 us; the launch traced here: 1620 us
  waiting for transfers between devices  639 us (39%)
  matrix products  447 us (27%)
  other arithmetic  224 us (14%)
  local copies, waits for them, and re-layouts  185 us (11%)
  starting transfers between devices  89.5 us (5%)
  between operations  33.2 us (2%)
    ppermute x40, waiting for transfers between devices, scatter_task(): arrived, = (yield ([lax.ppermute(joined(sent, axis), 'dp', pairs)], lag))  251 us
    all_gather x3, waiting for transfers between devices, gathered(): lax.all_gather(jnp.concatenate(members, axis=0), everywhere, axis=1, tile...  140 us
    dot_general x25, matrix products, product(): return jnp.dot(left_side, right_side, preferred_element_type=jnp.float32)  119 us
    all_to_all x1, waiting for transfers between devices, muon_steps(): lax.all_to_all(result.reshape(devices, highest, widest), ('dp', 'copy'),...  113 us
    dot_general x29, matrix products, product_left(): lax.dot_general(left_side, right_side, (((0,), (0,)), ((), ())), preferre...  98.8 us
    dot_general x17, matrix products, product_right(): lax.dot_general(left_side, right_side, (((1,), (1,)), ((), ())), preferre...  74.9 us
    all_to_all x2, waiting for transfers between devices, exchange_task(): arrived, = (yield ([lax.all_to_all(buffer, ('dp', 'copy'), 0, 0)], lag))  64.2 us
    sub x2, matrix products, block_backward(): soft_grad - jnp.sum(probability * soft_grad, axis=-1, keepdims=True)  62 us
  transfers between devices with their start and end apart: 93, of which 31 were waited for; matrix products, arithmetic and copies ran while one was open for 37% of the time, Pallas kernels for 0%

profile of v4, /device:TPU:0, one launch (start us, length us, event | category | flops | bytes accessed | tf_op | source)
XLA Modules:
  0.0 1617.2 jit_solution(4204663656196006969)
XLA Ops:
  31.4 55.4 %all-gather.6.cloned.1.call-done = bf16[6,768,768]{2,1,0:T(8,128)(2,1)} async-done(((bf16[6,24,768]{2,1,0:T(8,128)(2,1)}), bf16[6,768,768]{2,1,0:T(8,128)(2,1)}) %all-gather.6.cloned.1.call-update) | async-done | bytes 7077904 | tf_op jit(solution)/shard_map/all_gather | solution.py:540
  134.3 12.4 fusion.6
  146.8 12.5 fusion.4
  162.6 9.1 fusion.69
  192.2 84.1 %all-gather.10.cloned.1.call-done = bf16[12,768,768]{2,1,0:T(8,128)(2,1)} async-done(((bf16[12,24,768]{2,1,0:T(8,128)(2,1)}), bf16[12,768,768]{2,1,0:T(8,128)(2,1)}) %all-gather.10.cloned.1.call-update) | async-done | bytes 14155792 | tf_op jit(solution)/shard_map/all_gather | solution.py:540
  301.8 12.9 fusion.7
  314.7 12.4 fusion.5
  330.3 8.9 fusion.68
  351.5 51.1 %all-gather.12.cloned.1.call-done = bf16[9216,1024]{1,0:T(8,128)(2,1)} async-done(((bf16[288,1024]{1,0:T(8,128)(2,1)}), bf16[9216,1024]{1,0:T(8,128)(2,1)}) %all-gather.12.cloned.1.call-update) | async-done | bytes 18874384 | tf_op jit(solution)/shard_map/all_gather | solution.py:546
  408.7 10.8 slice.820
  432.0 16.3 %fusion.404 = f32[1024,5120]{0,1:T(8,128)} fusion(bf16[5120,1024]{1,0:T(8,128)(2,1)S(1)} %bitcast.652, bf16[1024,1024]{0,1:T(8,128)(2,1)} %get-tuple-element.401), kind=kOutput, calls=%fused_computation.892 | convolution fusion | flops 10737418240 | bytes 33554432 | tf_op jit(solution)/shard_map/dot_general | solution.py:48
  508.3 10.7 fusion.129
  525.6 20.7 %fusion.367 = (bf16[1024,1024]{0,1:T(8,128)(2,1)S(1)}, f32[1024,1024]{0,1:T(8,128)}) fusion(f32[1024,1024]{0,1:T(8,128)} %get-tuple-element.402, bf16[1024,1024]{0,1:T(8,128)(2,1)} %copy-done.154, bf16[1024,5120]{0,1:T(8,128)(2,1)} %copy-done.44, bf16[5120,1024]{1,0:T(8,128)(2,1)} %bitcast.649), kind=kOutput, calls=%fused_computation.859 | convolution fusion | flops 10750001152 | bytes 33554432 | tf_op jit(solution)/shard_map/dot_general | solution.py:38
  566.4 8.7 fusion.123
  575.6 64.2 %all-to-all-done = bf16[32,80,1024]{2,1,0:T(8,128)(2,1)} async-done(((bf16[32,80,1024]{2,1,0:T(8,128)(2,1)}), bf16[32,80,1024]{2,1,0:T(8,128)(2,1)}, u32[]{:S(2)}, u32[]{:S(2)}) %all-to-all-start) | async-done | bytes 5242912 | tf_op jit(solution)/shard_map/all_to_all | solution.py:456
  654.2 13.6 add_bitcast_fusion
  672.6 12.4 fusion.31
  750.1 13.2 collective-permute-done.20
  767.6 31.0 %multiply_convert_fusion.1 = bf16[12,512,1024]{2,1,0:T(8,128)(2,1)} fusion(f32[12,512]{1,0:T(8,128)S(1)} %copy-done.309, f32[12,512,1024]{2,1,0:T(8,128)} %get-tuple-element.394, pred[512,1024]{1,0:T(8,128)(4,1)S(1)} %copy-done.38, bf16[512,12,64]{0,2,1:T(8,128)(2,1)} %bitcast.739, bf16[1024,12,64]{0,2,1:T(8,128)(2,1)S(1)} %bitcast.733), kind=kOutput, calls=%fused_computation.5 | convolution fusion | flops 1679825920 | bytes 40656896 | tf_op jit(solution)/shard_map/sub | solution.py:360
  798.6 13.7 fusion.58
  857.2 32.9 %collective-permute-done.26 = bf16[4,2,2,48,384]{4,3,2,1,0:T(8,128)(2,1)S(1)} collective-permute-done((bf16[4,2,2,48,384]{4,3,2,1,0:T(8,128)(2,1)S(1)}, bf16[4,2,2,48,384]{4,3,2,1,0:T(8,128)(2,1)S(1)}, u32[]{:S(2)}, u32[]{:S(2)}) %collective-permute-start.26) | collective-permute-done | bytes 589856 | tf_op jit(solution)/shard_map/ppermute | solution.py:189
  996.7 10.0 collective-permute-done.47
  1006.8 31.1 %multiply_convert_fusion = bf16[12,512,1024]{2,1,0:T(8,128)(2,1)} fusion(f32[12,512]{1,0:T(8,128)S(1)} %copy-done.308, f32[12,512,1024]{2,1,0:T(8,128)} %get-tuple-element.388, pred[512,1024]{1,0:T(8,128)(4,1)S(1)} %copy-done.39, bf16[512,12,64]{0,2,1:T(8,128)(2,1)} %bitcast.743, bf16[1024,12,64]{0,2,1:T(8,128)(2,1)S(1)} %bitcast.731), kind=kOutput, calls=%fused_computation.2 | convolution fusion | flops 1679825920 | bytes 40656896 | tf_op jit(solution)/shard_map/sub | solution.py:360
  1037.9 13.8 fusion.61
  1082.5 31.1 %collective-permute-done.54 = bf16[5,2,2,2,48,384]{5,4,1,2,3,0:T(8,128)(2,1)S(1)} collective-permute-done((bf16[5,2,2,2,48,384]{5,4,1,2,3,0:T(8,128)(2,1)S(1)}, bf16[5,2,2,2,48,384]{5,4,1,2,3,0:T(8,128)(2,1)S(1)}, u32[]{:S(2)}, u32[]{:S(2)}) %collective-permute-start.54) | collective-permute-done | bytes 1474592 | tf_op jit(solution)/shard_map/ppermute | solution.py:189
  1161.9 15.1 collective-permute-done.64
  1183.4 9.1 collective-permute-done.69
  1209.1 88.6 %collective-permute-done.72 = bf16[2,2,48,550]{3,2,1,0:T(8,128)(2,1)S(1)} collective-permute-done((bf16[2,2,48,550]{3,2,1,0:T(8,128)(2,1)S(1)}, bf16[2,2,48,550]{3,2,1,0:T(8,128)(2,1)S(1)}, u32[]{:S(2)}, u32[]{:S(2)}) %collective-permute-start.72) | collective-permute-done | bytes 211232 | tf_op jit(solution)/shard_map/ppermute | solution.py:189
  1301.9 29.0 %collective-permute-done.73 = bf16[5,48,384]{2,1,0:T(8,128)(2,1)S(1)} collective-permute-done((bf16[5,48,384]{2,1,0:T(8,128)(2,1)S(1)}, bf16[5,48,384]{2,1,0:T(8,128)(2,1)S(1)}, u32[]{:S(2)}, u32[]{:S(2)}) %collective-permute-start.73) | collective-permute-done | bytes 184352 | tf_op jit(solution)/shard_map/ppermute | solution.py:189
  1444.2 13.9 multiply_add_fusion
  1458.0 16.7 %multiply_convert_fusion.2 = bf16[2560,1024]{1,0:T(8,128)(2,1)} fusion(bf16[2560,1024]{1,0:T(8,128)(2,1)} %bitcast.674, f32[]{:T(128)} %bitcast.245, f32[1024,1024]{1,0:T(8,128)} %copy-done.345, f32[1024,1024]{1,0:T(8,128)} %multiply_add_fusion), kind=kOutput, calls=%fused_computation.27 | convolution fusion | flops 7527727104 | bytes 18874372 | tf_op jit(solution)/shard_map/dot_general | solution.py:38
  1483.1 112.6 %all-to-all-done.3 = bf16[32,80,1024]{2,1,0:T(8,128)(2,1)} async-done(((bf16[32,80,1024]{2,1,0:T(8,128)(2,1)}), bf16[32,80,1024]{2,1,0:T(8,128)(2,1)}, u32[]{:S(2)}, u32[]{:S(2)}) %all-to-all-start.3) | async-done | bytes 5242912 | tf_op jit(solution)/shard_map/all_to_all | solution.py:470
  (1464 shorter events, 706.0 us)
Async XLA Ops:
  7.2 79.6 %all-gather.6.cloned.1.call-start = ((), (), s32[]{:S(2)}) async-start(), calls=%async_computation.4 | async-start | bytes 7299072 | tf_op jit(solution)/shard_map/all_gather | solution.py:540
  10.2 165.5 %all-gather.8.cloned.1.call-start = ((), (), s32[]{:S(2)}) async-start(), calls=%async_computation.5 | async-start | bytes 9732096 | tf_op jit(solution)/shard_map/all_gather | solution.py:540
  11.2 265.1 %all-gather.10.cloned.1.call-start = ((), (), s32[]{:S(2)}) async-start(), calls=%async_computation.6 | async-start | bytes 14598144 | tf_op jit(solution)/shard_map/all_gather | solution.py:540
  12.1 390.5 %all-gather.12.cloned.1.call-start = ((), (), s32[]{:S(2)}) async-start(), calls=%async_computation.7 | async-start | bytes 19464192 | tf_op jit(solution)/shard_map/all_gather | solution.py:546
  19.5 81.5 %collective-permute-start.5 = (f32[]{:T(128)}, f32[]{:T(128)}, u32[]{:S(2)}, u32[]{:S(2)}) collective-permute-start(f32[]{:T(128)} %reduce_sum.698), channel_id=1, source_target_pairs={{0,1},{1,0},{2,3},{3,2},{4,5},{5,4},{6,7},{7,6},{8,9},{9,8},{10,11... | collective-permute-start | bytes 20 | tf_op jit(solution)/shard_map/ppermute | solution.py:99
  519.1 120.7 %collective-permute-start.11 = (f32[5120,512]{1,0:T(8,128)}, f32[5120,512]{1,0:T(8,128)}, u32[]{:S(2)}, u32[]{:S(2)}) collective-permute-start(f32[5120,512]{1,0:T(8,128)} %fusion.129), channel_id=1, source_target_pairs={{0,1},{1,0},{2,3},{3,2},{4,5},{5,4},{6,7},{7,6},{8,9},{9,8},{10,11... | collective-permute-start | bytes 31457288 | tf_op jit(solution)/shard_map/ppermute | solution.py:99
  519.4 120.4 %all-to-all-start = ((bf16[32,80,1024]{2,1,0:T(8,128)(2,1)}), bf16[32,80,1024]{2,1,0:T(8,128)(2,1)}, u32[]{:S(2)}, u32[]{:S(2)}) async-start(bf16[32,80,1024]{2,1,0:T(8,128)(2,1)} %broadcast_dynamic-update-slice_fusion.6), calls=%async_computation | async-start | bytes 10485760 | tf_op jit(solution)/shard_map/all_to_all | solution.py:456
  550.6 137.8 %collective-permute-start.12 = (f32[1024,512]{1,0:T(8,128)}, f32[1024,512]{1,0:T(8,128)}, u32[]{:S(2)}, u32[]{:S(2)}) collective-permute-start(f32[1024,512]{1,0:T(8,128)} %fusion.127), channel_id=1, source_target_pairs={{0,1},{1,0},{2,3},{3,2},{4,5},{5,4},{6,7},{7,6},{8,9},{9,8},{10,11... | collective-permute-start | bytes 6291464 | tf_op jit(solution)/shard_map/ppermute | solution.py:99
  554.1 135.9 %collective-permute-start.13 = (f32[1024,512]{1,0:T(8,128)}, f32[1024,512]{1,0:T(8,128)}, u32[]{:S(2)}, u32[]{:S(2)}) collective-permute-start(f32[1024,512]{1,0:T(8,128)} %fusion.125), channel_id=1, source_target_pairs={{0,1},{1,0},{2,3},{3,2},{4,5},{5,4},{6,7},{7,6},{8,9},{9,8},{10,11... | collective-permute-start | bytes 6291464 | tf_op jit(solution)/shard_map/ppermute | solution.py:99
  558.7 128.8 %collective-permute-start.15 = (f32[1024,192]{0,1:T(8,128)}, f32[1024,192]{0,1:T(8,128)}, u32[]{:S(2)}, u32[]{:S(2)}) collective-permute-start(f32[1024,192]{0,1:T(8,128)} %constant_dynamic-slice_fusion.40), channel_id=1, source_target_pairs={{0,1},{1,0},{2,3},{3,2},{4,5},{5,4},{6,7},{7,6},{8,9},{9,8},{10,11... | collective-permute-start | bytes 2359304 | tf_op jit(solution)/shard_map/ppermute | solution.py:99
  646.0 44.0 %collective-permute-start.14 = (f32[1024,384]{1,0:T(8,128)}, f32[1024,384]{1,0:T(8,128)}, u32[]{:S(2)}, u32[]{:S(2)}) collective-permute-start(f32[1024,384]{1,0:T(8,128)} %fusion.212), channel_id=1, source_target_pairs={{0,1},{1,0},{2,3},{3,2},{4,5},{5,4},{6,7},{7,6},{8,9},{9,8},{10,11... | collective-permute-start | bytes 4718600 | tf_op jit(solution)/shard_map/ppermute | solution.py:99
  687.5 40.3 %collective-permute-start.17 = (bf16[1,2,2,2,320,256]{5,4,1,2,3,0:T(8,128)(2,1)}, bf16[1,2,2,2,320,256]{5,4,1,2,3,0:T(8,128)(2,1)}, u32[]{:S(2)}, u32[]{:S(2)}) collective-permute-start(bf16[1,2,2,2,320,256]{5,4,1,2,3,0:T(8,128)(2,1)} %fusion.73), channel_id=1, source_target_pairs={{0,2},{2,0},{4,6},{6,4},{8,10},{10,8},{12,14},{14,12},{16,18},{18,... | collective-permute-start | bytes 3932168 | tf_op jit(solution)/shard_map/ppermute | solution.py:189
  694.0 73.5 %collective-permute-start.21 = (f32[3072,384]{1,0:T(8,128)}, f32[3072,384]{1,0:T(8,128)}, u32[]{:S(2)}, u32[]{:S(2)}) collective-permute-start(f32[3072,384]{1,0:T(8,128)} %fusion.205), channel_id=1, source_target_pairs={{0,1},{1,0},{2,3},{3,2},{4,5},{5,4},{6,7},{7,6},{8,9},{9,8},{10,11... | collective-permute-start | bytes 14155784 | tf_op jit(solution)/shard_map/ppermute | solution.py:99
  724.4 43.2 %collective-permute-start.19 = (bf16[1,2,2,2,64,1792]{5,4,3,2,1,0:T(8,128)(2,1)}, bf16[1,2,2,2,64,1792]{5,4,3,2,1,0:T(8,128)(2,1)}, u32[]{:S(2)}, u32[]{:S(2)}) collective-permute-start(bf16[1,2,2,2,64,1792]{5,4,3,2,1,0:T(8,128)(2,1)} %concatenate.288), channel_id=1, source_target_pairs={{0,4},{2,6},{4,0},{6,2},{8,12},{10,14},{12,8},{14,10},{16,20},{18,... | collective-permute-start | bytes 5505032 | tf_op jit(solution)/shard_map/ppermute | solution.py:189
  744.6 67.7 %collective-permute-start.23 = (bf16[1,2,2,320,256]{4,3,1,2,0:T(8,128)(2,1)}, bf16[1,2,2,320,256]{4,3,1,2,0:T(8,128)(2,1)}, u32[]{:S(2)}, u32[]{:S(2)}) collective-permute-start(bf16[1,2,2,320,256]{4,3,1,2,0:T(8,128)(2,1)} %fusion.145), channel_id=1, source_target_pairs={{0,4},{2,6},{4,0},{6,2},{8,12},{10,14},{12,8},{14,10},{16,20},{18,... | collective-permute-start | bytes 1966088 | tf_op jit(solution)/shard_map/ppermute | solution.py:189
  763.4 49.0 %collective-permute-start.24 = (bf16[1,2,2,320,256]{4,3,1,2,0:T(8,128)(2,1)}, bf16[1,2,2,320,256]{4,3,1,2,0:T(8,128)(2,1)}, u32[]{:S(2)}, u32[]{:S(2)}) collective-permute-start(bf16[1,2,2,320,256]{4,3,1,2,0:T(8,128)(2,1)} %fusion.146), channel_id=1, source_target_pairs={{0,2},{2,0},{4,6},{6,4},{8,10},{10,8},{12,14},{14,12},{16,18},{18,... | collective-permute-start | bytes 1966088 | tf_op jit(solution)/shard_map/ppermute | solution.py:189
  835.6 54.5 %collective-permute-start.25 = (bf16[1,2,2,64,1792]{4,3,2,1,0:T(8,128)(2,1)}, bf16[1,2,2,64,1792]{4,3,2,1,0:T(8,128)(2,1)S(1)}, u32[]{:S(2)}, u32[]{:S(2)}) collective-permute-start(bf16[1,2,2,64,1792]{4,3,2,1,0:T(8,128)(2,1)} %concatenate.289), channel_id=1, source_target_pairs={{0,2},{2,0},{4,6},{6,4},{8,10},{10,8},{12,14},{14,12},{16,18},{18,... | collective-permute-start | bytes 2752520 | tf_op jit(solution)/shard_map/ppermute | solution.py:189
  844.2 46.0 %collective-permute-start.27 = (bf16[5,2,2,2,48,384]{5,4,1,2,3,0:T(8,128)(2,1)S(1)}, bf16[5,2,2,2,48,384]{5,4,1,2,3,0:T(8,128)(2,1)S(1)}, u32[]{:S(2)}, u32[]{:S(2)}) collective-permute-start(bf16[5,2,2,2,48,384]{5,4,1,2,3,0:T(8,128)(2,1)S(1)} %pad_maximum_fusion.6), channel_id=1, source_target_pairs={{0,4},{2,6},{4,0},{6,2},{8,12},{10,14},{12,8},{14,10},{16,20},{18,... | collective-permute-start | bytes 4423688 | tf_op jit(solution)/shard_map/ppermute | solution.py:189
  848.3 41.9 %collective-permute-start.26 = (bf16[4,2,2,48,384]{4,3,2,1,0:T(8,128)(2,1)S(1)}, bf16[4,2,2,48,384]{4,3,2,1,0:T(8,128)(2,1)S(1)}, u32[]{:S(2)}, u32[]{:S(2)}) collective-permute-start(bf16[4,2,2,48,384]{4,3,2,1,0:T(8,128)(2,1)S(1)} %fusion.159), channel_id=1, source_target_pairs={{0,4},{2,6},{4,0},{6,2},{8,12},{10,14},{12,8},{14,10},{16,20},{18,... | collective-permute-start | bytes 1769480 | tf_op jit(solution)/shard_map/ppermute | solution.py:189
  851.9 46.6 %collective-permute-start.30 = (bf16[1,2,320,256]{3,2,1,0:T(8,128)(2,1)}, bf16[1,2,320,256]{3,2,1,0:T(8,128)(2,1)}, u32[]{:S(2)}, u32[]{:S(2)}) collective-permute-start(bf16[1,2,320,256]{3,2,1,0:T(8,128)(2,1)} %fusion.215), channel_id=1, source_target_pairs={{0,8},{2,10},{4,12},{6,14},{8,0},{10,2},{12,4},{14,6},{16,24},{18,... | collective-permute-start | bytes 983048 | tf_op jit(solution)/shard_map/ppermute | solution.py:189
  854.1 44.4 %collective-permute-start.31 = (bf16[1,2,320,256]{3,2,1,0:T(8,128)(2,1)}, bf16[1,2,320,256]{3,2,1,0:T(8,128)(2,1)}, u32[]{:S(2)}, u32[]{:S(2)}) collective-permute-start(bf16[1,2,320,256]{3,2,1,0:T(8,128)(2,1)} %fusion.216), channel_id=1, source_target_pairs={{0,8},{2,10},{4,12},{6,14},{8,0},{10,2},{12,4},{14,6},{16,24},{18,... | collective-permute-start | bytes 983048 | tf_op jit(solution)/shard_map/ppermute | solution.py:189
  910.0 46.0 %collective-permute-start.36 = (bf16[1,320,256]{2,1,0:T(8,128)(2,1)}, bf16[1,320,256]{2,1,0:T(8,128)(2,1)}, u32[]{:S(2)}, u32[]{:S(2)}) collective-permute-start(bf16[1,320,256]{2,1,0:T(8,128)(2,1)} %fusion.248), channel_id=1, source_target_pairs={{0,16},{2,18},{4,20},{6,22},{8,24},{10,26},{12,28},{14,30},{16,0},... | collective-permute-start | bytes 491528 | tf_op jit(solution)/shard_map/ppermute | solution.py:189
  994.0 57.7 %collective-permute-start.50 = (bf16[5,48,384]{2,1,0:T(8,128)(2,1)}, bf16[5,48,384]{2,1,0:T(8,128)(2,1)}, u32[]{:S(2)}, u32[]{:S(2)}) collective-permute-start(bf16[5,48,384]{2,1,0:T(8,128)(2,1)} %pad_maximum_fusion.30), channel_id=1, source_target_pairs={{0,16},{2,18},{4,20},{6,22},{8,24},{10,26},{12,28},{14,30},{16,0},... | collective-permute-start | bytes 552968 | tf_op jit(solution)/shard_map/ppermute | solution.py:189
  995.6 56.1 %collective-permute-start.51 = (bf16[1,2,2,48,1152]{4,3,1,2,0:T(8,128)(2,1)}, bf16[1,2,2,48,1152]{4,3,1,2,0:T(8,128)(2,1)}, u32[]{:S(2)}, u32[]{:S(2)}) collective-permute-start(bf16[1,2,2,48,1152]{4,3,1,2,0:T(8,128)(2,1)} %fusion.177), channel_id=1, source_target_pairs={{0,4},{2,6},{4,0},{6,2},{8,12},{10,14},{12,8},{14,10},{16,20},{18,... | collective-permute-start | bytes 1327112 | tf_op jit(solution)/shard_map/ppermute | solution.py:189
  1073.9 39.8 %collective-permute-start.54 = (bf16[5,2,2,2,48,384]{5,4,1,2,3,0:T(8,128)(2,1)S(1)}, bf16[5,2,2,2,48,384]{5,4,1,2,3,0:T(8,128)(2,1)S(1)}, u32[]{:S(2)}, u32[]{:S(2)}) collective-permute-start(bf16[5,2,2,2,48,384]{5,4,1,2,3,0:T(8,128)(2,1)S(1)} %pad_maximum_fusion.7), channel_id=1, source_target_pairs={{0,4},{2,6},{4,0},{6,2},{8,12},{10,14},{12,8},{14,10},{16,20},{18,... | collective-permute-start | bytes 4423688 | tf_op jit(solution)/shard_map/ppermute | solution.py:189
  1077.1 41.5 %collective-permute-start.57 = (bf16[1,2,48,1152]{3,2,1,0:T(8,128)(2,1)S(1)}, bf16[1,2,48,1152]{3,2,1,0:T(8,128)(2,1)S(1)}, u32[]{:S(2)}, u32[]{:S(2)}) collective-permute-start(bf16[1,2,48,1152]{3,2,1,0:T(8,128)(2,1)S(1)} %fusion.241), channel_id=1, source_target_pairs={{0,8},{2,10},{4,12},{6,14},{8,0},{10,2},{12,4},{14,6},{16,24},{18,... | collective-permute-start | bytes 663560 | tf_op jit(solution)/shard_map/ppermute | solution.py:189
  1197.2 147.7 %all-to-all-start.1 = ((bf16[32,80,1024]{2,1,0:T(8,128)(2,1)}), bf16[32,80,1024]{2,1,0:T(8,128)(2,1)}, u32[]{:S(2)}, u32[]{:S(2)}) async-start(bf16[32,80,1024]{2,1,0:T(8,128)(2,1)} %broadcast_dynamic-update-slice_fusion.5), calls=%async_computation.1 | async-start | bytes 10485760 | tf_op jit(solution)/shard_map/all_to_all | solution.py:456
  1203.8 93.8 %collective-permute-start.71 = (bf16[1,2,48,1152]{3,2,1,0:T(8,128)(2,1)S(1)}, bf16[1,2,48,1152]{3,2,1,0:T(8,128)(2,1)S(1)}, u32[]{:S(2)}, u32[]{:S(2)}) collective-permute-start(bf16[1,2,48,1152]{3,2,1,0:T(8,128)(2,1)S(1)} %fusion.242), channel_id=1, source_target_pairs={{0,8},{2,10},{4,12},{6,14},{8,0},{10,2},{12,4},{14,6},{16,24},{18,... | collective-permute-start | bytes 663560 | tf_op jit(solution)/shard_map/ppermute | solution.py:189
  1205.8 91.9 %collective-permute-start.72 = (bf16[2,2,48,550]{3,2,1,0:T(8,128)(2,1)S(1)}, bf16[2,2,48,550]{3,2,1,0:T(8,128)(2,1)S(1)}, u32[]{:S(2)}, u32[]{:S(2)}) collective-permute-start(bf16[2,2,48,550]{3,2,1,0:T(8,128)(2,1)S(1)} %pad_maximum_fusion.28), channel_id=1, source_target_pairs={{0,8},{2,10},{4,12},{6,14},{8,0},{10,2},{12,4},{14,6},{16,24},{18,... | collective-permute-start | bytes 633608 | tf_op jit(solution)/shard_map/ppermute | solution.py:189
  1206.3 124.6 %collective-permute-start.73 = (bf16[5,48,384]{2,1,0:T(8,128)(2,1)S(1)}, bf16[5,48,384]{2,1,0:T(8,128)(2,1)S(1)}, u32[]{:S(2)}, u32[]{:S(2)}) collective-permute-start(bf16[5,48,384]{2,1,0:T(8,128)(2,1)S(1)} %pad_maximum_fusion.31), channel_id=1, source_target_pairs={{0,16},{2,18},{4,20},{6,22},{8,24},{10,26},{12,28},{14,30},{16,0},... | collective-permute-start | bytes 552968 | tf_op jit(solution)/shard_map/ppermute | solution.py:189
  1344.9 61.0 %all-to-all-start.2 = ((bf16[32,48,768]{2,1,0:T(8,128)(2,1)}), bf16[32,48,768]{2,1,0:T(8,128)(2,1)S(1)}, u32[]{:S(2)}, u32[]{:S(2)}) async-start(bf16[32,48,768]{2,1,0:T(8,128)(2,1)} %broadcast_dynamic-update-slice_fusion.9), calls=%async_computation.2 | async-start | bytes 4718592 | tf_op jit(solution)/shard_map/all_to_all | solution.py:783
  1474.8 120.9 %all-to-all-start.3 = ((bf16[32,80,1024]{2,1,0:T(8,128)(2,1)}), bf16[32,80,1024]{2,1,0:T(8,128)(2,1)}, u32[]{:S(2)}, u32[]{:S(2)}) async-start(bf16[32,80,1024]{2,1,0:T(8,128)(2,1)} %bitcast.673), calls=%async_computation.3 | async-start | bytes 10485760 | tf_op jit(solution)/shard_map/all_to_all | solution.py:470
  (446 other events, 5227.9 us)
Sparse Core Ops, SparseCore 0:
  11.6 75.1 all-gather.5
  90.3 80.5 all-gather.7
  174.4 101.8 all-gather.9
  279.6 122.8 all-gather.11

commit v5 on v4

--- a/solution.py
+++ b/solution.py
@@ -113,13 +113,10 @@
 
 class Flow:
     def __init__(self):
-        self.live, self.results, self.waiting = ([], {}, [])
+        self.live, self.results = ([], {})
 
     def begin(self, name, task):
         self.live.append([name, task, *next(task)])
-
-    def when(self, names, name, make):
-        self.waiting.append((names, name, make))
 
     def tick(self, *carry):
         due = [entry for entry in self.live if entry[3] <= 1]
@@ -132,10 +129,6 @@
             except StopIteration as stop:
                 self.results[entry[0]] = stop.value
                 self.live.remove(entry)
-        for entry in list(self.waiting):
-            if all(name in self.results for name in entry[0]):
-                self.waiting.remove(entry)
-                self.begin(entry[1], entry[2]())
         return carry if len(carry) > 1 else (carry[0] if carry else None)
 
     def take(self, *names):
@@ -411,7 +404,7 @@
     )
 
 
-muon_counts = (2, 8, 8, 2, 1)
+muon_counts = (4, 8, 8, 2, 1)
 
 
 def first_owner():
@@ -419,13 +412,14 @@
 
 
 def owner_tables():
-    matrices = [14, 14] + [8 + i // 2 for i in range(8)] + list(range(8)) + [12, 13, 15]
-    shared = [1.0] * 10 + [0.0] * 11
     devices, start = (lax.axis_size(("dp", "copy")), first_owner())
-    rest = devices - start - len(matrices)
+
+    def table(values, kind):
+        return jnp.asarray([0] * start + values + [0] * (devices - start - len(values)), kind)
+
     return (
-        jnp.asarray([0] * start + matrices + [0] * rest, jnp.int32),
-        jnp.asarray([0.0] * start + shared + [0.0] * rest, jnp.float32),
+        table([1] * 12 + [0] * 11, jnp.float32),
+        table([1] * 4 + [0] * 19, jnp.float32),
     )
 
 
@@ -448,26 +442,58 @@
     return jnp.concatenate(groups, axis=0)
 
 
-def two_parts(values):
-    return values.reshape(-1, values.shape[-2] // 2, values.shape[-1])
-
-
-def exchange_task(buffer, lag):
-    (arrived,) = yield ([lax.all_to_all(buffer, ("dp", "copy"), 0, 0)], lag)
-    return arrived
-
-
-def muon_steps(moments, held, inverse):
-    devices, highest, widest = held.shape
-    held = held.reshape(devices * highest, widest)
-    me = lax.axis_index(("dp", "copy"))
-    matrix_here, shared_here = owner_tables()
-    scale_here = inverse[matrix_here[me]]
+def in_parts(values, count):
+    return values.reshape(-1, values.shape[-2] // count, values.shape[-1])
+
+
+def muon_steps(moments):
+    attend, expand, dense, modulate, condition = moments
+    highest = max(
+        modulate.shape[0] // 4,
+        expand.shape[1] // 2,
+        attend.shape[1],
+        dense.shape[1],
+        condition.shape[0],
+    )
+    held = lax.all_to_all(
+        owner_buffer(
+            [in_parts(modulate, 4)],
+            [in_parts(expand, 2)],
+            [attend],
+            [dense],
+            [condition[None]],
+            highest,
+            HW,
+        ),
+        ("dp", "copy"),
+        0,
+        0,
+    )
+    devices = held.shape[0]
+    held = held.reshape(devices * highest, HW)
+    core, me = (lax.axis_index("copy"), lax.axis_index(("dp", "copy")))
+    shared_here, crossed_here = owner_tables()
     gram_matrix = product_left(held, held)
     gram_matrix = gram_matrix + shared_here[me] * swap_core(gram_matrix)
+    chips = [(i, i ^ 1) for i in range(lax.axis_size("dp"))]
+    near = lax.ppermute(to_low(columns_of(gram_matrix, core)), "dp", chips)
+    far = swap_core(near)
+    crossed = jnp.concatenate(
+        [jnp.where(core == 0, near, far), jnp.where(core == 0, far, near)], axis=1
+    )
+    gram_matrix = gram_matrix + crossed_here[me] * crossed.astype(jnp.float32)
+    rows = lax.broadcasted_iota(jnp.int32, gram_matrix.shape, 0)
+    columns = lax.broadcasted_iota(jnp.int32, gram_matrix.shape, 1)
+    trace = jnp.sum(jnp.where(rows == columns, gram_matrix, 0.0))
+    scale_here = 1.0 / (jnp.sqrt(trace) + 1e-07)
     extra = newton_extra(gram_matrix * (scale_here * scale_here))
     result = to_low(product(held, to_low(extra)) * scale_here)
-    back = lax.all_to_all(result.reshape(devices, highest, widest), ("dp", "copy"), 0, 0)
+    back = lax.all_to_all(result.reshape(devices, highest, HW), ("dp", "copy"), 0, 0)
+    squares = [
+        jnp.sum((member * member).reshape(-1, *member.shape[-2:]), axis=(1, 2))
+        for member in moments
+    ]
+    inverse = 1.0 / (jnp.sqrt(sum_all(jnp.concatenate(squares))) + 1e-07)
     scaled = newton_first * newton_first * inverse
     found, start = ([], first_owner())
     shapes = [moments[i].shape for i in (3, 1, 0, 2, 4)]
@@ -624,28 +650,6 @@
     latent_low = to_low(latent)
     condition_own = to_low(product_right(latent_low, condition_all))
     condition_rows = jnp.concatenate([condition_own, swap_core(condition_own)], axis=0)
-    highest = max(
-        modulate_weight.shape[0] // 2,
-        expand_weight.shape[1] // 2,
-        attend_weight.shape[1],
-        dense_weight.shape[1],
-        condition_weight.shape[0],
-    )
-    condition_rows, velocity_buffer = lax.optimization_barrier(
-        (
-            condition_rows,
-            owner_buffer(
-                [two_parts(modulate_velocity)],
-                [two_parts(expand_velocity)],
-                [attend_velocity],
-                [dense_velocity],
-                [condition_velocity[None]],
-                highest,
-                HW,
-            ),
-        )
-    )
-    flow.begin("velocity", exchange_task(velocity_buffer, 2))
     step_float = own_first(timesteps[0, 0]).astype(jnp.float32)
     alpha_row = alpha_bar(step_float)[:, None]
     target = own_first(noise_copies[0, 0]).astype(jnp.float32)
@@ -723,22 +727,6 @@
     def dense_whole():
         return jnp.concatenate(flow.results["head"][:2], axis=0)
 
-    flow.when(
-        ["head", "modulate.2", "modulate.3", "upper1", "lower1", "attend1"],
-        "early",
-        lambda: exchange_task(
-            owner_buffer(
-                [two_parts(modulate_whole())],
-                [4, two_parts(expand_whole(1))],
-                [4, attend_whole(1)],
-                [dense_whole()],
-                [flow.results["head"][2]],
-                highest,
-                HW,
-            ),
-            4,
-        ),
-    )
     gain_parts = [None, None]
     for depth_index in (1, 0):
         state_grad, gain_parts[depth_index] = block_backward(
@@ -778,16 +766,8 @@
         ],
         axis=1,
     ).T
-    flow.take("upper0", "lower0", "attend0")
-    late_rows = max(expand_weight.shape[1] // 2, attend_weight.shape[1])
-    late = lax.all_to_all(
-        owner_buffer(
-            [2], [two_parts(expand_whole(0)), 4], [attend_whole(0), 4], [2], [1], late_rows, D
-        ),
-        everywhere,
-        0,
-        0,
-    )
+    blocks = [name + str(i) for i in range(2) for name in ("upper", "lower", "attend")]
+    flow.take("head", "modulate.2", "modulate.3", *blocks)
     reduced = (
         jnp.concatenate([attend_whole(0), attend_whole(1)], axis=0),
         jnp.concatenate([expand_whole(0), expand_whole(1)], axis=0),
@@ -805,42 +785,13 @@
         condition_velocity,
     )
 
-    def pairs_of(left, right):
-        return jnp.concatenate(
-            [
-                jnp.sum((left[i] * right[i]).reshape(-1, *left[i].shape[-2:]), axis=(1, 2))
-                for i in range(5)
-            ]
-        )
-
-    table_squares = sum(jnp.sum(member * member) for member in reduced[5:])
-    totals = sum_all(
-        jnp.concatenate(
-            [
-                pairs_of(reduced, reduced),
-                pairs_of(velocities, reduced),
-                pairs_of(velocities, velocities),
-                jnp.stack([table_squares, loss_local]),
-            ]
-        )
-    )
-    loss_sum = totals[49]
-    clip_norm = jnp.sqrt(jnp.sum(totals[:16]) + totals[48])
+    squares = sum((jnp.sum(member * member) for member in reduced))
+    totals = sum_all(jnp.stack([squares, loss_local]))
+    square_total, loss_sum = (totals[0], totals[1])
+    clip_norm = jnp.sqrt(square_total)
     factor = jnp.minimum(1.0, clip_bound / (clip_norm + 1e-06))
-    moment_squares = (
-        factor * factor * totals[:16]
-        + 2.0 * muon_keep * factor * totals[16:32]
-        + muon_keep * muon_keep * totals[32:48]
-    )
-    inverse = 1.0 / (jnp.sqrt(jnp.maximum(moment_squares, 0.0)) + 1e-07)
     moments = tuple((muon_keep * velocities[i] + factor * reduced[i] for i in range(5)))
-    early, velocity_held = flow.take("early", "velocity")
-    held = to_low(
-        muon_keep * velocity_held.astype(jnp.float32)
-        + factor
-        * (early.astype(jnp.float32) + padded(late, highest, HW).astype(jnp.float32))
-    )
-    current = muon_steps(moments, held, inverse)
+    current = muon_steps(moments)
     devices = lax.axis_size(everywhere)
     masters = (attend_weight, expand_weight, dense_weight, modulate_weight, condition_weight)
     updated = tuple(

time: 1630 us -> 1460 us (0.90)
  waiting for transfers between devices: 639 us -> 458 us
  blocking collectives: 0 us -> 74.5 us
  other arithmetic: 224 us -> 194 us
  local copies, waits for them, and re-layouts: 185 us -> 158 us
    all_to_all x4 -> x1, waiting for transfers between devices: 177 us -> 0.01 us  [muon_steps(): lax.all_to_all(result.reshape(devices, highest, HW), ('dp', 'copy'), 0, 0)]
    ppermute x40, waiting for transfers between devices: 251 us -> 139 us  [scatter_task(): arrived, = (yield ([lax.ppermute(joined(sent, axis), 'dp', pairs)], lag))]
    all_to_all x0 -> x1, blocking collectives: none -> 74.5 us  [muon_steps(): lax.all_to_all(owner_buffer([in_parts(modulate, 4)], [in_parts(expand, 2)...]
    ppermute x8 -> x12, waiting for transfers between devices: 14.3 us -> 75.1 us  [sum_all(): lax.ppermute(values, 'dp', [(i, i ^ step) for i in range(count)])]
    ppermute x0 -> x1, waiting for transfers between devices: none -> 23.7 us  [muon_steps(): near = lax.ppermute(to_low(columns_of(gram_matrix, core)), 'dp', chips)]
    unnamed x785 -> x717, local copies, waits for them, and re-layouts: 60.5 us -> 43.4 us
    convert_element_type x38 -> x34, other arithmetic: 35.4 us -> 29.1 us  [to_low(): return values.astype(jnp.bfloat16)]
    add x58 -> x56, other arithmetic: 37.6 us -> 38.8 us  [scatter_task(): total = total + piece.astype(jnp.float32)]
  transfers between devices with their start and end apart: 93 -> 97, of which waited for: 31 -> 37; matrix products, arithmetic and copies ran while one was open for 37% -> 38% of each run, Pallas kernels for 0% -> 0%
where the time goes in v5:
time: 1460 us; the launch traced here: 1440 us
  waiting for transfers between devices  458 us (31%)
  matrix products  444 us (30%)
  other arithmetic  194 us (13%)
  local copies, waits for them, and re-layouts  158 us (11%)
  starting transfers between devices  82.1 us (6%)
  blocking collectives  74.5 us (5%)
  between operations  32.7 us (2%)
    all_gather x3, waiting for transfers between devices, gathered(): lax.all_gather(jnp.concatenate(members, axis=0), everywhere, axis=1, tile...  153 us
    ppermute x40, waiting for transfers between devices, scatter_task(): arrived, = (yield ([lax.ppermute(joined(sent, axis), 'dp', pairs)], lag))  139 us
    dot_general x25, matrix products, product(): return jnp.dot(left_side, right_side, preferred_element_type=jnp.float32)  114 us
    dot_general x29, matrix products, product_left(): lax.dot_general(left_side, right_side, (((0,), (0,)), ((), ())), preferre...  103 us
    ppermute x12, waiting for transfers between devices, sum_all(): lax.ppermute(values, 'dp', [(i, i ^ step) for i in range(count)])  75.1 us
    all_to_all x1, blocking collectives, muon_steps(): lax.all_to_all(owner_buffer([in_parts(modulate, 4)], [in_parts(expand, 2)...  74.5 us
    dot_general x17, matrix products, product_right(): lax.dot_general(left_side, right_side, (((1,), (1,)), ((), ())), preferre...  73.5 us
    sub x2, matrix products, block_backward(): soft_grad - jnp.sum(probability * soft_grad, axis=-1, keepdims=True)  62.9 us
  transfers between devices with their start and end apart: 97, of which 37 were waited for; matrix products, arithmetic and copies ran while one was open for 38% of the time, Pallas kernels for 0%

profile of v5, /device:TPU:0, one launch (start us, length us, event | category | flops | bytes accessed | tf_op | source)
XLA Modules:
  0.0 1443.9 jit_solution(11663131461805515800)
XLA Ops:
  21.1 65.7 %all-gather.6.cloned.1.call-done = bf16[6,768,768]{2,1,0:T(8,128)(2,1)} async-done(((bf16[6,24,768]{2,1,0:T(8,128)(2,1)}), bf16[6,768,768]{2,1,0:T(8,128)(2,1)}) %all-gather.6.cloned.1.call-update) | async-done | bytes 7077904 | tf_op jit(solution)/shard_map/all_gather | solution.py:566
  130.1 13.5 fusion.6
  143.7 12.4 fusion.4
  159.5 9.1 fusion.66
  189.5 86.8 %all-gather.10.cloned.1.call-done = bf16[12,768,768]{2,1,0:T(8,128)(2,1)} async-done(((bf16[12,24,768]{2,1,0:T(8,128)(2,1)}), bf16[12,768,768]{2,1,0:T(8,128)(2,1)}) %all-gather.10.cloned.1.call-update) | async-done | bytes 14155792 | tf_op jit(solution)/shard_map/all_gather | solution.py:566
  301.7 12.9 fusion.7
  314.6 12.4 fusion.5
  351.2 51.3 %all-gather.12.cloned.1.call-done = bf16[9216,1024]{1,0:T(8,128)(2,1)} async-done(((bf16[288,1024]{1,0:T(8,128)(2,1)}), bf16[9216,1024]{1,0:T(8,128)(2,1)}) %all-gather.12.cloned.1.call-update) | async-done | bytes 18874384 | tf_op jit(solution)/shard_map/all_gather | solution.py:572
  402.5 10.0 slice.809
  427.3 16.2 %fusion.367 = f32[1024,5120]{0,1:T(8,128)} fusion(bf16[5120,1024]{1,0:T(8,128)(2,1)S(1)} %bitcast.618, bf16[1024,1024]{0,1:T(8,128)(2,1)} %get-tuple-element.386), kind=kOutput, calls=%fused_computation.826 | convolution fusion | flops 10737418240 | bytes 33554432 | tf_op jit(solution)/shard_map/dot_general | solution.py:48
  506.9 12.7 fusion.120
  522.1 20.3 %fusion.330 = (bf16[1024,1024]{0,1:T(8,128)(2,1)S(1)}, f32[1024,1024]{0,1:T(8,128)}) fusion(f32[1024,1024]{0,1:T(8,128)} %get-tuple-element.387, bf16[512,1024]{0,1:T(8,128)(2,1)} %copy-done.313, bf16[512,1024]{0,1:T(8,128)(2,1)} %copy-done.312, bf16[1024,5120]{0,1:T(8,128)(2,1)} %add_convert_fusion, bf16[5120,1024]{1,0:T(8,128)(2,1)} %bitcast.615), kind=kOutput, calls=%fused_computation.793 | convolution fusion | flops 10753146880 | bytes 33554432 | tf_op jit(solution)/shard_map/dot_general | solution.py:38
  576.5 10.8 add_bitcast_fusion
  592.0 12.6 fusion.31
  677.0 13.3 collective-permute-done.20
  693.5 30.8 %multiply_convert_fusion.1 = bf16[12,512,1024]{2,1,0:T(8,128)(2,1)} fusion(f32[12,512]{1,0:T(8,128)S(1)} %copy-done.272, f32[12,512,1024]{2,1,0:T(8,128)} %get-tuple-element.381, pred[512,1024]{1,0:T(8,128)(4,1)S(1)} %copy-done.41, bf16[512,12,64]{0,2,1:T(8,128)(2,1)} %bitcast.696, bf16[1024,12,64]{0,2,1:T(8,128)(2,1)S(1)} %bitcast.692), kind=kOutput, calls=%fused_computation.5 | convolution fusion | flops 1679825920 | bytes 40656896 | tf_op jit(solution)/shard_map/sub | solution.py:353
  724.3 13.9 fusion.55
  783.8 33.0 %collective-permute-done.26 = bf16[4,2,2,48,384]{4,3,2,1,0:T(8,128)(2,1)S(1)} collective-permute-done((bf16[4,2,2,48,384]{4,3,2,1,0:T(8,128)(2,1)S(1)}, bf16[4,2,2,48,384]{4,3,2,1,0:T(8,128)(2,1)S(1)}, u32[]{:S(2)}, u32[]{:S(2)}) %collective-permute-start.26) | collective-permute-done | bytes 589856 | tf_op jit(solution)/shard_map/ppermute | solution.py:182
  933.0 32.1 %multiply_convert_fusion = bf16[12,512,1024]{2,1,0:T(8,128)(2,1)} fusion(f32[12,512]{1,0:T(8,128)S(1)} %copy-done.271, f32[12,512,1024]{2,1,0:T(8,128)} %get-tuple-element.375, pred[512,1024]{1,0:T(8,128)(4,1)S(1)} %copy-done.42, bf16[512,12,64]{0,2,1:T(8,128)(2,1)} %bitcast.698, bf16[1024,12,64]{0,2,1:T(8,128)(2,1)} %bitcast.690), kind=kOutput, calls=%fused_computation.2 | convolution fusion | flops 1679825920 | bytes 40656896 | tf_op jit(solution)/shard_map/sub | solution.py:353
  965.1 11.9 fusion.58
  1018.0 16.2 %collective-permute-done.54 = bf16[5,2,2,2,48,384]{5,4,1,2,3,0:T(8,128)(2,1)} collective-permute-done((bf16[5,2,2,2,48,384]{5,4,1,2,3,0:T(8,128)(2,1)}, bf16[5,2,2,2,48,384]{5,4,1,2,3,0:T(8,128)(2,1)}, u32[]{:S(2)}, u32[]{:S(2)}) %collective-permute-start.54) | collective-permute-done | bytes 1474592 | tf_op jit(solution)/shard_map/ppermute | solution.py:182
  1055.9 10.1 collective-permute-done.59
  1092.6 15.1 %collective-permute-done.64 = bf16[2,2,2,2,48,550]{5,4,3,2,1,0:T(8,128)(2,1)S(1)} collective-permute-done((bf16[2,2,2,2,48,550]{5,4,3,2,1,0:T(8,128)(2,1)S(1)}, bf16[2,2,2,2,48,550]{5,4,3,2,1,0:T(8,128)(2,1)S(1)}, u32[]{:S(2)}, u32[]{:S(2)}) %collective-permute-start.64) | collective-permute-done | bytes 844832 | tf_op jit(solution)/shard_map/ppermute | solution.py:182
  1127.8 13.5 collective-permute-done.72
  1144.7 9.1 collective-permute-done.75
  1188.6 74.5 %all_to_all.10 = bf16[32,48,1024]{2,1,0:T(8,128)(2,1)S(1)} all-to-all(bf16[32,48,1024]{2,1,0:T(8,128)(2,1)S(1)} %broadcast_dynamic-update-slice_fusion.1), channel_id=1, replica_groups=mesh['dp'=16,'copy'=2] {'dp','copy'}, dimensions={0} | all-to-all | bytes 6291456 | tf_op jit(solution)/shard_map/all_to_all | solution.py:458
  1282.7 23.7 %collective-permute-done.90 = bf16[1024,512]{1,0:T(8,128)(2,1)S(1)} collective-permute-done((bf16[1024,512]{1,0:T(8,128)(2,1)S(1)}, bf16[1024,512]{1,0:T(8,128)(2,1)S(1)}, u32[]{:S(2)}, u32[]{:S(2)}) %collective-permute-start.90) | collective-permute-done | bytes 1048608 | tf_op jit(solution)/shard_map/ppermute | solution.py:479
  1312.3 9.5 multiply_add_fusion.3
  1332.2 14.3 multiply_convert_fusion.2
  1354.6 16.8 %collective-permute-done.85 = f32[16]{0:T(128)S(1)} collective-permute-done((f32[16]{0:T(128)S(1)}, f32[16]{0:T(128)S(1)}, u32[]{:S(2)}, u32[]{:S(2)}) %collective-permute-start.85) | collective-permute-done | bytes 96 | tf_op jit(solution)/shard_map/ppermute | solution.py:109
  1376.1 26.1 %collective-permute-done.87 = f32[16]{0:T(128)S(1)} collective-permute-done((f32[16]{0:T(128)S(1)}, f32[16]{0:T(128)S(1)}, u32[]{:S(2)}, u32[]{:S(2)}) %collective-permute-start.87) | collective-permute-done | bytes 96 | tf_op jit(solution)/shard_map/ppermute | solution.py:109
  1407.1 14.7 %collective-permute-done.88 = f32[16]{0:T(128)S(1)} collective-permute-done((f32[16]{0:T(128)S(1)}, f32[16]{0:T(128)S(1)}, u32[]{:S(2)}, u32[]{:S(2)}) %collective-permute-start.88) | collective-permute-done | bytes 96 | tf_op jit(solution)/shard_map/ppermute | solution.py:109
  (1389 shorter events, 685.8 us)
Async XLA Ops:
  7.2 79.6 %all-gather.6.cloned.1.call-start = ((), (), s32[]{:S(2)}) async-start(), calls=%async_computation.2 | async-start | bytes 7299072 | tf_op jit(solution)/shard_map/all_gather | solution.py:566
  10.2 162.5 %all-gather.8.cloned.1.call-start = ((), (), s32[]{:S(2)}) async-start(), calls=%async_computation.3 | async-start | bytes 9732096 | tf_op jit(solution)/shard_map/all_gather | solution.py:566
  11.2 265.1 %all-gather.10.cloned.1.call-start = ((), (), s32[]{:S(2)}) async-start(), calls=%async_computation.4 | async-start | bytes 14598144 | tf_op jit(solution)/shard_map/all_gather | solution.py:566
  12.1 390.4 %all-gather.12.cloned.1.call-start = ((), (), s32[]{:S(2)}) async-start(), calls=%async_computation.5 | async-start | bytes 19464192 | tf_op jit(solution)/shard_map/all_gather | solution.py:572
  14.5 85.7 %collective-permute-start.5 = (f32[]{:T(128)}, f32[]{:T(128)}, u32[]{:S(2)}, u32[]{:S(2)}) collective-permute-start(f32[]{:T(128)} %reduce_sum.555), channel_id=1, source_target_pairs={{0,1},{1,0},{2,3},{3,2},{4,5},{5,4},{6,7},{7,6},{8,9},{9,8},{10,11... | collective-permute-start | bytes 20 | tf_op jit(solution)/shard_map/ppermute | solution.py:99
  519.6 45.9 %collective-permute-start.11 = (f32[5120,512]{1,0:T(8,128)}, f32[5120,512]{1,0:T(8,128)}, u32[]{:S(2)}, u32[]{:S(2)}) collective-permute-start(f32[5120,512]{1,0:T(8,128)} %fusion.120), channel_id=1, source_target_pairs={{0,1},{1,0},{2,3},{3,2},{4,5},{5,4},{6,7},{7,6},{8,9},{9,8},{10,11... | collective-permute-start | bytes 31457288 | tf_op jit(solution)/shard_map/ppermute | solution.py:99
  547.8 69.6 %collective-permute-start.12 = (f32[1024,512]{1,0:T(8,128)}, f32[1024,512]{1,0:T(8,128)}, u32[]{:S(2)}, u32[]{:S(2)}) collective-permute-start(f32[1024,512]{1,0:T(8,128)} %fusion.118), channel_id=1, source_target_pairs={{0,1},{1,0},{2,3},{3,2},{4,5},{5,4},{6,7},{7,6},{8,9},{9,8},{10,11... | collective-permute-start | bytes 6291464 | tf_op jit(solution)/shard_map/ppermute | solution.py:99
  550.9 67.1 %collective-permute-start.13 = (f32[1024,512]{1,0:T(8,128)}, f32[1024,512]{1,0:T(8,128)}, u32[]{:S(2)}, u32[]{:S(2)}) collective-permute-start(f32[1024,512]{1,0:T(8,128)} %fusion.116), channel_id=1, source_target_pairs={{0,1},{1,0},{2,3},{3,2},{4,5},{5,4},{6,7},{7,6},{8,9},{9,8},{10,11... | collective-permute-start | bytes 6291464 | tf_op jit(solution)/shard_map/ppermute | solution.py:99
  555.2 60.7 %collective-permute-start.15 = (f32[1024,192]{0,1:T(8,128)}, f32[1024,192]{0,1:T(8,128)}, u32[]{:S(2)}, u32[]{:S(2)}) collective-permute-start(f32[1024,192]{0,1:T(8,128)} %constant_dynamic-slice_fusion.46), channel_id=1, source_target_pairs={{0,1},{1,0},{2,3},{3,2},{4,5},{5,4},{6,7},{7,6},{8,9},{9,8},{10,11... | collective-permute-start | bytes 2359304 | tf_op jit(solution)/shard_map/ppermute | solution.py:99
  570.6 47.4 %collective-permute-start.14 = (f32[1024,384]{1,0:T(8,128)}, f32[1024,384]{1,0:T(8,128)}, u32[]{:S(2)}, u32[]{:S(2)}) collective-permute-start(f32[1024,384]{1,0:T(8,128)} %fusion.193), channel_id=1, source_target_pairs={{0,1},{1,0},{2,3},{3,2},{4,5},{5,4},{6,7},{7,6},{8,9},{9,8},{10,11... | collective-permute-start | bytes 4718600 | tf_op jit(solution)/shard_map/ppermute | solution.py:99
  575.4 42.6 %collective-permute-start.16 = (f32[3072,384]{1,0:T(8,128)}, f32[3072,384]{1,0:T(8,128)}, u32[]{:S(2)}, u32[]{:S(2)}) collective-permute-start(f32[3072,384]{1,0:T(8,128)} %fusion.191), channel_id=1, source_target_pairs={{0,1},{1,0},{2,3},{3,2},{4,5},{5,4},{6,7},{7,6},{8,9},{9,8},{10,11... | collective-permute-start | bytes 14155784 | tf_op jit(solution)/shard_map/ppermute | solution.py:99
  615.9 38.8 %collective-permute-start.17 = (bf16[1,2,2,2,320,256]{5,4,1,2,3,0:T(8,128)(2,1)}, bf16[1,2,2,2,320,256]{5,4,1,2,3,0:T(8,128)(2,1)}, u32[]{:S(2)}, u32[]{:S(2)}) collective-permute-start(bf16[1,2,2,2,320,256]{5,4,1,2,3,0:T(8,128)(2,1)} %fusion.70), channel_id=1, source_target_pairs={{0,2},{2,0},{4,6},{6,4},{8,10},{10,8},{12,14},{14,12},{16,18},{18,... | collective-permute-start | bytes 3932168 | tf_op jit(solution)/shard_map/ppermute | solution.py:182
  617.4 37.4 %collective-permute-start.18 = (bf16[1,2,2,2,320,256]{5,4,1,2,3,0:T(8,128)(2,1)}, bf16[1,2,2,2,320,256]{5,4,1,2,3,0:T(8,128)(2,1)}, u32[]{:S(2)}, u32[]{:S(2)}) collective-permute-start(bf16[1,2,2,2,320,256]{5,4,1,2,3,0:T(8,128)(2,1)} %fusion.71), channel_id=1, source_target_pairs={{0,4},{2,6},{4,0},{6,2},{8,12},{10,14},{12,8},{14,10},{16,20},{18,... | collective-permute-start | bytes 3932168 | tf_op jit(solution)/shard_map/ppermute | solution.py:182
  622.0 71.4 %collective-permute-start.21 = (f32[3072,384]{1,0:T(8,128)}, f32[3072,384]{1,0:T(8,128)}, u32[]{:S(2)}, u32[]{:S(2)}) collective-permute-start(f32[3072,384]{1,0:T(8,128)} %fusion.186), channel_id=1, source_target_pairs={{0,1},{1,0},{2,3},{3,2},{4,5},{5,4},{6,7},{7,6},{8,9},{9,8},{10,11... | collective-permute-start | bytes 14155784 | tf_op jit(solution)/shard_map/ppermute | solution.py:99
  650.2 43.2 %collective-permute-start.19 = (bf16[1,2,2,2,64,1792]{5,4,1,2,3,0:T(8,128)(2,1)}, bf16[1,2,2,2,64,1792]{5,4,1,2,3,0:T(8,128)(2,1)}, u32[]{:S(2)}, u32[]{:S(2)}) collective-permute-start(bf16[1,2,2,2,64,1792]{5,4,1,2,3,0:T(8,128)(2,1)} %concatenate.254), channel_id=1, source_target_pairs={{0,4},{2,6},{4,0},{6,2},{8,12},{10,14},{12,8},{14,10},{16,20},{18,... | collective-permute-start | bytes 5505032 | tf_op jit(solution)/shard_map/ppermute | solution.py:182
  670.9 67.3 %collective-permute-start.23 = (bf16[1,2,2,320,256]{4,3,1,2,0:T(8,128)(2,1)}, bf16[1,2,2,320,256]{4,3,1,2,0:T(8,128)(2,1)}, u32[]{:S(2)}, u32[]{:S(2)}) collective-permute-start(bf16[1,2,2,320,256]{4,3,1,2,0:T(8,128)(2,1)} %fusion.140), channel_id=1, source_target_pairs={{0,4},{2,6},{4,0},{6,2},{8,12},{10,14},{12,8},{14,10},{16,20},{18,... | collective-permute-start | bytes 1966088 | tf_op jit(solution)/shard_map/ppermute | solution.py:182
  690.3 47.9 %collective-permute-start.24 = (bf16[1,2,2,320,256]{4,3,1,2,0:T(8,128)(2,1)}, bf16[1,2,2,320,256]{4,3,1,2,0:T(8,128)(2,1)}, u32[]{:S(2)}, u32[]{:S(2)}) collective-permute-start(bf16[1,2,2,320,256]{4,3,1,2,0:T(8,128)(2,1)} %fusion.141), channel_id=1, source_target_pairs={{0,2},{2,0},{4,6},{6,4},{8,10},{10,8},{12,14},{14,12},{16,18},{18,... | collective-permute-start | bytes 1966088 | tf_op jit(solution)/shard_map/ppermute | solution.py:182
  761.1 55.6 %collective-permute-start.25 = (bf16[1,2,2,64,1792]{4,3,1,2,0:T(8,128)(2,1)}, bf16[1,2,2,64,1792]{4,3,1,2,0:T(8,128)(2,1)S(1)}, u32[]{:S(2)}, u32[]{:S(2)}) collective-permute-start(bf16[1,2,2,64,1792]{4,3,1,2,0:T(8,128)(2,1)} %concatenate.255), channel_id=1, source_target_pairs={{0,2},{2,0},{4,6},{6,4},{8,10},{10,8},{12,14},{14,12},{16,18},{18,... | collective-permute-start | bytes 2752520 | tf_op jit(solution)/shard_map/ppermute | solution.py:182
  770.8 46.0 %collective-permute-start.27 = (bf16[5,2,2,2,48,384]{5,4,1,2,3,0:T(8,128)(2,1)S(1)}, bf16[5,2,2,2,48,384]{5,4,1,2,3,0:T(8,128)(2,1)S(1)}, u32[]{:S(2)}, u32[]{:S(2)}) collective-permute-start(bf16[5,2,2,2,48,384]{5,4,1,2,3,0:T(8,128)(2,1)S(1)} %pad_maximum_fusion.6), channel_id=1, source_target_pairs={{0,4},{2,6},{4,0},{6,2},{8,12},{10,14},{12,8},{14,10},{16,20},{18,... | collective-permute-start | bytes 4423688 | tf_op jit(solution)/shard_map/ppermute | solution.py:182
  774.8 41.9 %collective-permute-start.26 = (bf16[4,2,2,48,384]{4,3,2,1,0:T(8,128)(2,1)S(1)}, bf16[4,2,2,48,384]{4,3,2,1,0:T(8,128)(2,1)S(1)}, u32[]{:S(2)}, u32[]{:S(2)}) collective-permute-start(bf16[4,2,2,48,384]{4,3,2,1,0:T(8,128)(2,1)S(1)} %fusion.144), channel_id=1, source_target_pairs={{0,4},{2,6},{4,0},{6,2},{8,12},{10,14},{12,8},{14,10},{16,20},{18,... | collective-permute-start | bytes 1769480 | tf_op jit(solution)/shard_map/ppermute | solution.py:182
  778.5 46.7 %collective-permute-start.30 = (bf16[1,2,320,256]{3,2,1,0:T(8,128)(2,1)}, bf16[1,2,320,256]{3,2,1,0:T(8,128)(2,1)}, u32[]{:S(2)}, u32[]{:S(2)}) collective-permute-start(bf16[1,2,320,256]{3,2,1,0:T(8,128)(2,1)} %fusion.196), channel_id=1, source_target_pairs={{0,8},{2,10},{4,12},{6,14},{8,0},{10,2},{12,4},{14,6},{16,24},{18,... | collective-permute-start | bytes 983048 | tf_op jit(solution)/shard_map/ppermute | solution.py:182
  780.9 44.3 %collective-permute-start.31 = (bf16[1,2,320,256]{3,2,1,0:T(8,128)(2,1)}, bf16[1,2,320,256]{3,2,1,0:T(8,128)(2,1)}, u32[]{:S(2)}, u32[]{:S(2)}) collective-permute-start(bf16[1,2,320,256]{3,2,1,0:T(8,128)(2,1)} %fusion.197), channel_id=1, source_target_pairs={{0,8},{2,10},{4,12},{6,14},{8,0},{10,2},{12,4},{14,6},{16,24},{18,... | collective-permute-start | bytes 983048 | tf_op jit(solution)/shard_map/ppermute | solution.py:182
  835.9 46.6 %collective-permute-start.36 = (bf16[1,320,256]{2,1,0:T(8,128)(2,1)}, bf16[1,320,256]{2,1,0:T(8,128)(2,1)}, u32[]{:S(2)}, u32[]{:S(2)}) collective-permute-start(bf16[1,320,256]{2,1,0:T(8,128)(2,1)} %fusion.225), channel_id=1, source_target_pairs={{0,16},{2,18},{4,20},{6,22},{8,24},{10,26},{12,28},{14,30},{16,0},... | collective-permute-start | bytes 491528 | tf_op jit(solution)/shard_map/ppermute | solution.py:182
  866.0 35.5 %collective-permute-start.41 = (bf16[1,64,1792]{2,1,0:T(8,128)(2,1)}, bf16[1,64,1792]{2,1,0:T(8,128)(2,1)S(1)}, u32[]{:S(2)}, u32[]{:S(2)}) collective-permute-start(bf16[1,64,1792]{2,1,0:T(8,128)(2,1)} %concatenate.260), channel_id=1, source_target_pairs={{0,16},{2,18},{4,20},{6,22},{8,24},{10,26},{12,28},{14,30},{16,0},... | collective-permute-start | bytes 688136 | tf_op jit(solution)/shard_map/ppermute | solution.py:182
  923.5 53.5 %collective-permute-start.50 = (bf16[5,48,384]{2,1,0:T(8,128)(2,1)}, bf16[5,48,384]{2,1,0:T(8,128)(2,1)S(1)}, u32[]{:S(2)}, u32[]{:S(2)}) collective-permute-start(bf16[5,48,384]{2,1,0:T(8,128)(2,1)} %pad_maximum_fusion.28), channel_id=1, source_target_pairs={{0,16},{2,18},{4,20},{6,22},{8,24},{10,26},{12,28},{14,30},{16,0},... | collective-permute-start | bytes 552968 | tf_op jit(solution)/shard_map/ppermute | solution.py:182
  924.9 52.1 %collective-permute-start.51 = (bf16[1,2,2,48,1152]{4,3,1,2,0:T(8,128)(2,1)}, bf16[1,2,2,48,1152]{4,3,1,2,0:T(8,128)(2,1)}, u32[]{:S(2)}, u32[]{:S(2)}) collective-permute-start(bf16[1,2,2,48,1152]{4,3,1,2,0:T(8,128)(2,1)} %fusion.158), channel_id=1, source_target_pairs={{0,4},{2,6},{4,0},{6,2},{8,12},{10,14},{12,8},{14,10},{16,20},{18,... | collective-permute-start | bytes 1327112 | tf_op jit(solution)/shard_map/ppermute | solution.py:182
  983.4 34.6 %collective-permute-start.52 = (f32[5,24,384]{2,1,0:T(8,128)}, f32[5,24,384]{2,1,0:T(8,128)}, u32[]{:S(2)}, u32[]{:S(2)}) collective-permute-start(f32[5,24,384]{2,1,0:T(8,128)} %fusion.224), channel_id=1, source_target_pairs={{0,1},{1,0},{2,3},{3,2},{4,5},{5,4},{6,7},{7,6},{8,9},{9,8},{10,11... | collective-permute-start | bytes 552968 | tf_op jit(solution)/shard_map/ppermute | solution.py:99
  999.0 35.2 %collective-permute-start.54 = (bf16[5,2,2,2,48,384]{5,4,1,2,3,0:T(8,128)(2,1)}, bf16[5,2,2,2,48,384]{5,4,1,2,3,0:T(8,128)(2,1)}, u32[]{:S(2)}, u32[]{:S(2)}) collective-permute-start(bf16[5,2,2,2,48,384]{5,4,1,2,3,0:T(8,128)(2,1)} %pad_maximum_fusion.7), channel_id=1, source_target_pairs={{0,4},{2,6},{4,0},{6,2},{8,12},{10,14},{12,8},{14,10},{16,20},{18,... | collective-permute-start | bytes 4423688 | tf_op jit(solution)/shard_map/ppermute | solution.py:182
  1008.3 33.7 %collective-permute-start.57 = (bf16[1,2,48,1152]{3,2,1,0:T(8,128)(2,1)S(1)}, bf16[1,2,48,1152]{3,2,1,0:T(8,128)(2,1)S(1)}, u32[]{:S(2)}, u32[]{:S(2)}) collective-permute-start(bf16[1,2,48,1152]{3,2,1,0:T(8,128)(2,1)S(1)} %fusion.218), channel_id=1, source_target_pairs={{0,8},{2,10},{4,12},{6,14},{8,0},{10,2},{12,4},{14,6},{16,24},{18,... | collective-permute-start | bytes 663560 | tf_op jit(solution)/shard_map/ppermute | solution.py:182
  1049.6 37.1 %collective-permute-start.61 = (bf16[1,48,1152]{2,1,0:T(8,128)(2,1)}, bf16[1,48,1152]{2,1,0:T(8,128)(2,1)}, u32[]{:S(2)}, u32[]{:S(2)}) collective-permute-start(bf16[1,48,1152]{2,1,0:T(8,128)(2,1)} %fusion.240), channel_id=1, source_target_pairs={{0,16},{2,18},{4,20},{6,22},{8,24},{10,26},{12,28},{14,30},{16,0},... | collective-permute-start | bytes 331784 | tf_op jit(solution)/shard_map/ppermute | solution.py:182
  1077.9 34.8 %collective-permute-start.66 = (bf16[4,48,384]{2,1,0:T(8,128)(2,1)}, bf16[4,48,384]{2,1,0:T(8,128)(2,1)}, u32[]{:S(2)}, u32[]{:S(2)}) collective-permute-start(bf16[4,48,384]{2,1,0:T(8,128)(2,1)} %fusion.231), channel_id=1, source_target_pairs={{0,16},{2,18},{4,20},{6,22},{8,24},{10,26},{12,28},{14,30},{16,0},... | collective-permute-start | bytes 442376 | tf_op jit(solution)/shard_map/ppermute | solution.py:182
  1346.6 76.0 %all-to-all-start.1 = ((bf16[32,48,1024]{2,1,0:T(8,128)(2,1)}), bf16[32,48,1024]{2,1,0:T(8,128)(2,1)}, u32[]{:S(2)}, u32[]{:S(2)}) async-start(bf16[32,48,1024]{2,1,0:T(8,128)(2,1)} %bitcast.671), calls=%async_computation.1 | async-start | bytes 6291456 | tf_op jit(solution)/shard_map/all_to_all | solution.py:491
  (422 other events, 5264.4 us)
Sparse Core Ops, SparseCore 0:
  11.6 75.2 all-gather.5
  90.3 80.5 all-gather.7
  174.5 101.8 all-gather.9
  279.7 122.8 all-gather.11

commit v6 on v5

--- a/solution.py
+++ b/solution.py
@@ -3,6 +3,8 @@
 import jax
 import jax.numpy as jnp
 from jax import lax
+from jax.experimental import pallas as pl
+from jax.experimental.pallas import tpu as pltpu
 from jax.sharding import PartitionSpec as P
 
 D = 768
@@ -249,6 +251,83 @@
     return None
 
 
+def attention_back_kernel(
+    query_ref, key_ref, value_ref, grad_ref, log_ref, query_id, key_id, dq_ref, dk_ref, dv_ref
+):
+    same = key_id[...] == query_id[...]
+    query, key, value, grad = (query_ref[...], key_ref[...], value_ref[...], grad_ref[...])
+    width = query.shape[1]
+    lane = lax.broadcasted_iota(jnp.int32, (1, width), 1)
+    query_grad, key_grad, value_grad = (None, None, None)
+    for head in range(width // HD):
+        inside = jnp.where((lane >= head * HD) & (lane < (head + 1) * HD), 1.0, 0.0)
+        query_here = to_low(query.astype(jnp.float32) * inside)
+        grad_here = to_low(grad.astype(jnp.float32) * inside)
+        key_here = to_low(key.astype(jnp.float32) * inside)
+        scores = product_right(key, query_here) * score_factor
+        chance = jnp.where(same, jnp.exp(scores - log_ref[head]), 0.0)
+        soft_grad = product_right(value, grad_here)
+        total = jnp.sum(chance * soft_grad, axis=0, keepdims=True)
+        score_low = to_low(chance * (soft_grad - total) * score_factor)
+        parts = (
+            product_left(key_here, score_low),
+            product(score_low, query_here),
+            product(to_low(chance), grad_here),
+        )
+        if head == 0:
+            query_grad, key_grad, value_grad = parts
+        else:
+            query_grad, key_grad, value_grad = (
+                query_grad + parts[0],
+                key_grad + parts[1],
+                value_grad + parts[2],
+            )
+    dq_ref[...] = to_low(query_grad.T)
+    first = pl.program_id(1) == 0
+
+    @pl.when(first)
+    def _():
+        dk_ref[...] = key_grad
+        dv_ref[...] = value_grad
+
+    @pl.when(jnp.logical_not(first))
+    def _():
+        dk_ref[...] += key_grad
+        dv_ref[...] += value_grad
+
+
+def attention_back(query, key, value, grad, log_total, query_ids, key_ids):
+    queries, keys = (query.shape[0], key.shape[0])
+    width, chunk = (2 * HD, 256)
+    own = pl.BlockSpec((chunk, width), lambda pair, part: (part, pair))
+    whole = pl.BlockSpec((keys, width), lambda pair, part: (0, pair))
+    return pl.pallas_call(
+        attention_back_kernel,
+        grid=(D // width, queries // chunk),
+        in_specs=[
+            own,
+            whole,
+            whole,
+            own,
+            pl.BlockSpec((2, 1, chunk), lambda pair, part: (pair, 0, part)),
+            pl.BlockSpec((1, chunk), lambda pair, part: (0, part)),
+            pl.BlockSpec((keys, 1), lambda pair, part: (0, 0)),
+        ],
+        out_specs=[own, whole, whole],
+        out_shape=[
+            jax.ShapeDtypeStruct((queries, D), jnp.bfloat16),
+            jax.ShapeDtypeStruct((keys, D), jnp.float32),
+            jax.ShapeDtypeStruct((keys, D), jnp.float32),
+        ],
+        compiler_params=pltpu.CompilerParams(vmem_limit_bytes=48 * 2**20),
+        cost_estimate=pl.CostEstimate(
+            flops=10 * queries * keys * D * 2,
+            bytes_accessed=12 * keys * D,
+            transcendentals=queries * keys * HEADS,
+        ),
+    )(query, key, value, grad, log_total, query_ids[None, :], key_ids[:, None])
+
+
 def attention_scores(query_heads, key_heads, same_image):
     raw_scores = jnp.einsum(
         "qhd,khd->hqk", query_heads, key_heads, preferred_element_type=jnp.float32
@@ -290,9 +369,9 @@
     kept = (
         first_back,
         normed_low,
-        query_heads,
-        key_heads,
-        value_heads,
+        query_low,
+        key_all,
+        value_all,
         log_total,
         attended,
         second_back,
@@ -304,13 +383,13 @@
     return (output_rows, kept)
 
 
-def block_backward(output_grad, kept, attend_low, flow, depth, same_image):
+def block_backward(output_grad, kept, attend_low, flow, depth, image_row):
     (
         first_back,
         normed_low,
-        query_heads,
-        key_heads,
-        value_heads,
+        query_low,
+        key_all,
+        value_all,
         log_total,
         attended,
         second_back,
@@ -339,32 +418,17 @@
             0,
         ),
     )
-    attended_grad = to_low(product_right(projected_low, attend_low[3])).reshape(halfway, HEADS, HD)
-    attended_grad = flow.tick(attended_grad)
-    probability = jnp.exp(attention_scores(query_heads, key_heads, same_image) - log_total)
-    soft_grad = jnp.einsum(
-        "qhd,khd->hqk", attended_grad, value_heads, preferred_element_type=jnp.float32
-    )
-    value_part = jnp.einsum(
-        "hqk,qhd->khd", to_low(probability), attended_grad, preferred_element_type=jnp.float32
-    )
-    score_low = to_low(
-        probability
-        * (soft_grad - jnp.sum(probability * soft_grad, axis=-1, keepdims=True))
-        * score_factor
-    )
-    score_low, value_part = flow.tick(score_low, value_part)
-    key_part = jnp.einsum(
-        "hqk,qhd->khd", score_low, query_heads, preferred_element_type=jnp.float32
-    )
-    key_part = flow.tick(key_part)
-    query_grad = to_low(
-        jnp.einsum(
-            "hqk,khd->qhd", score_low, key_heads, preferred_element_type=jnp.float32
-        ).reshape(halfway, D)
-    )
-    key_part = key_part.reshape(SEQ, D)
-    value_part = value_part.reshape(SEQ, D)
+    attended_grad = flow.tick(to_low(product_right(projected_low, attend_low[3])))
+    query_grad, key_part, value_part = attention_back(
+        query_low,
+        key_all,
+        value_all,
+        attended_grad,
+        log_total.reshape(HEADS, 1, halfway),
+        image_row[:halfway],
+        image_row,
+    )
+    key_part, value_part = flow.tick(key_part, value_part)
     value_grad = to_low(
         value_part[:halfway] + swap_core(to_low(value_part[halfway:])).astype(jnp.float32)
     )
@@ -566,8 +630,7 @@
         return lax.all_gather(jnp.concatenate(members, axis=0), everywhere, axis=1, tiled=True)
 
     entry_part = gathered([attend_low[:4], encoder_turned])
-    expand_part = gathered([expand_slots[0], expand_slots[1]])
-    later_part = gathered([attend_low[4:], expand_slots[2], expand_slots[3]])
+    later_part = gathered([expand_slots[0], expand_slots[1], attend_low[4:], *expand_slots[2:]])
     modulate_rows = modulate_weight.shape[0]
     head_part = lax.all_gather(
         jnp.concatenate(
@@ -588,13 +651,13 @@
     def rows_of(start, count):
         return head_part[:, start : start + count].reshape(-1, HW)
 
-    attend_all = [entry_part[:4], later_part[:4]]
+    attend_all = [entry_part[:4], later_part[2 * copies : 2 * copies + 4]]
     expand_all = [
         (
             member[: copies].reshape(copies * D, D),
             member[copies:].reshape(copies * D, D),
         )
-        for member in (expand_part, later_part[4:])
+        for member in (later_part[: 2 * copies], later_part[2 * copies + 4 :])
     ]
     encoder_all = jnp.concatenate([entry_part[4 + i] for i in range(table_slots)], axis=1).T[
         : encoder_table.shape[0]
@@ -735,7 +798,7 @@
             attend_all[depth_index],
             flow,
             depth_index,
-            same_image,
+            image_row,
         )
     embedded_grad, token_grad, position_grad = entry_back(state_grad)
     embed_delta = product_left(own_patch, to_low(embedded_grad))

time: 1460 us -> 1450 us (level)
  matrix products: 444 us -> 342 us
  Pallas kernels: 0 us -> 59 us
  waiting for transfers between devices: 458 us -> 487 us
    sub x2 -> x0, matrix products: 62.9 us -> none  [block_backward(): soft_grad - jnp.sum(probability * soft_grad, axis=-1, keepdims=True)]
    pallas_call x0 -> x2, Pallas kernels: none -> 59 us  [attention_back(): pl.pallas_call(attention_back_kernel, grid=(D // width, queries // chunk)...]
    all_gather x1, waiting for transfers between devices: 51.3 us -> 99.6 us  [per_device(): lax.all_gather(jnp.concatenate([to_low(modulate_weight), dense_low[0], de...]
    dot_general x6 -> x0, matrix products: 45.8 us -> none  [the longest x2 25.8 us: block_backward(): jnp.einsum('hqk,qhd->khd', to_low(probability), attended_grad, preferred_...]
    all_gather x3 -> x2, waiting for transfers between devices: 153 us -> 126 us  [gathered(): lax.all_gather(jnp.concatenate(members, axis=0), everywhere, axis=1, tile...]
    unnamed x717 -> x735, local copies, waits for them, and re-layouts: 43.4 us -> 41.4 us
  transfers between devices with their start and end apart: 97 -> 96, of which waited for: 37 -> 36; matrix products, arithmetic and copies ran while one was open for 38% -> 30% of each run, Pallas kernels for 0% -> 4%
where the time goes in v6:
time: 1450 us; the launch traced here: 1430 us
  waiting for transfers between devices  487 us (34%)
  matrix products  342 us (24%)
  other arithmetic  194 us (13%)
  local copies, waits for them, and re-layouts  161 us (11%)
  starting transfers between devices  82.5 us (6%)
  blocking collectives  74.7 us (5%)
  Pallas kernels  59 us (4%)
  between operations  32.5 us (2%)
    ppermute x40, waiting for transfers between devices, scatter_task(): arrived, = (yield ([lax.ppermute(joined(sent, axis), 'dp', pairs)], lag))  150 us
    all_gather x2, waiting for transfers between devices, gathered(): lax.all_gather(jnp.concatenate(members, axis=0), everywhere, axis=1, tile...  126 us
    dot_general x25, matrix products, product(): return jnp.dot(left_side, right_side, preferred_element_type=jnp.float32)  115 us
    dot_general x29, matrix products, product_left(): lax.dot_general(left_side, right_side, (((0,), (0,)), ((), ())), preferre...  104 us
    all_gather x1, waiting for transfers between devices, per_device(): lax.all_gather(jnp.concatenate([to_low(modulate_weight), dense_low[0], de...  99.6 us
    all_to_all x1, blocking collectives, muon_steps(): lax.all_to_all(owner_buffer([in_parts(modulate, 4)], [in_parts(expand, 2)...  74.7 us
    ppermute x12, waiting for transfers between devices, sum_all(): lax.ppermute(values, 'dp', [(i, i ^ step) for i in range(count)])  74.5 us
    dot_general x17, matrix products, product_right(): lax.dot_general(left_side, right_side, (((1,), (1,)), ((), ())), preferre...  74.4 us
  transfers between devices with their start and end apart: 96, of which 36 were waited for; matrix products, arithmetic and copies ran while one was open for 30% of the time, Pallas kernels for 4%

profile of v6, /device:TPU:0, one launch (start us, length us, event | category | flops | bytes accessed | tf_op | source)
XLA Modules:
  0.0 1432.7 jit_solution(1965880136170505678)
XLA Ops:
  19.6 67.2 %all-gather.5.cloned.1.call-done = bf16[6,768,768]{2,1,0:T(8,128)(2,1)} async-done(((bf16[6,24,768]{2,1,0:T(8,128)(2,1)}), bf16[6,768,768]{2,1,0:T(8,128)(2,1)}) %all-gather.5.cloned.1.call-update) | async-done | bytes 7077904 | tf_op jit(solution)/shard_map/all_gather | solution.py:630
  131.9 14.6 %fusion = (f32[12,512]{1,0:T(8,128)S(1)}, f32[12,512,1024]{2,1,0:T(8,128)}) fusion(pred[512,1024]{1,0:T(8,128)(4,1)} %broadcast_compare_fusion, bf16[512,12,64]{0,2,1:T(8,128)(2,1)} %bitcast.605, bf16[1024,12,64]{0,2,1:T(8,128)(2,1)} %bitcast.579), kind=kOutput, calls=%fused_computation.6 | convolution fusion | flops 824174592 | bytes 28073984 | tf_op jit(solution)/shard_map/qhd,khd->hqk/dot_general | solution.py:332
  146.5 13.0 fusion.2
  162.0 9.7 fusion.44
  177.0 58.4 %all-gather.7.cloned.1.call-done = bf16[20,768,768]{2,1,0:T(8,128)(2,1)} async-done(((bf16[20,24,768]{2,1,0:T(8,128)(2,1)}), bf16[20,768,768]{2,1,0:T(8,128)(2,1)}) %all-gather.7.cloned.1.call-update) | async-done | bytes 23592976 | tf_op jit(solution)/shard_map/all_gather | solution.py:630
  235.5 11.1 fusion.305
  262.2 99.6 %all-gather.9.cloned.1.call-done = bf16[9216,1024]{1,0:T(8,128)(2,1)} async-done(((bf16[288,1024]{1,0:T(8,128)(2,1)}), bf16[9216,1024]{1,0:T(8,128)(2,1)}) %all-gather.9.cloned.1.call-update) | async-done | bytes 18874384 | tf_op jit(solution)/shard_map/all_gather | solution.py:635
  368.1 10.0 slice.791
  396.1 14.4 %fusion.1 = (f32[12,512]{1,0:T(8,128)S(1)}, f32[12,512,1024]{2,1,0:T(8,128)}) fusion(pred[512,1024]{1,0:T(8,128)(4,1)} %broadcast_compare_fusion, bf16[512,12,64]{0,2,1:T(8,128)(2,1)} %bitcast.606, bf16[1024,12,64]{0,2,1:T(8,128)(2,1)} %bitcast.580), kind=kOutput, calls=%fused_computation.7 | convolution fusion | flops 824174592 | bytes 28073984 | tf_op jit(solution)/shard_map/qhd,khd->hqk/dot_general | solution.py:332
  410.5 12.3 fusion.3
  425.9 9.9 fusion.43
  457.9 16.6 %fusion.330 = f32[1024,5120]{0,1:T(8,128)} fusion(bf16[5120,1024]{1,0:T(8,128)(2,1)S(1)} %bitcast.562, bf16[1024,1024]{0,1:T(8,128)(2,1)} %get-tuple-element.394), kind=kOutput, calls=%fused_computation.796 | convolution fusion | flops 10737418240 | bytes 33554432 | tf_op jit(solution)/shard_map/dot_general | solution.py:50
  539.9 12.6 fusion.98
  557.8 20.6 %fusion.300 = (bf16[1024,1024]{0,1:T(8,128)(2,1)S(1)}, f32[1024,1024]{0,1:T(8,128)}) fusion(f32[1024,1024]{0,1:T(8,128)} %get-tuple-element.395, bf16[512,1024]{0,1:T(8,128)(2,1)} %copy-done.329, bf16[512,1024]{0,1:T(8,128)(2,1)} %copy-done.328, bf16[1024,5120]{0,1:T(8,128)(2,1)} %add_convert_fusion, bf16[5120,1024]{1,0:T(8,128)(2,1)} %bitcast.559), kind=kOutput, calls=%fused_computation.768 | convolution fusion | flops 10753146880 | bytes 33554432 | tf_op jit(solution)/shard_map/dot_general | solution.py:40
  613.8 10.8 add_bitcast_fusion
  629.3 12.4 fusion.19
  713.1 14.2 collective-permute-done.20
  733.3 29.5 %shard_map.375 = (bf16[512,768]{1,0:T(8,128)(2,1)S(1)}, f32[1024,768]{1,0:T(8,128)}, f32[1024,768]{1,0:T(8,128)}) custom-call(bf16[512,768]{1,0:T(8,128)(2,1)S(1)} %copy-done.4, bf16[1024,768]{1,0:T(8,128)(2,1)S(1)} %copy-done.1, bf16[1024,768]{1,0:T(8,128)(2,1)S(1)} %copy-done, bf16[512,768]{1,0:T(8,128)(2,1)S(1)} %convolution_convert_fusion.2.grad_ref, ...), custom_call_target="tpu_custom_call" | custom-call | flops 8053063680 | bytes 9437184 | tf_op jit(solution)/shard_map/pallas_call | solution.py:304
  791.7 33.6 %collective-permute-done.28 = bf16[4,2,2,48,384]{4,3,2,1,0:T(8,128)(2,1)S(1)} collective-permute-done((bf16[4,2,2,48,384]{4,3,2,1,0:T(8,128)(2,1)S(1)}, bf16[4,2,2,48,384]{4,3,2,1,0:T(8,128)(2,1)S(1)}, u32[]{:S(2)}, u32[]{:S(2)}) %collective-permute-start.28) | collective-permute-done | bytes 589856 | tf_op jit(solution)/shard_map/ppermute | solution.py:184
  890.9 11.9 collective-permute-done.39
  932.4 9.8 collective-permute-done.42
  964.1 29.5 %shard_map.376 = (bf16[512,768]{1,0:T(8,128)(2,1)S(1)}, f32[1024,768]{1,0:T(8,128)}, f32[1024,768]{1,0:T(8,128)}) custom-call(bf16[512,768]{1,0:T(8,128)(2,1)S(1)} %copy-done.3, bf16[1024,768]{1,0:T(8,128)(2,1)S(1)} %pad_maximum_fusion.1.key_ref, bf16[1024,768]{1,0:T(8,128)(2,1)S(1)} %pad_maximum_fusion.2.value_ref, bf16[512,768]{1,0:T(8,128)(2,1)S(1)} %copy-done.11, ...), custom_call_target="tpu_custom_call" | custom-call | flops 8053063680 | bytes 9437184 | tf_op jit(solution)/shard_map/pallas_call | solution.py:304
  1007.4 21.6 %collective-permute-done.55 = bf16[5,2,2,2,48,384]{5,4,1,2,3,0:T(8,128)(2,1)S(1)} collective-permute-done((bf16[5,2,2,2,48,384]{5,4,1,2,3,0:T(8,128)(2,1)S(1)}, bf16[5,2,2,2,48,384]{5,4,1,2,3,0:T(8,128)(2,1)S(1)}, u32[]{:S(2)}, u32[]{:S(2)}) %collective-permute-start.55) | collective-permute-done | bytes 1474592 | tf_op jit(solution)/shard_map/ppermute | solution.py:184
  1068.3 14.2 collective-permute-done.61
  1124.7 13.3 collective-permute-done.74
  1175.8 74.7 %all_to_all.10 = bf16[32,48,1024]{2,1,0:T(8,128)(2,1)S(1)} all-to-all(bf16[32,48,1024]{2,1,0:T(8,128)(2,1)S(1)} %constant_dynamic-update-slice_fusion.4), channel_id=1, replica_groups=mesh['dp'=16,'copy'=2] {'dp','copy'}, dimensions={0} | all-to-all | bytes 6291456 | tf_op jit(solution)/shard_map/all_to_all | solution.py:522
  1270.3 23.7 %collective-permute-done.90 = bf16[1024,512]{1,0:T(8,128)(2,1)S(1)} collective-permute-done((bf16[1024,512]{1,0:T(8,128)(2,1)S(1)}, bf16[1024,512]{1,0:T(8,128)(2,1)S(1)}, u32[]{:S(2)}, u32[]{:S(2)}) %collective-permute-start.90) | collective-permute-done | bytes 1048608 | tf_op jit(solution)/shard_map/ppermute | solution.py:543
  1300.3 10.4 multiply_add_fusion.3
  1321.1 14.3 multiply_convert_fusion
  1343.4 16.8 %collective-permute-done.85 = f32[16]{0:T(128)S(1)} collective-permute-done((f32[16]{0:T(128)S(1)}, f32[16]{0:T(128)S(1)}, u32[]{:S(2)}, u32[]{:S(2)}) %collective-permute-start.85) | collective-permute-done | bytes 96 | tf_op jit(solution)/shard_map/ppermute | solution.py:111
  1364.9 26.1 %collective-permute-done.87 = f32[16]{0:T(128)S(1)} collective-permute-done((f32[16]{0:T(128)S(1)}, f32[16]{0:T(128)S(1)}, u32[]{:S(2)}, u32[]{:S(2)}) %collective-permute-start.87) | collective-permute-done | bytes 96 | tf_op jit(solution)/shard_map/ppermute | solution.py:111
  1396.8 13.8 collective-permute-done.88
  (1387 shorter events, 649.6 us)
Async XLA Ops:
  7.2 79.6 %all-gather.5.cloned.1.call-start = ((), (), s32[]{:S(2)}) async-start(), calls=%async_computation.2 | async-start | bytes 7299072 | tf_op jit(solution)/shard_map/all_gather | solution.py:630
  10.7 224.8 %all-gather.7.cloned.1.call-start = ((), (), s32[]{:S(2)}) async-start(), calls=%async_computation.3 | async-start | bytes 24330240 | tf_op jit(solution)/shard_map/all_gather | solution.py:630
  11.7 350.1 %all-gather.9.cloned.1.call-start = ((), (), s32[]{:S(2)}) async-start(), calls=%async_computation.4 | async-start | bytes 19464192 | tf_op jit(solution)/shard_map/all_gather | solution.py:635
  14.1 89.3 %collective-permute-start.5 = (f32[]{:T(128)}, f32[]{:T(128)}, u32[]{:S(2)}, u32[]{:S(2)}) collective-permute-start(f32[]{:T(128)} %reduce_sum.539), channel_id=1, source_target_pairs={{0,1},{1,0},{2,3},{3,2},{4,5},{5,4},{6,7},{7,6},{8,9},{9,8},{10,11... | collective-permute-start | bytes 20 | tf_op jit(solution)/shard_map/ppermute | solution.py:101
  258.7 126.9 %collective-permute-start.2 = (bf16[512,768]{1,0:T(8,128)(2,1)}, bf16[512,768]{1,0:T(8,128)(2,1)}, u32[]{:S(2)}, u32[]{:S(2)}) collective-permute-start(bf16[512,768]{1,0:T(8,128)(2,1)} %convolution_convert_fusion.5), channel_id=1, source_target_pairs={{0,1},{1,0},{2,3},{3,2},{4,5},{5,4},{6,7},{7,6},{8,9},{9,8},{10,11... | collective-permute-start | bytes 2359304 | tf_op jit(solution)/shard_map/ppermute | solution.py:101
  262.0 128.8 %collective-permute-start.3 = (bf16[512,768]{1,0:T(8,128)(2,1)}, bf16[512,768]{1,0:T(8,128)(2,1)}, u32[]{:S(2)}, u32[]{:S(2)}) collective-permute-start(bf16[512,768]{1,0:T(8,128)(2,1)} %convolution_convert_fusion.3), channel_id=1, source_target_pairs={{0,1},{1,0},{2,3},{3,2},{4,5},{5,4},{6,7},{7,6},{8,9},{9,8},{10,11... | collective-permute-start | bytes 2359304 | tf_op jit(solution)/shard_map/ppermute | solution.py:101
  552.5 50.3 %collective-permute-start.11 = (f32[5120,512]{1,0:T(8,128)}, f32[5120,512]{1,0:T(8,128)}, u32[]{:S(2)}, u32[]{:S(2)}) collective-permute-start(f32[5120,512]{1,0:T(8,128)} %fusion.98), channel_id=1, source_target_pairs={{0,1},{1,0},{2,3},{3,2},{4,5},{5,4},{6,7},{7,6},{8,9},{9,8},{10,11... | collective-permute-start | bytes 31457288 | tf_op jit(solution)/shard_map/ppermute | solution.py:101
  583.8 70.7 %collective-permute-start.12 = (f32[1024,512]{1,0:T(8,128)}, f32[1024,512]{1,0:T(8,128)}, u32[]{:S(2)}, u32[]{:S(2)}) collective-permute-start(f32[1024,512]{1,0:T(8,128)} %fusion.96), channel_id=1, source_target_pairs={{0,1},{1,0},{2,3},{3,2},{4,5},{5,4},{6,7},{7,6},{8,9},{9,8},{10,11... | collective-permute-start | bytes 6291464 | tf_op jit(solution)/shard_map/ppermute | solution.py:101
  587.0 68.1 %collective-permute-start.13 = (f32[1024,512]{1,0:T(8,128)}, f32[1024,512]{1,0:T(8,128)}, u32[]{:S(2)}, u32[]{:S(2)}) collective-permute-start(f32[1024,512]{1,0:T(8,128)} %fusion.94), channel_id=1, source_target_pairs={{0,1},{1,0},{2,3},{3,2},{4,5},{5,4},{6,7},{7,6},{8,9},{9,8},{10,11... | collective-permute-start | bytes 6291464 | tf_op jit(solution)/shard_map/ppermute | solution.py:101
  592.6 60.5 %collective-permute-start.15 = (f32[1024,192]{0,1:T(8,128)}, f32[1024,192]{0,1:T(8,128)}, u32[]{:S(2)}, u32[]{:S(2)}) collective-permute-start(f32[1024,192]{0,1:T(8,128)} %constant_dynamic-slice_fusion.46), channel_id=1, source_target_pairs={{0,1},{1,0},{2,3},{3,2},{4,5},{5,4},{6,7},{7,6},{8,9},{9,8},{10,11... | collective-permute-start | bytes 2359304 | tf_op jit(solution)/shard_map/ppermute | solution.py:101
  607.9 47.2 %collective-permute-start.14 = (f32[1024,384]{1,0:T(8,128)}, f32[1024,384]{1,0:T(8,128)}, u32[]{:S(2)}, u32[]{:S(2)}) collective-permute-start(f32[1024,384]{1,0:T(8,128)} %fusion.171), channel_id=1, source_target_pairs={{0,1},{1,0},{2,3},{3,2},{4,5},{5,4},{6,7},{7,6},{8,9},{9,8},{10,11... | collective-permute-start | bytes 4718600 | tf_op jit(solution)/shard_map/ppermute | solution.py:101
  612.8 42.3 %collective-permute-start.16 = (f32[3072,384]{1,0:T(8,128)}, f32[3072,384]{1,0:T(8,128)}, u32[]{:S(2)}, u32[]{:S(2)}) collective-permute-start(f32[3072,384]{1,0:T(8,128)} %fusion.169), channel_id=1, source_target_pairs={{0,1},{1,0},{2,3},{3,2},{4,5},{5,4},{6,7},{7,6},{8,9},{9,8},{10,11... | collective-permute-start | bytes 14155784 | tf_op jit(solution)/shard_map/ppermute | solution.py:101
  653.1 40.1 %collective-permute-start.17 = (bf16[1,2,2,2,320,256]{5,4,1,2,3,0:T(8,128)(2,1)}, bf16[1,2,2,2,320,256]{5,4,1,2,3,0:T(8,128)(2,1)}, u32[]{:S(2)}, u32[]{:S(2)}) collective-permute-start(bf16[1,2,2,2,320,256]{5,4,1,2,3,0:T(8,128)(2,1)} %fusion.48), channel_id=1, source_target_pairs={{0,2},{2,0},{4,6},{6,4},{8,10},{10,8},{12,14},{14,12},{16,18},{18,... | collective-permute-start | bytes 3932168 | tf_op jit(solution)/shard_map/ppermute | solution.py:184
  654.5 38.7 %collective-permute-start.18 = (bf16[1,2,2,2,320,256]{5,4,1,2,3,0:T(8,128)(2,1)}, bf16[1,2,2,2,320,256]{5,4,1,2,3,0:T(8,128)(2,1)}, u32[]{:S(2)}, u32[]{:S(2)}) collective-permute-start(bf16[1,2,2,2,320,256]{5,4,1,2,3,0:T(8,128)(2,1)} %fusion.49), channel_id=1, source_target_pairs={{0,4},{2,6},{4,0},{6,2},{8,12},{10,14},{12,8},{14,10},{16,20},{18,... | collective-permute-start | bytes 3932168 | tf_op jit(solution)/shard_map/ppermute | solution.py:184
  659.3 72.7 %collective-permute-start.21 = (f32[3072,384]{1,0:T(8,128)}, f32[3072,384]{1,0:T(8,128)}, u32[]{:S(2)}, u32[]{:S(2)}) collective-permute-start(f32[3072,384]{1,0:T(8,128)} %fusion.164), channel_id=1, source_target_pairs={{0,1},{1,0},{2,3},{3,2},{4,5},{5,4},{6,7},{7,6},{8,9},{9,8},{10,11... | collective-permute-start | bytes 14155784 | tf_op jit(solution)/shard_map/ppermute | solution.py:101
  688.9 43.1 %collective-permute-start.19 = (bf16[1,2,2,2,64,1792]{5,4,1,2,3,0:T(8,128)(2,1)}, bf16[1,2,2,2,64,1792]{5,4,1,2,3,0:T(8,128)(2,1)S(1)}, u32[]{:S(2)}, u32[]{:S(2)}) collective-permute-start(bf16[1,2,2,2,64,1792]{5,4,1,2,3,0:T(8,128)(2,1)} %concatenate.263), channel_id=1, source_target_pairs={{0,4},{2,6},{4,0},{6,2},{8,12},{10,14},{12,8},{14,10},{16,20},{18,... | collective-permute-start | bytes 5505032 | tf_op jit(solution)/shard_map/ppermute | solution.py:184
  704.5 58.3 %collective-permute-start.23 = (bf16[1,2,2,320,256]{4,3,1,2,0:T(8,128)(2,1)}, bf16[1,2,2,320,256]{4,3,1,2,0:T(8,128)(2,1)}, u32[]{:S(2)}, u32[]{:S(2)}) collective-permute-start(bf16[1,2,2,320,256]{4,3,1,2,0:T(8,128)(2,1)} %fusion.118), channel_id=1, source_target_pairs={{0,4},{2,6},{4,0},{6,2},{8,12},{10,14},{12,8},{14,10},{16,20},{18,... | collective-permute-start | bytes 1966088 | tf_op jit(solution)/shard_map/ppermute | solution.py:184
  727.4 35.4 %collective-permute-start.24 = (bf16[1,2,2,320,256]{4,3,1,2,0:T(8,128)(2,1)}, bf16[1,2,2,320,256]{4,3,1,2,0:T(8,128)(2,1)}, u32[]{:S(2)}, u32[]{:S(2)}) collective-permute-start(bf16[1,2,2,320,256]{4,3,1,2,0:T(8,128)(2,1)} %fusion.119), channel_id=1, source_target_pairs={{0,2},{2,0},{4,6},{6,4},{8,10},{10,8},{12,14},{14,12},{16,18},{18,... | collective-permute-start | bytes 1966088 | tf_op jit(solution)/shard_map/ppermute | solution.py:184
  778.3 46.9 %collective-permute-start.29 = (bf16[5,2,2,2,48,384]{5,4,1,2,3,0:T(8,128)(2,1)}, bf16[5,2,2,2,48,384]{5,4,1,2,3,0:T(8,128)(2,1)}, u32[]{:S(2)}, u32[]{:S(2)}) collective-permute-start(bf16[5,2,2,2,48,384]{5,4,1,2,3,0:T(8,128)(2,1)} %pad_maximum_fusion.6), channel_id=1, source_target_pairs={{0,4},{2,6},{4,0},{6,2},{8,12},{10,14},{12,8},{14,10},{16,20},{18,... | collective-permute-start | bytes 4423688 | tf_op jit(solution)/shard_map/ppermute | solution.py:184
  783.8 41.4 %collective-permute-start.27 = (bf16[1,2,2,64,1792]{4,3,1,2,0:T(8,128)(2,1)}, bf16[1,2,2,64,1792]{4,3,1,2,0:T(8,128)(2,1)S(1)}, u32[]{:S(2)}, u32[]{:S(2)}) collective-permute-start(bf16[1,2,2,64,1792]{4,3,1,2,0:T(8,128)(2,1)} %concatenate.267), channel_id=1, source_target_pairs={{0,2},{2,0},{4,6},{6,4},{8,10},{10,8},{12,14},{14,12},{16,18},{18,... | collective-permute-start | bytes 2752520 | tf_op jit(solution)/shard_map/ppermute | solution.py:184
  787.1 38.1 %collective-permute-start.28 = (bf16[4,2,2,48,384]{4,3,2,1,0:T(8,128)(2,1)S(1)}, bf16[4,2,2,48,384]{4,3,2,1,0:T(8,128)(2,1)S(1)}, u32[]{:S(2)}, u32[]{:S(2)}) collective-permute-start(bf16[4,2,2,48,384]{4,3,2,1,0:T(8,128)(2,1)S(1)} %fusion.122), channel_id=1, source_target_pairs={{0,4},{2,6},{4,0},{6,2},{8,12},{10,14},{12,8},{14,10},{16,20},{18,... | collective-permute-start | bytes 1769480 | tf_op jit(solution)/shard_map/ppermute | solution.py:184
  904.7 39.0 %collective-permute-start.46 = (f32[3072,384]{1,0:T(8,128)}, f32[3072,384]{1,0:T(8,128)}, u32[]{:S(2)}, u32[]{:S(2)}) collective-permute-start(f32[3072,384]{1,0:T(8,128)} %fusion.147), channel_id=1, source_target_pairs={{0,1},{1,0},{2,3},{3,2},{4,5},{5,4},{6,7},{7,6},{8,9},{9,8},{10,11... | collective-permute-start | bytes 14155784 | tf_op jit(solution)/shard_map/ppermute | solution.py:101
  913.3 30.3 %collective-permute-start.45 = (bf16[4,2,2,2,48,384]{5,4,0,1,2,3:T(8,128)(2,1)}, bf16[4,2,2,2,48,384]{5,4,0,1,2,3:T(8,128)(2,1)}, u32[]{:S(2)}, u32[]{:S(2)}) collective-permute-start(bf16[4,2,2,2,48,384]{5,4,0,1,2,3:T(8,128)(2,1)} %fusion.52), channel_id=1, source_target_pairs={{0,2},{2,0},{4,6},{6,4},{8,10},{10,8},{12,14},{14,12},{16,18},{18,... | collective-permute-start | bytes 3538952 | tf_op jit(solution)/shard_map/ppermute | solution.py:184
  942.2 52.6 %collective-permute-start.50 = (bf16[1,2,2,48,1152]{4,3,1,2,0:T(8,128)(2,1)}, bf16[1,2,2,48,1152]{4,3,1,2,0:T(8,128)(2,1)}, u32[]{:S(2)}, u32[]{:S(2)}) collective-permute-start(bf16[1,2,2,48,1152]{4,3,1,2,0:T(8,128)(2,1)} %fusion.136), channel_id=1, source_target_pairs={{0,4},{2,6},{4,0},{6,2},{8,12},{10,14},{12,8},{14,10},{16,20},{18,... | collective-permute-start | bytes 1327112 | tf_op jit(solution)/shard_map/ppermute | solution.py:184
  949.7 46.6 %collective-permute-start.48 = (f32[1,32,1600]{2,1,0:T(8,128)}, f32[1,32,1600]{2,1,0:T(8,128)}, u32[]{:S(2)}, u32[]{:S(2)}) collective-permute-start(f32[1,32,1600]{2,1,0:T(8,128)} %constant_dynamic-slice_fusion.19), channel_id=1, source_target_pairs={{0,1},{1,0},{2,3},{3,2},{4,5},{5,4},{6,7},{7,6},{8,9},{9,8},{10,11... | collective-permute-start | bytes 614408 | tf_op jit(solution)/shard_map/ppermute | solution.py:101
  950.5 45.8 %collective-permute-start.49 = (f32[4,24,384]{2,1,0:T(8,128)}, f32[4,24,384]{2,1,0:T(8,128)}, u32[]{:S(2)}, u32[]{:S(2)}) collective-permute-start(f32[4,24,384]{2,1,0:T(8,128)} %constant_dynamic-slice_fusion.18), channel_id=1, source_target_pairs={{0,1},{1,0},{2,3},{3,2},{4,5},{5,4},{6,7},{7,6},{8,9},{9,8},{10,11... | collective-permute-start | bytes 442376 | tf_op jit(solution)/shard_map/ppermute | solution.py:101
  951.8 55.6 %collective-permute-start.53 = (bf16[5,48,384]{2,1,0:T(8,128)(2,1)}, bf16[5,48,384]{2,1,0:T(8,128)(2,1)}, u32[]{:S(2)}, u32[]{:S(2)}) collective-permute-start(bf16[5,48,384]{2,1,0:T(8,128)(2,1)} %pad_maximum_fusion.26), channel_id=1, source_target_pairs={{0,16},{2,18},{4,20},{6,22},{8,24},{10,26},{12,28},{14,30},{16,0},... | collective-permute-start | bytes 552968 | tf_op jit(solution)/shard_map/ppermute | solution.py:184
  955.1 52.2 %collective-permute-start.54 = (bf16[4,2,2,48,384]{4,3,0,1,2:T(8,128)(2,1)}, bf16[4,2,2,48,384]{4,3,0,1,2:T(8,128)(2,1)}, u32[]{:S(2)}, u32[]{:S(2)}) collective-permute-start(bf16[4,2,2,48,384]{4,3,0,1,2:T(8,128)(2,1)} %fusion.124), channel_id=1, source_target_pairs={{0,4},{2,6},{4,0},{6,2},{8,12},{10,14},{12,8},{14,10},{16,20},{18,... | collective-permute-start | bytes 1769480 | tf_op jit(solution)/shard_map/ppermute | solution.py:184
  994.9 34.1 %collective-permute-start.55 = (bf16[5,2,2,2,48,384]{5,4,1,2,3,0:T(8,128)(2,1)S(1)}, bf16[5,2,2,2,48,384]{5,4,1,2,3,0:T(8,128)(2,1)S(1)}, u32[]{:S(2)}, u32[]{:S(2)}) collective-permute-start(bf16[5,2,2,2,48,384]{5,4,1,2,3,0:T(8,128)(2,1)S(1)} %pad_maximum_fusion.7), channel_id=1, source_target_pairs={{0,4},{2,6},{4,0},{6,2},{8,12},{10,14},{12,8},{14,10},{16,20},{18,... | collective-permute-start | bytes 4423688 | tf_op jit(solution)/shard_map/ppermute | solution.py:184
  1003.8 44.0 %collective-permute-start.57 = (bf16[1,2,48,1152]{3,2,1,0:T(8,128)(2,1)S(1)}, bf16[1,2,48,1152]{3,2,1,0:T(8,128)(2,1)S(1)}, u32[]{:S(2)}, u32[]{:S(2)}) collective-permute-start(bf16[1,2,48,1152]{3,2,1,0:T(8,128)(2,1)S(1)} %fusion.196), channel_id=1, source_target_pairs={{0,8},{2,10},{4,12},{6,14},{8,0},{10,2},{12,4},{14,6},{16,24},{18,... | collective-permute-start | bytes 663560 | tf_op jit(solution)/shard_map/ppermute | solution.py:184
  1035.2 33.1 %collective-permute-start.59 = (bf16[4,2,48,384]{3,2,0,1:T(8,128)(2,1)}, bf16[4,2,48,384]{3,2,0,1:T(8,128)(2,1)}, u32[]{:S(2)}, u32[]{:S(2)}) collective-permute-start(bf16[4,2,48,384]{3,2,0,1:T(8,128)(2,1)} %fusion.178), channel_id=1, source_target_pairs={{0,8},{2,10},{4,12},{6,14},{8,0},{10,2},{12,4},{14,6},{16,24},{18,... | collective-permute-start | bytes 884744 | tf_op jit(solution)/shard_map/ppermute | solution.py:184
  1335.4 76.1 %all-to-all-start.1 = ((bf16[32,48,1024]{2,1,0:T(8,128)(2,1)}), bf16[32,48,1024]{2,1,0:T(8,128)(2,1)}, u32[]{:S(2)}, u32[]{:S(2)}) async-start(bf16[32,48,1024]{2,1,0:T(8,128)(2,1)} %bitcast.609), calls=%async_computation.1 | async-start | bytes 6291456 | tf_op jit(solution)/shard_map/all_to_all | solution.py:555
  (424 other events, 5057.6 us)
Sparse Core Ops, SparseCore 0:
  11.6 75.1 all-gather.4
  89.7 145.6 all-gather.6
  238.9 122.8 all-gather.8

commit v7 on v6

--- a/solution.py
+++ b/solution.py
@@ -246,8 +246,8 @@
     (arrived,) = yield ([swap_core(product_left(left_side, columns_of(right_side, 1 - core)))], 1)
     total = (product_left(left_side, columns_of(right_side, core)) + arrived)[None]
     quarter = total.shape[-1] // 2
-    flow.begin(names[0], scatter_task([total[..., :quarter]], False, 0, [False]))
-    flow.begin(names[1], scatter_task([total[..., quarter:]], True, 0, [False]))
+    flow.begin(names[0], scatter_task([total[..., :quarter]], False, 0, [False], 3))
+    flow.begin(names[1], scatter_task([total[..., quarter:]], True, 0, [False], 3))
     return None
 
 
@@ -662,10 +662,6 @@
     encoder_all = jnp.concatenate([entry_part[4 + i] for i in range(table_slots)], axis=1).T[
         : encoder_table.shape[0]
     ]
-    modulate_all = rows_of(0, modulate_rows)
-    dense_all = [rows_of(modulate_rows, wide), rows_of(modulate_rows + wide, wide)]
-    condition_all = rows_of(modulate_rows + 2 * wide, wide)[:, :D]
-    head_all = rows_of(modulate_rows + 3 * wide, wide)[:, : head_table.shape[0]].T
     halfway = SEQ // 2
     offset = core * halfway
 
@@ -680,6 +676,16 @@
     masked_row = own_first(loss_mask[0])
     weight_row = (masked_row * (1 - buffer_row)).astype(jnp.float32)
     token_count = sum_all(jnp.sum(weight_row))
+    step_float = own_first(timesteps[0, 0]).astype(jnp.float32)
+    alpha_row = alpha_bar(step_float)[:, None]
+    target = own_first(noise_copies[0, 0]).astype(jnp.float32)
+    noisy_low = to_low(
+        jnp.sqrt(alpha_row) * patch_seq.astype(jnp.float32) + jnp.sqrt(1.0 - alpha_row) * target
+    )
+    feature_low = to_low(time_features(step_float))
+    encoder_all, noisy_low, feature_low, target = lax.optimization_barrier(
+        (encoder_all, noisy_low, feature_low, target)
+    )
     own_patch = patch_seq[:halfway]
     buffer_on = buffer_row[:halfway, None] > 0
     masked_on = masked_row[:halfway, None] > 0
@@ -709,18 +715,16 @@
             same_image,
         )
         kept_all.append(kept)
+    state_rows, head_part = lax.optimization_barrier((state_rows, head_part))
+    modulate_all = rows_of(0, modulate_rows)
+    dense_all = [rows_of(modulate_rows, wide), rows_of(modulate_rows + wide, wide)]
+    condition_all = rows_of(modulate_rows + 2 * wide, wide)[:, :D]
+    head_all = rows_of(modulate_rows + 3 * wide, wide)[:, : head_table.shape[0]].T
     latent, third_back = jax.vjp(layer_norm, state_rows, gain_rows[8], gain_rows[9])
     latent_low = to_low(latent)
     condition_own = to_low(product_right(latent_low, condition_all))
     condition_rows = jnp.concatenate([condition_own, swap_core(condition_own)], axis=0)
-    step_float = own_first(timesteps[0, 0]).astype(jnp.float32)
-    alpha_row = alpha_bar(step_float)[:, None]
-    target = own_first(noise_copies[0, 0]).astype(jnp.float32)
-    noisy_low = to_low(
-        jnp.sqrt(alpha_row) * patch_seq.astype(jnp.float32) + jnp.sqrt(1.0 - alpha_row) * target
-    )
     lifted = product(noisy_low, head_all[:PATCH])
-    feature_low = to_low(time_features(step_float))
     summed = condition_rows.astype(jnp.float32) + product(
         feature_low, head_all[PATCH : PATCH + FREQ]
     )
@@ -770,6 +774,7 @@
             True,
             -1,
             [head_turned_grad],
+            3,
         ),
     )
     state_grad, gain_nine, gain_ten = third_back(product(condition_grad, condition_all))
@@ -814,21 +819,13 @@
     )
     small_delta = small_delta + swap_core(small_delta)
     small_half = small_delta.shape[0] // 2
-    encoder_half = jnp.concatenate(
-        [position_grad, lax.dynamic_slice_in_dim(small_delta, core * small_half, small_half, 0)],
-        axis=0,
-    ).T
-    flow.begin("encoder", scatter_task([encoder_half[None]], True, 0, [True], 1))
-    encoder_first_half, encoder_last_half = (m[0] for m in flow.take("encoder")[0][0])
-    encoder_delta = jnp.concatenate(
-        [
-            encoder_first_half[:, halfway:],
-            encoder_last_half[:, halfway:],
-            encoder_first_half[:, :halfway],
-            encoder_last_half[:, :halfway],
-        ],
-        axis=1,
-    ).T
+    small_own = lax.dynamic_slice_in_dim(small_delta, core * small_half, small_half, 0)
+    flow.begin(
+        "encoder",
+        scatter_task([small_own.T[None], position_grad.T[None]], True, -1, [True, False], 1),
+    )
+    small_pair, position_pair = flow.take("encoder")[0]
+    encoder_delta = jnp.concatenate([*small_pair, *position_pair], axis=-1)[0].T
     blocks = [name + str(i) for i in range(2) for name in ("upper", "lower", "attend")]
     flow.take("head", "modulate.2", "modulate.3", *blocks)
     reduced = (

time: 1450 us -> 1360 us (0.938)
  waiting for transfers between devices: 487 us -> 378 us
  other arithmetic: 194 us -> 214 us
    all_gather x1, waiting for transfers between devices: 99.6 us -> 8.56 us  [per_device(): lax.all_gather(jnp.concatenate([to_low(modulate_weight), dense_low[0], de...]
    ppermute x40, waiting for transfers between devices: 150 us -> 106 us  [scatter_task(): arrived, = (yield ([lax.ppermute(joined(sent, axis), 'dp', pairs)], lag))]
    all_gather x2, waiting for transfers between devices: 126 us -> 151 us  [gathered(): lax.all_gather(jnp.concatenate(members, axis=0), everywhere, axis=1, tile...]
    add x56 -> x60, other arithmetic: 35.3 us -> 49.7 us  [scatter_task(): total = total + piece.astype(jnp.float32)]
    unnamed x735 -> x739, local copies, waits for them, and re-layouts: 41.4 us -> 47.4 us
    convert_element_type x34 -> x35, other arithmetic: 29.8 us -> 32.8 us  [to_low(): return values.astype(jnp.bfloat16)]
  transfers between devices with their start and end apart: 96 -> 96, of which waited for: 36 -> 34; matrix products, arithmetic and copies ran while one was open for 30% -> 35% of each run, Pallas kernels for 4% -> 4%
where the time goes in v7:
time: 1360 us; the launch traced here: 1340 us
  waiting for transfers between devices  378 us (28%)
  matrix products  328 us (24%)
  other arithmetic  214 us (16%)
  local copies, waits for them, and re-layouts  171 us (13%)
  starting transfers between devices  84.4 us (6%)
  blocking collectives  75.7 us (6%)
  Pallas kernels  59.7 us (4%)
  between operations  33 us (2%)
    all_gather x2, waiting for transfers between devices, gathered(): lax.all_gather(jnp.concatenate(members, axis=0), everywhere, axis=1, tile...  151 us
    dot_general x25, matrix products, product(): return jnp.dot(left_side, right_side, preferred_element_type=jnp.float32)  108 us
    ppermute x40, waiting for transfers between devices, scatter_task(): arrived, = (yield ([lax.ppermute(joined(sent, axis), 'dp', pairs)], lag))  106 us
    dot_general x29, matrix products, product_left(): lax.dot_general(left_side, right_side, (((0,), (0,)), ((), ())), preferre...  98.5 us
    all_to_all x1, blocking collectives, muon_steps(): lax.all_to_all(owner_buffer([in_parts(modulate, 4)], [in_parts(expand, 2)...  75.7 us
    ppermute x12, waiting for transfers between devices, sum_all(): lax.ppermute(values, 'dp', [(i, i ^ step) for i in range(count)])  75.2 us
    dot_general x17, matrix products, product_right(): lax.dot_general(left_side, right_side, (((1,), (1,)), ((), ())), preferre...  72.4 us
    pallas_call x2, Pallas kernels, attention_back(): pl.pallas_call(attention_back_kernel, grid=(D // width, queries // chunk)...  59.7 us
  transfers between devices with their start and end apart: 96, of which 34 were waited for; matrix products, arithmetic and copies ran while one was open for 35% of the time, Pallas kernels for 4%

profile of v7, /device:TPU:0, one launch (start us, length us, event | category | flops | bytes accessed | tf_op | source)
XLA Modules:
  0.0 1344.1 jit_solution(17589283401170194318)
XLA Ops:
  19.7 67.1 %all-gather.5.cloned.1.call-done = bf16[6,768,768]{2,1,0:T(8,128)(2,1)} async-done(((bf16[6,24,768]{2,1,0:T(8,128)(2,1)}), bf16[6,768,768]{2,1,0:T(8,128)(2,1)}) %all-gather.5.cloned.1.call-update) | async-done | bytes 7077904 | tf_op jit(solution)/shard_map/all_gather | solution.py:630
  105.7 14.5 %fusion = (f32[12,512]{1,0:T(8,128)S(1)}, f32[12,512,1024]{2,1,0:T(8,128)}) fusion(pred[512,1024]{1,0:T(8,128)(4,1)} %broadcast_compare_fusion, bf16[512,12,64]{0,2,1:T(8,128)(2,1)} %bitcast.636, bf16[1024,12,64]{0,2,1:T(8,128)(2,1)} %bitcast.606), kind=kOutput, calls=%fused_computation.6 | convolution fusion | flops 824174592 | bytes 28073984 | tf_op jit(solution)/shard_map/qhd,khd->hqk/dot_general | solution.py:332
  120.2 13.7 %fusion.2 = f32[12,512]{1,0:T(8,128)S(1)} fusion(f32[12,512,1024]{2,1,0:T(8,128)} %get-tuple-element.398, f32[12,512]{1,0:T(8,128)S(1)} %get-tuple-element.397, pred[512,1024]{1,0:T(8,128)(4,1)S(1)} %copy-done.58), kind=kLoop, calls=%fused_computation.9 | loop fusion | flops 25159680 | bytes 25739264 | tf_op jit(solution)/shard_map/reduce_sum | solution.py:353
  136.4 9.9 fusion.44
  151.1 84.4 %all-gather.7.cloned.1.call-done = bf16[20,768,768]{2,1,0:T(8,128)(2,1)} async-done(((bf16[20,24,768]{2,1,0:T(8,128)(2,1)}), bf16[20,768,768]{2,1,0:T(8,128)(2,1)}) %all-gather.7.cloned.1.call-update) | async-done | bytes 23592976 | tf_op jit(solution)/shard_map/all_gather | solution.py:630
  235.4 11.2 fusion.307
  298.9 14.5 %fusion.1 = (f32[12,512]{1,0:T(8,128)S(1)}, f32[12,512,1024]{2,1,0:T(8,128)}) fusion(pred[512,1024]{1,0:T(8,128)(4,1)} %broadcast_compare_fusion, bf16[512,12,64]{0,2,1:T(8,128)(2,1)} %bitcast.637, bf16[1024,12,64]{0,2,1:T(8,128)(2,1)} %bitcast.607), kind=kOutput, calls=%fused_computation.7 | convolution fusion | flops 824174592 | bytes 28073984 | tf_op jit(solution)/shard_map/qhd,khd->hqk/dot_general | solution.py:332
  313.5 12.5 fusion.3
  329.1 10.0 fusion.43
  353.2 8.6 all-gather.9.cloned.1.call-done
  361.8 9.9 slice.672
  394.3 16.2 %fusion.332 = f32[1024,5120]{0,1:T(8,128)} fusion(bf16[5120,1024]{1,0:T(8,128)(2,1)S(1)} %bitcast.591, bf16[1024,1024]{0,1:T(8,128)(2,1)} %get-tuple-element.407), kind=kOutput, calls=%fused_computation.815 | convolution fusion | flops 10737418240 | bytes 33554432 | tf_op jit(solution)/shard_map/dot_general | solution.py:50
  442.3 9.4 add_multiply_fusion
  477.9 12.5 fusion.98
  491.8 20.6 %fusion.301 = (bf16[1024,1024]{0,1:T(8,128)(2,1)S(1)}, f32[1024,1024]{0,1:T(8,128)}) fusion(f32[1024,1024]{0,1:T(8,128)} %get-tuple-element.408, bf16[512,1024]{0,1:T(8,128)(2,1)} %copy-done.324, bf16[512,1024]{0,1:T(8,128)(2,1)} %copy-done.323, bf16[1024,5120]{0,1:T(8,128)(2,1)} %add_convert_fusion, bf16[5120,1024]{1,0:T(8,128)(2,1)} %bitcast.588), kind=kOutput, calls=%fused_computation.787 | convolution fusion | flops 10753146880 | bytes 33554432 | tf_op jit(solution)/shard_map/dot_general | solution.py:40
  544.8 10.7 add_bitcast_fusion
  560.3 12.2 fusion.19
  637.7 29.8 %shard_map.375 = (bf16[512,768]{1,0:T(8,128)(2,1)S(1)}, f32[1024,768]{1,0:T(8,128)}, f32[1024,768]{1,0:T(8,128)}) custom-call(bf16[512,768]{1,0:T(8,128)(2,1)S(1)} %copy-done.4, bf16[1024,768]{1,0:T(8,128)(2,1)S(1)} %copy-done.1, bf16[1024,768]{1,0:T(8,128)(2,1)S(1)} %copy-done, bf16[512,768]{1,0:T(8,128)(2,1)S(1)} %convolution_convert_fusion.2.grad_ref, ...), custom_call_target="tpu_custom_call" | custom-call | flops 8053063680 | bytes 9437184 | tf_op jit(solution)/shard_map/pallas_call | solution.py:304
  692.6 33.0 %collective-permute-done.25 = bf16[4,2,2,48,384]{4,3,2,1,0:T(8,128)(2,1)S(1)} collective-permute-done((bf16[4,2,2,48,384]{4,3,2,1,0:T(8,128)(2,1)S(1)}, bf16[4,2,2,48,384]{4,3,2,1,0:T(8,128)(2,1)S(1)}, u32[]{:S(2)}, u32[]{:S(2)}) %collective-permute-start.25) | collective-permute-done | bytes 589856 | tf_op jit(solution)/shard_map/ppermute | solution.py:184
  769.6 9.0 fusion.12
  785.6 13.6 %collective-permute-done.32 = bf16[5,2,2,48,384]{4,3,1,2,0:T(8,128)(2,1)S(1)} collective-permute-done((bf16[5,2,2,48,384]{4,3,1,2,0:T(8,128)(2,1)S(1)}, bf16[5,2,2,48,384]{4,3,1,2,0:T(8,128)(2,1)S(1)}, u32[]{:S(2)}, u32[]{:S(2)}) %collective-permute-start.32) | collective-permute-done | bytes 737312 | tf_op jit(solution)/shard_map/ppermute | solution.py:184
  808.1 9.6 collective-permute-done.34
  875.3 29.9 %shard_map.376 = (bf16[512,768]{1,0:T(8,128)(2,1)S(1)}, f32[1024,768]{1,0:T(8,128)}, f32[1024,768]{1,0:T(8,128)}) custom-call(bf16[512,768]{1,0:T(8,128)(2,1)S(1)} %copy-done.3, bf16[1024,768]{1,0:T(8,128)(2,1)S(1)} %pad_maximum_fusion.1.key_ref, bf16[1024,768]{1,0:T(8,128)(2,1)S(1)} %pad_maximum_fusion.2.value_ref, bf16[512,768]{1,0:T(8,128)(2,1)S(1)} %copy-done.13, ...), custom_call_target="tpu_custom_call" | custom-call | flops 8053063680 | bytes 9437184 | tf_op jit(solution)/shard_map/pallas_call | solution.py:304
  927.3 14.7 %collective-permute-done.49 = bf16[5,2,2,2,48,384]{5,4,1,2,3,0:T(8,128)(2,1)} collective-permute-done((bf16[5,2,2,2,48,384]{5,4,1,2,3,0:T(8,128)(2,1)S(1)}, bf16[5,2,2,2,48,384]{5,4,1,2,3,0:T(8,128)(2,1)}, u32[]{:S(2)}, u32[]{:S(2)}) %collective-permute-start.49) | collective-permute-done | bytes 1474592 | tf_op jit(solution)/shard_map/ppermute | solution.py:184
  1039.1 12.6 collective-permute-done.74
  1087.2 75.7 %all_to_all.10 = bf16[32,48,1024]{2,1,0:T(8,128)(2,1)S(1)} all-to-all(bf16[32,48,1024]{2,1,0:T(8,128)(2,1)S(1)} %constant_dynamic-update-slice_fusion.4), channel_id=1, replica_groups=mesh['dp'=16,'copy'=2] {'dp','copy'}, dimensions={0} | all-to-all | bytes 6291456 | tf_op jit(solution)/shard_map/all_to_all | solution.py:522
  1182.6 23.7 %collective-permute-done.90 = bf16[1024,512]{1,0:T(8,128)(2,1)S(1)} collective-permute-done((bf16[1024,512]{1,0:T(8,128)(2,1)S(1)}, bf16[1024,512]{1,0:T(8,128)(2,1)S(1)}, u32[]{:S(2)}, u32[]{:S(2)}) %collective-permute-start.90) | collective-permute-done | bytes 1048608 | tf_op jit(solution)/shard_map/ppermute | solution.py:543
  1212.2 9.5 multiply_add_fusion.3
  1232.1 14.4 %multiply_convert_fusion = bf16[1536,1024]{1,0:T(8,128)(2,1)} fusion(bf16[1536,1024]{1,0:T(8,128)(2,1)} %bitcast.643, f32[]{:T(128)S(6)} %div.323, f32[1024,1024]{1,0:T(8,128)} %copy-done.331, f32[1024,1024]{1,0:T(8,128)} %multiply_add_fusion), kind=kOutput, calls=%fused_computation.32 | convolution fusion | flops 5378146304 | bytes 14680068 | tf_op jit(solution)/shard_map/dot_general | solution.py:40
  1254.6 16.8 %collective-permute-done.85 = f32[16]{0:T(128)S(1)} collective-permute-done((f32[16]{0:T(128)S(1)}, f32[16]{0:T(128)S(1)}, u32[]{:S(2)}, u32[]{:S(2)}) %collective-permute-start.85) | collective-permute-done | bytes 96 | tf_op jit(solution)/shard_map/ppermute | solution.py:111
  1276.2 26.1 %collective-permute-done.87 = f32[16]{0:T(128)S(1)} collective-permute-done((f32[16]{0:T(128)S(1)}, f32[16]{0:T(128)S(1)}, u32[]{:S(2)}, u32[]{:S(2)}) %collective-permute-start.87) | collective-permute-done | bytes 96 | tf_op jit(solution)/shard_map/ppermute | solution.py:111
  1307.2 14.7 %collective-permute-done.88 = f32[16]{0:T(128)S(1)} collective-permute-done((f32[16]{0:T(128)S(1)}, f32[16]{0:T(128)S(1)}, u32[]{:S(2)}, u32[]{:S(2)}) %collective-permute-start.88) | collective-permute-done | bytes 96 | tf_op jit(solution)/shard_map/ppermute | solution.py:111
  (1407 shorter events, 639.9 us)
Async XLA Ops:
  7.2 79.6 %all-gather.5.cloned.1.call-start = ((), (), s32[]{:S(2)}) async-start(), calls=%async_computation.2 | async-start | bytes 7299072 | tf_op jit(solution)/shard_map/all_gather | solution.py:630
  10.7 224.8 %all-gather.7.cloned.1.call-start = ((), (), s32[]{:S(2)}) async-start(), calls=%async_computation.3 | async-start | bytes 24330240 | tf_op jit(solution)/shard_map/all_gather | solution.py:630
  11.6 350.1 %all-gather.9.cloned.1.call-start = ((), (), s32[]{:S(2)}) async-start(), calls=%async_computation.4 | async-start | bytes 19464192 | tf_op jit(solution)/shard_map/all_gather | solution.py:635
  490.5 41.1 %collective-permute-start.11 = (f32[5120,512]{1,0:T(8,128)}, f32[5120,512]{1,0:T(8,128)}, u32[]{:S(2)}, u32[]{:S(2)}) collective-permute-start(f32[5120,512]{1,0:T(8,128)} %fusion.98), channel_id=1, source_target_pairs={{0,1},{1,0},{2,3},{3,2},{4,5},{5,4},{6,7},{7,6},{8,9},{9,8},{10,11... | collective-permute-start | bytes 31457288 | tf_op jit(solution)/shard_map/ppermute | solution.py:101
  516.8 65.7 %collective-permute-start.12 = (f32[1024,512]{1,0:T(8,128)}, f32[1024,512]{1,0:T(8,128)}, u32[]{:S(2)}, u32[]{:S(2)}) collective-permute-start(f32[1024,512]{1,0:T(8,128)} %fusion.96), channel_id=1, source_target_pairs={{0,1},{1,0},{2,3},{3,2},{4,5},{5,4},{6,7},{7,6},{8,9},{9,8},{10,11... | collective-permute-start | bytes 6291464 | tf_op jit(solution)/shard_map/ppermute | solution.py:101
  520.0 63.2 %collective-permute-start.13 = (f32[1024,512]{1,0:T(8,128)}, f32[1024,512]{1,0:T(8,128)}, u32[]{:S(2)}, u32[]{:S(2)}) collective-permute-start(f32[1024,512]{1,0:T(8,128)} %fusion.94), channel_id=1, source_target_pairs={{0,1},{1,0},{2,3},{3,2},{4,5},{5,4},{6,7},{7,6},{8,9},{9,8},{10,11... | collective-permute-start | bytes 6291464 | tf_op jit(solution)/shard_map/ppermute | solution.py:101
  525.4 55.6 %collective-permute-start.15 = (f32[1024,192]{0,1:T(8,128)}, f32[1024,192]{0,1:T(8,128)}, u32[]{:S(2)}, u32[]{:S(2)}) collective-permute-start(f32[1024,192]{0,1:T(8,128)} %constant_dynamic-slice_fusion.50), channel_id=1, source_target_pairs={{0,1},{1,0},{2,3},{3,2},{4,5},{5,4},{6,7},{7,6},{8,9},{9,8},{10,11... | collective-permute-start | bytes 2359304 | tf_op jit(solution)/shard_map/ppermute | solution.py:101
  538.9 44.2 %collective-permute-start.14 = (f32[1024,384]{1,0:T(8,128)}, f32[1024,384]{1,0:T(8,128)}, u32[]{:S(2)}, u32[]{:S(2)}) collective-permute-start(f32[1024,384]{1,0:T(8,128)} %fusion.165), channel_id=1, source_target_pairs={{0,1},{1,0},{2,3},{3,2},{4,5},{5,4},{6,7},{7,6},{8,9},{9,8},{10,11... | collective-permute-start | bytes 4718600 | tf_op jit(solution)/shard_map/ppermute | solution.py:101
  543.7 39.4 %collective-permute-start.16 = (f32[3072,384]{1,0:T(8,128)}, f32[3072,384]{1,0:T(8,128)}, u32[]{:S(2)}, u32[]{:S(2)}) collective-permute-start(f32[3072,384]{1,0:T(8,128)} %fusion.163), channel_id=1, source_target_pairs={{0,1},{1,0},{2,3},{3,2},{4,5},{5,4},{6,7},{7,6},{8,9},{9,8},{10,11... | collective-permute-start | bytes 14155784 | tf_op jit(solution)/shard_map/ppermute | solution.py:101
  581.0 42.9 %collective-permute-start.17 = (bf16[1,2,2,2,320,256]{5,4,1,2,3,0:T(8,128)(2,1)}, bf16[1,2,2,2,320,256]{5,4,1,2,3,0:T(8,128)(2,1)}, u32[]{:S(2)}, u32[]{:S(2)}) collective-permute-start(bf16[1,2,2,2,320,256]{5,4,1,2,3,0:T(8,128)(2,1)} %fusion.48), channel_id=1, source_target_pairs={{0,2},{2,0},{4,6},{6,4},{8,10},{10,8},{12,14},{14,12},{16,18},{18,... | collective-permute-start | bytes 3932168 | tf_op jit(solution)/shard_map/ppermute | solution.py:184
  582.5 50.5 %collective-permute-start.18 = (bf16[1,2,2,2,320,256]{5,4,1,2,3,0:T(8,128)(2,1)}, bf16[1,2,2,2,320,256]{5,4,1,2,3,0:T(8,128)(2,1)}, u32[]{:S(2)}, u32[]{:S(2)}) collective-permute-start(bf16[1,2,2,2,320,256]{5,4,1,2,3,0:T(8,128)(2,1)} %fusion.49), channel_id=1, source_target_pairs={{0,4},{2,6},{4,0},{6,2},{8,12},{10,14},{12,8},{14,10},{16,20},{18,... | collective-permute-start | bytes 3932168 | tf_op jit(solution)/shard_map/ppermute | solution.py:184
  587.2 50.4 %collective-permute-start.20 = (f32[3072,384]{1,0:T(8,128)}, f32[3072,384]{1,0:T(8,128)}, u32[]{:S(2)}, u32[]{:S(2)}) collective-permute-start(f32[3072,384]{1,0:T(8,128)} %fusion.159), channel_id=1, source_target_pairs={{0,1},{1,0},{2,3},{3,2},{4,5},{5,4},{6,7},{7,6},{8,9},{9,8},{10,11... | collective-permute-start | bytes 14155784 | tf_op jit(solution)/shard_map/ppermute | solution.py:101
  600.3 37.3 %collective-permute-start.19 = (bf16[4,2,2,2,48,384]{5,4,3,2,1,0:T(8,128)(2,1)}, bf16[4,2,2,2,48,384]{5,4,3,2,1,0:T(8,128)(2,1)}, u32[]{:S(2)}, u32[]{:S(2)}) collective-permute-start(bf16[4,2,2,2,48,384]{5,4,3,2,1,0:T(8,128)(2,1)} %fusion.50), channel_id=1, source_target_pairs={{0,2},{2,0},{4,6},{6,4},{8,10},{10,8},{12,14},{14,12},{16,18},{18,... | collective-permute-start | bytes 3538952 | tf_op jit(solution)/shard_map/ppermute | solution.py:184
  603.4 34.2 %collective-permute-start.21 = (f32[768,384]{1,0:T(8,128)}, f32[768,384]{1,0:T(8,128)}, u32[]{:S(2)}, u32[]{:S(2)}) collective-permute-start(f32[768,384]{1,0:T(8,128)} %fusion.157), channel_id=1, source_target_pairs={{0,1},{1,0},{2,3},{3,2},{4,5},{5,4},{6,7},{7,6},{8,9},{9,8},{10,11... | collective-permute-start | bytes 3538952 | tf_op jit(solution)/shard_map/ppermute | solution.py:101
  623.9 43.7 %collective-permute-start.22 = (bf16[1,2,2,2,64,1792]{5,4,1,2,3,0:T(8,128)(2,1)}, bf16[1,2,2,2,64,1792]{5,4,1,2,3,0:T(8,128)(2,1)}, u32[]{:S(2)}, u32[]{:S(2)}) collective-permute-start(bf16[1,2,2,2,64,1792]{5,4,1,2,3,0:T(8,128)(2,1)} %concatenate.266), channel_id=1, source_target_pairs={{0,4},{2,6},{4,0},{6,2},{8,12},{10,14},{12,8},{14,10},{16,20},{18,... | collective-permute-start | bytes 5505032 | tf_op jit(solution)/shard_map/ppermute | solution.py:184
  678.1 47.6 %collective-permute-start.26 = (bf16[5,2,2,2,48,384]{5,4,1,2,3,0:T(8,128)(2,1)}, bf16[5,2,2,2,48,384]{5,4,1,2,3,0:T(8,128)(2,1)}, u32[]{:S(2)}, u32[]{:S(2)}) collective-permute-start(bf16[5,2,2,2,48,384]{5,4,1,2,3,0:T(8,128)(2,1)} %pad_maximum_fusion.6), channel_id=1, source_target_pairs={{0,4},{2,6},{4,0},{6,2},{8,12},{10,14},{12,8},{14,10},{16,20},{18,... | collective-permute-start | bytes 4423688 | tf_op jit(solution)/shard_map/ppermute | solution.py:184
  685.9 39.8 %collective-permute-start.25 = (bf16[4,2,2,48,384]{4,3,2,1,0:T(8,128)(2,1)S(1)}, bf16[4,2,2,48,384]{4,3,2,1,0:T(8,128)(2,1)S(1)}, u32[]{:S(2)}, u32[]{:S(2)}) collective-permute-start(bf16[4,2,2,48,384]{4,3,2,1,0:T(8,128)(2,1)S(1)} %fusion.120), channel_id=1, source_target_pairs={{0,4},{2,6},{4,0},{6,2},{8,12},{10,14},{12,8},{14,10},{16,20},{18,... | collective-permute-start | bytes 1769480 | tf_op jit(solution)/shard_map/ppermute | solution.py:184
  754.3 44.9 %collective-permute-start.33 = (f32[3072,384]{1,0:T(8,128)}, f32[3072,384]{1,0:T(8,128)}, u32[]{:S(2)}, u32[]{:S(2)}) collective-permute-start(f32[3072,384]{1,0:T(8,128)} %fusion.151), channel_id=1, source_target_pairs={{0,1},{1,0},{2,3},{3,2},{4,5},{5,4},{6,7},{7,6},{8,9},{9,8},{10,11... | collective-permute-start | bytes 14155784 | tf_op jit(solution)/shard_map/ppermute | solution.py:101
  778.8 38.9 %collective-permute-start.34 = (bf16[1,2,2,2,48,1152]{5,4,1,2,3,0:T(8,128)(2,1)S(1)}, bf16[1,2,2,2,48,1152]{5,4,1,2,3,0:T(8,128)(2,1)S(1)}, u32[]{:S(2)}, u32[]{:S(2)}) collective-permute-start(bf16[1,2,2,2,48,1152]{5,4,1,2,3,0:T(8,128)(2,1)S(1)} %fusion.106), channel_id=1, source_target_pairs={{0,2},{2,0},{4,6},{6,4},{8,10},{10,8},{12,14},{14,12},{16,18},{18,... | collective-permute-start | bytes 2654216 | tf_op jit(solution)/shard_map/ppermute | solution.py:184
  783.5 52.9 %collective-permute-start.35 = (bf16[1,2,320,256]{3,2,1,0:T(8,128)(2,1)S(1)}, bf16[1,2,320,256]{3,2,1,0:T(8,128)(2,1)S(1)}, u32[]{:S(2)}, u32[]{:S(2)}) collective-permute-start(bf16[1,2,320,256]{3,2,1,0:T(8,128)(2,1)S(1)} %fusion.167), channel_id=1, source_target_pairs={{0,8},{2,10},{4,12},{6,14},{8,0},{10,2},{12,4},{14,6},{16,24},{18,... | collective-permute-start | bytes 983048 | tf_op jit(solution)/shard_map/ppermute | solution.py:184
  785.4 55.9 %collective-permute-start.36 = (bf16[1,2,320,256]{3,2,1,0:T(8,128)(2,1)}, bf16[1,2,320,256]{3,2,1,0:T(8,128)(2,1)}, u32[]{:S(2)}, u32[]{:S(2)}) collective-permute-start(bf16[1,2,320,256]{3,2,1,0:T(8,128)(2,1)} %fusion.168), channel_id=1, source_target_pairs={{0,8},{2,10},{4,12},{6,14},{8,0},{10,2},{12,4},{14,6},{16,24},{18,... | collective-permute-start | bytes 983048 | tf_op jit(solution)/shard_map/ppermute | solution.py:184
  817.8 35.7 %collective-permute-start.40 = (f32[3072,384]{1,0:T(8,128)}, f32[3072,384]{1,0:T(8,128)}, u32[]{:S(2)}, u32[]{:S(2)}) collective-permute-start(f32[3072,384]{1,0:T(8,128)} %fusion.144), channel_id=1, source_target_pairs={{0,1},{1,0},{2,3},{3,2},{4,5},{5,4},{6,7},{7,6},{8,9},{9,8},{10,11... | collective-permute-start | bytes 14155784 | tf_op jit(solution)/shard_map/ppermute | solution.py:101
  849.0 59.3 %collective-permute-start.42 = (bf16[1,2,64,1792]{3,2,1,0:T(8,128)(2,1)}, bf16[1,2,64,1792]{3,2,1,0:T(8,128)(2,1)}, u32[]{:S(2)}, u32[]{:S(2)}) collective-permute-start(bf16[1,2,64,1792]{3,2,1,0:T(8,128)(2,1)} %concatenate.273), channel_id=1, source_target_pairs={{0,8},{2,10},{4,12},{6,14},{8,0},{10,2},{12,4},{14,6},{16,24},{18,... | collective-permute-start | bytes 1376264 | tf_op jit(solution)/shard_map/ppermute | solution.py:184
  852.3 55.1 %collective-permute-start.44 = (bf16[1,2,2,48,1152]{4,3,1,2,0:T(8,128)(2,1)}, bf16[1,2,2,48,1152]{4,3,1,2,0:T(8,128)(2,1)}, u32[]{:S(2)}, u32[]{:S(2)}) collective-permute-start(bf16[1,2,2,48,1152]{4,3,1,2,0:T(8,128)(2,1)} %fusion.132), channel_id=1, source_target_pairs={{0,4},{2,6},{4,0},{6,2},{8,12},{10,14},{12,8},{14,10},{16,20},{18,... | collective-permute-start | bytes 1327112 | tf_op jit(solution)/shard_map/ppermute | solution.py:184
  856.6 51.6 %collective-permute-start.43 = (f32[4,24,384]{2,1,0:T(8,128)}, f32[4,24,384]{2,1,0:T(8,128)}, u32[]{:S(2)}, u32[]{:S(2)}) collective-permute-start(f32[4,24,384]{2,1,0:T(8,128)} %constant_dynamic-slice_fusion.25), channel_id=1, source_target_pairs={{0,1},{1,0},{2,3},{3,2},{4,5},{5,4},{6,7},{7,6},{8,9},{9,8},{10,11... | collective-permute-start | bytes 442376 | tf_op jit(solution)/shard_map/ppermute | solution.py:101
  857.4 69.8 %collective-permute-start.47 = (bf16[5,48,384]{2,1,0:T(8,128)(2,1)}, bf16[5,48,384]{2,1,0:T(8,128)(2,1)}, u32[]{:S(2)}, u32[]{:S(2)}) collective-permute-start(bf16[5,48,384]{2,1,0:T(8,128)(2,1)} %pad_maximum_fusion.23), channel_id=1, source_target_pairs={{0,16},{2,18},{4,20},{6,22},{8,24},{10,26},{12,28},{14,30},{16,0},... | collective-permute-start | bytes 552968 | tf_op jit(solution)/shard_map/ppermute | solution.py:184
  863.2 64.1 %collective-permute-start.48 = (bf16[4,2,2,48,384]{4,3,0,1,2:T(8,128)(2,1)}, bf16[4,2,2,48,384]{4,3,0,1,2:T(8,128)(2,1)}, u32[]{:S(2)}, u32[]{:S(2)}) collective-permute-start(bf16[4,2,2,48,384]{4,3,0,1,2:T(8,128)(2,1)} %fusion.122), channel_id=1, source_target_pairs={{0,4},{2,6},{4,0},{6,2},{8,12},{10,14},{12,8},{14,10},{16,20},{18,... | collective-permute-start | bytes 1769480 | tf_op jit(solution)/shard_map/ppermute | solution.py:184
  907.4 34.6 %collective-permute-start.49 = (bf16[5,2,2,2,48,384]{5,4,1,2,3,0:T(8,128)(2,1)S(1)}, bf16[5,2,2,2,48,384]{5,4,1,2,3,0:T(8,128)(2,1)}, u32[]{:S(2)}, u32[]{:S(2)}) collective-permute-start(bf16[5,2,2,2,48,384]{5,4,1,2,3,0:T(8,128)(2,1)S(1)} %pad_maximum_fusion.7), channel_id=1, source_target_pairs={{0,4},{2,6},{4,0},{6,2},{8,12},{10,14},{12,8},{14,10},{16,20},{18,... | collective-permute-start | bytes 4423688 | tf_op jit(solution)/shard_map/ppermute | solution.py:184
  920.8 39.0 %collective-permute-start.50 = (bf16[1,320,256]{2,1,0:T(8,128)(2,1)}, bf16[1,320,256]{2,1,0:T(8,128)(2,1)S(1)}, u32[]{:S(2)}, u32[]{:S(2)}) collective-permute-start(bf16[1,320,256]{2,1,0:T(8,128)(2,1)} %fusion.195), channel_id=1, source_target_pairs={{0,16},{2,18},{4,20},{6,22},{8,24},{10,26},{12,28},{14,30},{16,0},... | collective-permute-start | bytes 491528 | tf_op jit(solution)/shard_map/ppermute | solution.py:184
  923.2 37.0 %collective-permute-start.51 = (bf16[1,320,256]{2,1,0:T(8,128)(2,1)}, bf16[1,320,256]{2,1,0:T(8,128)(2,1)S(1)}, u32[]{:S(2)}, u32[]{:S(2)}) collective-permute-start(bf16[1,320,256]{2,1,0:T(8,128)(2,1)} %fusion.196), channel_id=1, source_target_pairs={{0,16},{2,18},{4,20},{6,22},{8,24},{10,26},{12,28},{14,30},{16,0},... | collective-permute-start | bytes 491528 | tf_op jit(solution)/shard_map/ppermute | solution.py:184
  960.2 35.0 %collective-permute-start.59 = (bf16[5,2,2,48,384]{4,3,1,2,0:T(8,128)(2,1)}, bf16[5,2,2,48,384]{4,3,1,2,0:T(8,128)(2,1)}, u32[]{:S(2)}, u32[]{:S(2)}) collective-permute-start(bf16[5,2,2,48,384]{4,3,1,2,0:T(8,128)(2,1)} %pad_maximum_fusion.10), channel_id=1, source_target_pairs={{0,2},{2,0},{4,6},{6,4},{8,10},{10,8},{12,14},{14,12},{16,18},{18,... | collective-permute-start | bytes 2211848 | tf_op jit(solution)/shard_map/ppermute | solution.py:184
  1246.6 76.0 %all-to-all-start.1 = ((bf16[32,48,1024]{2,1,0:T(8,128)(2,1)}), bf16[32,48,1024]{2,1,0:T(8,128)(2,1)}, u32[]{:S(2)}, u32[]{:S(2)}) async-start(bf16[32,48,1024]{2,1,0:T(8,128)(2,1)} %bitcast.642), calls=%async_computation.1 | async-start | bytes 6291456 | tf_op jit(solution)/shard_map/all_to_all | solution.py:555
  (426 other events, 5166.4 us)
Sparse Core Ops, SparseCore 0:
  11.6 75.1 all-gather.4
  89.7 145.6 all-gather.6
  238.9 122.8 all-gather.8

commit v8 on v7

--- a/solution.py
+++ b/solution.py
@@ -414,7 +414,7 @@
         "lower%d" % depth,
         weight_task(
             [(copies, hidden_grad_low, [normed_two_low]), (1, attended, [projected_low])],
-            True,
+            False,
             0,
         ),
     )

time: 1360 us -> 1330 us (0.978)
  waiting for transfers between devices: 378 us -> 351 us
    ppermute x40, waiting for transfers between devices: 106 us -> 77.5 us  [scatter_task(): arrived, = (yield ([lax.ppermute(joined(sent, axis), 'dp', pairs)], lag))]
  transfers between devices with their start and end apart: 96 -> 96, of which waited for: 34 -> 33; matrix products, arithmetic and copies ran while one was open for 35% -> 35% of each run, Pallas kernels for 4% -> 5%
where the time goes in v8:
time: 1330 us; the launch traced here: 1310 us
  waiting for transfers between devices  351 us (26%)
  matrix products  328 us (25%)
  other arithmetic  214 us (16%)
  local copies, waits for them, and re-layouts  171 us (13%)
  starting transfers between devices  82.6 us (6%)
  blocking collectives  75.2 us (6%)
  Pallas kernels  59.7 us (4%)
  between operations  33 us (2%)
    all_gather x2, waiting for transfers between devices, gathered(): lax.all_gather(jnp.concatenate(members, axis=0), everywhere, axis=1, tile...  151 us
    dot_general x25, matrix products, product(): return jnp.dot(left_side, right_side, preferred_element_type=jnp.float32)  108 us
    dot_general x29, matrix products, product_left(): lax.dot_general(left_side, right_side, (((0,), (0,)), ((), ())), preferre...  98.5 us
    ppermute x40, waiting for transfers between devices, scatter_task(): arrived, = (yield ([lax.ppermute(joined(sent, axis), 'dp', pairs)], lag))  77.5 us
    ppermute x12, waiting for transfers between devices, sum_all(): lax.ppermute(values, 'dp', [(i, i ^ step) for i in range(count)])  76.7 us
    all_to_all x1, blocking collectives, muon_steps(): lax.all_to_all(owner_buffer([in_parts(modulate, 4)], [in_parts(expand, 2)...  75.2 us
    dot_general x17, matrix products, product_right(): lax.dot_general(left_side, right_side, (((1,), (1,)), ((), ())), preferre...  72.4 us
    pallas_call x2, Pallas kernels, attention_back(): pl.pallas_call(attention_back_kernel, grid=(D // width, queries // chunk)...  59.7 us
  transfers between devices with their start and end apart: 96, of which 33 were waited for; matrix products, arithmetic and copies ran while one was open for 35% of the time, Pallas kernels for 5%

profile of v8, /device:TPU:0, one launch (start us, length us, event | category | flops | bytes accessed | tf_op | source)
XLA Modules:
  0.0 1315.0 jit_solution(2855402298267647583)
XLA Ops:
  19.7 67.1 %all-gather.5.cloned.1.call-done = bf16[6,768,768]{2,1,0:T(8,128)(2,1)} async-done(((bf16[6,24,768]{2,1,0:T(8,128)(2,1)}), bf16[6,768,768]{2,1,0:T(8,128)(2,1)}) %all-gather.5.cloned.1.call-update) | async-done | bytes 7077904 | tf_op jit(solution)/shard_map/all_gather | solution.py:630
  105.7 14.5 %fusion = (f32[12,512]{1,0:T(8,128)S(1)}, f32[12,512,1024]{2,1,0:T(8,128)}) fusion(pred[512,1024]{1,0:T(8,128)(4,1)} %broadcast_compare_fusion, bf16[512,12,64]{0,2,1:T(8,128)(2,1)} %bitcast.636, bf16[1024,12,64]{0,2,1:T(8,128)(2,1)} %bitcast.606), kind=kOutput, calls=%fused_computation.6 | convolution fusion | flops 824174592 | bytes 28073984 | tf_op jit(solution)/shard_map/qhd,khd->hqk/dot_general | solution.py:332
  120.2 13.7 %fusion.2 = f32[12,512]{1,0:T(8,128)S(1)} fusion(f32[12,512,1024]{2,1,0:T(8,128)} %get-tuple-element.398, f32[12,512]{1,0:T(8,128)S(1)} %get-tuple-element.397, pred[512,1024]{1,0:T(8,128)(4,1)S(1)} %copy-done.58), kind=kLoop, calls=%fused_computation.9 | loop fusion | flops 25159680 | bytes 25739264 | tf_op jit(solution)/shard_map/reduce_sum | solution.py:353
  136.4 9.9 fusion.44
  151.1 84.4 %all-gather.7.cloned.1.call-done = bf16[20,768,768]{2,1,0:T(8,128)(2,1)} async-done(((bf16[20,24,768]{2,1,0:T(8,128)(2,1)}), bf16[20,768,768]{2,1,0:T(8,128)(2,1)}) %all-gather.7.cloned.1.call-update) | async-done | bytes 23592976 | tf_op jit(solution)/shard_map/all_gather | solution.py:630
  235.4 11.2 fusion.307
  298.9 14.5 %fusion.1 = (f32[12,512]{1,0:T(8,128)S(1)}, f32[12,512,1024]{2,1,0:T(8,128)}) fusion(pred[512,1024]{1,0:T(8,128)(4,1)} %broadcast_compare_fusion, bf16[512,12,64]{0,2,1:T(8,128)(2,1)} %bitcast.637, bf16[1024,12,64]{0,2,1:T(8,128)(2,1)} %bitcast.607), kind=kOutput, calls=%fused_computation.7 | convolution fusion | flops 824174592 | bytes 28073984 | tf_op jit(solution)/shard_map/qhd,khd->hqk/dot_general | solution.py:332
  313.5 12.5 fusion.3
  329.1 10.0 fusion.43
  353.2 8.6 all-gather.9.cloned.1.call-done
  361.8 9.9 slice.672
  394.3 16.2 %fusion.332 = f32[1024,5120]{0,1:T(8,128)} fusion(bf16[5120,1024]{1,0:T(8,128)(2,1)S(1)} %bitcast.591, bf16[1024,1024]{0,1:T(8,128)(2,1)} %get-tuple-element.407), kind=kOutput, calls=%fused_computation.815 | convolution fusion | flops 10737418240 | bytes 33554432 | tf_op jit(solution)/shard_map/dot_general | solution.py:50
  418.3 7.5 fusion.304
  442.3 9.4 add_multiply_fusion
  477.9 12.5 fusion.98
  491.8 20.6 %fusion.301 = (bf16[1024,1024]{0,1:T(8,128)(2,1)S(1)}, f32[1024,1024]{0,1:T(8,128)}) fusion(f32[1024,1024]{0,1:T(8,128)} %get-tuple-element.408, bf16[512,1024]{0,1:T(8,128)(2,1)} %copy-done.324, bf16[512,1024]{0,1:T(8,128)(2,1)} %copy-done.323, bf16[1024,5120]{0,1:T(8,128)(2,1)} %add_convert_fusion, bf16[5120,1024]{1,0:T(8,128)(2,1)} %bitcast.588), kind=kOutput, calls=%fused_computation.787 | convolution fusion | flops 10753146880 | bytes 33554432 | tf_op jit(solution)/shard_map/dot_general | solution.py:40
  544.8 10.7 add_bitcast_fusion
  560.3 12.2 fusion.19
  637.7 29.8 %shard_map.375 = (bf16[512,768]{1,0:T(8,128)(2,1)S(1)}, f32[1024,768]{1,0:T(8,128)}, f32[1024,768]{1,0:T(8,128)}) custom-call(bf16[512,768]{1,0:T(8,128)(2,1)S(1)} %copy-done.4, bf16[1024,768]{1,0:T(8,128)(2,1)S(1)} %copy-done.1, bf16[1024,768]{1,0:T(8,128)(2,1)S(1)} %copy-done, bf16[512,768]{1,0:T(8,128)(2,1)S(1)} %convolution_convert_fusion.2.grad_ref, ...), custom_call_target="tpu_custom_call" | custom-call | flops 8053063680 | bytes 9437184 | tf_op jit(solution)/shard_map/pallas_call | solution.py:304
  692.6 8.7 collective-permute-done.25
  701.3 11.8 collective-permute-done.26
  757.0 9.0 fusion.12
  846.9 29.9 %shard_map.376 = (bf16[512,768]{1,0:T(8,128)(2,1)S(1)}, f32[1024,768]{1,0:T(8,128)}, f32[1024,768]{1,0:T(8,128)}) custom-call(bf16[512,768]{1,0:T(8,128)(2,1)S(1)} %copy-done.3, bf16[1024,768]{1,0:T(8,128)(2,1)S(1)} %pad_maximum_fusion.1.key_ref, bf16[1024,768]{1,0:T(8,128)(2,1)S(1)} %pad_maximum_fusion.2.value_ref, bf16[512,768]{1,0:T(8,128)(2,1)S(1)} %copy-done.13, ...), custom_call_target="tpu_custom_call" | custom-call | flops 8053063680 | bytes 9437184 | tf_op jit(solution)/shard_map/pallas_call | solution.py:304
  898.8 14.7 %collective-permute-done.49 = bf16[5,2,2,2,48,384]{5,4,1,2,3,0:T(8,128)(2,1)} collective-permute-done((bf16[5,2,2,2,48,384]{5,4,1,2,3,0:T(8,128)(2,1)S(1)}, bf16[5,2,2,2,48,384]{5,4,1,2,3,0:T(8,128)(2,1)}, u32[]{:S(2)}, u32[]{:S(2)}) %collective-permute-start.49) | collective-permute-done | bytes 1474592 | tf_op jit(solution)/shard_map/ppermute | solution.py:184
  1010.0 13.2 %collective-permute-done.74 = bf16[1,48,588]{2,1,0:T(8,128)(2,1)S(1)} collective-permute-done((bf16[1,48,588]{2,1,0:T(8,128)(2,1)S(1)}, bf16[1,48,588]{2,1,0:T(8,128)(2,1)S(1)}, u32[]{:S(2)}, u32[]{:S(2)}) %collective-permute-start.74) | collective-permute-done | bytes 56480 | tf_op jit(solution)/shard_map/ppermute | solution.py:184
  1058.7 75.2 %all_to_all.10 = bf16[32,48,1024]{2,1,0:T(8,128)(2,1)S(1)} all-to-all(bf16[32,48,1024]{2,1,0:T(8,128)(2,1)S(1)} %constant_dynamic-update-slice_fusion.4), channel_id=1, replica_groups=mesh['dp'=16,'copy'=2] {'dp','copy'}, dimensions={0} | all-to-all | bytes 6291456 | tf_op jit(solution)/shard_map/all_to_all | solution.py:522
  1153.6 23.7 %collective-permute-done.90 = bf16[1024,512]{1,0:T(8,128)(2,1)S(1)} collective-permute-done((bf16[1024,512]{1,0:T(8,128)(2,1)S(1)}, bf16[1024,512]{1,0:T(8,128)(2,1)S(1)}, u32[]{:S(2)}, u32[]{:S(2)}) %collective-permute-start.90) | collective-permute-done | bytes 1048608 | tf_op jit(solution)/shard_map/ppermute | solution.py:543
  1183.2 9.5 multiply_add_fusion.3
  1203.1 14.4 %multiply_convert_fusion = bf16[1536,1024]{1,0:T(8,128)(2,1)} fusion(bf16[1536,1024]{1,0:T(8,128)(2,1)} %bitcast.643, f32[]{:T(128)S(6)} %div.323, f32[1024,1024]{1,0:T(8,128)} %copy-done.331, f32[1024,1024]{1,0:T(8,128)} %multiply_add_fusion), kind=kOutput, calls=%fused_computation.32 | convolution fusion | flops 5378146304 | bytes 14680068 | tf_op jit(solution)/shard_map/dot_general | solution.py:40
  1225.5 16.8 %collective-permute-done.85 = f32[16]{0:T(128)S(1)} collective-permute-done((f32[16]{0:T(128)S(1)}, f32[16]{0:T(128)S(1)}, u32[]{:S(2)}, u32[]{:S(2)}) %collective-permute-start.85) | collective-permute-done | bytes 96 | tf_op jit(solution)/shard_map/ppermute | solution.py:111
  1247.1 26.1 %collective-permute-done.87 = f32[16]{0:T(128)S(1)} collective-permute-done((f32[16]{0:T(128)S(1)}, f32[16]{0:T(128)S(1)}, u32[]{:S(2)}, u32[]{:S(2)}) %collective-permute-start.87) | collective-permute-done | bytes 96 | tf_op jit(solution)/shard_map/ppermute | solution.py:111
  1278.1 14.7 %collective-permute-done.88 = f32[16]{0:T(128)S(1)} collective-permute-done((f32[16]{0:T(128)S(1)}, f32[16]{0:T(128)S(1)}, u32[]{:S(2)}, u32[]{:S(2)}) %collective-permute-start.88) | collective-permute-done | bytes 96 | tf_op jit(solution)/shard_map/ppermute | solution.py:111
  (1407 shorter events, 639.1 us)
Async XLA Ops:
  7.2 79.6 %all-gather.5.cloned.1.call-start = ((), (), s32[]{:S(2)}) async-start(), calls=%async_computation.2 | async-start | bytes 7299072 | tf_op jit(solution)/shard_map/all_gather | solution.py:630
  10.7 224.8 %all-gather.7.cloned.1.call-start = ((), (), s32[]{:S(2)}) async-start(), calls=%async_computation.3 | async-start | bytes 24330240 | tf_op jit(solution)/shard_map/all_gather | solution.py:630
  11.6 350.1 %all-gather.9.cloned.1.call-start = ((), (), s32[]{:S(2)}) async-start(), calls=%async_computation.4 | async-start | bytes 19464192 | tf_op jit(solution)/shard_map/all_gather | solution.py:635
  261.2 32.3 %collective-permute-start.3 = (bf16[512,768]{1,0:T(8,128)(2,1)}, bf16[512,768]{1,0:T(8,128)(2,1)}, u32[]{:S(2)}, u32[]{:S(2)}) collective-permute-start(bf16[512,768]{1,0:T(8,128)(2,1)} %convolution_convert_fusion.3), channel_id=1, source_target_pairs={{0,1},{1,0},{2,3},{3,2},{4,5},{5,4},{6,7},{7,6},{8,9},{9,8},{10,11... | collective-permute-start | bytes 2359304 | tf_op jit(solution)/shard_map/ppermute | solution.py:101
  490.5 41.1 %collective-permute-start.11 = (f32[5120,512]{1,0:T(8,128)}, f32[5120,512]{1,0:T(8,128)}, u32[]{:S(2)}, u32[]{:S(2)}) collective-permute-start(f32[5120,512]{1,0:T(8,128)} %fusion.98), channel_id=1, source_target_pairs={{0,1},{1,0},{2,3},{3,2},{4,5},{5,4},{6,7},{7,6},{8,9},{9,8},{10,11... | collective-permute-start | bytes 31457288 | tf_op jit(solution)/shard_map/ppermute | solution.py:101
  516.8 65.7 %collective-permute-start.12 = (f32[1024,512]{1,0:T(8,128)}, f32[1024,512]{1,0:T(8,128)}, u32[]{:S(2)}, u32[]{:S(2)}) collective-permute-start(f32[1024,512]{1,0:T(8,128)} %fusion.96), channel_id=1, source_target_pairs={{0,1},{1,0},{2,3},{3,2},{4,5},{5,4},{6,7},{7,6},{8,9},{9,8},{10,11... | collective-permute-start | bytes 6291464 | tf_op jit(solution)/shard_map/ppermute | solution.py:101
  520.0 63.2 %collective-permute-start.13 = (f32[1024,512]{1,0:T(8,128)}, f32[1024,512]{1,0:T(8,128)}, u32[]{:S(2)}, u32[]{:S(2)}) collective-permute-start(f32[1024,512]{1,0:T(8,128)} %fusion.94), channel_id=1, source_target_pairs={{0,1},{1,0},{2,3},{3,2},{4,5},{5,4},{6,7},{7,6},{8,9},{9,8},{10,11... | collective-permute-start | bytes 6291464 | tf_op jit(solution)/shard_map/ppermute | solution.py:101
  525.4 55.6 %collective-permute-start.15 = (f32[1024,192]{0,1:T(8,128)}, f32[1024,192]{0,1:T(8,128)}, u32[]{:S(2)}, u32[]{:S(2)}) collective-permute-start(f32[1024,192]{0,1:T(8,128)} %constant_dynamic-slice_fusion.50), channel_id=1, source_target_pairs={{0,1},{1,0},{2,3},{3,2},{4,5},{5,4},{6,7},{7,6},{8,9},{9,8},{10,11... | collective-permute-start | bytes 2359304 | tf_op jit(solution)/shard_map/ppermute | solution.py:101
  538.9 44.2 %collective-permute-start.14 = (f32[1024,384]{1,0:T(8,128)}, f32[1024,384]{1,0:T(8,128)}, u32[]{:S(2)}, u32[]{:S(2)}) collective-permute-start(f32[1024,384]{1,0:T(8,128)} %fusion.165), channel_id=1, source_target_pairs={{0,1},{1,0},{2,3},{3,2},{4,5},{5,4},{6,7},{7,6},{8,9},{9,8},{10,11... | collective-permute-start | bytes 4718600 | tf_op jit(solution)/shard_map/ppermute | solution.py:101
  543.7 39.4 %collective-permute-start.16 = (f32[3072,384]{1,0:T(8,128)}, f32[3072,384]{1,0:T(8,128)}, u32[]{:S(2)}, u32[]{:S(2)}) collective-permute-start(f32[3072,384]{1,0:T(8,128)} %fusion.163), channel_id=1, source_target_pairs={{0,1},{1,0},{2,3},{3,2},{4,5},{5,4},{6,7},{7,6},{8,9},{9,8},{10,11... | collective-permute-start | bytes 14155784 | tf_op jit(solution)/shard_map/ppermute | solution.py:101
  581.0 42.9 %collective-permute-start.17 = (bf16[1,2,2,2,320,256]{5,4,1,2,3,0:T(8,128)(2,1)}, bf16[1,2,2,2,320,256]{5,4,1,2,3,0:T(8,128)(2,1)}, u32[]{:S(2)}, u32[]{:S(2)}) collective-permute-start(bf16[1,2,2,2,320,256]{5,4,1,2,3,0:T(8,128)(2,1)} %fusion.48), channel_id=1, source_target_pairs={{0,2},{2,0},{4,6},{6,4},{8,10},{10,8},{12,14},{14,12},{16,18},{18,... | collective-permute-start | bytes 3932168 | tf_op jit(solution)/shard_map/ppermute | solution.py:184
  582.5 50.5 %collective-permute-start.18 = (bf16[1,2,2,2,320,256]{5,4,1,2,3,0:T(8,128)(2,1)}, bf16[1,2,2,2,320,256]{5,4,1,2,3,0:T(8,128)(2,1)}, u32[]{:S(2)}, u32[]{:S(2)}) collective-permute-start(bf16[1,2,2,2,320,256]{5,4,1,2,3,0:T(8,128)(2,1)} %fusion.49), channel_id=1, source_target_pairs={{0,4},{2,6},{4,0},{6,2},{8,12},{10,14},{12,8},{14,10},{16,20},{18,... | collective-permute-start | bytes 3932168 | tf_op jit(solution)/shard_map/ppermute | solution.py:184
  587.2 50.4 %collective-permute-start.20 = (f32[3072,384]{1,0:T(8,128)}, f32[3072,384]{1,0:T(8,128)}, u32[]{:S(2)}, u32[]{:S(2)}) collective-permute-start(f32[3072,384]{1,0:T(8,128)} %fusion.159), channel_id=1, source_target_pairs={{0,1},{1,0},{2,3},{3,2},{4,5},{5,4},{6,7},{7,6},{8,9},{9,8},{10,11... | collective-permute-start | bytes 14155784 | tf_op jit(solution)/shard_map/ppermute | solution.py:101
  600.3 37.3 %collective-permute-start.19 = (bf16[4,2,2,2,48,384]{5,4,3,2,1,0:T(8,128)(2,1)}, bf16[4,2,2,2,48,384]{5,4,3,2,1,0:T(8,128)(2,1)}, u32[]{:S(2)}, u32[]{:S(2)}) collective-permute-start(bf16[4,2,2,2,48,384]{5,4,3,2,1,0:T(8,128)(2,1)} %fusion.50), channel_id=1, source_target_pairs={{0,2},{2,0},{4,6},{6,4},{8,10},{10,8},{12,14},{14,12},{16,18},{18,... | collective-permute-start | bytes 3538952 | tf_op jit(solution)/shard_map/ppermute | solution.py:184
  603.4 34.2 %collective-permute-start.21 = (f32[768,384]{1,0:T(8,128)}, f32[768,384]{1,0:T(8,128)}, u32[]{:S(2)}, u32[]{:S(2)}) collective-permute-start(f32[768,384]{1,0:T(8,128)} %fusion.157), channel_id=1, source_target_pairs={{0,1},{1,0},{2,3},{3,2},{4,5},{5,4},{6,7},{7,6},{8,9},{9,8},{10,11... | collective-permute-start | bytes 3538952 | tf_op jit(solution)/shard_map/ppermute | solution.py:101
  623.9 43.7 %collective-permute-start.22 = (bf16[1,2,2,2,64,1792]{5,4,1,2,3,0:T(8,128)(2,1)}, bf16[1,2,2,2,64,1792]{5,4,1,2,3,0:T(8,128)(2,1)}, u32[]{:S(2)}, u32[]{:S(2)}) collective-permute-start(bf16[1,2,2,2,64,1792]{5,4,1,2,3,0:T(8,128)(2,1)} %concatenate.266), channel_id=1, source_target_pairs={{0,4},{2,6},{4,0},{6,2},{8,12},{10,14},{12,8},{14,10},{16,20},{18,... | collective-permute-start | bytes 5505032 | tf_op jit(solution)/shard_map/ppermute | solution.py:184
  678.1 35.0 %collective-permute-start.26 = (bf16[5,2,2,2,48,384]{5,4,1,2,3,0:T(8,128)(2,1)}, bf16[5,2,2,2,48,384]{5,4,1,2,3,0:T(8,128)(2,1)}, u32[]{:S(2)}, u32[]{:S(2)}) collective-permute-start(bf16[5,2,2,2,48,384]{5,4,1,2,3,0:T(8,128)(2,1)} %pad_maximum_fusion.6), channel_id=1, source_target_pairs={{0,2},{2,0},{4,6},{6,4},{8,10},{10,8},{12,14},{14,12},{16,18},{18,... | collective-permute-start | bytes 4423688 | tf_op jit(solution)/shard_map/ppermute | solution.py:184
  741.6 31.3 %collective-permute-start.33 = (f32[3072,384]{1,0:T(8,128)}, f32[3072,384]{1,0:T(8,128)}, u32[]{:S(2)}, u32[]{:S(2)}) collective-permute-start(f32[3072,384]{1,0:T(8,128)} %fusion.151), channel_id=1, source_target_pairs={{0,1},{1,0},{2,3},{3,2},{4,5},{5,4},{6,7},{7,6},{8,9},{9,8},{10,11... | collective-permute-start | bytes 14155784 | tf_op jit(solution)/shard_map/ppermute | solution.py:101
  770.9 37.1 %collective-permute-start.35 = (bf16[1,2,320,256]{3,2,1,0:T(8,128)(2,1)S(1)}, bf16[1,2,320,256]{3,2,1,0:T(8,128)(2,1)S(1)}, u32[]{:S(2)}, u32[]{:S(2)}) collective-permute-start(bf16[1,2,320,256]{3,2,1,0:T(8,128)(2,1)S(1)} %fusion.167), channel_id=1, source_target_pairs={{0,8},{2,10},{4,12},{6,14},{8,0},{10,2},{12,4},{14,6},{16,24},{18,... | collective-permute-start | bytes 983048 | tf_op jit(solution)/shard_map/ppermute | solution.py:184
  772.8 40.2 %collective-permute-start.36 = (bf16[1,2,320,256]{3,2,1,0:T(8,128)(2,1)}, bf16[1,2,320,256]{3,2,1,0:T(8,128)(2,1)}, u32[]{:S(2)}, u32[]{:S(2)}) collective-permute-start(bf16[1,2,320,256]{3,2,1,0:T(8,128)(2,1)} %fusion.168), channel_id=1, source_target_pairs={{0,8},{2,10},{4,12},{6,14},{8,0},{10,2},{12,4},{14,6},{16,24},{18,... | collective-permute-start | bytes 983048 | tf_op jit(solution)/shard_map/ppermute | solution.py:184
  789.4 35.7 %collective-permute-start.40 = (f32[3072,384]{1,0:T(8,128)}, f32[3072,384]{1,0:T(8,128)}, u32[]{:S(2)}, u32[]{:S(2)}) collective-permute-start(f32[3072,384]{1,0:T(8,128)} %fusion.144), channel_id=1, source_target_pairs={{0,1},{1,0},{2,3},{3,2},{4,5},{5,4},{6,7},{7,6},{8,9},{9,8},{10,11... | collective-permute-start | bytes 14155784 | tf_op jit(solution)/shard_map/ppermute | solution.py:101
  820.5 59.2 %collective-permute-start.42 = (bf16[1,2,64,1792]{3,2,1,0:T(8,128)(2,1)}, bf16[1,2,64,1792]{3,2,1,0:T(8,128)(2,1)}, u32[]{:S(2)}, u32[]{:S(2)}) collective-permute-start(bf16[1,2,64,1792]{3,2,1,0:T(8,128)(2,1)} %concatenate.273), channel_id=1, source_target_pairs={{0,8},{2,10},{4,12},{6,14},{8,0},{10,2},{12,4},{14,6},{16,24},{18,... | collective-permute-start | bytes 1376264 | tf_op jit(solution)/shard_map/ppermute | solution.py:184
  823.9 55.1 %collective-permute-start.44 = (bf16[1,2,2,48,1152]{4,3,1,2,0:T(8,128)(2,1)}, bf16[1,2,2,48,1152]{4,3,1,2,0:T(8,128)(2,1)}, u32[]{:S(2)}, u32[]{:S(2)}) collective-permute-start(bf16[1,2,2,48,1152]{4,3,1,2,0:T(8,128)(2,1)} %fusion.132), channel_id=1, source_target_pairs={{0,4},{2,6},{4,0},{6,2},{8,12},{10,14},{12,8},{14,10},{16,20},{18,... | collective-permute-start | bytes 1327112 | tf_op jit(solution)/shard_map/ppermute | solution.py:184
  828.2 51.6 %collective-permute-start.43 = (f32[4,24,384]{2,1,0:T(8,128)}, f32[4,24,384]{2,1,0:T(8,128)}, u32[]{:S(2)}, u32[]{:S(2)}) collective-permute-start(f32[4,24,384]{2,1,0:T(8,128)} %constant_dynamic-slice_fusion.25), channel_id=1, source_target_pairs={{0,1},{1,0},{2,3},{3,2},{4,5},{5,4},{6,7},{7,6},{8,9},{9,8},{10,11... | collective-permute-start | bytes 442376 | tf_op jit(solution)/shard_map/ppermute | solution.py:101
  828.9 69.8 %collective-permute-start.47 = (bf16[5,48,384]{2,1,0:T(8,128)(2,1)}, bf16[5,48,384]{2,1,0:T(8,128)(2,1)}, u32[]{:S(2)}, u32[]{:S(2)}) collective-permute-start(bf16[5,48,384]{2,1,0:T(8,128)(2,1)} %pad_maximum_fusion.23), channel_id=1, source_target_pairs={{0,16},{2,18},{4,20},{6,22},{8,24},{10,26},{12,28},{14,30},{16,0},... | collective-permute-start | bytes 552968 | tf_op jit(solution)/shard_map/ppermute | solution.py:184
  834.7 64.1 %collective-permute-start.48 = (bf16[4,2,2,48,384]{4,3,0,1,2:T(8,128)(2,1)}, bf16[4,2,2,48,384]{4,3,0,1,2:T(8,128)(2,1)}, u32[]{:S(2)}, u32[]{:S(2)}) collective-permute-start(bf16[4,2,2,48,384]{4,3,0,1,2:T(8,128)(2,1)} %fusion.122), channel_id=1, source_target_pairs={{0,4},{2,6},{4,0},{6,2},{8,12},{10,14},{12,8},{14,10},{16,20},{18,... | collective-permute-start | bytes 1769480 | tf_op jit(solution)/shard_map/ppermute | solution.py:184
  878.9 34.6 %collective-permute-start.49 = (bf16[5,2,2,2,48,384]{5,4,1,2,3,0:T(8,128)(2,1)S(1)}, bf16[5,2,2,2,48,384]{5,4,1,2,3,0:T(8,128)(2,1)}, u32[]{:S(2)}, u32[]{:S(2)}) collective-permute-start(bf16[5,2,2,2,48,384]{5,4,1,2,3,0:T(8,128)(2,1)S(1)} %pad_maximum_fusion.7), channel_id=1, source_target_pairs={{0,2},{2,0},{4,6},{6,4},{8,10},{10,8},{12,14},{14,12},{16,18},{18,... | collective-permute-start | bytes 4423688 | tf_op jit(solution)/shard_map/ppermute | solution.py:184
  892.3 39.0 %collective-permute-start.50 = (bf16[1,320,256]{2,1,0:T(8,128)(2,1)}, bf16[1,320,256]{2,1,0:T(8,128)(2,1)S(1)}, u32[]{:S(2)}, u32[]{:S(2)}) collective-permute-start(bf16[1,320,256]{2,1,0:T(8,128)(2,1)} %fusion.195), channel_id=1, source_target_pairs={{0,16},{2,18},{4,20},{6,22},{8,24},{10,26},{12,28},{14,30},{16,0},... | collective-permute-start | bytes 491528 | tf_op jit(solution)/shard_map/ppermute | solution.py:184
  894.7 37.0 %collective-permute-start.51 = (bf16[1,320,256]{2,1,0:T(8,128)(2,1)}, bf16[1,320,256]{2,1,0:T(8,128)(2,1)S(1)}, u32[]{:S(2)}, u32[]{:S(2)}) collective-permute-start(bf16[1,320,256]{2,1,0:T(8,128)(2,1)} %fusion.196), channel_id=1, source_target_pairs={{0,16},{2,18},{4,20},{6,22},{8,24},{10,26},{12,28},{14,30},{16,0},... | collective-permute-start | bytes 491528 | tf_op jit(solution)/shard_map/ppermute | solution.py:184
  898.7 33.0 %collective-permute-start.53 = (bf16[1,2,48,1152]{3,2,1,0:T(8,128)(2,1)S(1)}, bf16[1,2,48,1152]{3,2,1,0:T(8,128)(2,1)S(1)}, u32[]{:S(2)}, u32[]{:S(2)}) collective-permute-start(bf16[1,2,48,1152]{3,2,1,0:T(8,128)(2,1)S(1)} %fusion.185), channel_id=1, source_target_pairs={{0,8},{2,10},{4,12},{6,14},{8,0},{10,2},{12,4},{14,6},{16,24},{18,... | collective-permute-start | bytes 663560 | tf_op jit(solution)/shard_map/ppermute | solution.py:184
  931.8 35.0 %collective-permute-start.59 = (bf16[5,2,2,48,384]{4,3,1,2,0:T(8,128)(2,1)}, bf16[5,2,2,48,384]{4,3,1,2,0:T(8,128)(2,1)}, u32[]{:S(2)}, u32[]{:S(2)}) collective-permute-start(bf16[5,2,2,48,384]{4,3,1,2,0:T(8,128)(2,1)} %pad_maximum_fusion.10), channel_id=1, source_target_pairs={{0,4},{2,6},{4,0},{6,2},{8,12},{10,14},{12,8},{14,10},{16,20},{18,... | collective-permute-start | bytes 2211848 | tf_op jit(solution)/shard_map/ppermute | solution.py:184
  1217.5 76.0 %all-to-all-start.1 = ((bf16[32,48,1024]{2,1,0:T(8,128)(2,1)}), bf16[32,48,1024]{2,1,0:T(8,128)(2,1)}, u32[]{:S(2)}, u32[]{:S(2)}) async-start(bf16[32,48,1024]{2,1,0:T(8,128)(2,1)} %bitcast.642), calls=%async_computation.1 | async-start | bytes 6291456 | tf_op jit(solution)/shard_map/all_to_all | solution.py:555
  (426 other events, 4941.7 us)
Sparse Core Ops, SparseCore 0:
  11.6 75.1 all-gather.4
  89.7 145.6 all-gather.6
  238.9 122.8 all-gather.8

commit v9 on v8

--- a/solution.py
+++ b/solution.py
@@ -403,7 +403,7 @@
     upper_low = to_low(output_grad)
     flow.begin(
         "upper%d" % depth,
-        weight_task([(copies, hidden_low, [upper_low])], False, 0),
+        weight_task([(copies, hidden_low, [upper_low])], False, 0, (), 2 + depth),
     )
     (hidden_grad,) = gelu_back(product_right(upper_low, expand_low[1]))
     hidden_grad_low = flow.tick(to_low(hidden_grad))
@@ -416,6 +416,8 @@
             [(copies, hidden_grad_low, [normed_two_low]), (1, attended, [projected_low])],
             False,
             0,
+            (),
+            2 + depth,
         ),
     )
     attended_grad = flow.tick(to_low(product_right(projected_low, attend_low[3])))

time: 1330 us -> 1320 us (level)
    unnamed x739 -> x757, local copies, waits for them, and re-layouts: 47.4 us -> 43.3 us
  transfers between devices with their start and end apart: 96 -> 96, of which waited for: 33 -> 34; matrix products, arithmetic and copies ran while one was open for 35% -> 35% of each run, Pallas kernels for 5% -> 5%
where the time goes in v9:
time: 1320 us; the launch traced here: 1310 us
  waiting for transfers between devices  358 us (27%)
  matrix products  326 us (25%)
  other arithmetic  207 us (16%)
  local copies, waits for them, and re-layouts  171 us (13%)
  starting transfers between devices  82 us (6%)
  blocking collectives  75.3 us (6%)
  Pallas kernels  59.5 us (5%)
  between operations  32.6 us (2%)
    all_gather x2, waiting for transfers between devices, gathered(): lax.all_gather(jnp.concatenate(members, axis=0), everywhere, axis=1, tile...  151 us
    dot_general x25, matrix products, product(): return jnp.dot(left_side, right_side, preferred_element_type=jnp.float32)  109 us
    dot_general x29, matrix products, product_left(): lax.dot_general(left_side, right_side, (((0,), (0,)), ((), ())), preferre...  96.1 us
    ppermute x40, waiting for transfers between devices, scatter_task(): arrived, = (yield ([lax.ppermute(joined(sent, axis), 'dp', pairs)], lag))  84.3 us
    ppermute x12, waiting for transfers between devices, sum_all(): lax.ppermute(values, 'dp', [(i, i ^ step) for i in range(count)])  78.5 us
    all_to_all x1, blocking collectives, muon_steps(): lax.all_to_all(owner_buffer([in_parts(modulate, 4)], [in_parts(expand, 2)...  75.3 us
    dot_general x17, matrix products, product_right(): lax.dot_general(left_side, right_side, (((1,), (1,)), ((), ())), preferre...  72.4 us
    pallas_call x2, Pallas kernels, attention_back(): pl.pallas_call(attention_back_kernel, grid=(D // width, queries // chunk)...  59.5 us
  transfers between devices with their start and end apart: 96, of which 34 were waited for; matrix products, arithmetic and copies ran while one was open for 35% of the time, Pallas kernels for 5%

profile of v9, /device:TPU:0, one launch (start us, length us, event | category | flops | bytes accessed | tf_op | source)
XLA Modules:
  0.0 1311.8 jit_solution(4636770982014558116)
XLA Ops:
  19.6 67.1 %all-gather.5.cloned.1.call-done = bf16[6,768,768]{2,1,0:T(8,128)(2,1)} async-done(((bf16[6,24,768]{2,1,0:T(8,128)(2,1)}), bf16[6,768,768]{2,1,0:T(8,128)(2,1)}) %all-gather.5.cloned.1.call-update) | async-done | bytes 7077904 | tf_op jit(solution)/shard_map/all_gather | solution.py:632
  105.7 14.4 %fusion = (f32[12,512]{1,0:T(8,128)S(1)}, f32[12,512,1024]{2,1,0:T(8,128)}) fusion(pred[512,1024]{1,0:T(8,128)(4,1)} %broadcast_compare_fusion, bf16[512,12,64]{0,2,1:T(8,128)(2,1)} %bitcast.638, bf16[1024,12,64]{0,2,1:T(8,128)(2,1)} %bitcast.608), kind=kOutput, calls=%fused_computation.6 | convolution fusion | flops 824174592 | bytes 28073984 | tf_op jit(solution)/shard_map/qhd,khd->hqk/dot_general | solution.py:332
  120.2 13.3 %fusion.2 = f32[12,512]{1,0:T(8,128)S(1)} fusion(f32[12,512,1024]{2,1,0:T(8,128)} %get-tuple-element.398, f32[12,512]{1,0:T(8,128)S(1)} %get-tuple-element.397, pred[512,1024]{1,0:T(8,128)(4,1)S(1)} %copy-done.55), kind=kLoop, calls=%fused_computation.9 | loop fusion | flops 25159680 | bytes 25739264 | tf_op jit(solution)/shard_map/reduce_sum | solution.py:353
  136.4 9.9 fusion.44
  151.1 84.3 %all-gather.7.cloned.1.call-done = bf16[20,768,768]{2,1,0:T(8,128)(2,1)} async-done(((bf16[20,24,768]{2,1,0:T(8,128)(2,1)}), bf16[20,768,768]{2,1,0:T(8,128)(2,1)}) %all-gather.7.cloned.1.call-update) | async-done | bytes 23592976 | tf_op jit(solution)/shard_map/all_gather | solution.py:632
  235.4 11.1 fusion.303
  300.2 14.6 %fusion.1 = (f32[12,512]{1,0:T(8,128)S(1)}, f32[12,512,1024]{2,1,0:T(8,128)}) fusion(pred[512,1024]{1,0:T(8,128)(4,1)} %broadcast_compare_fusion, bf16[512,12,64]{0,2,1:T(8,128)(2,1)} %bitcast.639, bf16[1024,12,64]{0,2,1:T(8,128)(2,1)} %bitcast.609), kind=kOutput, calls=%fused_computation.7 | convolution fusion | flops 824174592 | bytes 28073984 | tf_op jit(solution)/shard_map/qhd,khd->hqk/dot_general | solution.py:332
  314.8 12.5 fusion.3
  330.4 10.0 fusion.43
  354.2 7.6 all-gather.9.cloned.1.call-done
  361.8 10.0 slice.672
  393.8 16.2 %fusion.328 = f32[1024,5120]{0,1:T(8,128)} fusion(bf16[5120,1024]{1,0:T(8,128)(2,1)S(1)} %bitcast.593, bf16[1024,1024]{0,1:T(8,128)(2,1)} %get-tuple-element.407), kind=kOutput, calls=%fused_computation.813 | convolution fusion | flops 10737418240 | bytes 33554432 | tf_op jit(solution)/shard_map/dot_general | solution.py:50
  417.7 7.8 fusion.300
  442.0 9.4 add_multiply_fusion
  477.8 12.5 fusion.95
  496.4 20.4 %fusion.297 = (bf16[1024,1024]{0,1:T(8,128)(2,1)S(1)}, f32[1024,1024]{0,1:T(8,128)}) fusion(f32[1024,1024]{0,1:T(8,128)} %get-tuple-element.408, bf16[512,1024]{0,1:T(8,128)(2,1)} %copy-done.328, bf16[512,1024]{0,1:T(8,128)(2,1)} %copy-done.327, bf16[1024,5120]{0,1:T(8,128)(2,1)} %add_convert_fusion, bf16[5120,1024]{1,0:T(8,128)(2,1)} %bitcast.590), kind=kOutput, calls=%fused_computation.785 | convolution fusion | flops 10753146880 | bytes 33554432 | tf_op jit(solution)/shard_map/dot_general | solution.py:40
  551.9 10.8 add_bitcast_fusion
  567.5 12.4 fusion.19
  637.5 29.7 %shard_map.375 = (bf16[512,768]{1,0:T(8,128)(2,1)S(1)}, f32[1024,768]{1,0:T(8,128)}, f32[1024,768]{1,0:T(8,128)}) custom-call(bf16[512,768]{1,0:T(8,128)(2,1)S(1)} %copy-done.4, bf16[1024,768]{1,0:T(8,128)(2,1)S(1)} %copy-done.1, bf16[1024,768]{1,0:T(8,128)(2,1)S(1)} %copy-done, bf16[512,768]{1,0:T(8,128)(2,1)S(1)} %convolution_convert_fusion.2.grad_ref, ...), custom_call_target="tpu_custom_call" | custom-call | flops 8053063680 | bytes 9437184 | tf_op jit(solution)/shard_map/pallas_call | solution.py:304
  705.8 20.4 %collective-permute-done.27 = bf16[5,2,2,2,48,384]{5,4,1,2,3,0:T(8,128)(2,1)S(1)} collective-permute-done((bf16[5,2,2,2,48,384]{5,4,1,2,3,0:T(8,128)(2,1)S(1)}, bf16[5,2,2,2,48,384]{5,4,1,2,3,0:T(8,128)(2,1)S(1)}, u32[]{:S(2)}, u32[]{:S(2)}) %collective-permute-start.27) | collective-permute-done | bytes 1474592 | tf_op jit(solution)/shard_map/ppermute | solution.py:184
  751.3 9.5 fusion.12
  805.1 7.7 collective-permute-done.36
  813.9 29.9 %shard_map.376 = (bf16[512,768]{1,0:T(8,128)(2,1)S(1)}, f32[1024,768]{1,0:T(8,128)}, f32[1024,768]{1,0:T(8,128)}) custom-call(bf16[512,768]{1,0:T(8,128)(2,1)S(1)} %copy-done.3, bf16[1024,768]{1,0:T(8,128)(2,1)S(1)} %pad_maximum_fusion.1.key_ref, bf16[1024,768]{1,0:T(8,128)(2,1)S(1)} %pad_maximum_fusion.2.value_ref, ...), custom_call_target="tpu_custom_call" | custom-call | flops 8053063680 | bytes 9437184 | tf_op jit(solution)/shard_map/pallas_call | solution.py:304
  888.6 10.3 collective-permute-done.45
  1008.0 9.6 collective-permute-done.74
  1055.3 75.3 %all_to_all.10 = bf16[32,48,1024]{2,1,0:T(8,128)(2,1)S(1)} all-to-all(bf16[32,48,1024]{2,1,0:T(8,128)(2,1)S(1)} %constant_dynamic-update-slice_fusion.4), channel_id=1, replica_groups=mesh['dp'=16,'copy'=2] {'dp','copy'}, dimensions={0} | all-to-all | bytes 6291456 | tf_op jit(solution)/shard_map/all_to_all | solution.py:524
  1150.2 23.7 %collective-permute-done.90 = bf16[1024,512]{1,0:T(8,128)(2,1)S(1)} collective-permute-done((bf16[1024,512]{1,0:T(8,128)(2,1)S(1)}, bf16[1024,512]{1,0:T(8,128)(2,1)S(1)}, u32[]{:S(2)}, u32[]{:S(2)}) %collective-permute-start.90) | collective-permute-done | bytes 1048608 | tf_op jit(solution)/shard_map/ppermute | solution.py:545
  1179.8 9.4 multiply_add_fusion.3
  1199.7 14.4 %multiply_convert_fusion = bf16[1536,1024]{1,0:T(8,128)(2,1)} fusion(bf16[1536,1024]{1,0:T(8,128)(2,1)} %bitcast.645, f32[]{:T(128)S(6)} %div.323, f32[1024,1024]{1,0:T(8,128)} %copy-done.334, f32[1024,1024]{1,0:T(8,128)} %multiply_add_fusion), kind=kOutput, calls=%fused_computation.32 | convolution fusion | flops 5378146304 | bytes 14680068 | tf_op jit(solution)/shard_map/dot_general | solution.py:40
  1222.1 16.8 %collective-permute-done.85 = f32[16]{0:T(128)S(1)} collective-permute-done((f32[16]{0:T(128)S(1)}, f32[16]{0:T(128)S(1)}, u32[]{:S(2)}, u32[]{:S(2)}) %collective-permute-start.85) | collective-permute-done | bytes 96 | tf_op jit(solution)/shard_map/ppermute | solution.py:111
  1243.7 26.1 %collective-permute-done.87 = f32[16]{0:T(128)S(1)} collective-permute-done((f32[16]{0:T(128)S(1)}, f32[16]{0:T(128)S(1)}, u32[]{:S(2)}, u32[]{:S(2)}) %collective-permute-start.87) | collective-permute-done | bytes 96 | tf_op jit(solution)/shard_map/ppermute | solution.py:111
  1274.7 14.7 %collective-permute-done.88 = f32[16]{0:T(128)S(1)} collective-permute-done((f32[16]{0:T(128)S(1)}, f32[16]{0:T(128)S(1)}, u32[]{:S(2)}, u32[]{:S(2)}) %collective-permute-start.88) | collective-permute-done | bytes 96 | tf_op jit(solution)/shard_map/ppermute | solution.py:111
  (1429 shorter events, 637.6 us)
Async XLA Ops:
  7.2 79.6 %all-gather.5.cloned.1.call-start = ((), (), s32[]{:S(2)}) async-start(), calls=%async_computation.2 | async-start | bytes 7299072 | tf_op jit(solution)/shard_map/all_gather | solution.py:632
  10.7 224.8 %all-gather.7.cloned.1.call-start = ((), (), s32[]{:S(2)}) async-start(), calls=%async_computation.3 | async-start | bytes 24330240 | tf_op jit(solution)/shard_map/all_gather | solution.py:632
  11.6 350.2 %all-gather.9.cloned.1.call-start = ((), (), s32[]{:S(2)}) async-start(), calls=%async_computation.4 | async-start | bytes 19464192 | tf_op jit(solution)/shard_map/all_gather | solution.py:637
  261.2 33.4 %collective-permute-start.3 = (bf16[512,768]{1,0:T(8,128)(2,1)}, bf16[512,768]{1,0:T(8,128)(2,1)}, u32[]{:S(2)}, u32[]{:S(2)}) collective-permute-start(bf16[512,768]{1,0:T(8,128)(2,1)} %convolution_convert_fusion.3), channel_id=1, source_target_pairs={{0,1},{1,0},{2,3},{3,2},{4,5},{5,4},{6,7},{7,6},{8,9},{9,8},{10,11... | collective-permute-start | bytes 2359304 | tf_op jit(solution)/shard_map/ppermute | solution.py:101
  490.3 50.7 %collective-permute-start.11 = (f32[5120,512]{1,0:T(8,128)}, f32[5120,512]{1,0:T(8,128)}, u32[]{:S(2)}, u32[]{:S(2)}) collective-permute-start(f32[5120,512]{1,0:T(8,128)} %fusion.95), channel_id=1, source_target_pairs={{0,1},{1,0},{2,3},{3,2},{4,5},{5,4},{6,7},{7,6},{8,9},{9,8},{10,11... | collective-permute-start | bytes 31457288 | tf_op jit(solution)/shard_map/ppermute | solution.py:101
  522.2 61.8 %collective-permute-start.12 = (f32[1024,512]{1,0:T(8,128)}, f32[1024,512]{1,0:T(8,128)}, u32[]{:S(2)}, u32[]{:S(2)}) collective-permute-start(f32[1024,512]{1,0:T(8,128)} %fusion.93), channel_id=1, source_target_pairs={{0,1},{1,0},{2,3},{3,2},{4,5},{5,4},{6,7},{7,6},{8,9},{9,8},{10,11... | collective-permute-start | bytes 6291464 | tf_op jit(solution)/shard_map/ppermute | solution.py:101
  525.3 59.3 %collective-permute-start.13 = (f32[1024,512]{1,0:T(8,128)}, f32[1024,512]{1,0:T(8,128)}, u32[]{:S(2)}, u32[]{:S(2)}) collective-permute-start(f32[1024,512]{1,0:T(8,128)} %fusion.91), channel_id=1, source_target_pairs={{0,1},{1,0},{2,3},{3,2},{4,5},{5,4},{6,7},{7,6},{8,9},{9,8},{10,11... | collective-permute-start | bytes 6291464 | tf_op jit(solution)/shard_map/ppermute | solution.py:101
  530.8 51.7 %collective-permute-start.15 = (f32[1024,192]{0,1:T(8,128)}, f32[1024,192]{0,1:T(8,128)}, u32[]{:S(2)}, u32[]{:S(2)}) collective-permute-start(f32[1024,192]{0,1:T(8,128)} %constant_dynamic-slice_fusion.50), channel_id=1, source_target_pairs={{0,1},{1,0},{2,3},{3,2},{4,5},{5,4},{6,7},{7,6},{8,9},{9,8},{10,11... | collective-permute-start | bytes 2359304 | tf_op jit(solution)/shard_map/ppermute | solution.py:101
  546.0 38.6 %collective-permute-start.14 = (f32[1024,384]{1,0:T(8,128)}, f32[1024,384]{1,0:T(8,128)}, u32[]{:S(2)}, u32[]{:S(2)}) collective-permute-start(f32[1024,384]{1,0:T(8,128)} %fusion.161), channel_id=1, source_target_pairs={{0,1},{1,0},{2,3},{3,2},{4,5},{5,4},{6,7},{7,6},{8,9},{9,8},{10,11... | collective-permute-start | bytes 4718600 | tf_op jit(solution)/shard_map/ppermute | solution.py:101
  551.1 33.5 %collective-permute-start.16 = (f32[3072,384]{1,0:T(8,128)}, f32[3072,384]{1,0:T(8,128)}, u32[]{:S(2)}, u32[]{:S(2)}) collective-permute-start(f32[3072,384]{1,0:T(8,128)} %fusion.159), channel_id=1, source_target_pairs={{0,1},{1,0},{2,3},{3,2},{4,5},{5,4},{6,7},{7,6},{8,9},{9,8},{10,11... | collective-permute-start | bytes 14155784 | tf_op jit(solution)/shard_map/ppermute | solution.py:101
  582.5 50.3 %collective-permute-start.17 = (bf16[1,2,2,2,320,256]{5,4,1,2,3,0:T(8,128)(2,1)}, bf16[1,2,2,2,320,256]{5,4,1,2,3,0:T(8,128)(2,1)}, u32[]{:S(2)}, u32[]{:S(2)}) collective-permute-start(bf16[1,2,2,2,320,256]{5,4,1,2,3,0:T(8,128)(2,1)} %fusion.48), channel_id=1, source_target_pairs={{0,2},{2,0},{4,6},{6,4},{8,10},{10,8},{12,14},{14,12},{16,18},{18,... | collective-permute-start | bytes 3932168 | tf_op jit(solution)/shard_map/ppermute | solution.py:184
  584.0 53.4 %collective-permute-start.18 = (bf16[1,2,2,2,320,256]{5,4,1,2,3,0:T(8,128)(2,1)}, bf16[1,2,2,2,320,256]{5,4,1,2,3,0:T(8,128)(2,1)}, u32[]{:S(2)}, u32[]{:S(2)}) collective-permute-start(bf16[1,2,2,2,320,256]{5,4,1,2,3,0:T(8,128)(2,1)} %fusion.49), channel_id=1, source_target_pairs={{0,4},{2,6},{4,0},{6,2},{8,12},{10,14},{12,8},{14,10},{16,20},{18,... | collective-permute-start | bytes 3932168 | tf_op jit(solution)/shard_map/ppermute | solution.py:184
  588.7 48.7 %collective-permute-start.19 = (f32[3072,384]{1,0:T(8,128)}, f32[3072,384]{1,0:T(8,128)}, u32[]{:S(2)}, u32[]{:S(2)}) collective-permute-start(f32[3072,384]{1,0:T(8,128)} %fusion.157), channel_id=1, source_target_pairs={{0,1},{1,0},{2,3},{3,2},{4,5},{5,4},{6,7},{7,6},{8,9},{9,8},{10,11... | collective-permute-start | bytes 14155784 | tf_op jit(solution)/shard_map/ppermute | solution.py:101
  598.6 38.8 %collective-permute-start.20 = (f32[768,384]{1,0:T(8,128)}, f32[768,384]{1,0:T(8,128)}, u32[]{:S(2)}, u32[]{:S(2)}) collective-permute-start(f32[768,384]{1,0:T(8,128)} %fusion.155), channel_id=1, source_target_pairs={{0,1},{1,0},{2,3},{3,2},{4,5},{5,4},{6,7},{7,6},{8,9},{9,8},{10,11... | collective-permute-start | bytes 3538952 | tf_op jit(solution)/shard_map/ppermute | solution.py:101
  621.3 45.8 %collective-permute-start.21 = (bf16[1,2,2,2,64,1792]{5,4,1,2,3,0:T(8,128)(2,1)}, bf16[1,2,2,2,64,1792]{5,4,1,2,3,0:T(8,128)(2,1)}, u32[]{:S(2)}, u32[]{:S(2)}) collective-permute-start(bf16[1,2,2,2,64,1792]{5,4,1,2,3,0:T(8,128)(2,1)} %concatenate.266), channel_id=1, source_target_pairs={{0,4},{2,6},{4,0},{6,2},{8,12},{10,14},{12,8},{14,10},{16,20},{18,... | collective-permute-start | bytes 5505032 | tf_op jit(solution)/shard_map/ppermute | solution.py:184
  632.8 34.3 %collective-permute-start.22 = (bf16[4,2,2,2,48,384]{5,4,3,2,1,0:T(8,128)(2,1)}, bf16[4,2,2,2,48,384]{5,4,3,2,1,0:T(8,128)(2,1)}, u32[]{:S(2)}, u32[]{:S(2)}) collective-permute-start(bf16[4,2,2,2,48,384]{5,4,3,2,1,0:T(8,128)(2,1)} %fusion.50), channel_id=1, source_target_pairs={{0,2},{2,0},{4,6},{6,4},{8,10},{10,8},{12,14},{14,12},{16,18},{18,... | collective-permute-start | bytes 3538952 | tf_op jit(solution)/shard_map/ppermute | solution.py:184
  672.6 33.2 %collective-permute-start.25 = (bf16[1,2,2,320,256]{4,3,1,2,0:T(8,128)(2,1)S(1)}, bf16[1,2,2,320,256]{4,3,1,2,0:T(8,128)(2,1)S(1)}, u32[]{:S(2)}, u32[]{:S(2)}) collective-permute-start(bf16[1,2,2,320,256]{4,3,1,2,0:T(8,128)(2,1)S(1)} %fusion.112), channel_id=1, source_target_pairs={{0,4},{2,6},{4,0},{6,2},{8,12},{10,14},{12,8},{14,10},{16,20},{18,... | collective-permute-start | bytes 1966088 | tf_op jit(solution)/shard_map/ppermute | solution.py:184
  682.9 43.2 %collective-permute-start.28 = (f32[768,1152]{1,0:T(8,128)S(1)}, f32[768,1152]{1,0:T(8,128)}, u32[]{:S(2)}, u32[]{:S(2)}) collective-permute-start(f32[768,1152]{1,0:T(8,128)S(1)} %fusion.54), channel_id=1, source_target_pairs={{0,1},{1,0},{2,3},{3,2},{4,5},{5,4},{6,7},{7,6},{8,9},{9,8},{10,11... | collective-permute-start | bytes 10616840 | tf_op jit(solution)/shard_map/ppermute | solution.py:101
  691.6 34.6 %collective-permute-start.27 = (bf16[5,2,2,2,48,384]{5,4,1,2,3,0:T(8,128)(2,1)S(1)}, bf16[5,2,2,2,48,384]{5,4,1,2,3,0:T(8,128)(2,1)S(1)}, u32[]{:S(2)}, u32[]{:S(2)}) collective-permute-start(bf16[5,2,2,2,48,384]{5,4,1,2,3,0:T(8,128)(2,1)S(1)} %pad_maximum_fusion.6), channel_id=1, source_target_pairs={{0,2},{2,0},{4,6},{6,4},{8,10},{10,8},{12,14},{14,12},{16,18},{18,... | collective-permute-start | bytes 4423688 | tf_op jit(solution)/shard_map/ppermute | solution.py:184
  730.8 33.0 %collective-permute-start.31 = (f32[3072,384]{1,0:T(8,128)}, f32[3072,384]{1,0:T(8,128)}, u32[]{:S(2)}, u32[]{:S(2)}) collective-permute-start(f32[3072,384]{1,0:T(8,128)} %fusion.147), channel_id=1, source_target_pairs={{0,1},{1,0},{2,3},{3,2},{4,5},{5,4},{6,7},{7,6},{8,9},{9,8},{10,11... | collective-permute-start | bytes 14155784 | tf_op jit(solution)/shard_map/ppermute | solution.py:101
  750.2 42.5 %collective-permute-start.33 = (bf16[1,2,320,256]{3,2,1,0:T(8,128)(2,1)S(1)}, bf16[1,2,320,256]{3,2,1,0:T(8,128)(2,1)}, u32[]{:S(2)}, u32[]{:S(2)}) collective-permute-start(bf16[1,2,320,256]{3,2,1,0:T(8,128)(2,1)S(1)} %fusion.163), channel_id=1, source_target_pairs={{0,8},{2,10},{4,12},{6,14},{8,0},{10,2},{12,4},{14,6},{16,24},{18,... | collective-permute-start | bytes 983048 | tf_op jit(solution)/shard_map/ppermute | solution.py:184
  762.9 40.4 %collective-permute-start.35 = (bf16[5,2,2,48,384]{4,3,1,2,0:T(8,128)(2,1)}, bf16[5,2,2,48,384]{4,3,1,2,0:T(8,128)(2,1)}, u32[]{:S(2)}, u32[]{:S(2)}) collective-permute-start(bf16[5,2,2,48,384]{4,3,1,2,0:T(8,128)(2,1)} %pad_maximum_fusion.9), channel_id=1, source_target_pairs={{0,4},{2,6},{4,0},{6,2},{8,12},{10,14},{12,8},{14,10},{16,20},{18,... | collective-permute-start | bytes 2211848 | tf_op jit(solution)/shard_map/ppermute | solution.py:184
  770.9 43.0 %collective-permute-start.37 = (f32[3072,384]{1,0:T(8,128)}, f32[3072,384]{1,0:T(8,128)}, u32[]{:S(2)}, u32[]{:S(2)}) collective-permute-start(f32[3072,384]{1,0:T(8,128)} %fusion.140), channel_id=1, source_target_pairs={{0,1},{1,0},{2,3},{3,2},{4,5},{5,4},{6,7},{7,6},{8,9},{9,8},{10,11... | collective-permute-start | bytes 14155784 | tf_op jit(solution)/shard_map/ppermute | solution.py:101
  803.0 43.4 %collective-permute-start.39 = (bf16[1,2,64,1792]{3,2,1,0:T(8,128)(2,1)}, bf16[1,2,64,1792]{3,2,1,0:T(8,128)(2,1)S(1)}, u32[]{:S(2)}, u32[]{:S(2)}) collective-permute-start(bf16[1,2,64,1792]{3,2,1,0:T(8,128)(2,1)} %concatenate.272), channel_id=1, source_target_pairs={{0,8},{2,10},{4,12},{6,14},{8,0},{10,2},{12,4},{14,6},{16,24},{18,... | collective-permute-start | bytes 1376264 | tf_op jit(solution)/shard_map/ppermute | solution.py:184
  803.3 43.1 %collective-permute-start.40 = (bf16[4,2,48,384]{3,2,1,0:T(8,128)(2,1)}, bf16[4,2,48,384]{3,2,1,0:T(8,128)(2,1)S(1)}, u32[]{:S(2)}, u32[]{:S(2)}) collective-permute-start(bf16[4,2,48,384]{3,2,1,0:T(8,128)(2,1)} %fusion.165), channel_id=1, source_target_pairs={{0,8},{2,10},{4,12},{6,14},{8,0},{10,2},{12,4},{14,6},{16,24},{18,... | collective-permute-start | bytes 884744 | tf_op jit(solution)/shard_map/ppermute | solution.py:184
  812.8 33.6 %collective-permute-start.41 = (bf16[1,2,2,48,1152]{4,3,1,2,0:T(8,128)(2,1)}, bf16[1,2,2,48,1152]{4,3,1,2,0:T(8,128)(2,1)S(1)}, u32[]{:S(2)}, u32[]{:S(2)}) collective-permute-start(bf16[1,2,2,48,1152]{4,3,1,2,0:T(8,128)(2,1)} %fusion.128), channel_id=1, source_target_pairs={{0,4},{2,6},{4,0},{6,2},{8,12},{10,14},{12,8},{14,10},{16,20},{18,... | collective-permute-start | bytes 1327112 | tf_op jit(solution)/shard_map/ppermute | solution.py:184
  849.4 32.1 %collective-permute-start.42 = (bf16[512,768]{1,0:T(8,128)(2,1)}, bf16[512,768]{1,0:T(8,128)(2,1)}, u32[]{:S(2)}, u32[]{:S(2)}) collective-permute-start(bf16[512,768]{1,0:T(8,128)(2,1)} %slice.1038), channel_id=1, source_target_pairs={{0,1},{1,0},{2,3},{3,2},{4,5},{5,4},{6,7},{7,6},{8,9},{9,8},{10,11... | collective-permute-start | bytes 2359304 | tf_op jit(solution)/shard_map/ppermute | solution.py:101
  851.8 33.2 %collective-permute-start.43 = (bf16[512,768]{1,0:T(8,128)(2,1)}, bf16[512,768]{1,0:T(8,128)(2,1)}, u32[]{:S(2)}, u32[]{:S(2)}) collective-permute-start(bf16[512,768]{1,0:T(8,128)(2,1)} %slice.1037), channel_id=1, source_target_pairs={{0,1},{1,0},{2,3},{3,2},{4,5},{5,4},{6,7},{7,6},{8,9},{9,8},{10,11... | collective-permute-start | bytes 2359304 | tf_op jit(solution)/shard_map/ppermute | solution.py:101
  864.5 34.4 %collective-permute-start.45 = (bf16[5,2,2,2,48,384]{5,4,1,2,3,0:T(8,128)(2,1)}, bf16[5,2,2,2,48,384]{5,4,1,2,3,0:T(8,128)(2,1)}, u32[]{:S(2)}, u32[]{:S(2)}) collective-permute-start(bf16[5,2,2,2,48,384]{5,4,1,2,3,0:T(8,128)(2,1)} %pad_maximum_fusion.7), channel_id=1, source_target_pairs={{0,2},{2,0},{4,6},{6,4},{8,10},{10,8},{12,14},{14,12},{16,18},{18,... | collective-permute-start | bytes 4423688 | tf_op jit(solution)/shard_map/ppermute | solution.py:184
  868.6 45.0 %collective-permute-start.46 = (bf16[1,320,256]{2,1,0:T(8,128)(2,1)}, bf16[1,320,256]{2,1,0:T(8,128)(2,1)}, u32[]{:S(2)}, u32[]{:S(2)}) collective-permute-start(bf16[1,320,256]{2,1,0:T(8,128)(2,1)} %fusion.191), channel_id=1, source_target_pairs={{0,16},{2,18},{4,20},{6,22},{8,24},{10,26},{12,28},{14,30},{16,0},... | collective-permute-start | bytes 491528 | tf_op jit(solution)/shard_map/ppermute | solution.py:184
  881.6 33.5 %collective-permute-start.47 = (bf16[1,320,256]{2,1,0:T(8,128)(2,1)}, bf16[1,320,256]{2,1,0:T(8,128)(2,1)S(1)}, u32[]{:S(2)}, u32[]{:S(2)}) collective-permute-start(bf16[1,320,256]{2,1,0:T(8,128)(2,1)} %fusion.192), channel_id=1, source_target_pairs={{0,16},{2,18},{4,20},{6,22},{8,24},{10,26},{12,28},{14,30},{16,0},... | collective-permute-start | bytes 491528 | tf_op jit(solution)/shard_map/ppermute | solution.py:184
  1214.1 76.1 %all-to-all-start.1 = ((bf16[32,48,1024]{2,1,0:T(8,128)(2,1)}), bf16[32,48,1024]{2,1,0:T(8,128)(2,1)}, u32[]{:S(2)}, u32[]{:S(2)}) async-start(bf16[32,48,1024]{2,1,0:T(8,128)(2,1)} %bitcast.644), calls=%async_computation.1 | async-start | bytes 6291456 | tf_op jit(solution)/shard_map/all_to_all | solution.py:557
  (435 other events, 5367.8 us)
Sparse Core Ops, SparseCore 0:
  11.6 75.1 all-gather.4
  89.7 145.6 all-gather.6
  238.9 122.8 all-gather.8
